TPU v7x, 32 devices: a whole 2x2x4 slice. The times are simulated.
32 devices in a mesh: section: 2 (over y), ep: 16 (over z, x, core).
Axes of the slice: x: 2, y: 2, z: 4, core: 2. Of those that a mesh axis runs over, the one named last changes fastest.
Arguments:
- entering_rising: bfloat16 [8, 128, 3584], P(None, 'ep'), may hold values from -6 to 6
- entering_falling: bfloat16 [8, 128, 3584], P(None, 'ep'), may hold values from -6 to 6
- norm_gain: float32 [2, 3584], P('section'), may hold values from 0.1 to 1.9
- router: bfloat16 [2, 3584, 8], P('section'), may hold values from -0.09375 to 0.09375
- w_gate: bfloat16 [2, 3584, 8192], P('section', None, 'ep'), may hold values from -0.09375 to 0.09375
- w_up: bfloat16 [2, 3584, 8192], P('section', None, 'ep'), may hold values from -0.09375 to 0.09375
- w_down: bfloat16 [2, 8192, 3584], P('section', 'ep'), may hold values from -0.1875 to 0.1875
- routes_rising: int32 [2, 8, 128, 2], P('section', None, 'ep'), may hold values from 0 to 7, all different within a row; in each aligned block of 8 rows (0 to 7, 8 to 15, ..., all dimensions but the last counted through in order) at most 4 rows name the same one
- routes_falling: int32 [2, 8, 128, 2], P('section', None, 'ep'), may hold values from 0 to 7, all different within a row; in each aligned block of 8 rows (0 to 7, 8 to 15, ..., all dimensions but the last counted through in order) at most 4 rows name the same one
Outputs:
- states_rising: bfloat16 [2, 8, 128, 3584], P('section', None, 'ep')
- states_falling: bfloat16 [2, 8, 128, 3584], P('section', None, 'ep')
Inputs may be any that keep to these rules, and one draw needn't show every extreme that they name: `routes_rising`: in each aligned block of 8 tokens (one micro-batch on one device of ep, within one layer) no expert is chosen by more than 4 tokens, a bound that some block reaches; the 2 experts of a token differ. `routes_falling`: in each aligned block of 8 tokens (one micro-batch on one device of ep, within one layer) no expert is chosen by more than 4 tokens, a bound that some block reaches; the 2 experts of a token differ.
All inputs are finite; a program needn't handle non-finite values.
Results may differ from a plain program's by a relative error of at most 0.0081.
Values may be sent and summed in bfloat16 or wider, within the bound.
No kernel may reach another device: no remote copies, remote signals or barrier semaphores. Data moves between devices by JAX's collectives and lax.ppermute only.
A program may use at most 64 MiB of HBM per device.

v0:
```python
import jax
import jax.numpy as jnp
from jax import lax
from jax.sharding import PartitionSpec as P

route_scale = 2.5
epsilon = 1e-06


def shortened(array):
    return jax.tree.map(lambda a: a.astype(jnp.bfloat16) if a.dtype == jnp.float32 else a, array)


def shifted(value, axis, steps):
    count = lax.axis_size(axis)
    initial, last = (max(0, -steps), min(count, count - steps))
    return lax.ppermute(value, axis, [(source, source + steps) for source in range(initial, last)])


def run_expert(flat_rows, gate_w, up_w, down_w):
    gate_act = jnp.dot(flat_rows, gate_w, preferred_element_type=jnp.float32)
    upward = jnp.dot(flat_rows, up_w, preferred_element_type=jnp.float32)
    hidden = (jax.nn.silu(gate_act) * upward).astype(jnp.bfloat16)
    return jnp.dot(hidden, down_w, preferred_element_type=jnp.float32).astype(jnp.bfloat16)


def shards(
    entering_rising,
    entering_falling,
    norm_gain,
    router,
    w_gate,
    w_up,
    w_down,
    routes_rising,
    routes_falling,
):
    n_section = lax.axis_size("section")
    n_ep = lax.axis_size("ep")
    section_index = lax.axis_index("section")
    micro_count, tok_count, features = entering_rising.shape
    experts = router.shape[2]
    sharers = n_ep // experts
    top_count = routes_rising.shape[3]
    capacity = 2 * max(1, tok_count * top_count // experts)
    gain_row = norm_gain[0]
    scorer = router[0]
    gate_w = w_gate[0]
    up_w = w_up[0]
    down_w = w_down[0]
    slots_all = jnp.arange(experts * capacity, dtype=jnp.int32)
    expert_ids = jnp.arange(experts, dtype=jnp.int32)

    def prepare(current, picks):
        widened = current.astype(jnp.float32)
        normed = (
            widened
            * lax.rsqrt(jnp.mean(widened * widened, axis=-1, keepdims=True) + epsilon)
            * gain_row
        ).astype(jnp.bfloat16)
        scores = jax.nn.sigmoid(jnp.dot(normed, scorer, preferred_element_type=jnp.float32))
        onehot = picks[:, :, None] == expert_ids[None, None, :]
        chosen = jnp.sum(jnp.where(onehot, scores[:, None, :], 0.0), axis=2)
        gate_vals = route_scale * chosen / jnp.sum(chosen, axis=1, keepdims=True)
        counts = onehot.reshape(tok_count * top_count, experts).astype(jnp.int32)
        before = jnp.cumsum(counts, axis=0) - counts
        slot_index = jnp.sum(before * counts, axis=1)
        target = picks.reshape(-1) * capacity + slot_index
        placed = (target[:, None] == slots_all[None, :]).reshape(
            tok_count, top_count, experts * capacity
        )
        sender = jnp.any(placed, axis=1).T.astype(jnp.bfloat16)
        outgoing = jnp.dot(sender, normed, preferred_element_type=jnp.float32).astype(jnp.bfloat16)
        mixing = jnp.sum(jnp.where(placed, gate_vals[:, :, None], 0.0), axis=1)
        return (widened, outgoing, mixing)

    def serve_rows(arrived, active):

        def compute(rows_in):
            flat_rows = rows_in.reshape(-1, features)
            return run_expert(flat_rows, gate_w, up_w, down_w).reshape(rows_in.shape)

        def skipped(rows_in):
            return jnp.zeros_like(rows_in)

        return lax.cond(active, compute, skipped, arrived)

    def route_rows(outgoing, actives):
        outbound = tuple(
            (
                jnp.broadcast_to(
                    buffer.reshape(experts, 1, capacity, features),
                    (experts, sharers, capacity, features),
                ).reshape(n_ep, capacity, features)
                for buffer in outgoing
            )
        )
        arrived = (lax.all_to_all(outbound[0], "ep", split_axis=0, concat_axis=0, tiled=True),)
        partials = tuple((serve_rows(rows_in, active) for rows_in, active in zip(arrived, actives)))
        returned = jax.tree.map(
            lambda part, own: part.astype(own.dtype),
            lax.all_to_all(shortened(partials), "ep", split_axis=0, concat_axis=0, tiled=True),
            partials,
        )
        return tuple(
            (
                returned_part.reshape(experts, sharers, capacity, features)
                .astype(jnp.float32)
                .sum(axis=1)
                .reshape(experts * capacity, features)
                for returned_part in returned
            )
        )

    def finish(widened, mixing, totals):
        mixed_rows = jnp.dot(
            mixing, totals, precision=lax.Precision.HIGHEST, preferred_element_type=jnp.float32
        )
        return (widened + mixed_rows).astype(jnp.bfloat16)

    def advance(tick_index, carry):
        held_rising, held_falling, kept_rising, kept_falling = carry
        index_rising = tick_index - section_index
        index_falling = tick_index - (n_section - 1 - section_index)
        live_rising = (index_rising >= 0) & (index_rising < micro_count)
        live_falling = (index_falling >= 0) & (index_falling < micro_count)
        pick_rising = jnp.clip(index_rising, 0, micro_count - 1)
        pick_falling = jnp.clip(index_falling, 0, micro_count - 1)
        start_rising = lax.dynamic_index_in_dim(entering_rising, pick_rising, 0, keepdims=False)
        start_falling = lax.dynamic_index_in_dim(entering_falling, pick_falling, 0, keepdims=False)
        current_rising = jnp.where(section_index == 0, start_rising, held_rising)
        current_falling = jnp.where(section_index == n_section - 1, start_falling, held_falling)
        picks_rising = lax.dynamic_index_in_dim(routes_rising[0], pick_rising, 0, keepdims=False)
        picks_falling = lax.dynamic_index_in_dim(routes_falling[0], pick_falling, 0, keepdims=False)
        wide_rising, out_rising, mix_rising = prepare(current_rising, picks_rising)
        wide_falling, out_falling, mix_falling = prepare(current_falling, picks_falling)
        (totals_rising,) = route_rows((out_rising,), (live_rising,))
        (totals_falling,) = route_rows((out_falling,), (live_falling,))
        next_rising = finish(wide_rising, mix_rising, totals_rising)
        next_falling = finish(wide_falling, mix_falling, totals_falling)
        stored_rising = jnp.where(
            live_rising,
            next_rising,
            lax.dynamic_index_in_dim(kept_rising, pick_rising, 0, keepdims=False),
        )
        stored_falling = jnp.where(
            live_falling,
            next_falling,
            lax.dynamic_index_in_dim(kept_falling, pick_falling, 0, keepdims=False),
        )
        kept_rising = lax.dynamic_update_index_in_dim(kept_rising, stored_rising, pick_rising, 0)
        kept_falling = lax.dynamic_update_index_in_dim(
            kept_falling, stored_falling, pick_falling, 0
        )
        held_rising = shifted(next_rising, "section", 1)
        held_falling = shifted(next_falling, "section", -1)
        return (held_rising, held_falling, kept_rising, kept_falling)

    empty_state = jnp.zeros((tok_count, features), jnp.bfloat16)
    empty_store = jnp.zeros((micro_count, tok_count, features), jnp.bfloat16)
    carry = (empty_state, empty_state, empty_store, empty_store)
    carry = lax.fori_loop(0, micro_count + n_section - 1, advance, carry)
    return (carry[2][None], carry[3][None])


def solution(mesh):
    return jax.shard_map(
        shards,
        mesh=mesh,
        in_specs=(
            P(None, "ep", None),
            P(None, "ep", None),
            P("section", None),
            P("section", None, None),
            P("section", None, "ep"),
            P("section", None, "ep"),
            P("section", "ep", None),
            P("section", None, "ep", None),
            P("section", None, "ep", None),
        ),
        out_specs=(P("section", None, "ep", None), P("section", None, "ep", None)),
        check_vma=False,
    )
```

profile of v0, /device:TPU:0, one launch (start us, length us, event | category | flops | bytes accessed | tf_op | source)
XLA Modules:
  0.0 737.0 jit_solution(773221978236334101)
XLA Ops:
  0.7 735.3 %while.22 = (s32[]{:T(128)}, bf16[8,3584]{1,0:T(8,128)(2,1)S(1)}, bf16[8,3584]{1,0:T(8,128)(2,1)S(1)}, bf16[8,8,3584]{2,1,0:T(8,128)(2,1)S(1)}, bf16[8,8,3584]{2...) while((s32[]{:T(128)}, bf16[8,3584]{1,0:T(8,128)(2,1)S(1)}, ...), condition=%wide.region_21.22_spmd.clone.clone, body=%wide.region_0.21_spmd.clone.clone.sunk | while | flops 1438592000 | bytes 43983104 | solution.py:162
  5.8 7.4 all-to-all-start.2
  17.3 9.1 %all-to-all-done.2 = bf16[16,4,3584]{2,1,0:T(4,128)(2,1)S(1)} async-done(((bf16[16,4,3584]{2,1,0:T(4,128)(2,1)}), bf16[16,4,3584]{2,1,0:T(4,128)(2,1)S(1)}, u32[]{:S(2)}, u32[]{:S(2)}) %all-to-all-start.2) | async-done | bytes 458784 | tf_op jit(solution)/shard_map/while/body/eval_jaxpr/all_to_all | solution.py:98
  33.5 11.0 %all-to-all-done = bf16[16,4,3584]{2,1,0:T(4,128)(2,1)S(1)} async-done(((bf16[16,4,3584]{2,1,0:T(4,128)(2,1)}), bf16[16,4,3584]{2,1,0:T(4,128)(2,1)S(1)}, u32[]{:S(2)}, u32[]{:S(2)}) %all-to-all-start) | async-done | bytes 458784 | tf_op jit(solution)/shard_map/while/body/eval_jaxpr/all_to_all | solution.py:98
  48.7 8.4 %conditional.8 = (bf16[16,4,3584]{2,1,0:T(4,128)(2,1)}) conditional(s32[]{:T(128)} %convert_element_type.248, () %tuple.87, (bf16[16,4,3584]{2,1,0:T(4,128)(2,1)S(1)}, bf16[3584,512]{1,0:T(8,128)(2,1)}, bf16[3584,512]{1,0:T(8,128)(2,1)}, bf16[512,3584]{1,0:T(8,128)(2,1)}) %tuple.88), branch_computations={%region_8.8_spmd, %region_9.9_spmd} | conditional | flops 705069056 | bytes 14483464 | solution.py:86
  51.6 4.6 convolution_convert_fusion
  57.1 4.5 all-to-all-done.3
  67.7 11.1 %all-to-all-done.1 = bf16[16,4,3584]{2,1,0:T(4,128)(2,1)S(1)} async-done(((bf16[16,4,3584]{2,1,0:T(4,128)(2,1)}), bf16[16,4,3584]{2,1,0:T(4,128)(2,1)S(1)}, u32[]{:S(2)}, u32[]{:S(2)}) %all-to-all-start.1) | async-done | bytes 458784 | tf_op jit(solution)/shard_map/while/body/eval_jaxpr/all_to_all | solution.py:102
  97.9 9.1 %all-to-all-done.2 = bf16[16,4,3584]{2,1,0:T(4,128)(2,1)S(1)} async-done(((bf16[16,4,3584]{2,1,0:T(4,128)(2,1)}), bf16[16,4,3584]{2,1,0:T(4,128)(2,1)S(1)}, u32[]{:S(2)}, u32[]{:S(2)}) %all-to-all-start.2) | async-done | bytes 458784 | tf_op jit(solution)/shard_map/while/body/eval_jaxpr/all_to_all | solution.py:98
  113.2 8.4 %conditional.9 = (bf16[16,4,3584]{2,1,0:T(4,128)(2,1)}) conditional(s32[]{:T(128)} %convert_element_type.249, () %tuple.89, (bf16[16,4,3584]{2,1,0:T(4,128)(2,1)S(1)}, bf16[3584,512]{1,0:T(8,128)(2,1)}, bf16[3584,512]{1,0:T(8,128)(2,1)}, bf16[512,3584]{1,0:T(8,128)(2,1)}) %tuple.90), branch_computations={%region_18.18_spmd, %region_19.19_spmd} | conditional | flops 705069056 | bytes 14483464 | solution.py:86
  116.1 4.6 convolution_convert_fusion.1
  129.3 8.4 %conditional.8 = (bf16[16,4,3584]{2,1,0:T(4,128)(2,1)}) conditional(s32[]{:T(128)} %convert_element_type.248, () %tuple.87, (bf16[16,4,3584]{2,1,0:T(4,128)(2,1)S(1)}, bf16[3584,512]{1,0:T(8,128)(2,1)}, bf16[3584,512]{1,0:T(8,128)(2,1)}, bf16[512,3584]{1,0:T(8,128)(2,1)}) %tuple.88), branch_computations={%region_8.8_spmd, %region_9.9_spmd} | conditional | flops 705069056 | bytes 14483464 | solution.py:86
  132.2 4.6 convolution_convert_fusion
  137.7 4.5 all-to-all-done.3
  148.3 11.1 %all-to-all-done.1 = bf16[16,4,3584]{2,1,0:T(4,128)(2,1)S(1)} async-done(((bf16[16,4,3584]{2,1,0:T(4,128)(2,1)}), bf16[16,4,3584]{2,1,0:T(4,128)(2,1)S(1)}, u32[]{:S(2)}, u32[]{:S(2)}) %all-to-all-start.1) | async-done | bytes 458784 | tf_op jit(solution)/shard_map/while/body/eval_jaxpr/all_to_all | solution.py:102
  160.2 4.3 collective-permute-start
  179.3 9.1 %all-to-all-done.2 = bf16[16,4,3584]{2,1,0:T(4,128)(2,1)S(1)} async-done(((bf16[16,4,3584]{2,1,0:T(4,128)(2,1)}), bf16[16,4,3584]{2,1,0:T(4,128)(2,1)S(1)}, u32[]{:S(2)}, u32[]{:S(2)}) %all-to-all-start.2) | async-done | bytes 458784 | tf_op jit(solution)/shard_map/while/body/eval_jaxpr/all_to_all | solution.py:98
  194.6 8.4 %conditional.9 = (bf16[16,4,3584]{2,1,0:T(4,128)(2,1)}) conditional(s32[]{:T(128)} %convert_element_type.249, () %tuple.89, (bf16[16,4,3584]{2,1,0:T(4,128)(2,1)S(1)}, bf16[3584,512]{1,0:T(8,128)(2,1)}, bf16[3584,512]{1,0:T(8,128)(2,1)}, bf16[512,3584]{1,0:T(8,128)(2,1)}) %tuple.90), branch_computations={%region_18.18_spmd, %region_19.19_spmd} | conditional | flops 705069056 | bytes 14483464 | solution.py:86
  197.5 4.6 convolution_convert_fusion.1
  210.7 8.4 %conditional.8 = (bf16[16,4,3584]{2,1,0:T(4,128)(2,1)}) conditional(s32[]{:T(128)} %convert_element_type.248, () %tuple.87, (bf16[16,4,3584]{2,1,0:T(4,128)(2,1)S(1)}, bf16[3584,512]{1,0:T(8,128)(2,1)}, bf16[3584,512]{1,0:T(8,128)(2,1)}, bf16[512,3584]{1,0:T(8,128)(2,1)}) %tuple.88), branch_computations={%region_8.8_spmd, %region_9.9_spmd} | conditional | flops 705069056 | bytes 14483464 | solution.py:86
  213.6 4.6 convolution_convert_fusion
  219.1 4.5 all-to-all-done.3
  229.7 11.1 %all-to-all-done.1 = bf16[16,4,3584]{2,1,0:T(4,128)(2,1)S(1)} async-done(((bf16[16,4,3584]{2,1,0:T(4,128)(2,1)}), bf16[16,4,3584]{2,1,0:T(4,128)(2,1)S(1)}, u32[]{:S(2)}, u32[]{:S(2)}) %all-to-all-start.1) | async-done | bytes 458784 | tf_op jit(solution)/shard_map/while/body/eval_jaxpr/all_to_all | solution.py:102
  241.6 4.3 collective-permute-start
  260.7 9.1 %all-to-all-done.2 = bf16[16,4,3584]{2,1,0:T(4,128)(2,1)S(1)} async-done(((bf16[16,4,3584]{2,1,0:T(4,128)(2,1)}), bf16[16,4,3584]{2,1,0:T(4,128)(2,1)S(1)}, u32[]{:S(2)}, u32[]{:S(2)}) %all-to-all-start.2) | async-done | bytes 458784 | tf_op jit(solution)/shard_map/while/body/eval_jaxpr/all_to_all | solution.py:98
  276.0 8.4 %conditional.9 = (bf16[16,4,3584]{2,1,0:T(4,128)(2,1)}) conditional(s32[]{:T(128)} %convert_element_type.249, () %tuple.89, (bf16[16,4,3584]{2,1,0:T(4,128)(2,1)S(1)}, bf16[3584,512]{1,0:T(8,128)(2,1)}, bf16[3584,512]{1,0:T(8,128)(2,1)}, bf16[512,3584]{1,0:T(8,128)(2,1)}) %tuple.90), branch_computations={%region_18.18_spmd, %region_19.19_spmd} | conditional | flops 705069056 | bytes 14483464 | solution.py:86
  278.9 4.6 convolution_convert_fusion.1
  292.1 8.4 %conditional.8 = (bf16[16,4,3584]{2,1,0:T(4,128)(2,1)}) conditional(s32[]{:T(128)} %convert_element_type.248, () %tuple.87, (bf16[16,4,3584]{2,1,0:T(4,128)(2,1)S(1)}, bf16[3584,512]{1,0:T(8,128)(2,1)}, bf16[3584,512]{1,0:T(8,128)(2,1)}, bf16[512,3584]{1,0:T(8,128)(2,1)}) %tuple.88), branch_computations={%region_8.8_spmd, %region_9.9_spmd} | conditional | flops 705069056 | bytes 14483464 | solution.py:86
  295.0 4.6 convolution_convert_fusion
  300.5 4.5 all-to-all-done.3
  311.1 11.1 %all-to-all-done.1 = bf16[16,4,3584]{2,1,0:T(4,128)(2,1)S(1)} async-done(((bf16[16,4,3584]{2,1,0:T(4,128)(2,1)}), bf16[16,4,3584]{2,1,0:T(4,128)(2,1)S(1)}, u32[]{:S(2)}, u32[]{:S(2)}) %all-to-all-start.1) | async-done | bytes 458784 | tf_op jit(solution)/shard_map/while/body/eval_jaxpr/all_to_all | solution.py:102
  342.1 9.1 %all-to-all-done.2 = bf16[16,4,3584]{2,1,0:T(4,128)(2,1)S(1)} async-done(((bf16[16,4,3584]{2,1,0:T(4,128)(2,1)}), bf16[16,4,3584]{2,1,0:T(4,128)(2,1)S(1)}, u32[]{:S(2)}, u32[]{:S(2)}) %all-to-all-start.2) | async-done | bytes 458784 | tf_op jit(solution)/shard_map/while/body/eval_jaxpr/all_to_all | solution.py:98
  357.4 8.4 %conditional.9 = (bf16[16,4,3584]{2,1,0:T(4,128)(2,1)}) conditional(s32[]{:T(128)} %convert_element_type.249, () %tuple.89, (bf16[16,4,3584]{2,1,0:T(4,128)(2,1)S(1)}, bf16[3584,512]{1,0:T(8,128)(2,1)}, bf16[3584,512]{1,0:T(8,128)(2,1)}, bf16[512,3584]{1,0:T(8,128)(2,1)}) %tuple.90), branch_computations={%region_18.18_spmd, %region_19.19_spmd} | conditional | flops 705069056 | bytes 14483464 | solution.py:86
  360.3 4.6 convolution_convert_fusion.1
  373.5 8.4 %conditional.8 = (bf16[16,4,3584]{2,1,0:T(4,128)(2,1)}) conditional(s32[]{:T(128)} %convert_element_type.248, () %tuple.87, (bf16[16,4,3584]{2,1,0:T(4,128)(2,1)S(1)}, bf16[3584,512]{1,0:T(8,128)(2,1)}, bf16[3584,512]{1,0:T(8,128)(2,1)}, bf16[512,3584]{1,0:T(8,128)(2,1)}) %tuple.88), branch_computations={%region_8.8_spmd, %region_9.9_spmd} | conditional | flops 705069056 | bytes 14483464 | solution.py:86
  376.4 4.6 convolution_convert_fusion
  381.9 4.5 all-to-all-done.3
  392.5 11.1 %all-to-all-done.1 = bf16[16,4,3584]{2,1,0:T(4,128)(2,1)S(1)} async-done(((bf16[16,4,3584]{2,1,0:T(4,128)(2,1)}), bf16[16,4,3584]{2,1,0:T(4,128)(2,1)S(1)}, u32[]{:S(2)}, u32[]{:S(2)}) %all-to-all-start.1) | async-done | bytes 458784 | tf_op jit(solution)/shard_map/while/body/eval_jaxpr/all_to_all | solution.py:102
  423.5 9.1 %all-to-all-done.2 = bf16[16,4,3584]{2,1,0:T(4,128)(2,1)S(1)} async-done(((bf16[16,4,3584]{2,1,0:T(4,128)(2,1)}), bf16[16,4,3584]{2,1,0:T(4,128)(2,1)S(1)}, u32[]{:S(2)}, u32[]{:S(2)}) %all-to-all-start.2) | async-done | bytes 458784 | tf_op jit(solution)/shard_map/while/body/eval_jaxpr/all_to_all | solution.py:98
  438.8 8.4 %conditional.9 = (bf16[16,4,3584]{2,1,0:T(4,128)(2,1)}) conditional(s32[]{:T(128)} %convert_element_type.249, () %tuple.89, (bf16[16,4,3584]{2,1,0:T(4,128)(2,1)S(1)}, bf16[3584,512]{1,0:T(8,128)(2,1)}, bf16[3584,512]{1,0:T(8,128)(2,1)}, bf16[512,3584]{1,0:T(8,128)(2,1)}) %tuple.90), branch_computations={%region_18.18_spmd, %region_19.19_spmd} | conditional | flops 705069056 | bytes 14483464 | solution.py:86
  441.7 4.6 convolution_convert_fusion.1
  454.9 8.4 %conditional.8 = (bf16[16,4,3584]{2,1,0:T(4,128)(2,1)}) conditional(s32[]{:T(128)} %convert_element_type.248, () %tuple.87, (bf16[16,4,3584]{2,1,0:T(4,128)(2,1)S(1)}, bf16[3584,512]{1,0:T(8,128)(2,1)}, bf16[3584,512]{1,0:T(8,128)(2,1)}, bf16[512,3584]{1,0:T(8,128)(2,1)}) %tuple.88), branch_computations={%region_8.8_spmd, %region_9.9_spmd} | conditional | flops 705069056 | bytes 14483464 | solution.py:86
  457.8 4.6 convolution_convert_fusion
  463.3 4.5 all-to-all-done.3
  473.9 11.1 %all-to-all-done.1 = bf16[16,4,3584]{2,1,0:T(4,128)(2,1)S(1)} async-done(((bf16[16,4,3584]{2,1,0:T(4,128)(2,1)}), bf16[16,4,3584]{2,1,0:T(4,128)(2,1)S(1)}, u32[]{:S(2)}, u32[]{:S(2)}) %all-to-all-start.1) | async-done | bytes 458784 | tf_op jit(solution)/shard_map/while/body/eval_jaxpr/all_to_all | solution.py:102
  504.9 9.1 %all-to-all-done.2 = bf16[16,4,3584]{2,1,0:T(4,128)(2,1)S(1)} async-done(((bf16[16,4,3584]{2,1,0:T(4,128)(2,1)}), bf16[16,4,3584]{2,1,0:T(4,128)(2,1)S(1)}, u32[]{:S(2)}, u32[]{:S(2)}) %all-to-all-start.2) | async-done | bytes 458784 | tf_op jit(solution)/shard_map/while/body/eval_jaxpr/all_to_all | solution.py:98
  520.2 8.4 %conditional.9 = (bf16[16,4,3584]{2,1,0:T(4,128)(2,1)}) conditional(s32[]{:T(128)} %convert_element_type.249, () %tuple.89, (bf16[16,4,3584]{2,1,0:T(4,128)(2,1)S(1)}, bf16[3584,512]{1,0:T(8,128)(2,1)}, bf16[3584,512]{1,0:T(8,128)(2,1)}, bf16[512,3584]{1,0:T(8,128)(2,1)}) %tuple.90), branch_computations={%region_18.18_spmd, %region_19.19_spmd} | conditional | flops 705069056 | bytes 14483464 | solution.py:86
  523.1 4.6 convolution_convert_fusion.1
  536.3 8.4 %conditional.8 = (bf16[16,4,3584]{2,1,0:T(4,128)(2,1)}) conditional(s32[]{:T(128)} %convert_element_type.248, () %tuple.87, (bf16[16,4,3584]{2,1,0:T(4,128)(2,1)S(1)}, bf16[3584,512]{1,0:T(8,128)(2,1)}, bf16[3584,512]{1,0:T(8,128)(2,1)}, bf16[512,3584]{1,0:T(8,128)(2,1)}) %tuple.88), branch_computations={%region_8.8_spmd, %region_9.9_spmd} | conditional | flops 705069056 | bytes 14483464 | solution.py:86
  539.2 4.6 convolution_convert_fusion
  544.7 4.5 all-to-all-done.3
  555.3 11.1 %all-to-all-done.1 = bf16[16,4,3584]{2,1,0:T(4,128)(2,1)S(1)} async-done(((bf16[16,4,3584]{2,1,0:T(4,128)(2,1)}), bf16[16,4,3584]{2,1,0:T(4,128)(2,1)S(1)}, u32[]{:S(2)}, u32[]{:S(2)}) %all-to-all-start.1) | async-done | bytes 458784 | tf_op jit(solution)/shard_map/while/body/eval_jaxpr/all_to_all | solution.py:102
  586.3 9.1 %all-to-all-done.2 = bf16[16,4,3584]{2,1,0:T(4,128)(2,1)S(1)} async-done(((bf16[16,4,3584]{2,1,0:T(4,128)(2,1)}), bf16[16,4,3584]{2,1,0:T(4,128)(2,1)S(1)}, u32[]{:S(2)}, u32[]{:S(2)}) %all-to-all-start.2) | async-done | bytes 458784 | tf_op jit(solution)/shard_map/while/body/eval_jaxpr/all_to_all | solution.py:98
  601.6 8.4 %conditional.9 = (bf16[16,4,3584]{2,1,0:T(4,128)(2,1)}) conditional(s32[]{:T(128)} %convert_element_type.249, () %tuple.89, (bf16[16,4,3584]{2,1,0:T(4,128)(2,1)S(1)}, bf16[3584,512]{1,0:T(8,128)(2,1)}, bf16[3584,512]{1,0:T(8,128)(2,1)}, bf16[512,3584]{1,0:T(8,128)(2,1)}) %tuple.90), branch_computations={%region_18.18_spmd, %region_19.19_spmd} | conditional | flops 705069056 | bytes 14483464 | solution.py:86
  604.5 4.6 convolution_convert_fusion.1
  617.7 8.4 %conditional.8 = (bf16[16,4,3584]{2,1,0:T(4,128)(2,1)}) conditional(s32[]{:T(128)} %convert_element_type.248, () %tuple.87, (bf16[16,4,3584]{2,1,0:T(4,128)(2,1)S(1)}, bf16[3584,512]{1,0:T(8,128)(2,1)}, bf16[3584,512]{1,0:T(8,128)(2,1)}, bf16[512,3584]{1,0:T(8,128)(2,1)}) %tuple.88), branch_computations={%region_8.8_spmd, %region_9.9_spmd} | conditional | flops 705069056 | bytes 14483464 | solution.py:86
  620.6 4.6 convolution_convert_fusion
  626.1 4.5 all-to-all-done.3
  636.7 11.1 %all-to-all-done.1 = bf16[16,4,3584]{2,1,0:T(4,128)(2,1)S(1)} async-done(((bf16[16,4,3584]{2,1,0:T(4,128)(2,1)}), bf16[16,4,3584]{2,1,0:T(4,128)(2,1)S(1)}, u32[]{:S(2)}, u32[]{:S(2)}) %all-to-all-start.1) | async-done | bytes 458784 | tf_op jit(solution)/shard_map/while/body/eval_jaxpr/all_to_all | solution.py:102
  667.7 9.1 %all-to-all-done.2 = bf16[16,4,3584]{2,1,0:T(4,128)(2,1)S(1)} async-done(((bf16[16,4,3584]{2,1,0:T(4,128)(2,1)}), bf16[16,4,3584]{2,1,0:T(4,128)(2,1)S(1)}, u32[]{:S(2)}, u32[]{:S(2)}) %all-to-all-start.2) | async-done | bytes 458784 | tf_op jit(solution)/shard_map/while/body/eval_jaxpr/all_to_all | solution.py:98
  683.0 8.4 %conditional.9 = (bf16[16,4,3584]{2,1,0:T(4,128)(2,1)}) conditional(s32[]{:T(128)} %convert_element_type.249, () %tuple.89, (bf16[16,4,3584]{2,1,0:T(4,128)(2,1)S(1)}, bf16[3584,512]{1,0:T(8,128)(2,1)}, bf16[3584,512]{1,0:T(8,128)(2,1)}, bf16[512,3584]{1,0:T(8,128)(2,1)}) %tuple.90), branch_computations={%region_18.18_spmd, %region_19.19_spmd} | conditional | flops 705069056 | bytes 14483464 | solution.py:86
  685.9 4.6 convolution_convert_fusion.1
  700.0 12.0 %all-to-all-done.3 = bf16[16,4,3584]{2,1,0:T(4,128)(2,1)S(1)} async-done(((bf16[16,4,3584]{2,1,0:T(4,128)(2,1)}), bf16[16,4,3584]{2,1,0:T(4,128)(2,1)S(1)}, u32[]{:S(2)}, u32[]{:S(2)}) %all-to-all-start.3) | async-done | bytes 458784 | tf_op jit(solution)/shard_map/while/body/eval_jaxpr/all_to_all | solution.py:102
  718.1 11.1 %all-to-all-done.1 = bf16[16,4,3584]{2,1,0:T(4,128)(2,1)S(1)} async-done(((bf16[16,4,3584]{2,1,0:T(4,128)(2,1)}), bf16[16,4,3584]{2,1,0:T(4,128)(2,1)S(1)}, u32[]{:S(2)}, u32[]{:S(2)}) %all-to-all-start.1) | async-done | bytes 458784 | tf_op jit(solution)/shard_map/while/body/eval_jaxpr/all_to_all | solution.py:102
  (596 shorter events, 404.9 us)
Async XLA Ops:
  0.8 31.2 %copy-start.2 = (bf16[3584,8]{0,1:T(8,128)(2,1)S(1)}, bf16[3584,8]{0,1:T(8,128)(2,1)}, u32[]{:S(2)}) copy-start(bf16[3584,8]{0,1:T(8,128)(2,1)} %get-tuple-element.789) | copy-start | bytes 172036 | tf_op jit(solution)/shard_map/while
  5.8 20.6 %all-to-all-start.2 = ((bf16[16,4,3584]{2,1,0:T(4,128)(2,1)}), bf16[16,4,3584]{2,1,0:T(4,128)(2,1)S(1)}, u32[]{:S(2)}, u32[]{:S(2)}) async-start(bf16[16,4,3584]{2,1,0:T(4,128)(2,1)} %bitcast.99), calls=%async_computation.2 | async-start | bytes 917504 | tf_op jit(solution)/shard_map/while/body/eval_jaxpr/all_to_all | solution.py:98
  27.3 17.2 %all-to-all-start = ((bf16[16,4,3584]{2,1,0:T(4,128)(2,1)}), bf16[16,4,3584]{2,1,0:T(4,128)(2,1)S(1)}, u32[]{:S(2)}, u32[]{:S(2)}) async-start(bf16[16,4,3584]{2,1,0:T(4,128)(2,1)} %bitcast.98), calls=%async_computation | async-start | bytes 917504 | tf_op jit(solution)/shard_map/while/body/eval_jaxpr/all_to_all | solution.py:98
  44.5 17.2 %all-to-all-start.3 = ((bf16[16,4,3584]{2,1,0:T(4,128)(2,1)}), bf16[16,4,3584]{2,1,0:T(4,128)(2,1)S(1)}, u32[]{:S(2)}, u32[]{:S(2)}) async-start(bf16[16,4,3584]{2,1,0:T(4,128)(2,1)} %get-tuple-element.803), calls=%async_computation.3 | async-start | bytes 917504 | tf_op jit(solution)/shard_map/while/body/eval_jaxpr/all_to_all | solution.py:102
  61.6 17.2 %all-to-all-start.1 = ((bf16[16,4,3584]{2,1,0:T(4,128)(2,1)}), bf16[16,4,3584]{2,1,0:T(4,128)(2,1)S(1)}, u32[]{:S(2)}, u32[]{:S(2)}) async-start(bf16[16,4,3584]{2,1,0:T(4,128)(2,1)} %get-tuple-element.802), calls=%async_computation.1 | async-start | bytes 917504 | tf_op jit(solution)/shard_map/while/body/eval_jaxpr/all_to_all | solution.py:102
  66.4 16.6 %collective-permute-start.1 = (bf16[8,3584]{1,0:T(8,128)(2,1)S(1)}, bf16[8,3584]{1,0:T(8,128)(2,1)S(1)}, u32[]{:S(2)}, u32[]{:S(2)}) collective-permute-start(bf16[8,3584]{1,0:T(8,128)(2,1)S(1)} %get-tuple-element.730), channel_id=1, source_target_pairs={{16,0},{17,1},{18,2},{19,3},{20,4},{21,5},{22,6},{23,7},{24,8},{25... | collective-permute-start | bytes 172040 | tf_op jit(solution)/shard_map/while/body/eval_jaxpr/ppermute | solution.py:17
  79.6 5.2 collective-permute-start
  84.8 27.7 %copy-start.2 = (bf16[3584,8]{0,1:T(8,128)(2,1)S(1)}, bf16[3584,8]{0,1:T(8,128)(2,1)}, u32[]{:S(2)}) copy-start(bf16[3584,8]{0,1:T(8,128)(2,1)} %get-tuple-element.789) | copy-start | bytes 172036 | tf_op jit(solution)/shard_map/while
  89.9 17.2 %all-to-all-start.2 = ((bf16[16,4,3584]{2,1,0:T(4,128)(2,1)}), bf16[16,4,3584]{2,1,0:T(4,128)(2,1)S(1)}, u32[]{:S(2)}, u32[]{:S(2)}) async-start(bf16[16,4,3584]{2,1,0:T(4,128)(2,1)} %bitcast.99), calls=%async_computation.2 | async-start | bytes 917504 | tf_op jit(solution)/shard_map/while/body/eval_jaxpr/all_to_all | solution.py:98
  107.9 17.2 %all-to-all-start = ((bf16[16,4,3584]{2,1,0:T(4,128)(2,1)}), bf16[16,4,3584]{2,1,0:T(4,128)(2,1)S(1)}, u32[]{:S(2)}, u32[]{:S(2)}) async-start(bf16[16,4,3584]{2,1,0:T(4,128)(2,1)} %bitcast.98), calls=%async_computation | async-start | bytes 917504 | tf_op jit(solution)/shard_map/while/body/eval_jaxpr/all_to_all | solution.py:98
  125.1 17.2 %all-to-all-start.3 = ((bf16[16,4,3584]{2,1,0:T(4,128)(2,1)}), bf16[16,4,3584]{2,1,0:T(4,128)(2,1)S(1)}, u32[]{:S(2)}, u32[]{:S(2)}) async-start(bf16[16,4,3584]{2,1,0:T(4,128)(2,1)} %get-tuple-element.803), calls=%async_computation.3 | async-start | bytes 917504 | tf_op jit(solution)/shard_map/while/body/eval_jaxpr/all_to_all | solution.py:102
  142.2 17.2 %all-to-all-start.1 = ((bf16[16,4,3584]{2,1,0:T(4,128)(2,1)}), bf16[16,4,3584]{2,1,0:T(4,128)(2,1)S(1)}, u32[]{:S(2)}, u32[]{:S(2)}) async-start(bf16[16,4,3584]{2,1,0:T(4,128)(2,1)} %get-tuple-element.802), calls=%async_computation.1 | async-start | bytes 917504 | tf_op jit(solution)/shard_map/while/body/eval_jaxpr/all_to_all | solution.py:102
  147.0 17.4 %collective-permute-start.1 = (bf16[8,3584]{1,0:T(8,128)(2,1)S(1)}, bf16[8,3584]{1,0:T(8,128)(2,1)S(1)}, u32[]{:S(2)}, u32[]{:S(2)}) collective-permute-start(bf16[8,3584]{1,0:T(8,128)(2,1)S(1)} %get-tuple-element.730), channel_id=1, source_target_pairs={{16,0},{17,1},{18,2},{19,3},{20,4},{21,5},{22,6},{23,7},{24,8},{25... | collective-permute-start | bytes 172040 | tf_op jit(solution)/shard_map/while/body/eval_jaxpr/ppermute | solution.py:17
  160.2 6.1 collective-permute-start
  166.2 27.7 %copy-start.2 = (bf16[3584,8]{0,1:T(8,128)(2,1)S(1)}, bf16[3584,8]{0,1:T(8,128)(2,1)}, u32[]{:S(2)}) copy-start(bf16[3584,8]{0,1:T(8,128)(2,1)} %get-tuple-element.789) | copy-start | bytes 172036 | tf_op jit(solution)/shard_map/while
  171.3 17.2 %all-to-all-start.2 = ((bf16[16,4,3584]{2,1,0:T(4,128)(2,1)}), bf16[16,4,3584]{2,1,0:T(4,128)(2,1)S(1)}, u32[]{:S(2)}, u32[]{:S(2)}) async-start(bf16[16,4,3584]{2,1,0:T(4,128)(2,1)} %bitcast.99), calls=%async_computation.2 | async-start | bytes 917504 | tf_op jit(solution)/shard_map/while/body/eval_jaxpr/all_to_all | solution.py:98
  189.3 17.2 %all-to-all-start = ((bf16[16,4,3584]{2,1,0:T(4,128)(2,1)}), bf16[16,4,3584]{2,1,0:T(4,128)(2,1)S(1)}, u32[]{:S(2)}, u32[]{:S(2)}) async-start(bf16[16,4,3584]{2,1,0:T(4,128)(2,1)} %bitcast.98), calls=%async_computation | async-start | bytes 917504 | tf_op jit(solution)/shard_map/while/body/eval_jaxpr/all_to_all | solution.py:98
  206.5 17.2 %all-to-all-start.3 = ((bf16[16,4,3584]{2,1,0:T(4,128)(2,1)}), bf16[16,4,3584]{2,1,0:T(4,128)(2,1)S(1)}, u32[]{:S(2)}, u32[]{:S(2)}) async-start(bf16[16,4,3584]{2,1,0:T(4,128)(2,1)} %get-tuple-element.803), calls=%async_computation.3 | async-start | bytes 917504 | tf_op jit(solution)/shard_map/while/body/eval_jaxpr/all_to_all | solution.py:102
  223.6 17.2 %all-to-all-start.1 = ((bf16[16,4,3584]{2,1,0:T(4,128)(2,1)}), bf16[16,4,3584]{2,1,0:T(4,128)(2,1)S(1)}, u32[]{:S(2)}, u32[]{:S(2)}) async-start(bf16[16,4,3584]{2,1,0:T(4,128)(2,1)} %get-tuple-element.802), calls=%async_computation.1 | async-start | bytes 917504 | tf_op jit(solution)/shard_map/while/body/eval_jaxpr/all_to_all | solution.py:102
  228.4 17.4 %collective-permute-start.1 = (bf16[8,3584]{1,0:T(8,128)(2,1)S(1)}, bf16[8,3584]{1,0:T(8,128)(2,1)S(1)}, u32[]{:S(2)}, u32[]{:S(2)}) collective-permute-start(bf16[8,3584]{1,0:T(8,128)(2,1)S(1)} %get-tuple-element.730), channel_id=1, source_target_pairs={{16,0},{17,1},{18,2},{19,3},{20,4},{21,5},{22,6},{23,7},{24,8},{25... | collective-permute-start | bytes 172040 | tf_op jit(solution)/shard_map/while/body/eval_jaxpr/ppermute | solution.py:17
  241.6 6.1 collective-permute-start
  247.6 27.7 %copy-start.2 = (bf16[3584,8]{0,1:T(8,128)(2,1)S(1)}, bf16[3584,8]{0,1:T(8,128)(2,1)}, u32[]{:S(2)}) copy-start(bf16[3584,8]{0,1:T(8,128)(2,1)} %get-tuple-element.789) | copy-start | bytes 172036 | tf_op jit(solution)/shard_map/while
  252.7 17.2 %all-to-all-start.2 = ((bf16[16,4,3584]{2,1,0:T(4,128)(2,1)}), bf16[16,4,3584]{2,1,0:T(4,128)(2,1)S(1)}, u32[]{:S(2)}, u32[]{:S(2)}) async-start(bf16[16,4,3584]{2,1,0:T(4,128)(2,1)} %bitcast.99), calls=%async_computation.2 | async-start | bytes 917504 | tf_op jit(solution)/shard_map/while/body/eval_jaxpr/all_to_all | solution.py:98
  270.7 17.2 %all-to-all-start = ((bf16[16,4,3584]{2,1,0:T(4,128)(2,1)}), bf16[16,4,3584]{2,1,0:T(4,128)(2,1)S(1)}, u32[]{:S(2)}, u32[]{:S(2)}) async-start(bf16[16,4,3584]{2,1,0:T(4,128)(2,1)} %bitcast.98), calls=%async_computation | async-start | bytes 917504 | tf_op jit(solution)/shard_map/while/body/eval_jaxpr/all_to_all | solution.py:98
  287.9 17.2 %all-to-all-start.3 = ((bf16[16,4,3584]{2,1,0:T(4,128)(2,1)}), bf16[16,4,3584]{2,1,0:T(4,128)(2,1)S(1)}, u32[]{:S(2)}, u32[]{:S(2)}) async-start(bf16[16,4,3584]{2,1,0:T(4,128)(2,1)} %get-tuple-element.803), calls=%async_computation.3 | async-start | bytes 917504 | tf_op jit(solution)/shard_map/while/body/eval_jaxpr/all_to_all | solution.py:102
  305.0 17.2 %all-to-all-start.1 = ((bf16[16,4,3584]{2,1,0:T(4,128)(2,1)}), bf16[16,4,3584]{2,1,0:T(4,128)(2,1)S(1)}, u32[]{:S(2)}, u32[]{:S(2)}) async-start(bf16[16,4,3584]{2,1,0:T(4,128)(2,1)} %get-tuple-element.802), calls=%async_computation.1 | async-start | bytes 917504 | tf_op jit(solution)/shard_map/while/body/eval_jaxpr/all_to_all | solution.py:102
  309.8 17.4 %collective-permute-start.1 = (bf16[8,3584]{1,0:T(8,128)(2,1)S(1)}, bf16[8,3584]{1,0:T(8,128)(2,1)S(1)}, u32[]{:S(2)}, u32[]{:S(2)}) collective-permute-start(bf16[8,3584]{1,0:T(8,128)(2,1)S(1)} %get-tuple-element.730), channel_id=1, source_target_pairs={{16,0},{17,1},{18,2},{19,3},{20,4},{21,5},{22,6},{23,7},{24,8},{25... | collective-permute-start | bytes 172040 | tf_op jit(solution)/shard_map/while/body/eval_jaxpr/ppermute | solution.py:17
  323.0 6.1 collective-permute-start
  329.0 27.7 %copy-start.2 = (bf16[3584,8]{0,1:T(8,128)(2,1)S(1)}, bf16[3584,8]{0,1:T(8,128)(2,1)}, u32[]{:S(2)}) copy-start(bf16[3584,8]{0,1:T(8,128)(2,1)} %get-tuple-element.789) | copy-start | bytes 172036 | tf_op jit(solution)/shard_map/while
  334.1 17.2 %all-to-all-start.2 = ((bf16[16,4,3584]{2,1,0:T(4,128)(2,1)}), bf16[16,4,3584]{2,1,0:T(4,128)(2,1)S(1)}, u32[]{:S(2)}, u32[]{:S(2)}) async-start(bf16[16,4,3584]{2,1,0:T(4,128)(2,1)} %bitcast.99), calls=%async_computation.2 | async-start | bytes 917504 | tf_op jit(solution)/shard_map/while/body/eval_jaxpr/all_to_all | solution.py:98
  352.1 17.2 %all-to-all-start = ((bf16[16,4,3584]{2,1,0:T(4,128)(2,1)}), bf16[16,4,3584]{2,1,0:T(4,128)(2,1)S(1)}, u32[]{:S(2)}, u32[]{:S(2)}) async-start(bf16[16,4,3584]{2,1,0:T(4,128)(2,1)} %bitcast.98), calls=%async_computation | async-start | bytes 917504 | tf_op jit(solution)/shard_map/while/body/eval_jaxpr/all_to_all | solution.py:98
  369.3 17.2 %all-to-all-start.3 = ((bf16[16,4,3584]{2,1,0:T(4,128)(2,1)}), bf16[16,4,3584]{2,1,0:T(4,128)(2,1)S(1)}, u32[]{:S(2)}, u32[]{:S(2)}) async-start(bf16[16,4,3584]{2,1,0:T(4,128)(2,1)} %get-tuple-element.803), calls=%async_computation.3 | async-start | bytes 917504 | tf_op jit(solution)/shard_map/while/body/eval_jaxpr/all_to_all | solution.py:102
  386.4 17.2 %all-to-all-start.1 = ((bf16[16,4,3584]{2,1,0:T(4,128)(2,1)}), bf16[16,4,3584]{2,1,0:T(4,128)(2,1)S(1)}, u32[]{:S(2)}, u32[]{:S(2)}) async-start(bf16[16,4,3584]{2,1,0:T(4,128)(2,1)} %get-tuple-element.802), calls=%async_computation.1 | async-start | bytes 917504 | tf_op jit(solution)/shard_map/while/body/eval_jaxpr/all_to_all | solution.py:102
  391.2 17.4 %collective-permute-start.1 = (bf16[8,3584]{1,0:T(8,128)(2,1)S(1)}, bf16[8,3584]{1,0:T(8,128)(2,1)S(1)}, u32[]{:S(2)}, u32[]{:S(2)}) collective-permute-start(bf16[8,3584]{1,0:T(8,128)(2,1)S(1)} %get-tuple-element.730), channel_id=1, source_target_pairs={{16,0},{17,1},{18,2},{19,3},{20,4},{21,5},{22,6},{23,7},{24,8},{25... | collective-permute-start | bytes 172040 | tf_op jit(solution)/shard_map/while/body/eval_jaxpr/ppermute | solution.py:17
  404.4 6.1 collective-permute-start
  410.4 27.7 %copy-start.2 = (bf16[3584,8]{0,1:T(8,128)(2,1)S(1)}, bf16[3584,8]{0,1:T(8,128)(2,1)}, u32[]{:S(2)}) copy-start(bf16[3584,8]{0,1:T(8,128)(2,1)} %get-tuple-element.789) | copy-start | bytes 172036 | tf_op jit(solution)/shard_map/while
  415.5 17.2 %all-to-all-start.2 = ((bf16[16,4,3584]{2,1,0:T(4,128)(2,1)}), bf16[16,4,3584]{2,1,0:T(4,128)(2,1)S(1)}, u32[]{:S(2)}, u32[]{:S(2)}) async-start(bf16[16,4,3584]{2,1,0:T(4,128)(2,1)} %bitcast.99), calls=%async_computation.2 | async-start | bytes 917504 | tf_op jit(solution)/shard_map/while/body/eval_jaxpr/all_to_all | solution.py:98
  433.5 17.2 %all-to-all-start = ((bf16[16,4,3584]{2,1,0:T(4,128)(2,1)}), bf16[16,4,3584]{2,1,0:T(4,128)(2,1)S(1)}, u32[]{:S(2)}, u32[]{:S(2)}) async-start(bf16[16,4,3584]{2,1,0:T(4,128)(2,1)} %bitcast.98), calls=%async_computation | async-start | bytes 917504 | tf_op jit(solution)/shard_map/while/body/eval_jaxpr/all_to_all | solution.py:98
  450.7 17.2 %all-to-all-start.3 = ((bf16[16,4,3584]{2,1,0:T(4,128)(2,1)}), bf16[16,4,3584]{2,1,0:T(4,128)(2,1)S(1)}, u32[]{:S(2)}, u32[]{:S(2)}) async-start(bf16[16,4,3584]{2,1,0:T(4,128)(2,1)} %get-tuple-element.803), calls=%async_computation.3 | async-start | bytes 917504 | tf_op jit(solution)/shard_map/while/body/eval_jaxpr/all_to_all | solution.py:102
  467.8 17.2 %all-to-all-start.1 = ((bf16[16,4,3584]{2,1,0:T(4,128)(2,1)}), bf16[16,4,3584]{2,1,0:T(4,128)(2,1)S(1)}, u32[]{:S(2)}, u32[]{:S(2)}) async-start(bf16[16,4,3584]{2,1,0:T(4,128)(2,1)} %get-tuple-element.802), calls=%async_computation.1 | async-start | bytes 917504 | tf_op jit(solution)/shard_map/while/body/eval_jaxpr/all_to_all | solution.py:102
  472.6 17.4 %collective-permute-start.1 = (bf16[8,3584]{1,0:T(8,128)(2,1)S(1)}, bf16[8,3584]{1,0:T(8,128)(2,1)S(1)}, u32[]{:S(2)}, u32[]{:S(2)}) collective-permute-start(bf16[8,3584]{1,0:T(8,128)(2,1)S(1)} %get-tuple-element.730), channel_id=1, source_target_pairs={{16,0},{17,1},{18,2},{19,3},{20,4},{21,5},{22,6},{23,7},{24,8},{25... | collective-permute-start | bytes 172040 | tf_op jit(solution)/shard_map/while/body/eval_jaxpr/ppermute | solution.py:17
  485.8 6.1 collective-permute-start
  491.9 27.7 %copy-start.2 = (bf16[3584,8]{0,1:T(8,128)(2,1)S(1)}, bf16[3584,8]{0,1:T(8,128)(2,1)}, u32[]{:S(2)}) copy-start(bf16[3584,8]{0,1:T(8,128)(2,1)} %get-tuple-element.789) | copy-start | bytes 172036 | tf_op jit(solution)/shard_map/while
  496.9 17.2 %all-to-all-start.2 = ((bf16[16,4,3584]{2,1,0:T(4,128)(2,1)}), bf16[16,4,3584]{2,1,0:T(4,128)(2,1)S(1)}, u32[]{:S(2)}, u32[]{:S(2)}) async-start(bf16[16,4,3584]{2,1,0:T(4,128)(2,1)} %bitcast.99), calls=%async_computation.2 | async-start | bytes 917504 | tf_op jit(solution)/shard_map/while/body/eval_jaxpr/all_to_all | solution.py:98
  514.9 17.2 %all-to-all-start = ((bf16[16,4,3584]{2,1,0:T(4,128)(2,1)}), bf16[16,4,3584]{2,1,0:T(4,128)(2,1)S(1)}, u32[]{:S(2)}, u32[]{:S(2)}) async-start(bf16[16,4,3584]{2,1,0:T(4,128)(2,1)} %bitcast.98), calls=%async_computation | async-start | bytes 917504 | tf_op jit(solution)/shard_map/while/body/eval_jaxpr/all_to_all | solution.py:98
  532.1 17.2 %all-to-all-start.3 = ((bf16[16,4,3584]{2,1,0:T(4,128)(2,1)}), bf16[16,4,3584]{2,1,0:T(4,128)(2,1)S(1)}, u32[]{:S(2)}, u32[]{:S(2)}) async-start(bf16[16,4,3584]{2,1,0:T(4,128)(2,1)} %get-tuple-element.803), calls=%async_computation.3 | async-start | bytes 917504 | tf_op jit(solution)/shard_map/while/body/eval_jaxpr/all_to_all | solution.py:102
  549.3 17.2 %all-to-all-start.1 = ((bf16[16,4,3584]{2,1,0:T(4,128)(2,1)}), bf16[16,4,3584]{2,1,0:T(4,128)(2,1)S(1)}, u32[]{:S(2)}, u32[]{:S(2)}) async-start(bf16[16,4,3584]{2,1,0:T(4,128)(2,1)} %get-tuple-element.802), calls=%async_computation.1 | async-start | bytes 917504 | tf_op jit(solution)/shard_map/while/body/eval_jaxpr/all_to_all | solution.py:102
  554.0 17.4 %collective-permute-start.1 = (bf16[8,3584]{1,0:T(8,128)(2,1)S(1)}, bf16[8,3584]{1,0:T(8,128)(2,1)S(1)}, u32[]{:S(2)}, u32[]{:S(2)}) collective-permute-start(bf16[8,3584]{1,0:T(8,128)(2,1)S(1)} %get-tuple-element.730), channel_id=1, source_target_pairs={{16,0},{17,1},{18,2},{19,3},{20,4},{21,5},{22,6},{23,7},{24,8},{25... | collective-permute-start | bytes 172040 | tf_op jit(solution)/shard_map/while/body/eval_jaxpr/ppermute | solution.py:17
  567.2 6.1 collective-permute-start
  573.3 27.7 %copy-start.2 = (bf16[3584,8]{0,1:T(8,128)(2,1)S(1)}, bf16[3584,8]{0,1:T(8,128)(2,1)}, u32[]{:S(2)}) copy-start(bf16[3584,8]{0,1:T(8,128)(2,1)} %get-tuple-element.789) | copy-start | bytes 172036 | tf_op jit(solution)/shard_map/while
  578.3 17.2 %all-to-all-start.2 = ((bf16[16,4,3584]{2,1,0:T(4,128)(2,1)}), bf16[16,4,3584]{2,1,0:T(4,128)(2,1)S(1)}, u32[]{:S(2)}, u32[]{:S(2)}) async-start(bf16[16,4,3584]{2,1,0:T(4,128)(2,1)} %bitcast.99), calls=%async_computation.2 | async-start | bytes 917504 | tf_op jit(solution)/shard_map/while/body/eval_jaxpr/all_to_all | solution.py:98
  596.4 17.2 %all-to-all-start = ((bf16[16,4,3584]{2,1,0:T(4,128)(2,1)}), bf16[16,4,3584]{2,1,0:T(4,128)(2,1)S(1)}, u32[]{:S(2)}, u32[]{:S(2)}) async-start(bf16[16,4,3584]{2,1,0:T(4,128)(2,1)} %bitcast.98), calls=%async_computation | async-start | bytes 917504 | tf_op jit(solution)/shard_map/while/body/eval_jaxpr/all_to_all | solution.py:98
  613.5 17.2 %all-to-all-start.3 = ((bf16[16,4,3584]{2,1,0:T(4,128)(2,1)}), bf16[16,4,3584]{2,1,0:T(4,128)(2,1)S(1)}, u32[]{:S(2)}, u32[]{:S(2)}) async-start(bf16[16,4,3584]{2,1,0:T(4,128)(2,1)} %get-tuple-element.803), calls=%async_computation.3 | async-start | bytes 917504 | tf_op jit(solution)/shard_map/while/body/eval_jaxpr/all_to_all | solution.py:102
  630.7 17.2 %all-to-all-start.1 = ((bf16[16,4,3584]{2,1,0:T(4,128)(2,1)}), bf16[16,4,3584]{2,1,0:T(4,128)(2,1)S(1)}, u32[]{:S(2)}, u32[]{:S(2)}) async-start(bf16[16,4,3584]{2,1,0:T(4,128)(2,1)} %get-tuple-element.802), calls=%async_computation.1 | async-start | bytes 917504 | tf_op jit(solution)/shard_map/while/body/eval_jaxpr/all_to_all | solution.py:102
  635.4 17.4 %collective-permute-start.1 = (bf16[8,3584]{1,0:T(8,128)(2,1)S(1)}, bf16[8,3584]{1,0:T(8,128)(2,1)S(1)}, u32[]{:S(2)}, u32[]{:S(2)}) collective-permute-start(bf16[8,3584]{1,0:T(8,128)(2,1)S(1)} %get-tuple-element.730), channel_id=1, source_target_pairs={{16,0},{17,1},{18,2},{19,3},{20,4},{21,5},{22,6},{23,7},{24,8},{25... | collective-permute-start | bytes 172040 | tf_op jit(solution)/shard_map/while/body/eval_jaxpr/ppermute | solution.py:17
  648.6 6.1 collective-permute-start
  654.7 27.7 %copy-start.2 = (bf16[3584,8]{0,1:T(8,128)(2,1)S(1)}, bf16[3584,8]{0,1:T(8,128)(2,1)}, u32[]{:S(2)}) copy-start(bf16[3584,8]{0,1:T(8,128)(2,1)} %get-tuple-element.789) | copy-start | bytes 172036 | tf_op jit(solution)/shard_map/while
  659.7 17.2 %all-to-all-start.2 = ((bf16[16,4,3584]{2,1,0:T(4,128)(2,1)}), bf16[16,4,3584]{2,1,0:T(4,128)(2,1)S(1)}, u32[]{:S(2)}, u32[]{:S(2)}) async-start(bf16[16,4,3584]{2,1,0:T(4,128)(2,1)} %bitcast.99), calls=%async_computation.2 | async-start | bytes 917504 | tf_op jit(solution)/shard_map/while/body/eval_jaxpr/all_to_all | solution.py:98
  677.8 17.2 %all-to-all-start = ((bf16[16,4,3584]{2,1,0:T(4,128)(2,1)}), bf16[16,4,3584]{2,1,0:T(4,128)(2,1)S(1)}, u32[]{:S(2)}, u32[]{:S(2)}) async-start(bf16[16,4,3584]{2,1,0:T(4,128)(2,1)} %bitcast.98), calls=%async_computation | async-start | bytes 917504 | tf_op jit(solution)/shard_map/while/body/eval_jaxpr/all_to_all | solution.py:98
  694.9 17.2 %all-to-all-start.3 = ((bf16[16,4,3584]{2,1,0:T(4,128)(2,1)}), bf16[16,4,3584]{2,1,0:T(4,128)(2,1)S(1)}, u32[]{:S(2)}, u32[]{:S(2)}) async-start(bf16[16,4,3584]{2,1,0:T(4,128)(2,1)} %get-tuple-element.803), calls=%async_computation.3 | async-start | bytes 917504 | tf_op jit(solution)/shard_map/while/body/eval_jaxpr/all_to_all | solution.py:102
  712.1 17.2 %all-to-all-start.1 = ((bf16[16,4,3584]{2,1,0:T(4,128)(2,1)}), bf16[16,4,3584]{2,1,0:T(4,128)(2,1)S(1)}, u32[]{:S(2)}, u32[]{:S(2)}) async-start(bf16[16,4,3584]{2,1,0:T(4,128)(2,1)} %get-tuple-element.802), calls=%async_computation.1 | async-start | bytes 917504 | tf_op jit(solution)/shard_map/while/body/eval_jaxpr/all_to_all | solution.py:102
  716.8 17.4 %collective-permute-start.1 = (bf16[8,3584]{1,0:T(8,128)(2,1)S(1)}, bf16[8,3584]{1,0:T(8,128)(2,1)S(1)}, u32[]{:S(2)}, u32[]{:S(2)}) collective-permute-start(bf16[8,3584]{1,0:T(8,128)(2,1)S(1)} %get-tuple-element.730), channel_id=1, source_target_pairs={{16,0},{17,1},{18,2},{19,3},{20,4},{21,5},{22,6},{23,7},{24,8},{25... | collective-permute-start | bytes 172040 | tf_op jit(solution)/shard_map/while/body/eval_jaxpr/ppermute | solution.py:17
  730.0 6.1 collective-permute-start
  736.1 0.9 copy-start.1
  (1 other events, 0.8 us)
where the time goes:
time: 744 us; the launch traced here: 737 us
  waiting for transfers between devices  285 us (38%)
  starting transfers between devices  193 us (26%)
  matrix products  133 us (18%)
  local copies, waits for them, and re-layouts  69.4 us (9%)
  other arithmetic  53.3 us (7%)
    all_to_all x18, waiting for transfers between devices, route_rows(): lax.all_to_all(shortened(partials), 'ep', split_axis=0, concat_axis=0, ti...  148 us
    all_to_all x18, waiting for transfers between devices, route_rows(): lax.all_to_all(outbound[0], 'ep', split_axis=0, concat_axis=0, tiled=True)  121 us
    dot_general x16, matrix products, run_expert(): jnp.dot(hidden, down_w, preferred_element_type=jnp.float32)  73.8 us
    all_to_all x18, starting transfers between devices, route_rows(): lax.all_to_all(outbound[0], 'ep', split_axis=0, concat_axis=0, tiled=True)  73.6 us
    all_to_all x18, starting transfers between devices, route_rows(): lax.all_to_all(shortened(partials), 'ep', split_axis=0, concat_axis=0, ti...  70.1 us
    ppermute x18, starting transfers between devices, shifted(): lax.ppermute(value, axis, [(source, source + steps) for source in range(i...  49.1 us
    dot_general x16, matrix products, run_expert(): gate_act = jnp.dot(flat_rows, gate_w, preferred_element_type=jnp.float32)  44.4 us
    reduce_sum x18, other arithmetic, prepare(): jnp.mean(widened * widened, axis=-1, keepdims=True) + epsilon  17.4 us
  transfers between devices with their start and end apart: 54, of which 45 were waited for; matrix products, arithmetic and copies ran while one was open for 27% of the time, Pallas kernels for 0%

commit v1 on v0

v1 whole, which is shorter than its diff:
```python
import jax
import jax.numpy as jnp
from jax import lax
from jax.sharding import PartitionSpec as P

route_scale = 2.5
epsilon = 1e-06
CHUNKS = 1


def flipped(value, axis, mask):
    count = lax.axis_size(axis)
    return lax.ppermute(value, axis, [(i, i ^ mask) for i in range(count)])


def shards(
    entering_rising,
    entering_falling,
    norm_gain,
    router,
    w_gate,
    w_up,
    w_down,
    routes_rising,
    routes_falling,
):
    n_section = lax.axis_size("section")
    n_ep = lax.axis_size("ep")
    section_index = lax.axis_index("section")
    ep_index = lax.axis_index("ep")
    micro_count, tok_count, features = entering_rising.shape
    experts = router.shape[2]
    top_count = routes_rising.shape[3]
    sharers = n_ep // experts
    capacity = 2 * max(1, tok_count * top_count // experts)
    half = n_ep // 2
    chips = half // sharers
    my_half = ep_index // half
    my_chip = (ep_index % half) // sharers
    gain_row = norm_gain[0]
    scorer = router[0]
    gate_w = w_gate[0]
    up_w = w_up[0]
    down_w = w_down[0]
    expert_ids = jnp.arange(experts, dtype=jnp.int32)

    group = micro_count // CHUNKS
    tokens = group * tok_count
    room = group * capacity
    slots = jnp.arange(chips * room, dtype=jnp.int32)

    def columns(picks):
        flat = picks.reshape(picks.shape[:-2] + (tok_count * top_count,))
        same = flat[..., :, None] == flat[..., None, :]
        earlier = jnp.tril(jnp.ones((tok_count * top_count,) * 2, bool), -1)
        place = jnp.sum((same & earlier).astype(jnp.int32), axis=-1)
        local = flat - my_half * chips
        inside = (local >= 0) & (local < chips)
        turn = jnp.arange(micro_count, dtype=jnp.int32)[:, None] % group
        column = (local ^ my_chip) * room + turn * capacity + place
        return jnp.where(inside, column, -1).reshape(picks.shape)

    def normalise(current):
        widened = current.astype(jnp.float32)
        normed = (
            widened
            * lax.rsqrt(jnp.mean(widened * widened, axis=-1, keepdims=True) + epsilon)
            * gain_row
        ).astype(jnp.bfloat16)
        return widened, normed

    def pack(normed, column):
        sender = jnp.any(column[:, :, None] == slots, axis=1).astype(jnp.bfloat16)
        rows = lax.dot_general(
            sender, normed, (((0,), (0,)), ((), ())), preferred_element_type=jnp.float32
        )
        return rows.astype(jnp.bfloat16).reshape(chips, room, features)

    def gates(normed, picks, column):
        scores = jax.nn.sigmoid(jnp.dot(normed, scorer, preferred_element_type=jnp.float32))
        onehot = picks[:, :, None] == expert_ids
        chosen = jnp.sum(jnp.where(onehot, scores[:, None, :], 0.0), axis=2)
        gate_vals = route_scale * chosen / jnp.sum(chosen, axis=1, keepdims=True)
        mixing = jnp.sum(
            jnp.where(column[:, :, None] == slots, gate_vals[:, :, None], 0.0), axis=1
        )
        high = lax.reduce_precision(mixing, 8, 7)
        return jnp.concatenate([high, mixing - high], axis=1).astype(jnp.bfloat16)

    def spread(rows):
        return [rows[0]] + [
            flipped(rows[k], "ep", sharers * k) for k in range(1, chips)
        ]

    def experts_of(blocks):
        mine = jnp.concatenate(blocks, axis=0)
        other = flipped(mine, "ep", 1)
        rows = jnp.concatenate([mine, other], axis=0)
        gate_act = jnp.dot(rows, gate_w, preferred_element_type=jnp.float32)
        upward = jnp.dot(rows, up_w, preferred_element_type=jnp.float32)
        hidden = (jax.nn.silu(gate_act) * upward).astype(jnp.bfloat16)
        part = jnp.dot(hidden, down_w, preferred_element_type=jnp.float32).astype(jnp.bfloat16)
        count = mine.shape[0]
        returned = flipped(part[count:], "ep", 1)
        total = (part[:count].astype(jnp.float32) + returned.astype(jnp.float32)).astype(
            jnp.bfloat16
        )
        return total.reshape(chips, room, features)

    def mix(mixing, blocks):
        rows = jnp.concatenate(blocks, axis=0)
        return jnp.dot(
            mixing, jnp.concatenate([rows, rows], axis=0), preferred_element_type=jnp.float32
        )

    def layer(current, picks, column, far_picks, far_column):
        widened, normed = normalise(current)
        far_normed = flipped(normed, "ep", half)
        near_in = spread(pack(normed, column))
        near_out = experts_of(near_in)
        far_in = spread(pack(far_normed, far_column))
        far_out = experts_of(far_in)
        far_part = mix(gates(far_normed, far_picks, far_column), spread(far_out))
        beyond = flipped(far_part.astype(jnp.bfloat16), "ep", half)
        near_part = mix(gates(normed, picks, column), spread(near_out))
        return (widened + (near_part + beyond.astype(jnp.float32))).astype(jnp.bfloat16)

    ticks = jnp.arange(n_section, dtype=jnp.int32)[:, None, None, None]
    picks = jnp.where(section_index == ticks, routes_rising, routes_falling)
    far_picks = flipped(picks, "ep", half)
    column = columns(picks)
    far_column = columns(far_picks)

    shape = (CHUNKS, tokens, features)
    tables = [a.reshape(n_section, CHUNKS, tokens, top_count) for a in (picks, column, far_picks, far_column)]

    def advance(tick, carry, moved):
        current, kept_rising, kept_falling = carry
        rising, falling = section_index == tick, section_index == n_section - 1 - tick
        here = [lax.dynamic_index_in_dim(a, tick, 0, keepdims=False) for a in tables]
        done = [layer(current[c], *[a[c] for a in here]) for c in range(CHUNKS)]
        kept_rising = [jnp.where(rising, d, k) for d, k in zip(done, kept_rising)]
        kept_falling = [jnp.where(falling, d, k) for d, k in zip(done, kept_falling)]
        return [moved(d, rising) for d in done], kept_rising, kept_falling

    def swapped(done, rising):
        return flipped(done, "section", 1)

    entered = jnp.where(section_index == 0, entering_rising, entering_falling).reshape(shape)
    empty = [jnp.zeros((tokens, features), jnp.bfloat16)] * CHUNKS
    carry = ([entered[c] for c in range(CHUNKS)], empty, empty)
    if n_section == 2:
        carry = advance(0, carry, swapped)
        carry = advance(1, carry, lambda done, rising: done)
    else:

        def body(tick, carry):
            def shifted(done, rising):
                up = lax.ppermute(done, "section", [(i, i + 1) for i in range(n_section - 1)])
                down = lax.ppermute(done, "section", [(i + 1, i) for i in range(n_section - 1)])
                return jnp.where(section_index == tick + 1, up, down)

            return advance(tick, carry, shifted)

        carry = lax.fori_loop(0, n_section, body, carry)
    _, kept_rising, kept_falling = carry
    out = (1, micro_count, tok_count, features)
    return (
        jnp.concatenate(kept_rising, axis=0).reshape(out),
        jnp.concatenate(kept_falling, axis=0).reshape(out),
    )


def solution(mesh):
    return jax.shard_map(
        shards,
        mesh=mesh,
        in_specs=(
            P(None, "ep", None),
            P(None, "ep", None),
            P("section", None),
            P("section", None, None),
            P("section", None, "ep"),
            P("section", None, "ep"),
            P("section", "ep", None),
            P("section", None, "ep", None),
            P("section", None, "ep", None),
        ),
        out_specs=(P("section", None, "ep", None), P("section", None, "ep", None)),
        check_vma=False,
    )
```

time: 744 us -> 261 us (0.35)
  waiting for transfers between devices: 285 us -> 138 us
  starting transfers between devices: 193 us -> 46.1 us
  matrix products: 133 us -> 45.3 us
  local copies, waits for them, and re-layouts: 69.4 us -> 22.2 us
  other arithmetic: 53.3 us -> 7.53 us
    all_to_all x36 -> x0, waiting for transfers between devices: 269 us -> none  [the longest x18 148 us: route_rows(): lax.all_to_all(shortened(partials), 'ep', split_axis=0, concat_axis=0, ti...]
    all_to_all x36 -> x0, starting transfers between devices: 144 us -> none  [the longest x18 73.6 us: route_rows(): lax.all_to_all(outbound[0], 'ep', split_axis=0, concat_axis=0, tiled=True)]
    ppermute x18 -> x38, waiting for transfers between devices: 16.2 us -> 138 us  [flipped(): return lax.ppermute(value, axis, [(i, i ^ mask) for i in range(count)])]
    dot_general x86 -> x20, matrix products: 133 us -> 45.3 us  [the longest x4 26.7 us: experts_of(): jnp.dot(hidden, down_w, preferred_element_type=jnp.float32)]
    reshape x68 -> x0, local copies, waits for them, and re-layouts: 31.1 us -> none  [the longest x16 14 us: compute(): return run_expert(flat_rows, gate_w, up_w, down_w).reshape(rows_in.shape)]
    reduce_sum x90 -> x11, other arithmetic: 30.4 us -> 2.72 us  [the longest x2 1.45 us: normalise(): jnp.mean(widened * widened, axis=-1, keepdims=True) + epsilon]
    broadcast_in_dim x40 -> x5, local copies, waits for them, and re-layouts: 17.1 us -> 1.12 us  [shards(): picks = jnp.where(section_index == ticks, routes_rising, routes_falling)]
    add x18 -> x1, other arithmetic: 12.5 us -> 0.01 us  [columns(): earlier = jnp.tril(jnp.ones((tok_count * top_count,) * 2, bool), -1)]
  transfers between devices with their start and end apart: 54 -> 38, of which waited for: 45 -> 18; matrix products, arithmetic and copies ran while one was open for 27% -> 23% of each run, Pallas kernels for 0% -> 0%
where the time goes in v1:
time: 261 us
  waiting for transfers between devices  138 us (53%)
  starting transfers between devices  46.1 us (18%)
  matrix products  45.3 us (17%)
  local copies, waits for them, and re-layouts  22.2 us (9%)
  other arithmetic  7.53 us (3%)
    ppermute x38, waiting for transfers between devices, flipped(): return lax.ppermute(value, axis, [(i, i ^ mask) for i in range(count)])  138 us
    ppermute x38, starting transfers between devices, flipped(): return lax.ppermute(value, axis, [(i, i ^ mask) for i in range(count)])  46.1 us
    dot_general x4, matrix products, experts_of(): jnp.dot(hidden, down_w, preferred_element_type=jnp.float32)  26.7 us
    dot_general x4, matrix products, experts_of(): upward = jnp.dot(rows, up_w, preferred_element_type=jnp.float32)  13 us
    unnamed x88, local copies, waits for them, and re-layouts  9.87 us
  transfers between devices with their start and end apart: 38, of which 18 were waited for; matrix products, arithmetic and copies ran while one was open for 23% of the time, Pallas kernels for 0%

profile of v1, /device:TPU:0, one launch (start us, length us, event | category | flops | bytes accessed | tf_op | source)
XLA Modules:
  0.0 260.6 jit_solution(4565354473219410001)
XLA Ops:
  0.7 0.7 copy_bitcast_fusion
  1.5 4.0 %collective-permute-start.8 = (s32[2,8,8,2]{2,1,3,0:T(8,128)S(1)}, s32[2,8,8,2]{2,1,3,0:T(8,128)S(1)}, u32[]{:S(2)}, u32[]{:S(2)}) collective-permute-start(s32[2,8,8,2]{2,1,3,0:T(8,128)S(1)} %broadcast_select_fusion.2), channel_id=1, source_target_pairs={{0,8},{1,9},{2,10},{3,11},{4,12},{5,13},{6,14},{7,15},{8,0},{9,1},... | collective-permute-start | bytes 3080 | tf_op jit(solution)/shard_map/ppermute | solution.py:13
  5.5 1.3 fusion.42
  6.9 0.8 reduce.5
  9.7 0.7 convert_reduce_fusion
  12.9 0.8 fusion.111
  13.6 2.8 %collective-permute-start.2 = (bf16[32,3584]{1,0:T(8,128)(2,1)S(1)}, bf16[32,3584]{1,0:T(8,128)(2,1)S(1)}, u32[]{:S(2)}, u32[]{:S(2)}) collective-permute-start(bf16[32,3584]{1,0:T(8,128)(2,1)S(1)} %get-tuple-element.51), channel_id=1, source_target_pairs={{0,6},{1,7},{2,4},{3,5},{4,2},{5,3},{6,0},{7,1},{8,14},{9,15},{10,... | collective-permute-start | bytes 688136 | tf_op jit(solution)/shard_map/ppermute | solution.py:13
  17.9 13.9 %collective-permute-done.2 = bf16[32,3584]{1,0:T(8,128)(2,1)S(1)} collective-permute-done((bf16[32,3584]{1,0:T(8,128)(2,1)S(1)}, bf16[32,3584]{1,0:T(8,128)(2,1)S(1)}, u32[]{:S(2)}, u32[]{:S(2)}) %collective-permute-start.2) | collective-permute-done | bytes 229408 | tf_op jit(solution)/shard_map/ppermute | solution.py:13
  31.8 3.5 %collective-permute-done.1 = bf16[32,3584]{1,0:T(8,128)(2,1)S(1)} collective-permute-done((bf16[32,3584]{1,0:T(8,128)(2,1)S(1)}, bf16[32,3584]{1,0:T(8,128)(2,1)S(1)}, u32[]{:S(2)}, u32[]{:S(2)}) %collective-permute-start.1) | collective-permute-done | bytes 229408 | tf_op jit(solution)/shard_map/ppermute | solution.py:13
  36.2 2.0 collective-permute-start.11
  38.2 1.5 collective-permute-start.10
  40.7 4.8 %collective-permute-done.12 = bf16[32,3584]{1,0:T(8,128)(2,1)S(1)} collective-permute-done((bf16[32,3584]{1,0:T(8,128)(2,1)S(1)}, bf16[32,3584]{1,0:T(8,128)(2,1)S(1)}, u32[]{:S(2)}, u32[]{:S(2)}) %collective-permute-start.12) | collective-permute-done | bytes 229408 | tf_op jit(solution)/shard_map/ppermute | solution.py:13
  45.5 3.6 %collective-permute-done.11 = bf16[32,3584]{1,0:T(8,128)(2,1)S(1)} collective-permute-done((bf16[32,3584]{1,0:T(8,128)(2,1)S(1)}, bf16[32,3584]{1,0:T(8,128)(2,1)S(1)}, u32[]{:S(2)}, u32[]{:S(2)}) %collective-permute-start.11) | collective-permute-done | bytes 229408 | tf_op jit(solution)/shard_map/ppermute | solution.py:13
  49.1 0.9 collective-permute-done.10
  50.3 1.2 copy-done.14
  51.4 1.2 copy-done.22
  52.6 0.7 copy-done.23
  53.3 1.9 fusion.14
  55.2 6.1 %convolution_convert_fusion.3 = bf16[256,3584]{1,0:T(8,128)(2,1)S(1)} fusion(bf16[1,512,3584]{2,1,0:T(8,128)(2,1)} %param.15, f32[256,512]{1,0:T(8,128)} %fusion.14, bf16[256,3584]{1,0:T(8,128)(2,1)} %copy-done.22, bf16[1,3584,512]{2,1,0:T(8,128)(2,1)} %param.13), kind=kOutput, calls=%fused_computation.3 | convolution fusion | flops 1880752128 | bytes 11534336 | tf_op jit(solution)/shard_map/dot_general | solution.py:102
  61.5 1.3 copy-done.15
  62.9 1.2 constant_dynamic-update-slice_fusion.11
  64.1 4.6 %fusion.12 = f32[256,512]{1,0:T(8,128)} fusion(bf16[256,3584]{1,0:T(8,128)(2,1)S(1)} %constant_dynamic-update-slice_fusion.11, bf16[1,3584,512]{2,1,0:T(8,128)(2,1)} %param.14), kind=kOutput, calls=%fused_computation.24 | convolution fusion | flops 939524096 | bytes 6029312 | tf_op jit(solution)/shard_map/dot_general | solution.py:100
  68.9 0.9 fusion.110
  70.4 7.3 %convolution_convert_fusion.2 = bf16[256,3584]{1,0:T(8,128)(2,1)} fusion(bf16[1,512,3584]{2,1,0:T(8,128)(2,1)} %param.15, f32[256,512]{1,0:T(8,128)} %fusion.12, bf16[256,3584]{1,0:T(8,128)(2,1)} %copy-done.16, bf16[1,3584,512]{2,1,0:T(8,128)(2,1)} %param.13), kind=kOutput, calls=%fused_computation.2 | convolution fusion | flops 1880752128 | bytes 11534336 | tf_op jit(solution)/shard_map/dot_general | solution.py:102
  77.7 1.4 slice.217
  79.6 2.5 collective-permute-start.6
  82.1 11.0 %collective-permute-done.6 = bf16[32,3584]{1,0:T(8,128)(2,1)S(1)} collective-permute-done((bf16[32,3584]{1,0:T(8,128)(2,1)}, bf16[32,3584]{1,0:T(8,128)(2,1)S(1)}, u32[]{:S(2)}, u32[]{:S(2)}) %collective-permute-start.6) | collective-permute-done | bytes 229408 | tf_op jit(solution)/shard_map/ppermute | solution.py:13
  93.6 0.7 collective-permute-start.15
  94.8 2.4 collective-permute-start.16
  97.2 8.5 %collective-permute-done.15 = bf16[32,3584]{1,0:T(8,128)(2,1)S(1)} collective-permute-done((bf16[32,3584]{1,0:T(8,128)(2,1)S(1)}, bf16[32,3584]{1,0:T(8,128)(2,1)S(1)}, u32[]{:S(2)}, u32[]{:S(2)}) %collective-permute-start.15) | collective-permute-done | bytes 229408 | tf_op jit(solution)/shard_map/ppermute | solution.py:13
  105.7 1.3 collective-permute-done.16
  107.7 2.8 %collective-permute-start.18 = (bf16[64,3584]{1,0:T(8,128)(2,1)S(1)}, bf16[64,3584]{1,0:T(8,128)(2,1)S(1)}, u32[]{:S(2)}, u32[]{:S(2)}) collective-permute-start(bf16[64,3584]{1,0:T(8,128)(2,1)S(1)} %convolution_convert_fusion.9), channel_id=1, source_target_pairs={{0,8},{1,9},{2,10},{3,11},{4,12},{5,13},{6,14},{7,15},{8,0},{9,1},... | collective-permute-start | bytes 1376264 | tf_op jit(solution)/shard_map/ppermute | solution.py:13
  110.6 19.0 %collective-permute-done.18 = bf16[64,3584]{1,0:T(8,128)(2,1)S(1)} collective-permute-done((bf16[64,3584]{1,0:T(8,128)(2,1)S(1)}, bf16[64,3584]{1,0:T(8,128)(2,1)S(1)}, u32[]{:S(2)}, u32[]{:S(2)}) %collective-permute-start.18) | collective-permute-done | bytes 458784 | tf_op jit(solution)/shard_map/ppermute | solution.py:13
  130.0 1.6 collective-permute-start.19
  132.1 8.5 %collective-permute-done.19 = bf16[64,3584]{1,0:T(8,128)(2,1)S(1)} collective-permute-done((bf16[64,3584]{1,0:T(8,128)(2,1)S(1)}, bf16[64,3584]{1,0:T(8,128)(2,1)S(1)}, u32[]{:S(2)}, u32[]{:S(2)}) %collective-permute-start.19) | collective-permute-done | bytes 458784 | tf_op jit(solution)/shard_map/ppermute | solution.py:13
  141.8 6.7 %collective-permute-start.22 = (bf16[32,3584]{1,0:T(8,128)(2,1)S(1)}, bf16[32,3584]{1,0:T(8,128)(2,1)S(1)}, u32[]{:S(2)}, u32[]{:S(2)}) collective-permute-start(bf16[32,3584]{1,0:T(8,128)(2,1)S(1)} %get-tuple-element.33), channel_id=1, source_target_pairs={{0,6},{1,7},{2,4},{3,5},{4,2},{5,3},{6,0},{7,1},{8,14},{9,15},{10,... | collective-permute-start | bytes 688136 | tf_op jit(solution)/shard_map/ppermute | solution.py:13
  148.5 0.8 collective-permute-start.20
  149.5 5.5 %collective-permute-done.22 = bf16[32,3584]{1,0:T(8,128)(2,1)S(1)} collective-permute-done((bf16[32,3584]{1,0:T(8,128)(2,1)S(1)}, bf16[32,3584]{1,0:T(8,128)(2,1)S(1)}, u32[]{:S(2)}, u32[]{:S(2)}) %collective-permute-start.22) | collective-permute-done | bytes 229408 | tf_op jit(solution)/shard_map/ppermute | solution.py:13
  155.0 7.4 %collective-permute-done.21 = bf16[32,3584]{1,0:T(8,128)(2,1)S(1)} collective-permute-done((bf16[32,3584]{1,0:T(8,128)(2,1)S(1)}, bf16[32,3584]{1,0:T(8,128)(2,1)S(1)}, u32[]{:S(2)}, u32[]{:S(2)}) %collective-permute-start.21) | collective-permute-done | bytes 229408 | tf_op jit(solution)/shard_map/ppermute | solution.py:13
  163.4 1.4 collective-permute-start.31
  164.8 2.5 collective-permute-start.30
  168.3 4.5 %collective-permute-done.31 = bf16[32,3584]{1,0:T(8,128)(2,1)S(1)} collective-permute-done((bf16[32,3584]{1,0:T(8,128)(2,1)S(1)}, bf16[32,3584]{1,0:T(8,128)(2,1)S(1)}, u32[]{:S(2)}, u32[]{:S(2)}) %collective-permute-start.31) | collective-permute-done | bytes 229408 | tf_op jit(solution)/shard_map/ppermute | solution.py:13
  172.8 5.5 %collective-permute-done.30 = bf16[32,3584]{1,0:T(8,128)(2,1)S(1)} collective-permute-done((bf16[32,3584]{1,0:T(8,128)(2,1)S(1)}, bf16[32,3584]{1,0:T(8,128)(2,1)S(1)}, u32[]{:S(2)}, u32[]{:S(2)}) %collective-permute-start.30) | collective-permute-done | bytes 229408 | tf_op jit(solution)/shard_map/ppermute | solution.py:13
  178.5 1.2 copy-done.17
  179.7 1.2 copy-done.20
  180.9 0.7 copy-done.24
  181.6 1.9 fusion.10
  183.5 6.1 %convolution_convert_fusion.1 = bf16[256,3584]{1,0:T(8,128)(2,1)S(1)} fusion(bf16[1,512,3584]{2,1,0:T(8,128)(2,1)} %param.15, f32[256,512]{1,0:T(8,128)} %fusion.10, bf16[256,3584]{1,0:T(8,128)(2,1)} %copy-done.20, bf16[1,3584,512]{2,1,0:T(8,128)(2,1)} %param.13), kind=kOutput, calls=%fused_computation.1 | convolution fusion | flops 1880752128 | bytes 11534336 | tf_op jit(solution)/shard_map/dot_general | solution.py:102
  189.7 1.3 copy-done.18
  191.1 1.2 constant_dynamic-update-slice_fusion.33
  192.4 4.6 %fusion.8 = f32[256,512]{1,0:T(8,128)} fusion(bf16[256,3584]{1,0:T(8,128)(2,1)S(1)} %constant_dynamic-update-slice_fusion.33, bf16[1,3584,512]{2,1,0:T(8,128)(2,1)} %param.14), kind=kOutput, calls=%fused_computation.20 | convolution fusion | flops 939524096 | bytes 6029312 | tf_op jit(solution)/shard_map/dot_general | solution.py:100
  197.2 0.9 fusion.106
  198.1 1.4 collective-permute-start.25
  199.5 7.3 %convolution_convert_fusion = bf16[256,3584]{1,0:T(8,128)(2,1)} fusion(bf16[1,512,3584]{2,1,0:T(8,128)(2,1)} %param.15, f32[256,512]{1,0:T(8,128)} %fusion.8, bf16[256,3584]{1,0:T(8,128)(2,1)} %copy-done.19, bf16[1,3584,512]{2,1,0:T(8,128)(2,1)} %param.13), kind=kOutput, calls=%fused_computation | convolution fusion | flops 1880752128 | bytes 11534336 | tf_op jit(solution)/shard_map/dot_general | solution.py:102
  206.8 1.4 slice.237
  208.6 1.8 collective-permute-start.26
  210.4 11.0 %collective-permute-done.26 = bf16[32,3584]{1,0:T(8,128)(2,1)S(1)} collective-permute-done((bf16[32,3584]{1,0:T(8,128)(2,1)}, bf16[32,3584]{1,0:T(8,128)(2,1)S(1)}, u32[]{:S(2)}, u32[]{:S(2)}) %collective-permute-start.26) | collective-permute-done | bytes 229408 | tf_op jit(solution)/shard_map/ppermute | solution.py:13
  221.8 1.5 collective-permute-start.34
  223.7 1.8 collective-permute-start.35
  225.5 8.5 %collective-permute-done.34 = bf16[32,3584]{1,0:T(8,128)(2,1)S(1)} collective-permute-done((bf16[32,3584]{1,0:T(8,128)(2,1)S(1)}, bf16[32,3584]{1,0:T(8,128)(2,1)S(1)}, u32[]{:S(2)}, u32[]{:S(2)}) %collective-permute-start.34) | collective-permute-done | bytes 229408 | tf_op jit(solution)/shard_map/ppermute | solution.py:13
  234.0 1.3 collective-permute-done.35
  235.9 4.2 %collective-permute-start.37 = (bf16[64,3584]{1,0:T(8,128)(2,1)S(1)}, bf16[64,3584]{1,0:T(8,128)(2,1)S(1)}, u32[]{:S(2)}, u32[]{:S(2)}) collective-permute-start(bf16[64,3584]{1,0:T(8,128)(2,1)S(1)} %convolution_convert_fusion.8), channel_id=1, source_target_pairs={{0,8},{1,9},{2,10},{3,11},{4,12},{5,13},{6,14},{7,15},{8,0},{9,1},... | collective-permute-start | bytes 1376264 | tf_op jit(solution)/shard_map/ppermute | solution.py:13
  240.2 19.0 %collective-permute-done.37 = bf16[64,3584]{1,0:T(8,128)(2,1)S(1)} collective-permute-done((bf16[64,3584]{1,0:T(8,128)(2,1)S(1)}, bf16[64,3584]{1,0:T(8,128)(2,1)S(1)}, u32[]{:S(2)}, u32[]{:S(2)}) %collective-permute-start.37) | collective-permute-done | bytes 458784 | tf_op jit(solution)/shard_map/ppermute | solution.py:13
  259.1 1.5 select_bitcast_fusion
  (211 shorter events, 17.6 us)
Async XLA Ops:
  0.6 8.0 %copy-start = (bf16[1,3584,8]{1,2,0:T(8,128)(2,1)S(1)}, bf16[1,3584,8]{1,2,0:T(8,128)(2,1)}, u32[]{:S(2)}) copy-start(bf16[1,3584,8]{1,2,0:T(8,128)(2,1)} %param.12) | copy-start | bytes 172036
  0.6 7.4 %copy-start.8 = (s32[1,8,8,2]{2,3,1,0:T(2,128)S(1)}, s32[1,8,8,2]{2,3,1,0:T(2,128)}, u32[]{:S(2)}) copy-start(s32[1,8,8,2]{2,3,1,0:T(2,128)} %param.17) | copy-start | bytes 1540
  0.7 7.3 %copy-start.7 = (s32[1,8,8,2]{2,3,1,0:T(2,128)S(1)}, s32[1,8,8,2]{2,3,1,0:T(2,128)}, u32[]{:S(2)}) copy-start(s32[1,8,8,2]{2,3,1,0:T(2,128)} %param.16) | copy-start | bytes 1540
  1.5 7.6 %collective-permute-start.8 = (s32[2,8,8,2]{2,1,3,0:T(8,128)S(1)}, s32[2,8,8,2]{2,1,3,0:T(8,128)S(1)}, u32[]{:S(2)}, u32[]{:S(2)}) collective-permute-start(s32[2,8,8,2]{2,1,3,0:T(8,128)S(1)} %broadcast_select_fusion.2), channel_id=1, source_target_pairs={{0,8},{1,9},{2,10},{3,11},{4,12},{5,13},{6,14},{7,15},{8,0},{9,1},... | collective-permute-start | bytes 3080 | tf_op jit(solution)/shard_map/ppermute | solution.py:13
  7.8 27.7 %collective-permute-start.9 = (bf16[64,3584]{1,0:T(8,128)(2,1)S(1)}, bf16[64,3584]{1,0:T(8,128)(2,1)S(1)}, u32[]{:S(2)}, u32[]{:S(2)}) collective-permute-start(bf16[64,3584]{1,0:T(8,128)(2,1)S(1)} %fusion.38), channel_id=1, source_target_pairs={{0,8},{1,9},{2,10},{3,11},{4,12},{5,13},{6,14},{7,15},{8,0},{9,1},... | collective-permute-start | bytes 1376264 | tf_op jit(solution)/shard_map/ppermute | solution.py:13
  13.6 18.2 %collective-permute-start.2 = (bf16[32,3584]{1,0:T(8,128)(2,1)S(1)}, bf16[32,3584]{1,0:T(8,128)(2,1)S(1)}, u32[]{:S(2)}, u32[]{:S(2)}) collective-permute-start(bf16[32,3584]{1,0:T(8,128)(2,1)S(1)} %get-tuple-element.51), channel_id=1, source_target_pairs={{0,6},{1,7},{2,4},{3,5},{4,2},{5,3},{6,0},{7,1},{8,14},{9,15},{10,... | collective-permute-start | bytes 688136 | tf_op jit(solution)/shard_map/ppermute | solution.py:13
  16.4 18.9 %collective-permute-start.1 = (bf16[32,3584]{1,0:T(8,128)(2,1)S(1)}, bf16[32,3584]{1,0:T(8,128)(2,1)S(1)}, u32[]{:S(2)}, u32[]{:S(2)}) collective-permute-start(bf16[32,3584]{1,0:T(8,128)(2,1)S(1)} %get-tuple-element.52), channel_id=1, source_target_pairs={{0,4},{1,5},{2,6},{3,7},{4,0},{5,1},{6,2},{7,3},{8,12},{9,13},{10,... | collective-permute-start | bytes 688136 | tf_op jit(solution)/shard_map/ppermute | solution.py:13
  16.9 18.4 %collective-permute-start = (bf16[32,3584]{1,0:T(8,128)(2,1)S(1)}, bf16[32,3584]{1,0:T(8,128)(2,1)S(1)}, u32[]{:S(2)}, u32[]{:S(2)}) collective-permute-start(bf16[32,3584]{1,0:T(8,128)(2,1)S(1)} %get-tuple-element.53), channel_id=1, source_target_pairs={{0,2},{1,3},{2,0},{3,1},{4,6},{5,7},{6,4},{7,5},{8,10},{9,11},{10,... | collective-permute-start | bytes 688136 | tf_op jit(solution)/shard_map/ppermute | solution.py:13
  17.3 18.2 %copy-start.21 = (bf16[256,3584]{1,0:T(8,128)(2,1)S(1)}, bf16[256,3584]{1,0:T(8,128)(2,1)}, u32[]{:S(2)}) copy-start(bf16[256,3584]{1,0:T(8,128)(2,1)} %get-tuple-element.50) | copy-start | bytes 5505028
  35.4 14.8 %collective-permute-start.3 = (bf16[128,3584]{1,0:T(8,128)(2,1)S(1)}, bf16[128,3584]{1,0:T(8,128)(2,1)S(1)}, u32[]{:S(2)}, u32[]{:S(2)}) collective-permute-start(bf16[128,3584]{1,0:T(8,128)(2,1)S(1)} %pad_maximum_fusion), channel_id=1, source_target_pairs={{0,1},{1,0},{2,3},{3,2},{4,5},{5,4},{6,7},{7,6},{8,9},{9,8},{10,11... | collective-permute-start | bytes 2752520 | tf_op jit(solution)/shard_map/ppermute | solution.py:13
  36.1 9.4 %collective-permute-start.12 = (bf16[32,3584]{1,0:T(8,128)(2,1)S(1)}, bf16[32,3584]{1,0:T(8,128)(2,1)S(1)}, u32[]{:S(2)}, u32[]{:S(2)}) collective-permute-start(bf16[32,3584]{1,0:T(8,128)(2,1)S(1)} %get-tuple-element.42), channel_id=1, source_target_pairs={{0,6},{1,7},{2,4},{3,5},{4,2},{5,3},{6,0},{7,1},{8,14},{9,15},{10,... | collective-permute-start | bytes 688136 | tf_op jit(solution)/shard_map/ppermute | solution.py:13
  36.2 12.9 %collective-permute-start.11 = (bf16[32,3584]{1,0:T(8,128)(2,1)S(1)}, bf16[32,3584]{1,0:T(8,128)(2,1)S(1)}, u32[]{:S(2)}, u32[]{:S(2)}) collective-permute-start(bf16[32,3584]{1,0:T(8,128)(2,1)S(1)} %get-tuple-element.43), channel_id=1, source_target_pairs={{0,4},{1,5},{2,6},{3,7},{4,0},{5,1},{6,2},{7,3},{8,12},{9,13},{10,... | collective-permute-start | bytes 688136 | tf_op jit(solution)/shard_map/ppermute | solution.py:13
  38.2 11.8 %collective-permute-start.10 = (bf16[32,3584]{1,0:T(8,128)(2,1)S(1)}, bf16[32,3584]{1,0:T(8,128)(2,1)S(1)}, u32[]{:S(2)}, u32[]{:S(2)}) collective-permute-start(bf16[32,3584]{1,0:T(8,128)(2,1)S(1)} %get-tuple-element.44), channel_id=1, source_target_pairs={{0,2},{1,3},{2,0},{3,1},{4,6},{5,7},{6,4},{7,5},{8,10},{9,11},{10,... | collective-permute-start | bytes 688136 | tf_op jit(solution)/shard_map/ppermute | solution.py:13
  50.0 3.4 %copy-start.23 = (bf16[1,3584,512]{2,1,0:T(8,128)(2,1)S(1)}, bf16[1,3584,512]{2,1,0:T(8,128)(2,1)}, u32[]{:S(2)}) copy-start(bf16[1,3584,512]{2,1,0:T(8,128)(2,1)} %param.14) | copy-start | bytes 11010052
  50.0 12.8 %collective-permute-start.13 = (bf16[128,3584]{1,0:T(8,128)(2,1)S(1)}, bf16[128,3584]{1,0:T(8,128)(2,1)}, u32[]{:S(2)}, u32[]{:S(2)}) collective-permute-start(bf16[128,3584]{1,0:T(8,128)(2,1)S(1)} %pad_maximum_fusion.1), channel_id=1, source_target_pairs={{0,1},{1,0},{2,3},{3,2},{4,5},{5,4},{6,7},{7,6},{8,9},{9,8},{10,11... | collective-permute-start | bytes 2752520 | tf_op jit(solution)/shard_map/ppermute | solution.py:13
  50.2 1.3 copy-start.14
  51.4 1.2 copy-start.22
  61.3 1.5 copy-start.15
  61.4 7.3 %collective-permute-start.4 = (bf16[128,3584]{1,0:T(8,128)(2,1)S(1)}, bf16[128,3584]{1,0:T(8,128)(2,1)S(1)}, u32[]{:S(2)}, u32[]{:S(2)}) collective-permute-start(bf16[128,3584]{1,0:T(8,128)(2,1)S(1)} %slice.207), channel_id=1, source_target_pairs={{0,1},{1,0},{2,3},{3,2},{4,5},{5,4},{6,7},{7,6},{8,9},{9,8},{10,11... | collective-permute-start | bytes 2752520 | tf_op jit(solution)/shard_map/ppermute | solution.py:13
  64.1 4.6 %copy-start.16 = (bf16[256,3584]{1,0:T(8,128)(2,1)}, bf16[256,3584]{1,0:T(8,128)(2,1)S(1)}, u32[]{:S(2)}) copy-start(bf16[256,3584]{1,0:T(8,128)(2,1)S(1)} %constant_dynamic-update-slice_fusion.11) | copy-start | bytes 5505028
  69.8 12.3 %collective-permute-start.5 = (bf16[32,3584]{1,0:T(8,128)(2,1)}, bf16[32,3584]{1,0:T(8,128)(2,1)S(1)}, u32[]{:S(2)}, u32[]{:S(2)}) collective-permute-start(bf16[32,3584]{1,0:T(8,128)(2,1)} %get-tuple-element.48), channel_id=1, source_target_pairs={{0,2},{1,3},{2,0},{3,1},{4,6},{5,7},{6,4},{7,5},{8,10},{9,11},{10,... | collective-permute-start | bytes 688136 | tf_op jit(solution)/shard_map/ppermute | solution.py:13
  77.7 15.6 %copy-start.3 = (bf16[256,3584]{1,0:T(8,128)(2,1)S(1)}, bf16[256,3584]{1,0:T(8,128)(2,1)}, u32[]{:S(2)}) copy-start(bf16[256,3584]{1,0:T(8,128)(2,1)} %convolution_convert_fusion.2) | copy-start | bytes 5505028
  79.1 14.2 %collective-permute-start.14 = (bf16[128,3584]{1,0:T(8,128)(2,1)S(1)}, bf16[128,3584]{1,0:T(8,128)(2,1)S(1)}, u32[]{:S(2)}, u32[]{:S(2)}) collective-permute-start(bf16[128,3584]{1,0:T(8,128)(2,1)S(1)} %slice.217), channel_id=1, source_target_pairs={{0,1},{1,0},{2,3},{3,2},{4,5},{5,4},{6,7},{7,6},{8,9},{9,8},{10,11... | collective-permute-start | bytes 2752520 | tf_op jit(solution)/shard_map/ppermute | solution.py:13
  79.2 14.0 %collective-permute-start.7 = (bf16[32,3584]{1,0:T(8,128)(2,1)}, bf16[32,3584]{1,0:T(8,128)(2,1)S(1)}, u32[]{:S(2)}, u32[]{:S(2)}) collective-permute-start(bf16[32,3584]{1,0:T(8,128)(2,1)} %get-tuple-element.45), channel_id=1, source_target_pairs={{0,6},{1,7},{2,4},{3,5},{4,2},{5,3},{6,0},{7,1},{8,14},{9,15},{10,... | collective-permute-start | bytes 688136 | tf_op jit(solution)/shard_map/ppermute | solution.py:13
  79.6 13.5 %collective-permute-start.6 = (bf16[32,3584]{1,0:T(8,128)(2,1)}, bf16[32,3584]{1,0:T(8,128)(2,1)S(1)}, u32[]{:S(2)}, u32[]{:S(2)}) collective-permute-start(bf16[32,3584]{1,0:T(8,128)(2,1)} %get-tuple-element.47), channel_id=1, source_target_pairs={{0,4},{1,5},{2,6},{3,7},{4,0},{5,1},{6,2},{7,3},{8,12},{9,13},{10,... | collective-permute-start | bytes 688136 | tf_op jit(solution)/shard_map/ppermute | solution.py:13
  93.6 13.7 %copy-start.11 = (bf16[64,128]{1,0:T(8,128)(2,1)S(1)}, bf16[64,128]{1,0:T(8,128)(2,1)}, u32[]{:S(2)}) copy-start(bf16[64,128]{1,0:T(8,128)(2,1)} %get-tuple-element.66) | copy-start | bytes 49156
  93.6 13.7 %copy-start.12 = (bf16[64,128]{1,0:T(8,128)(2,1)S(1)}, bf16[64,128]{1,0:T(8,128)(2,1)}, u32[]{:S(2)}) copy-start(bf16[64,128]{1,0:T(8,128)(2,1)} %get-tuple-element.67) | copy-start | bytes 49156
  93.6 12.1 %collective-permute-start.15 = (bf16[32,3584]{1,0:T(8,128)(2,1)S(1)}, bf16[32,3584]{1,0:T(8,128)(2,1)S(1)}, u32[]{:S(2)}, u32[]{:S(2)}) collective-permute-start(bf16[32,3584]{1,0:T(8,128)(2,1)S(1)} %get-tuple-element.39), channel_id=1, source_target_pairs={{0,2},{1,3},{2,0},{3,1},{4,6},{5,7},{6,4},{7,5},{8,10},{9,11},{10,... | collective-permute-start | bytes 688136 | tf_op jit(solution)/shard_map/ppermute | solution.py:13
  94.3 12.8 %collective-permute-start.17 = (bf16[32,3584]{1,0:T(8,128)(2,1)S(1)}, bf16[32,3584]{1,0:T(8,128)(2,1)S(1)}, u32[]{:S(2)}, u32[]{:S(2)}) collective-permute-start(bf16[32,3584]{1,0:T(8,128)(2,1)S(1)} %get-tuple-element.36), channel_id=1, source_target_pairs={{0,6},{1,7},{2,4},{3,5},{4,2},{5,3},{6,0},{7,1},{8,14},{9,15},{10,... | collective-permute-start | bytes 688136 | tf_op jit(solution)/shard_map/ppermute | solution.py:13
  94.8 12.2 %collective-permute-start.16 = (bf16[32,3584]{1,0:T(8,128)(2,1)S(1)}, bf16[32,3584]{1,0:T(8,128)(2,1)S(1)}, u32[]{:S(2)}, u32[]{:S(2)}) collective-permute-start(bf16[32,3584]{1,0:T(8,128)(2,1)S(1)} %get-tuple-element.38), channel_id=1, source_target_pairs={{0,4},{1,5},{2,6},{3,7},{4,0},{5,1},{6,2},{7,3},{8,12},{9,13},{10,... | collective-permute-start | bytes 688136 | tf_op jit(solution)/shard_map/ppermute | solution.py:13
  107.2 22.4 %copy-start.9 = (bf16[64,128]{1,0:T(8,128)(2,1)S(1)}, bf16[64,128]{1,0:T(8,128)(2,1)}, u32[]{:S(2)}) copy-start(bf16[64,128]{1,0:T(8,128)(2,1)} %get-tuple-element.64) | copy-start | bytes 49156
  107.2 22.3 %copy-start.10 = (bf16[64,128]{1,0:T(8,128)(2,1)S(1)}, bf16[64,128]{1,0:T(8,128)(2,1)}, u32[]{:S(2)}) copy-start(bf16[64,128]{1,0:T(8,128)(2,1)} %get-tuple-element.65) | copy-start | bytes 49156
  107.7 21.8 %collective-permute-start.18 = (bf16[64,3584]{1,0:T(8,128)(2,1)S(1)}, bf16[64,3584]{1,0:T(8,128)(2,1)S(1)}, u32[]{:S(2)}, u32[]{:S(2)}) collective-permute-start(bf16[64,3584]{1,0:T(8,128)(2,1)S(1)} %convolution_convert_fusion.9), channel_id=1, source_target_pairs={{0,8},{1,9},{2,10},{3,11},{4,12},{5,13},{6,14},{7,15},{8,0},{9,1},... | collective-permute-start | bytes 1376264 | tf_op jit(solution)/shard_map/ppermute | solution.py:13
  110.5 21.2 %copy-start.5 = (s32[1,1,64,2]{3,2,0,1:T(8,128)S(1)}, s32[1,1,64,2]{3,2,0,1:T(8,128)}, u32[]{:S(2)}) copy-start(s32[1,1,64,2]{3,2,0,1:T(8,128)} %get-tuple-element.54) | copy-start | bytes 1540
  110.5 21.3 %copy-start.6 = (s32[1,1,64,2]{3,2,0,1:T(8,128)S(1)}, s32[1,1,64,2]{3,2,0,1:T(8,128)}, u32[]{:S(2)}) copy-start(s32[1,1,64,2]{3,2,0,1:T(8,128)} %get-tuple-element.56) | copy-start | bytes 1540
  130.0 10.8 %copy-start.1 = (bf16[64,3584]{1,0:T(8,128)(2,1)}, bf16[64,3584]{1,0:T(8,128)(2,1)S(1)}, u32[]{:S(2)}) copy-start(bf16[64,3584]{1,0:T(8,128)(2,1)S(1)} %fusion.2) | copy-start | bytes 1376260
  130.0 10.6 %collective-permute-start.19 = (bf16[64,3584]{1,0:T(8,128)(2,1)S(1)}, bf16[64,3584]{1,0:T(8,128)(2,1)S(1)}, u32[]{:S(2)}, u32[]{:S(2)}) collective-permute-start(bf16[64,3584]{1,0:T(8,128)(2,1)S(1)} %fusion.2), channel_id=1, source_target_pairs={{0,16},{16,0},{1,17},{17,1},{2,18},{18,2},{3,19},{19,3},{4,20},{20... | collective-permute-start | bytes 1376264 | tf_op jit(solution)/shard_map/ppermute | solution.py:13
  141.2 21.6 %collective-permute-start.28 = (bf16[64,3584]{1,0:T(8,128)(2,1)S(1)}, bf16[64,3584]{1,0:T(8,128)(2,1)S(1)}, u32[]{:S(2)}, u32[]{:S(2)}) collective-permute-start(bf16[64,3584]{1,0:T(8,128)(2,1)S(1)} %fusion.41), channel_id=1, source_target_pairs={{0,8},{1,9},{2,10},{3,11},{4,12},{5,13},{6,14},{7,15},{8,0},{9,1},... | collective-permute-start | bytes 1376264 | tf_op jit(solution)/shard_map/ppermute | solution.py:13
  141.8 13.2 %collective-permute-start.22 = (bf16[32,3584]{1,0:T(8,128)(2,1)S(1)}, bf16[32,3584]{1,0:T(8,128)(2,1)S(1)}, u32[]{:S(2)}, u32[]{:S(2)}) collective-permute-start(bf16[32,3584]{1,0:T(8,128)(2,1)S(1)} %get-tuple-element.33), channel_id=1, source_target_pairs={{0,6},{1,7},{2,4},{3,5},{4,2},{5,3},{6,0},{7,1},{8,14},{9,15},{10,... | collective-permute-start | bytes 688136 | tf_op jit(solution)/shard_map/ppermute | solution.py:13
  148.5 13.9 %collective-permute-start.21 = (bf16[32,3584]{1,0:T(8,128)(2,1)S(1)}, bf16[32,3584]{1,0:T(8,128)(2,1)S(1)}, u32[]{:S(2)}, u32[]{:S(2)}) collective-permute-start(bf16[32,3584]{1,0:T(8,128)(2,1)S(1)} %get-tuple-element.34), channel_id=1, source_target_pairs={{0,4},{1,5},{2,6},{3,7},{4,0},{5,1},{6,2},{7,3},{8,12},{9,13},{10,... | collective-permute-start | bytes 688136 | tf_op jit(solution)/shard_map/ppermute | solution.py:13
  148.5 13.9 %collective-permute-start.20 = (bf16[32,3584]{1,0:T(8,128)(2,1)S(1)}, bf16[32,3584]{1,0:T(8,128)(2,1)S(1)}, u32[]{:S(2)}, u32[]{:S(2)}) collective-permute-start(bf16[32,3584]{1,0:T(8,128)(2,1)S(1)} %get-tuple-element.35), channel_id=1, source_target_pairs={{0,2},{1,3},{2,0},{3,1},{4,6},{5,7},{6,4},{7,5},{8,10},{9,11},{10,... | collective-permute-start | bytes 688136 | tf_op jit(solution)/shard_map/ppermute | solution.py:13
  162.5 16.0 %collective-permute-start.23 = (bf16[128,3584]{1,0:T(8,128)(2,1)S(1)}, bf16[128,3584]{1,0:T(8,128)(2,1)S(1)}, u32[]{:S(2)}, u32[]{:S(2)}) collective-permute-start(bf16[128,3584]{1,0:T(8,128)(2,1)S(1)} %pad_maximum_fusion.2), channel_id=1, source_target_pairs={{0,1},{1,0},{2,3},{3,2},{4,5},{5,4},{6,7},{7,6},{8,9},{9,8},{10,11... | collective-permute-start | bytes 2752520 | tf_op jit(solution)/shard_map/ppermute | solution.py:13
  163.4 9.4 %collective-permute-start.31 = (bf16[32,3584]{1,0:T(8,128)(2,1)S(1)}, bf16[32,3584]{1,0:T(8,128)(2,1)S(1)}, u32[]{:S(2)}, u32[]{:S(2)}) collective-permute-start(bf16[32,3584]{1,0:T(8,128)(2,1)S(1)} %get-tuple-element.24), channel_id=1, source_target_pairs={{0,6},{1,7},{2,4},{3,5},{4,2},{5,3},{6,0},{7,1},{8,14},{9,15},{10,... | collective-permute-start | bytes 688136 | tf_op jit(solution)/shard_map/ppermute | solution.py:13
  164.8 13.4 %collective-permute-start.30 = (bf16[32,3584]{1,0:T(8,128)(2,1)S(1)}, bf16[32,3584]{1,0:T(8,128)(2,1)S(1)}, u32[]{:S(2)}, u32[]{:S(2)}) collective-permute-start(bf16[32,3584]{1,0:T(8,128)(2,1)S(1)} %get-tuple-element.25), channel_id=1, source_target_pairs={{0,4},{1,5},{2,6},{3,7},{4,0},{5,1},{6,2},{7,3},{8,12},{9,13},{10,... | collective-permute-start | bytes 688136 | tf_op jit(solution)/shard_map/ppermute | solution.py:13
  167.3 10.9 %collective-permute-start.29 = (bf16[32,3584]{1,0:T(8,128)(2,1)S(1)}, bf16[32,3584]{1,0:T(8,128)(2,1)S(1)}, u32[]{:S(2)}, u32[]{:S(2)}) collective-permute-start(bf16[32,3584]{1,0:T(8,128)(2,1)S(1)} %get-tuple-element.26), channel_id=1, source_target_pairs={{0,2},{1,3},{2,0},{3,1},{4,6},{5,7},{6,4},{7,5},{8,10},{9,11},{10,... | collective-permute-start | bytes 688136 | tf_op jit(solution)/shard_map/ppermute | solution.py:13
  178.2 3.4 %copy-start.24 = (bf16[1,3584,512]{2,1,0:T(8,128)(2,1)S(1)}, bf16[1,3584,512]{2,1,0:T(8,128)(2,1)}, u32[]{:S(2)}) copy-start(bf16[1,3584,512]{2,1,0:T(8,128)(2,1)} %param.14) | copy-start | bytes 11010052
  178.3 12.8 %collective-permute-start.32 = (bf16[128,3584]{1,0:T(8,128)(2,1)S(1)}, bf16[128,3584]{1,0:T(8,128)(2,1)}, u32[]{:S(2)}, u32[]{:S(2)}) collective-permute-start(bf16[128,3584]{1,0:T(8,128)(2,1)S(1)} %pad_maximum_fusion.3), channel_id=1, source_target_pairs={{0,1},{1,0},{2,3},{3,2},{4,5},{5,4},{6,7},{7,6},{8,9},{9,8},{10,11... | collective-permute-start | bytes 2752520 | tf_op jit(solution)/shard_map/ppermute | solution.py:13
  178.4 1.3 copy-start.17
  179.7 1.2 copy-start.20
  189.6 1.5 copy-start.18
  189.7 7.3 %collective-permute-start.24 = (bf16[128,3584]{1,0:T(8,128)(2,1)S(1)}, bf16[128,3584]{1,0:T(8,128)(2,1)S(1)}, u32[]{:S(2)}, u32[]{:S(2)}) collective-permute-start(bf16[128,3584]{1,0:T(8,128)(2,1)S(1)} %slice.227), channel_id=1, source_target_pairs={{0,1},{1,0},{2,3},{3,2},{4,5},{5,4},{6,7},{7,6},{8,9},{9,8},{10,11... | collective-permute-start | bytes 2752520 | tf_op jit(solution)/shard_map/ppermute | solution.py:13
  192.4 4.6 %copy-start.19 = (bf16[256,3584]{1,0:T(8,128)(2,1)}, bf16[256,3584]{1,0:T(8,128)(2,1)S(1)}, u32[]{:S(2)}) copy-start(bf16[256,3584]{1,0:T(8,128)(2,1)S(1)} %constant_dynamic-update-slice_fusion.33) | copy-start | bytes 5505028
  198.1 12.3 %collective-permute-start.25 = (bf16[32,3584]{1,0:T(8,128)(2,1)}, bf16[32,3584]{1,0:T(8,128)(2,1)S(1)}, u32[]{:S(2)}, u32[]{:S(2)}) collective-permute-start(bf16[32,3584]{1,0:T(8,128)(2,1)} %get-tuple-element.30), channel_id=1, source_target_pairs={{0,2},{1,3},{2,0},{3,1},{4,6},{5,7},{6,4},{7,5},{8,10},{9,11},{10,... | collective-permute-start | bytes 688136 | tf_op jit(solution)/shard_map/ppermute | solution.py:13
  206.8 14.7 %copy-start.4 = (bf16[256,3584]{1,0:T(8,128)(2,1)S(1)}, bf16[256,3584]{1,0:T(8,128)(2,1)}, u32[]{:S(2)}) copy-start(bf16[256,3584]{1,0:T(8,128)(2,1)} %convolution_convert_fusion) | copy-start | bytes 5505028
  208.2 13.3 %collective-permute-start.33 = (bf16[128,3584]{1,0:T(8,128)(2,1)S(1)}, bf16[128,3584]{1,0:T(8,128)(2,1)S(1)}, u32[]{:S(2)}, u32[]{:S(2)}) collective-permute-start(bf16[128,3584]{1,0:T(8,128)(2,1)S(1)} %slice.237), channel_id=1, source_target_pairs={{0,1},{1,0},{2,3},{3,2},{4,5},{5,4},{6,7},{7,6},{8,9},{9,8},{10,11... | collective-permute-start | bytes 2752520 | tf_op jit(solution)/shard_map/ppermute | solution.py:13
  208.2 13.2 %collective-permute-start.27 = (bf16[32,3584]{1,0:T(8,128)(2,1)}, bf16[32,3584]{1,0:T(8,128)(2,1)S(1)}, u32[]{:S(2)}, u32[]{:S(2)}) collective-permute-start(bf16[32,3584]{1,0:T(8,128)(2,1)} %get-tuple-element.27), channel_id=1, source_target_pairs={{0,6},{1,7},{2,4},{3,5},{4,2},{5,3},{6,0},{7,1},{8,14},{9,15},{10,... | collective-permute-start | bytes 688136 | tf_op jit(solution)/shard_map/ppermute | solution.py:13
  208.6 12.8 %collective-permute-start.26 = (bf16[32,3584]{1,0:T(8,128)(2,1)}, bf16[32,3584]{1,0:T(8,128)(2,1)S(1)}, u32[]{:S(2)}, u32[]{:S(2)}) collective-permute-start(bf16[32,3584]{1,0:T(8,128)(2,1)} %get-tuple-element.29), channel_id=1, source_target_pairs={{0,4},{1,5},{2,6},{3,7},{4,0},{5,1},{6,2},{7,3},{8,12},{9,13},{10,... | collective-permute-start | bytes 688136 | tf_op jit(solution)/shard_map/ppermute | solution.py:13
  221.8 13.6 %copy-start.13 = (bf16[64,128]{1,0:T(8,128)(2,1)S(1)}, bf16[64,128]{1,0:T(8,128)(2,1)}, u32[]{:S(2)}) copy-start(bf16[64,128]{1,0:T(8,128)(2,1)} %get-tuple-element.63) | copy-start | bytes 49156
  221.8 12.1 %collective-permute-start.34 = (bf16[32,3584]{1,0:T(8,128)(2,1)S(1)}, bf16[32,3584]{1,0:T(8,128)(2,1)S(1)}, u32[]{:S(2)}, u32[]{:S(2)}) collective-permute-start(bf16[32,3584]{1,0:T(8,128)(2,1)S(1)} %get-tuple-element.21), channel_id=1, source_target_pairs={{0,2},{1,3},{2,0},{3,1},{4,6},{5,7},{6,4},{7,5},{8,10},{9,11},{10,... | collective-permute-start | bytes 688136 | tf_op jit(solution)/shard_map/ppermute | solution.py:13
  223.3 12.0 %collective-permute-start.36 = (bf16[32,3584]{1,0:T(8,128)(2,1)S(1)}, bf16[32,3584]{1,0:T(8,128)(2,1)S(1)}, u32[]{:S(2)}, u32[]{:S(2)}) collective-permute-start(bf16[32,3584]{1,0:T(8,128)(2,1)S(1)} %get-tuple-element.18), channel_id=1, source_target_pairs={{0,6},{1,7},{2,4},{3,5},{4,2},{5,3},{6,0},{7,1},{8,14},{9,15},{10,... | collective-permute-start | bytes 688136 | tf_op jit(solution)/shard_map/ppermute | solution.py:13
  223.7 11.6 %collective-permute-start.35 = (bf16[32,3584]{1,0:T(8,128)(2,1)S(1)}, bf16[32,3584]{1,0:T(8,128)(2,1)S(1)}, u32[]{:S(2)}, u32[]{:S(2)}) collective-permute-start(bf16[32,3584]{1,0:T(8,128)(2,1)S(1)} %get-tuple-element.20), channel_id=1, source_target_pairs={{0,4},{1,5},{2,6},{3,7},{4,0},{5,1},{6,2},{7,3},{8,12},{9,13},{10,... | collective-permute-start | bytes 688136 | tf_op jit(solution)/shard_map/ppermute | solution.py:13
  235.4 23.7 %copy-start.2 = (bf16[64,3584]{1,0:T(8,128)(2,1)S(1)}, bf16[64,3584]{1,0:T(8,128)(2,1)}, u32[]{:S(2)}) copy-start(bf16[64,3584]{1,0:T(8,128)(2,1)} %copy-done.1) | copy-start | bytes 1376260
  235.9 23.2 %collective-permute-start.37 = (bf16[64,3584]{1,0:T(8,128)(2,1)S(1)}, bf16[64,3584]{1,0:T(8,128)(2,1)S(1)}, u32[]{:S(2)}, u32[]{:S(2)}) collective-permute-start(bf16[64,3584]{1,0:T(8,128)(2,1)S(1)} %convolution_convert_fusion.8), channel_id=1, source_target_pairs={{0,8},{1,9},{2,10},{3,11},{4,12},{5,13},{6,14},{7,15},{8,0},{9,1},... | collective-permute-start | bytes 1376264 | tf_op jit(solution)/shard_map/ppermute | solution.py:13

commit v2 on v1

v2 whole, which is shorter than its diff:
```python
import functools

import jax
import jax.numpy as jnp
from jax import lax
from jax.experimental import pallas as pl
from jax.experimental.pallas import tpu as pltpu
from jax.sharding import PartitionSpec as P

route_scale = 2.5
epsilon = 1e-06
CHUNKS = 1
F32 = jnp.float32
BF16 = jnp.bfloat16


def flipped(value, axis, mask):
    count = lax.axis_size(axis)
    return lax.ppermute(value, axis, [(i, i ^ mask) for i in range(count)])


def tiles_of(width, wanted=512):
    step = wanted if width % wanted == 0 else width
    return [pl.ds(low, step) for low in range(0, width, step)]


def slot_columns(picks, where, geometry):
    tok_count, capacity, room, chips = geometry
    tokens = picks.shape[0]
    base, chip = where[0], where[1]
    down = lax.broadcasted_iota(jnp.int32, (tokens, tokens), 0)
    across = lax.broadcasted_iota(jnp.int32, (tokens, tokens), 1)
    earlier = (down // tok_count == across // tok_count) & (across < down)
    chosen = [picks[:, k : k + 1].astype(F32) for k in range(picks.shape[1])]
    rows = [as_row(c, down == across) for c in chosen]
    turn = lax.broadcasted_iota(jnp.int32, (tokens, 1), 0) // tok_count
    columns = []
    for k, own in enumerate(chosen):
        before = sum(jnp.where(earlier & (own == row), 1.0, 0.0) for row in rows)
        place = jnp.sum(before, axis=1, keepdims=True).astype(jnp.int32)
        local = picks[:, k : k + 1] - base
        column = (local ^ chip) * room + turn * capacity + place
        columns.append(jnp.where((local >= 0) & (local < chips), column, -1))
    return columns


def as_row(column, diagonal):
    return jnp.sum(jnp.where(diagonal, column, 0.0), axis=0, keepdims=True)


def pack_rows(normed_ref, picks, where, block_refs, geometry):
    tokens, features = normed_ref.shape
    room = geometry[2]
    down = lax.broadcasted_iota(jnp.int32, (tokens, tokens), 0)
    across = lax.broadcasted_iota(jnp.int32, (tokens, tokens), 1)
    slots = lax.broadcasted_iota(jnp.int32, (len(block_refs) * room, tokens), 0).astype(F32)
    sender = jnp.zeros(slots.shape, F32)
    for column in slot_columns(picks, where, geometry):
        sender += jnp.where(slots == as_row(column.astype(F32), down == across), 1.0, 0.0)
    sender = sender.astype(BF16)
    for part in tiles_of(features):
        rows = jnp.dot(sender, normed_ref[:, part], preferred_element_type=F32).astype(BF16)
        for k, block in enumerate(block_refs):
            block[:, part] = rows[k * room : (k + 1) * room]


def start_kernel(geometry, where, current, picks, gain, normed, *blocks):
    wide = current[...].astype(F32)
    scale = lax.rsqrt(jnp.mean(wide * wide, axis=-1, keepdims=True) + epsilon)
    normed[...] = (wide * scale * gain[...]).astype(BF16)
    pack_rows(normed, picks[...], where, blocks, geometry)


def relay_kernel(geometry, where, normed, picks, *blocks):
    pack_rows(normed, picks[...], where, blocks, geometry)


def gate_kernel(geometry, where, near, near_picks, far, far_picks, scorer, mixing):
    room, chips = geometry[2:]
    for place, (normed, picks_ref) in enumerate(((near, near_picks), (far, far_picks))):
        picks = picks_ref[...]
        tokens, top_count = picks.shape
        raw = lax.dot_general(
            normed[...], scorer[...], (((1,), (1,)), ((), ())), preferred_element_type=F32
        )
        scores = jax.nn.sigmoid(raw)
        ids = lax.broadcasted_iota(jnp.int32, scores.shape, 1)
        chosen = [
            jnp.sum(jnp.where(ids == picks[:, k : k + 1], scores, 0.0), axis=1, keepdims=True)
            for k in range(top_count)
        ]
        total = sum(chosen)
        slots = lax.broadcasted_iota(jnp.int32, (tokens, chips * room), 1)
        mixed = jnp.zeros(slots.shape, F32)
        for score, column in zip(chosen, slot_columns(picks, where, geometry)):
            mixed += jnp.where(slots == column, route_scale * score / total, 0.0)
        high = mixed.astype(BF16)
        mixing[place, 0] = high
        mixing[place, 1] = (mixed - high.astype(F32)).astype(BF16)


def mixed_rows(mixing, place, blocks, part):
    rows = jnp.concatenate([block[:, part] for block in blocks], axis=0)
    return jnp.dot(mixing[place, 0], rows, preferred_element_type=F32) + jnp.dot(
        mixing[place, 1], rows, preferred_element_type=F32
    )


def far_mix_kernel(mixing, *refs):
    *blocks, out = refs
    for part in tiles_of(out.shape[1]):
        out[:, part] = mixed_rows(mixing, 1, blocks, part).astype(BF16)


def finish_kernel(mixing, current, beyond, *refs):
    *blocks, out = refs
    for part in tiles_of(out.shape[1]):
        near = mixed_rows(mixing, 0, blocks, part)
        out[:, part] = (
            current[:, part].astype(F32) + (near + beyond[:, part].astype(F32))
        ).astype(BF16)


def expert_kernel(count, *refs):
    blocks, weights = refs[:count], refs[count : count + 6]
    outs = refs[count + 6 : 2 * count + 6]
    gate_buf, up_buf, down_buf, hidden, sems = refs[2 * count + 6 :]
    features, units = gate_buf.shape[1:]
    room = blocks[0].shape[0]
    inner = tiles_of(units, 256)
    copies = []
    for side in range(2):
        gate_w, up_w, _ = weights[3 * side : 3 * side + 3]
        for part in inner:
            copies.append((gate_w.at[:, part], gate_buf.at[side, :, part]))
            copies.append((up_w.at[:, part], up_buf.at[side, :, part]))
    for side in range(2):
        copies.append((weights[3 * side + 2], down_buf.at[side]))
    copies = [pltpu.make_async_copy(a, b, sems.at[n]) for n, (a, b) in enumerate(copies)]
    for copy in copies:
        copy.start()
    pending = iter(copies)
    rows = jnp.concatenate([block[...] for block in blocks], axis=0)
    for side in range(2):
        for part in inner:
            next(pending).wait()
            next(pending).wait()
            gate_act = jnp.dot(rows, gate_buf[side, :, part], preferred_element_type=F32)
            upward = jnp.dot(rows, up_buf[side, :, part], preferred_element_type=F32)
            hidden[side, :, part] = (jax.nn.silu(gate_act) * upward).astype(BF16)
    next(pending).wait()
    next(pending).wait()
    for part in tiles_of(features):
        total = jnp.dot(hidden[0], down_buf[0, :, part], preferred_element_type=F32) + jnp.dot(
            hidden[1], down_buf[1, :, part], preferred_element_type=F32
        )
        total = total.astype(BF16)
        for k, out in enumerate(outs):
            out[:, part] = total[k * room : (k + 1) * room]


VMEM = pl.BlockSpec(memory_space=pltpu.VMEM)
SMEM = pl.BlockSpec(memory_space=pltpu.SMEM)
HBM = pl.BlockSpec(memory_space=pl.ANY)


def shards(
    entering_rising,
    entering_falling,
    norm_gain,
    router,
    w_gate,
    w_up,
    w_down,
    routes_rising,
    routes_falling,
):
    n_section = lax.axis_size("section")
    n_ep = lax.axis_size("ep")
    section_index = lax.axis_index("section")
    ep_index = lax.axis_index("ep")
    micro_count, tok_count, features = entering_rising.shape
    experts = router.shape[2]
    units = w_gate.shape[2]
    top_count = routes_rising.shape[3]
    sharers = n_ep // experts
    capacity = 2 * max(1, tok_count * top_count // experts)
    half = n_ep // 2
    chips = half // sharers
    where = jnp.stack([ep_index // half * chips, ep_index % half // sharers]).astype(jnp.int32)
    scorer = router[0].T
    own = (w_gate[0], w_up[0], w_down[0])
    weights = own + tuple(flipped(w, "ep", 1) for w in own)

    chunks = CHUNKS if micro_count // CHUNKS * capacity % 16 == 0 else 1
    group = micro_count // chunks
    tokens = group * tok_count
    room = group * capacity
    geometry = (tok_count, capacity, room, chips)
    block = jax.ShapeDtypeStruct((room, features), BF16)
    state = jax.ShapeDtypeStruct((tokens, features), BF16)
    params = pltpu.CompilerParams(vmem_limit_bytes=48 << 20)

    def call(kernel, out_shape, in_specs, flops, moved, scratch=()):
        return pl.pallas_call(
            kernel,
            out_shape=out_shape,
            in_specs=in_specs,
            out_specs=jax.tree.map(lambda _: VMEM, out_shape),
            scratch_shapes=scratch,
            compiler_params=params,
            cost_estimate=pl.CostEstimate(flops=flops, bytes_accessed=moved, transcendentals=0),
        )

    row_bytes = 2 * tokens * features
    pack_flops = 2 * chips * room * tokens * features
    start = call(
        functools.partial(start_kernel, geometry),
        [state] + [block] * chips,
        [SMEM, VMEM, VMEM, VMEM],
        pack_flops,
        4 * row_bytes,
    )
    relay = call(
        functools.partial(relay_kernel, geometry), [block] * chips, [SMEM, VMEM, VMEM], pack_flops, 3 * row_bytes
    )
    gates = call(
        functools.partial(gate_kernel, geometry),
        jax.ShapeDtypeStruct((2, 2, tokens, chips * room), BF16),
        [SMEM, VMEM, VMEM, VMEM, VMEM, VMEM],
        4 * tokens * features * 128,
        2 * row_bytes,
    )
    far_mix = call(far_mix_kernel, state, [VMEM] * (1 + chips), 2 * pack_flops, 3 * row_bytes)
    finish = call(finish_kernel, state, [VMEM] * (3 + chips), 2 * pack_flops, 5 * row_bytes)
    expert = call(
        functools.partial(expert_kernel, chips),
        [block] * chips,
        [VMEM] * chips + [HBM] * 6,
        12 * chips * room * features * units,
        12 * features * units,
        [
            pltpu.VMEM((2, features, units), BF16),
            pltpu.VMEM((2, features, units), BF16),
            pltpu.VMEM((2, units, features), BF16),
            pltpu.VMEM((2, chips * room, units), BF16),
            pltpu.SemaphoreType.DMA((4 * len(tiles_of(units, 256)) + 2,)),
        ],
    )

    def spread(blocks):
        return [blocks[0]] + [flipped(blocks[k], "ep", sharers * k) for k in range(1, chips)]

    def layer(current, picks, far_picks):
        normed, *near_rows = start(where, current, picks, norm_gain)
        far_normed = flipped(normed, "ep", half)
        near_out = expert(*spread(near_rows), *weights)
        far_out = expert(*spread(relay(where, far_normed, far_picks)), *weights)
        mixing = gates(where, normed, picks, far_normed, far_picks, scorer)
        beyond = flipped(far_mix(mixing, *spread(far_out)), "ep", half)
        return finish(mixing, current, beyond, *spread(near_out))

    ticks = jnp.arange(n_section, dtype=jnp.int32)[:, None, None, None]
    picks = jnp.where(section_index == ticks, routes_rising, routes_falling)
    tables = [
        a.reshape(n_section, chunks, tokens, top_count) for a in (picks, flipped(picks, "ep", half))
    ]

    def advance(tick, carry, moved):
        current, kept_rising, kept_falling = carry
        rising, falling = section_index == tick, section_index == n_section - 1 - tick
        here = [lax.dynamic_index_in_dim(a, tick, 0, keepdims=False) for a in tables]
        done = [layer(current[c], *[a[c] for a in here]) for c in range(chunks)]
        kept_rising = [jnp.where(rising, d, k) for d, k in zip(done, kept_rising)]
        kept_falling = [jnp.where(falling, d, k) for d, k in zip(done, kept_falling)]
        return [moved(d, tick) for d in done], kept_rising, kept_falling

    def swapped(done, tick):
        return flipped(done, "section", 1)

    def shifted(done, tick):
        up = lax.ppermute(done, "section", [(i, i + 1) for i in range(n_section - 1)])
        down = lax.ppermute(done, "section", [(i + 1, i) for i in range(n_section - 1)])
        return jnp.where(section_index == tick + 1, up, down)

    shape = (chunks, tokens, features)
    entered = jnp.where(section_index == 0, entering_rising, entering_falling).reshape(shape)
    empty = [jnp.zeros((tokens, features), BF16)] * chunks
    carry = ([entered[c] for c in range(chunks)], empty, empty)
    if n_section == 2:
        carry = advance(0, carry, swapped)
        carry = advance(1, carry, lambda done, tick: done)
    else:
        carry = lax.fori_loop(0, n_section, lambda t, c: advance(t, c, shifted), carry)
    _, kept_rising, kept_falling = carry
    out = (1, micro_count, tok_count, features)
    return (
        jnp.concatenate(kept_rising, axis=0).reshape(out),
        jnp.concatenate(kept_falling, axis=0).reshape(out),
    )


def solution(mesh):
    return jax.shard_map(
        shards,
        mesh=mesh,
        in_specs=(
            P(None, "ep", None),
            P(None, "ep", None),
            P("section", None),
            P("section", None, None),
            P("section", None, "ep"),
            P("section", None, "ep"),
            P("section", "ep", None),
            P("section", None, "ep", None),
            P("section", None, "ep", None),
        ),
        out_specs=(P("section", None, "ep", None), P("section", None, "ep", None)),
        check_vma=False,
    )
```

time: 261 us -> 211 us (0.81)
  matrix products: 45.3 us -> 0 us
  Pallas kernels: 0 us -> 40.2 us
  waiting for transfers between devices: 138 us -> 121 us
  local copies, waits for them, and re-layouts: 22.2 us -> 6.12 us
  starting transfers between devices: 46.1 us -> 40.5 us
  other arithmetic: 7.53 us -> 2.29 us
    dot_general x20 -> x0, matrix products: 45.3 us -> none  [the longest x4 26.7 us: experts_of(): jnp.dot(hidden, down_w, preferred_element_type=jnp.float32)]
    pallas_call x0 -> x14, Pallas kernels: none -> 40.2 us  [the longest x4 18 us: layer(): far_out = expert(*spread(relay(where, far_normed, far_picks)), *weights)]
    ppermute x38 -> x33, waiting for transfers between devices: 138 us -> 121 us  [flipped(): return lax.ppermute(value, axis, [(i, i ^ mask) for i in range(count)])]
    slice x12 -> x0, local copies, waits for them, and re-layouts: 5.75 us -> none  [the longest x4 2.87 us: experts_of(): returned = flipped(part[count:], 'ep', 1)]
    ppermute x38 -> x33, starting transfers between devices: 46.1 us -> 40.5 us  [flipped(): return lax.ppermute(value, axis, [(i, i ^ mask) for i in range(count)])]
    unnamed x88 -> x14, local copies, waits for them, and re-layouts: 9.87 us -> 4.79 us
    reduce_sum x11 -> x0, other arithmetic: 2.72 us -> none  [the longest x2 1.45 us: normalise(): jnp.mean(widened * widened, axis=-1, keepdims=True) + epsilon]
    concatenate x8 -> x0, local copies, waits for them, and re-layouts: 2.67 us -> none  [the longest x4 2.6 us: experts_of(): rows = jnp.concatenate([mine, other], axis=0)]
  transfers between devices with their start and end apart: 38 -> 33, of which waited for: 18 -> 23; matrix products, arithmetic and copies ran while one was open for 23% -> 1% of each run, Pallas kernels for 0% -> 10%
where the time goes in v2:
time: 211 us
  waiting for transfers between devices  121 us (57%)
  starting transfers between devices  40.5 us (19%)
  Pallas kernels  40.2 us (19%)
  local copies, waits for them, and re-layouts  6.12 us (3%)
  other arithmetic  2.29 us (1%)
    ppermute x33, waiting for transfers between devices, flipped(): return lax.ppermute(value, axis, [(i, i ^ mask) for i in range(count)])  121 us
    ppermute x33, starting transfers between devices, flipped(): return lax.ppermute(value, axis, [(i, i ^ mask) for i in range(count)])  40.5 us
    pallas_call x4, Pallas kernels, layer(): far_out = expert(*spread(relay(where, far_normed, far_picks)), *weights)  18 us
    pallas_call x2, Pallas kernels, layer(): near_out = expert(*spread(near_rows), *weights)  16 us
    unnamed x14, local copies, waits for them, and re-layouts  4.79 us
  transfers between devices with their start and end apart: 33, of which 23 were waited for; matrix products, arithmetic and copies ran while one was open for 1% of the time, Pallas kernels for 10%

profile of v2, /device:TPU:0, one launch (start us, length us, event | category | flops | bytes accessed | tf_op | source)
XLA Modules:
  0.0 211.1 jit_solution(3999743055578435795)
XLA Ops:
  0.6 0.5 collective-permute-start.5
  1.2 0.4 collective-permute-start.7
  1.7 0.7 copy_bitcast_fusion
  2.8 1.1 select_bitcast_fusion.2.current
  3.9 0.7 copy-done.5
  4.6 1.2 shard_map.104
  5.8 3.7 %collective-permute-start = (bf16[64,3584]{1,0:T(8,128)(2,1)S(1)}, bf16[64,3584]{1,0:T(8,128)(2,1)S(1)}, u32[]{:S(2)}, u32[]{:S(2)}) collective-permute-start(bf16[64,3584]{1,0:T(8,128)(2,1)S(1)} %get-tuple-element.36.near), channel_id=1, source_target_pairs={{0,8},{1,9},{2,10},{3,11},{4,12},{5,13},{6,14},{7,15},{8,0},{9,1},... | collective-permute-start | bytes 1376264 | tf_op jit(solution)/shard_map/ppermute | solution.py:19
  9.6 21.5 %collective-permute-done.1 = s32[2,8,8,2]{2,1,3,0:T(8,128)S(1)} collective-permute-done((s32[2,8,8,2]{2,1,3,0:T(8,128)S(1)}, s32[2,8,8,2]{2,1,3,0:T(8,128)S(1)}, u32[]{:S(2)}, u32[]{:S(2)}) %collective-permute-start.1) | collective-permute-done | bytes 1056 | tf_op jit(solution)/shard_map/ppermute | solution.py:19
  31.3 1.2 shard_map.106
  32.5 1.6 collective-permute-start.2
  34.1 0.7 collective-permute-start.3
  34.8 5.1 %collective-permute-done.2.refs_1_ = bf16[32,3584]{1,0:T(8,128)(2,1)S(1)} collective-permute-done((bf16[32,3584]{1,0:T(8,128)(2,1)S(1)}, bf16[32,3584]{1,0:T(8,128)(2,1)S(1)}, u32[]{:S(2)}, u32[]{:S(2)}) %collective-permute-start.2) | collective-permute-done | bytes 229408 | tf_op jit(solution)/shard_map/ppermute | solution.py:19
  39.9 1.9 collective-permute-start.4
  41.8 5.5 %collective-permute-done.4.refs_3_ = bf16[32,3584]{1,0:T(8,128)(2,1)S(1)} collective-permute-done((bf16[32,3584]{1,0:T(8,128)(2,1)S(1)}, bf16[32,3584]{1,0:T(8,128)(2,1)S(1)}, u32[]{:S(2)}, u32[]{:S(2)}) %collective-permute-start.4) | collective-permute-done | bytes 229408 | tf_op jit(solution)/shard_map/ppermute | solution.py:19
  47.3 2.0 copy-done
  49.4 7.8 %shard_map.107 = (bf16[32,3584]{1,0:T(8,128)(2,1)S(1)}, bf16[32,3584]{1,0:T(8,128)(2,1)S(1)}, bf16[32,3584]{1,0:T(8,128)(2,1)S(1)}, bf16[32,3584]{1,0:T(8,128)(2,1)S(1)}) custom-call(bf16[32,3584]{1,0:T(8,128)(2,1)S(1)} %get-tuple-element.37.refs_0_, bf16[32,3584]{1,0:T(8,128)(2,1)S(1)} %collective-permute-done.2.refs_1_, ...), custom_call_target="tpu_custom_call" | custom-call | flops 2818572288 | bytes 22020096 | tf_op jit(solution)/shard_map/pallas_call | solution.py:258
  57.1 1.2 collective-permute-start.8
  58.3 1.6 collective-permute-start.9
  59.9 0.8 collective-permute-start.10
  60.7 1.1 collective-permute-start.12
  61.8 1.6 collective-permute-start.13
  63.4 5.1 %collective-permute-done.8.refs_1_ = bf16[32,3584]{1,0:T(8,128)(2,1)S(1)} collective-permute-done((bf16[32,3584]{1,0:T(8,128)(2,1)S(1)}, bf16[32,3584]{1,0:T(8,128)(2,1)S(1)}, u32[]{:S(2)}, u32[]{:S(2)}) %collective-permute-start.8) | collective-permute-done | bytes 229408 | tf_op jit(solution)/shard_map/ppermute | solution.py:19
  68.5 2.6 %collective-permute-start.14 = (bf16[32,3584]{1,0:T(8,128)(2,1)S(1)}, bf16[32,3584]{1,0:T(8,128)(2,1)S(1)}, u32[]{:S(2)}, u32[]{:S(2)}) collective-permute-start(bf16[32,3584]{1,0:T(8,128)(2,1)S(1)} %get-tuple-element.48), channel_id=1, source_target_pairs={{0,6},{1,7},{2,4},{3,5},{4,2},{5,3},{6,0},{7,1},{8,14},{9,15},{10,... | collective-permute-start | bytes 688136 | tf_op jit(solution)/shard_map/ppermute | solution.py:19
  71.1 1.1 shard_map.105.mixing
  72.3 4.8 %collective-permute-done.10.refs_3_ = bf16[32,3584]{1,0:T(8,128)(2,1)S(1)} collective-permute-done((bf16[32,3584]{1,0:T(8,128)(2,1)S(1)}, bf16[32,3584]{1,0:T(8,128)(2,1)S(1)}, u32[]{:S(2)}, u32[]{:S(2)}) %collective-permute-start.10) | collective-permute-done | bytes 229408 | tf_op jit(solution)/shard_map/ppermute | solution.py:19
  77.5 2.2 %collective-permute-start.11 = (bf16[64,3584]{1,0:T(8,128)(2,1)S(1)}, bf16[64,3584]{1,0:T(8,128)(2,1)S(1)}, u32[]{:S(2)}, u32[]{:S(2)}) collective-permute-start(bf16[64,3584]{1,0:T(8,128)(2,1)S(1)} %shard_map.108), channel_id=1, source_target_pairs={{0,8},{1,9},{2,10},{3,11},{4,12},{5,13},{6,14},{7,15},{8,0},{9,1},... | collective-permute-start | bytes 1376264 | tf_op jit(solution)/shard_map/ppermute | solution.py:19
  79.6 1.2 collective-permute-done.13.refs_2_
  80.9 3.7 %collective-permute-done.14.refs_3_ = bf16[32,3584]{1,0:T(8,128)(2,1)S(1)} collective-permute-done((bf16[32,3584]{1,0:T(8,128)(2,1)S(1)}, bf16[32,3584]{1,0:T(8,128)(2,1)S(1)}, u32[]{:S(2)}, u32[]{:S(2)}) %collective-permute-start.14) | collective-permute-done | bytes 229408 | tf_op jit(solution)/shard_map/ppermute | solution.py:19
  84.6 7.7 %shard_map.109 = (bf16[32,3584]{1,0:T(8,128)(2,1)S(1)}, bf16[32,3584]{1,0:T(8,128)(2,1)S(1)}, bf16[32,3584]{1,0:T(8,128)(2,1)S(1)}, bf16[32,3584]{1,0:T(8,128)(2,1)S(1)}) custom-call(bf16[32,3584]{1,0:T(8,128)(2,1)S(1)} %get-tuple-element.45.refs_0_, bf16[32,3584]{1,0:T(8,128)(2,1)S(1)} %collective-permute-done.12.refs_1_, ...), custom_call_target="tpu_custom_call" | custom-call | flops 2818572288 | bytes 22020096 | tf_op jit(solution)/shard_map/pallas_call | solution.py:257
  92.3 1.4 collective-permute-start.15
  93.7 2.2 %collective-permute-start.17 = (bf16[32,3584]{1,0:T(8,128)(2,1)S(1)}, bf16[32,3584]{1,0:T(8,128)(2,1)S(1)}, u32[]{:S(2)}, u32[]{:S(2)}) collective-permute-start(bf16[32,3584]{1,0:T(8,128)(2,1)S(1)} %get-tuple-element.52), channel_id=1, source_target_pairs={{0,6},{1,7},{2,4},{3,5},{4,2},{5,3},{6,0},{7,1},{8,14},{9,15},{10,... | collective-permute-start | bytes 688136 | tf_op jit(solution)/shard_map/ppermute | solution.py:19
  95.8 2.6 %collective-permute-done.15.refs_1_ = bf16[32,3584]{1,0:T(8,128)(2,1)S(1)} collective-permute-done((bf16[32,3584]{1,0:T(8,128)(2,1)S(1)}, bf16[32,3584]{1,0:T(8,128)(2,1)S(1)}, u32[]{:S(2)}, u32[]{:S(2)}) %collective-permute-start.15) | collective-permute-done | bytes 229408 | tf_op jit(solution)/shard_map/ppermute | solution.py:19
  98.4 3.8 %collective-permute-done.16.refs_2_ = bf16[32,3584]{1,0:T(8,128)(2,1)S(1)} collective-permute-done((bf16[32,3584]{1,0:T(8,128)(2,1)S(1)}, bf16[32,3584]{1,0:T(8,128)(2,1)S(1)}, u32[]{:S(2)}, u32[]{:S(2)}) %collective-permute-start.16) | collective-permute-done | bytes 229408 | tf_op jit(solution)/shard_map/ppermute | solution.py:19
  102.2 3.0 %collective-permute-done.17.refs_3_ = bf16[32,3584]{1,0:T(8,128)(2,1)S(1)} collective-permute-done((bf16[32,3584]{1,0:T(8,128)(2,1)S(1)}, bf16[32,3584]{1,0:T(8,128)(2,1)S(1)}, u32[]{:S(2)}, u32[]{:S(2)}) %collective-permute-start.17) | collective-permute-done | bytes 229408 | tf_op jit(solution)/shard_map/ppermute | solution.py:19
  105.2 0.4 shard_map.110
  105.6 1.6 collective-permute-start.18
  107.3 9.1 %collective-permute-done.18.current = bf16[64,3584]{1,0:T(8,128)(2,1)S(1)} collective-permute-done((bf16[64,3584]{1,0:T(8,128)(2,1)S(1)}, bf16[64,3584]{1,0:T(8,128)(2,1)S(1)}, u32[]{:S(2)}, u32[]{:S(2)}) %collective-permute-start.18) | collective-permute-done | bytes 458784 | tf_op jit(solution)/shard_map/ppermute | solution.py:19
  116.4 1.2 shard_map.111
  117.8 18.0 %collective-permute-done.19.far.normed = bf16[64,3584]{1,0:T(8,128)(2,1)S(1)} collective-permute-done((bf16[64,3584]{1,0:T(8,128)(2,1)S(1)}, bf16[64,3584]{1,0:T(8,128)(2,1)S(1)}, u32[]{:S(2)}, u32[]{:S(2)}) %collective-permute-start.19) | collective-permute-done | bytes 458784 | tf_op jit(solution)/shard_map/ppermute | solution.py:19
  135.8 1.2 shard_map.113
  137.0 2.0 collective-permute-start.20
  139.0 1.5 collective-permute-start.22
  140.6 4.2 %collective-permute-done.20.refs_1_ = bf16[32,3584]{1,0:T(8,128)(2,1)S(1)} collective-permute-done((bf16[32,3584]{1,0:T(8,128)(2,1)S(1)}, bf16[32,3584]{1,0:T(8,128)(2,1)S(1)}, u32[]{:S(2)}, u32[]{:S(2)}) %collective-permute-start.20) | collective-permute-done | bytes 229408 | tf_op jit(solution)/shard_map/ppermute | solution.py:19
  144.8 2.7 %collective-permute-done.21.refs_2_ = bf16[32,3584]{1,0:T(8,128)(2,1)S(1)} collective-permute-done((bf16[32,3584]{1,0:T(8,128)(2,1)S(1)}, bf16[32,3584]{1,0:T(8,128)(2,1)S(1)}, u32[]{:S(2)}, u32[]{:S(2)}) %collective-permute-start.21) | collective-permute-done | bytes 229408 | tf_op jit(solution)/shard_map/ppermute | solution.py:19
  147.5 3.4 %collective-permute-done.22.refs_3_ = bf16[32,3584]{1,0:T(8,128)(2,1)S(1)} collective-permute-done((bf16[32,3584]{1,0:T(8,128)(2,1)S(1)}, bf16[32,3584]{1,0:T(8,128)(2,1)S(1)}, u32[]{:S(2)}, u32[]{:S(2)}) %collective-permute-start.22) | collective-permute-done | bytes 229408 | tf_op jit(solution)/shard_map/ppermute | solution.py:19
  151.0 2.0 copy-done.2
  153.0 7.8 %shard_map.114 = (bf16[32,3584]{1,0:T(8,128)(2,1)S(1)}, bf16[32,3584]{1,0:T(8,128)(2,1)S(1)}, bf16[32,3584]{1,0:T(8,128)(2,1)S(1)}, bf16[32,3584]{1,0:T(8,128)(2,1)S(1)}) custom-call(bf16[32,3584]{1,0:T(8,128)(2,1)S(1)} %get-tuple-element.54.refs_0_, bf16[32,3584]{1,0:T(8,128)(2,1)S(1)} %collective-permute-done.20.refs_1_, ...), custom_call_target="tpu_custom_call" | custom-call | flops 2818572288 | bytes 22020096 | tf_op jit(solution)/shard_map/pallas_call | solution.py:258
  160.9 1.7 collective-permute-start.23
  162.9 1.5 collective-permute-start.25
  164.4 1.7 collective-permute-start.27
  166.4 6.5 %collective-permute-done.23.refs_1_ = bf16[32,3584]{1,0:T(8,128)(2,1)S(1)} collective-permute-done((bf16[32,3584]{1,0:T(8,128)(2,1)S(1)}, bf16[32,3584]{1,0:T(8,128)(2,1)S(1)}, u32[]{:S(2)}, u32[]{:S(2)}) %collective-permute-start.23) | collective-permute-done | bytes 229408 | tf_op jit(solution)/shard_map/ppermute | solution.py:19
  172.9 1.4 collective-permute-start.29
  174.3 1.1 shard_map.112.mixing
  175.5 0.4 collective-permute-done.25.refs_3_
  176.3 1.1 collective-permute-done.27.refs_1_
  177.4 10.4 %collective-permute-done.28.refs_2_ = bf16[32,3584]{1,0:T(8,128)(2,1)S(1)} collective-permute-done((bf16[32,3584]{1,0:T(8,128)(2,1)S(1)}, bf16[32,3584]{1,0:T(8,128)(2,1)S(1)}, u32[]{:S(2)}, u32[]{:S(2)}) %collective-permute-start.28) | collective-permute-done | bytes 229408 | tf_op jit(solution)/shard_map/ppermute | solution.py:19
  187.8 0.8 collective-permute-done.29.refs_3_
  188.6 8.3 %shard_map.116 = (bf16[32,3584]{1,0:T(8,128)(2,1)S(1)}, bf16[32,3584]{1,0:T(8,128)(2,1)}, bf16[32,3584]{1,0:T(8,128)(2,1)S(1)}, bf16[32,3584]{1,0:T(8,128)(2,1)S(1)}) custom-call(bf16[32,3584]{1,0:T(8,128)(2,1)S(1)} %get-tuple-element.62.refs_0_, bf16[32,3584]{1,0:T(8,128)(2,1)S(1)} %collective-permute-done.27.refs_1_, ...), custom_call_target="tpu_custom_call" | custom-call | flops 2818572288 | bytes 22020096 | tf_op jit(solution)/shard_map/pallas_call | solution.py:257
  196.9 3.2 %collective-permute-start.30 = (bf16[32,3584]{1,0:T(8,128)(2,1)}, bf16[32,3584]{1,0:T(8,128)(2,1)S(1)}, u32[]{:S(2)}, u32[]{:S(2)}) collective-permute-start(bf16[32,3584]{1,0:T(8,128)(2,1)} %get-tuple-element.67), channel_id=1, source_target_pairs={{0,2},{1,3},{2,0},{3,1},{4,6},{5,7},{6,4},{7,5},{8,10},{9,11},{10,... | collective-permute-start | bytes 688136 | tf_op jit(solution)/shard_map/ppermute | solution.py:19
  200.1 1.5 collective-permute-start.32
  201.7 5.1 %collective-permute-done.30.refs_1_ = bf16[32,3584]{1,0:T(8,128)(2,1)S(1)} collective-permute-done((bf16[32,3584]{1,0:T(8,128)(2,1)}, bf16[32,3584]{1,0:T(8,128)(2,1)S(1)}, u32[]{:S(2)}, u32[]{:S(2)}) %collective-permute-start.30) | collective-permute-done | bytes 229408 | tf_op jit(solution)/shard_map/ppermute | solution.py:19
  206.8 0.7 collective-permute-done.31.refs_2_
  207.5 2.2 %collective-permute-done.32.refs_3_ = bf16[32,3584]{1,0:T(8,128)(2,1)S(1)} collective-permute-done((bf16[32,3584]{1,0:T(8,128)(2,1)S(1)}, bf16[32,3584]{1,0:T(8,128)(2,1)S(1)}, u32[]{:S(2)}, u32[]{:S(2)}) %collective-permute-start.32) | collective-permute-done | bytes 229408 | tf_op jit(solution)/shard_map/ppermute | solution.py:19
  210.1 1.0 select_bitcast_fusion
  (45 shorter events, 2.9 us)
Async XLA Ops:
  0.6 46.7 %collective-permute-start.5 = (bf16[3584,512]{1,0:T(8,128)(2,1)}, bf16[3584,512]{1,0:T(8,128)(2,1)}, u32[]{:S(2)}, u32[]{:S(2)}) collective-permute-start(bf16[3584,512]{1,0:T(8,128)(2,1)} %bitcast.32), channel_id=1, source_target_pairs={{0,1},{1,0},{2,3},{3,2},{4,5},{5,4},{6,7},{7,6},{8,9},{9,8},{10,11... | collective-permute-start | bytes 11010056 | tf_op jit(solution)/shard_map/ppermute | solution.py:19
  1.1 46.2 %collective-permute-start.6 = (bf16[3584,512]{1,0:T(8,128)(2,1)}, bf16[3584,512]{1,0:T(8,128)(2,1)}, u32[]{:S(2)}, u32[]{:S(2)}) collective-permute-start(bf16[3584,512]{1,0:T(8,128)(2,1)} %bitcast.43), channel_id=1, source_target_pairs={{0,1},{1,0},{2,3},{3,2},{4,5},{5,4},{6,7},{7,6},{8,9},{9,8},{10,11... | collective-permute-start | bytes 11010056 | tf_op jit(solution)/shard_map/ppermute | solution.py:19
  1.2 46.1 %collective-permute-start.7 = (bf16[512,3584]{1,0:T(8,128)(2,1)}, bf16[512,3584]{1,0:T(8,128)(2,1)}, u32[]{:S(2)}, u32[]{:S(2)}) collective-permute-start(bf16[512,3584]{1,0:T(8,128)(2,1)} %bitcast.48), channel_id=1, source_target_pairs={{0,1},{1,0},{2,3},{3,2},{4,5},{5,4},{6,7},{7,6},{8,9},{9,8},{10,11... | collective-permute-start | bytes 11010056 | tf_op jit(solution)/shard_map/ppermute | solution.py:19
  3.9 0.7 copy-start.5
  5.8 25.5 %collective-permute-start = (bf16[64,3584]{1,0:T(8,128)(2,1)S(1)}, bf16[64,3584]{1,0:T(8,128)(2,1)S(1)}, u32[]{:S(2)}, u32[]{:S(2)}) collective-permute-start(bf16[64,3584]{1,0:T(8,128)(2,1)S(1)} %get-tuple-element.36.near), channel_id=1, source_target_pairs={{0,8},{1,9},{2,10},{3,11},{4,12},{5,13},{6,14},{7,15},{8,0},{9,1},... | collective-permute-start | bytes 1376264 | tf_op jit(solution)/shard_map/ppermute | solution.py:19
  9.6 21.6 %collective-permute-start.1 = (s32[2,8,8,2]{2,1,3,0:T(8,128)S(1)}, s32[2,8,8,2]{2,1,3,0:T(8,128)S(1)}, u32[]{:S(2)}, u32[]{:S(2)}) collective-permute-start(s32[2,8,8,2]{2,1,3,0:T(8,128)S(1)} %broadcast_select_fusion), channel_id=1, source_target_pairs={{0,8},{1,9},{2,10},{3,11},{4,12},{5,13},{6,14},{7,15},{8,0},{9,1},... | collective-permute-start | bytes 3080 | tf_op jit(solution)/shard_map/ppermute | solution.py:19
  32.5 7.4 %collective-permute-start.2 = (bf16[32,3584]{1,0:T(8,128)(2,1)S(1)}, bf16[32,3584]{1,0:T(8,128)(2,1)S(1)}, u32[]{:S(2)}, u32[]{:S(2)}) collective-permute-start(bf16[32,3584]{1,0:T(8,128)(2,1)S(1)} %get-tuple-element.38), channel_id=1, source_target_pairs={{0,2},{1,3},{2,0},{3,1},{4,6},{5,7},{6,4},{7,5},{8,10},{9,11},{10,... | collective-permute-start | bytes 688136 | tf_op jit(solution)/shard_map/ppermute | solution.py:19
  34.1 7.7 %collective-permute-start.3 = (bf16[32,3584]{1,0:T(8,128)(2,1)S(1)}, bf16[32,3584]{1,0:T(8,128)(2,1)S(1)}, u32[]{:S(2)}, u32[]{:S(2)}) collective-permute-start(bf16[32,3584]{1,0:T(8,128)(2,1)S(1)} %get-tuple-element.39), channel_id=1, source_target_pairs={{0,4},{1,5},{2,6},{3,7},{4,0},{5,1},{6,2},{7,3},{8,12},{9,13},{10,... | collective-permute-start | bytes 688136 | tf_op jit(solution)/shard_map/ppermute | solution.py:19
  39.9 7.4 %collective-permute-start.4 = (bf16[32,3584]{1,0:T(8,128)(2,1)S(1)}, bf16[32,3584]{1,0:T(8,128)(2,1)S(1)}, u32[]{:S(2)}, u32[]{:S(2)}) collective-permute-start(bf16[32,3584]{1,0:T(8,128)(2,1)S(1)} %get-tuple-element.40), channel_id=1, source_target_pairs={{0,6},{1,7},{2,4},{3,5},{4,2},{5,3},{6,0},{7,1},{8,14},{9,15},{10,... | collective-permute-start | bytes 688136 | tf_op jit(solution)/shard_map/ppermute | solution.py:19
  47.3 2.0 copy-start
  49.4 21.8 %copy-start.4 = (bf16[1,3584,8]{1,2,0:T(8,128)(2,1)S(1)}, bf16[1,3584,8]{1,2,0:T(8,128)(2,1)}, u32[]{:S(2)}) copy-start(bf16[1,3584,8]{1,2,0:T(8,128)(2,1)} %param.12) | copy-start | bytes 172036
  49.4 35.2 %copy-start.1 = (bf16[1,3584,512]{2,1,0:T(8,128)(2,1)S(1)}, bf16[1,3584,512]{2,1,0:T(8,128)(2,1)}, u32[]{:S(2)}) copy-start(bf16[1,3584,512]{2,1,0:T(8,128)(2,1)} %param.13) | copy-start | bytes 11010052
  57.1 11.4 %collective-permute-start.8 = (bf16[32,3584]{1,0:T(8,128)(2,1)S(1)}, bf16[32,3584]{1,0:T(8,128)(2,1)S(1)}, u32[]{:S(2)}, u32[]{:S(2)}) collective-permute-start(bf16[32,3584]{1,0:T(8,128)(2,1)S(1)} %get-tuple-element.42), channel_id=1, source_target_pairs={{0,2},{1,3},{2,0},{3,1},{4,6},{5,7},{6,4},{7,5},{8,10},{9,11},{10,... | collective-permute-start | bytes 688136 | tf_op jit(solution)/shard_map/ppermute | solution.py:19
  58.3 13.9 %collective-permute-start.9 = (bf16[32,3584]{1,0:T(8,128)(2,1)S(1)}, bf16[32,3584]{1,0:T(8,128)(2,1)S(1)}, u32[]{:S(2)}, u32[]{:S(2)}) collective-permute-start(bf16[32,3584]{1,0:T(8,128)(2,1)S(1)} %get-tuple-element.43), channel_id=1, source_target_pairs={{0,4},{1,5},{2,6},{3,7},{4,0},{5,1},{6,2},{7,3},{8,12},{9,13},{10,... | collective-permute-start | bytes 688136 | tf_op jit(solution)/shard_map/ppermute | solution.py:19
  59.9 17.2 %collective-permute-start.10 = (bf16[32,3584]{1,0:T(8,128)(2,1)S(1)}, bf16[32,3584]{1,0:T(8,128)(2,1)S(1)}, u32[]{:S(2)}, u32[]{:S(2)}) collective-permute-start(bf16[32,3584]{1,0:T(8,128)(2,1)S(1)} %get-tuple-element.44), channel_id=1, source_target_pairs={{0,6},{1,7},{2,4},{3,5},{4,2},{5,3},{6,0},{7,1},{8,14},{9,15},{10,... | collective-permute-start | bytes 688136 | tf_op jit(solution)/shard_map/ppermute | solution.py:19
  60.7 18.9 %collective-permute-start.12 = (bf16[32,3584]{1,0:T(8,128)(2,1)S(1)}, bf16[32,3584]{1,0:T(8,128)(2,1)S(1)}, u32[]{:S(2)}, u32[]{:S(2)}) collective-permute-start(bf16[32,3584]{1,0:T(8,128)(2,1)S(1)} %get-tuple-element.46), channel_id=1, source_target_pairs={{0,2},{1,3},{2,0},{3,1},{4,6},{5,7},{6,4},{7,5},{8,10},{9,11},{10,... | collective-permute-start | bytes 688136 | tf_op jit(solution)/shard_map/ppermute | solution.py:19
  61.8 19.1 %collective-permute-start.13 = (bf16[32,3584]{1,0:T(8,128)(2,1)S(1)}, bf16[32,3584]{1,0:T(8,128)(2,1)S(1)}, u32[]{:S(2)}, u32[]{:S(2)}) collective-permute-start(bf16[32,3584]{1,0:T(8,128)(2,1)S(1)} %get-tuple-element.47), channel_id=1, source_target_pairs={{0,4},{1,5},{2,6},{3,7},{4,0},{5,1},{6,2},{7,3},{8,12},{9,13},{10,... | collective-permute-start | bytes 688136 | tf_op jit(solution)/shard_map/ppermute | solution.py:19
  68.5 16.0 %collective-permute-start.14 = (bf16[32,3584]{1,0:T(8,128)(2,1)S(1)}, bf16[32,3584]{1,0:T(8,128)(2,1)S(1)}, u32[]{:S(2)}, u32[]{:S(2)}) collective-permute-start(bf16[32,3584]{1,0:T(8,128)(2,1)S(1)} %get-tuple-element.48), channel_id=1, source_target_pairs={{0,6},{1,7},{2,4},{3,5},{4,2},{5,3},{6,0},{7,1},{8,14},{9,15},{10,... | collective-permute-start | bytes 688136 | tf_op jit(solution)/shard_map/ppermute | solution.py:19
  77.5 27.8 %collective-permute-start.11 = (bf16[64,3584]{1,0:T(8,128)(2,1)S(1)}, bf16[64,3584]{1,0:T(8,128)(2,1)S(1)}, u32[]{:S(2)}, u32[]{:S(2)}) collective-permute-start(bf16[64,3584]{1,0:T(8,128)(2,1)S(1)} %shard_map.108), channel_id=1, source_target_pairs={{0,8},{1,9},{2,10},{3,11},{4,12},{5,13},{6,14},{7,15},{8,0},{9,1},... | collective-permute-start | bytes 1376264 | tf_op jit(solution)/shard_map/ppermute | solution.py:19
  84.6 31.8 %copy-start.6 = (f32[1,3584]{1,0:T(1,128)S(1)}, f32[1,3584]{1,0:T(1,128)}, u32[]{:S(2)}) copy-start(f32[1,3584]{1,0:T(1,128)} %gain.3) | copy-start | bytes 43012
  92.3 6.2 %collective-permute-start.15 = (bf16[32,3584]{1,0:T(8,128)(2,1)S(1)}, bf16[32,3584]{1,0:T(8,128)(2,1)S(1)}, u32[]{:S(2)}, u32[]{:S(2)}) collective-permute-start(bf16[32,3584]{1,0:T(8,128)(2,1)S(1)} %get-tuple-element.50), channel_id=1, source_target_pairs={{0,2},{1,3},{2,0},{3,1},{4,6},{5,7},{6,4},{7,5},{8,10},{9,11},{10,... | collective-permute-start | bytes 688136 | tf_op jit(solution)/shard_map/ppermute | solution.py:19
  93.7 8.5 %collective-permute-start.16 = (bf16[32,3584]{1,0:T(8,128)(2,1)S(1)}, bf16[32,3584]{1,0:T(8,128)(2,1)S(1)}, u32[]{:S(2)}, u32[]{:S(2)}) collective-permute-start(bf16[32,3584]{1,0:T(8,128)(2,1)S(1)} %get-tuple-element.51), channel_id=1, source_target_pairs={{0,4},{1,5},{2,6},{3,7},{4,0},{5,1},{6,2},{7,3},{8,12},{9,13},{10,... | collective-permute-start | bytes 688136 | tf_op jit(solution)/shard_map/ppermute | solution.py:19
  93.7 11.6 %collective-permute-start.17 = (bf16[32,3584]{1,0:T(8,128)(2,1)S(1)}, bf16[32,3584]{1,0:T(8,128)(2,1)S(1)}, u32[]{:S(2)}, u32[]{:S(2)}) collective-permute-start(bf16[32,3584]{1,0:T(8,128)(2,1)S(1)} %get-tuple-element.52), channel_id=1, source_target_pairs={{0,6},{1,7},{2,4},{3,5},{4,2},{5,3},{6,0},{7,1},{8,14},{9,15},{10,... | collective-permute-start | bytes 688136 | tf_op jit(solution)/shard_map/ppermute | solution.py:19
  105.6 10.8 %collective-permute-start.18 = (bf16[64,3584]{1,0:T(8,128)(2,1)S(1)}, bf16[64,3584]{1,0:T(8,128)(2,1)S(1)}, u32[]{:S(2)}, u32[]{:S(2)}) collective-permute-start(bf16[64,3584]{1,0:T(8,128)(2,1)S(1)} %shard_map.110), channel_id=1, source_target_pairs={{0,16},{16,0},{1,17},{17,1},{2,18},{18,2},{3,19},{19,3},{4,20},{20... | collective-permute-start | bytes 1376264 | tf_op jit(solution)/shard_map/ppermute | solution.py:19
  117.6 18.2 %collective-permute-start.19 = (bf16[64,3584]{1,0:T(8,128)(2,1)S(1)}, bf16[64,3584]{1,0:T(8,128)(2,1)S(1)}, u32[]{:S(2)}, u32[]{:S(2)}) collective-permute-start(bf16[64,3584]{1,0:T(8,128)(2,1)S(1)} %get-tuple-element.53.near), channel_id=1, source_target_pairs={{0,8},{1,9},{2,10},{3,11},{4,12},{5,13},{6,14},{7,15},{8,0},{9,1},... | collective-permute-start | bytes 1376264 | tf_op jit(solution)/shard_map/ppermute | solution.py:19
  137.0 7.8 %collective-permute-start.20 = (bf16[32,3584]{1,0:T(8,128)(2,1)S(1)}, bf16[32,3584]{1,0:T(8,128)(2,1)S(1)}, u32[]{:S(2)}, u32[]{:S(2)}) collective-permute-start(bf16[32,3584]{1,0:T(8,128)(2,1)S(1)} %get-tuple-element.55), channel_id=1, source_target_pairs={{0,2},{1,3},{2,0},{3,1},{4,6},{5,7},{6,4},{7,5},{8,10},{9,11},{10,... | collective-permute-start | bytes 688136 | tf_op jit(solution)/shard_map/ppermute | solution.py:19
  139.0 8.5 %collective-permute-start.21 = (bf16[32,3584]{1,0:T(8,128)(2,1)S(1)}, bf16[32,3584]{1,0:T(8,128)(2,1)S(1)}, u32[]{:S(2)}, u32[]{:S(2)}) collective-permute-start(bf16[32,3584]{1,0:T(8,128)(2,1)S(1)} %get-tuple-element.56), channel_id=1, source_target_pairs={{0,4},{1,5},{2,6},{3,7},{4,0},{5,1},{6,2},{7,3},{8,12},{9,13},{10,... | collective-permute-start | bytes 688136 | tf_op jit(solution)/shard_map/ppermute | solution.py:19
  139.0 11.9 %collective-permute-start.22 = (bf16[32,3584]{1,0:T(8,128)(2,1)S(1)}, bf16[32,3584]{1,0:T(8,128)(2,1)S(1)}, u32[]{:S(2)}, u32[]{:S(2)}) collective-permute-start(bf16[32,3584]{1,0:T(8,128)(2,1)S(1)} %get-tuple-element.57), channel_id=1, source_target_pairs={{0,6},{1,7},{2,4},{3,5},{4,2},{5,3},{6,0},{7,1},{8,14},{9,15},{10,... | collective-permute-start | bytes 688136 | tf_op jit(solution)/shard_map/ppermute | solution.py:19
  151.0 2.0 copy-start.2
  153.0 35.5 %copy-start.3 = (bf16[1,3584,512]{2,1,0:T(8,128)(2,1)S(1)}, bf16[1,3584,512]{2,1,0:T(8,128)(2,1)}, u32[]{:S(2)}) copy-start(bf16[1,3584,512]{2,1,0:T(8,128)(2,1)} %param.13) | copy-start | bytes 11010052
  160.9 12.1 %collective-permute-start.23 = (bf16[32,3584]{1,0:T(8,128)(2,1)S(1)}, bf16[32,3584]{1,0:T(8,128)(2,1)S(1)}, u32[]{:S(2)}, u32[]{:S(2)}) collective-permute-start(bf16[32,3584]{1,0:T(8,128)(2,1)S(1)} %get-tuple-element.59), channel_id=1, source_target_pairs={{0,2},{1,3},{2,0},{3,1},{4,6},{5,7},{6,4},{7,5},{8,10},{9,11},{10,... | collective-permute-start | bytes 688136 | tf_op jit(solution)/shard_map/ppermute | solution.py:19
  162.6 12.8 %collective-permute-start.24 = (bf16[32,3584]{1,0:T(8,128)(2,1)S(1)}, bf16[32,3584]{1,0:T(8,128)(2,1)S(1)}, u32[]{:S(2)}, u32[]{:S(2)}) collective-permute-start(bf16[32,3584]{1,0:T(8,128)(2,1)S(1)} %get-tuple-element.60), channel_id=1, source_target_pairs={{0,4},{1,5},{2,6},{3,7},{4,0},{5,1},{6,2},{7,3},{8,12},{9,13},{10,... | collective-permute-start | bytes 688136 | tf_op jit(solution)/shard_map/ppermute | solution.py:19
  162.9 13.0 %collective-permute-start.25 = (bf16[32,3584]{1,0:T(8,128)(2,1)S(1)}, bf16[32,3584]{1,0:T(8,128)(2,1)S(1)}, u32[]{:S(2)}, u32[]{:S(2)}) collective-permute-start(bf16[32,3584]{1,0:T(8,128)(2,1)S(1)} %get-tuple-element.61), channel_id=1, source_target_pairs={{0,6},{1,7},{2,4},{3,5},{4,2},{5,3},{6,0},{7,1},{8,14},{9,15},{10,... | collective-permute-start | bytes 688136 | tf_op jit(solution)/shard_map/ppermute | solution.py:19
  164.4 13.0 %collective-permute-start.27 = (bf16[32,3584]{1,0:T(8,128)(2,1)S(1)}, bf16[32,3584]{1,0:T(8,128)(2,1)S(1)}, u32[]{:S(2)}, u32[]{:S(2)}) collective-permute-start(bf16[32,3584]{1,0:T(8,128)(2,1)S(1)} %get-tuple-element.63), channel_id=1, source_target_pairs={{0,2},{1,3},{2,0},{3,1},{4,6},{5,7},{6,4},{7,5},{8,10},{9,11},{10,... | collective-permute-start | bytes 688136 | tf_op jit(solution)/shard_map/ppermute | solution.py:19
  166.1 21.7 %collective-permute-start.28 = (bf16[32,3584]{1,0:T(8,128)(2,1)S(1)}, bf16[32,3584]{1,0:T(8,128)(2,1)S(1)}, u32[]{:S(2)}, u32[]{:S(2)}) collective-permute-start(bf16[32,3584]{1,0:T(8,128)(2,1)S(1)} %get-tuple-element.64), channel_id=1, source_target_pairs={{0,4},{1,5},{2,6},{3,7},{4,0},{5,1},{6,2},{7,3},{8,12},{9,13},{10,... | collective-permute-start | bytes 688136 | tf_op jit(solution)/shard_map/ppermute | solution.py:19
  172.9 15.6 %collective-permute-start.29 = (bf16[32,3584]{1,0:T(8,128)(2,1)S(1)}, bf16[32,3584]{1,0:T(8,128)(2,1)S(1)}, u32[]{:S(2)}, u32[]{:S(2)}) collective-permute-start(bf16[32,3584]{1,0:T(8,128)(2,1)S(1)} %get-tuple-element.65), channel_id=1, source_target_pairs={{0,6},{1,7},{2,4},{3,5},{4,2},{5,3},{6,0},{7,1},{8,14},{9,15},{10,... | collective-permute-start | bytes 688136 | tf_op jit(solution)/shard_map/ppermute | solution.py:19
  176.3 33.5 %collective-permute-start.26 = (bf16[64,3584]{1,0:T(8,128)(2,1)S(1)}, bf16[64,3584]{1,0:T(8,128)(2,1)S(1)}, u32[]{:S(2)}, u32[]{:S(2)}) collective-permute-start(bf16[64,3584]{1,0:T(8,128)(2,1)S(1)} %shard_map.115), channel_id=1, source_target_pairs={{0,8},{1,9},{2,10},{3,11},{4,12},{5,13},{6,14},{7,15},{8,0},{9,1},... | collective-permute-start | bytes 1376264 | tf_op jit(solution)/shard_map/ppermute | solution.py:19
  196.9 9.9 %collective-permute-start.30 = (bf16[32,3584]{1,0:T(8,128)(2,1)}, bf16[32,3584]{1,0:T(8,128)(2,1)S(1)}, u32[]{:S(2)}, u32[]{:S(2)}) collective-permute-start(bf16[32,3584]{1,0:T(8,128)(2,1)} %get-tuple-element.67), channel_id=1, source_target_pairs={{0,2},{1,3},{2,0},{3,1},{4,6},{5,7},{6,4},{7,5},{8,10},{9,11},{10,... | collective-permute-start | bytes 688136 | tf_op jit(solution)/shard_map/ppermute | solution.py:19
  200.1 7.4 %collective-permute-start.31 = (bf16[32,3584]{1,0:T(8,128)(2,1)S(1)}, bf16[32,3584]{1,0:T(8,128)(2,1)S(1)}, u32[]{:S(2)}, u32[]{:S(2)}) collective-permute-start(bf16[32,3584]{1,0:T(8,128)(2,1)S(1)} %get-tuple-element.68), channel_id=1, source_target_pairs={{0,4},{1,5},{2,6},{3,7},{4,0},{5,1},{6,2},{7,3},{8,12},{9,13},{10,... | collective-permute-start | bytes 688136 | tf_op jit(solution)/shard_map/ppermute | solution.py:19
  200.1 9.6 %collective-permute-start.32 = (bf16[32,3584]{1,0:T(8,128)(2,1)S(1)}, bf16[32,3584]{1,0:T(8,128)(2,1)S(1)}, u32[]{:S(2)}, u32[]{:S(2)}) collective-permute-start(bf16[32,3584]{1,0:T(8,128)(2,1)S(1)} %get-tuple-element.69), channel_id=1, source_target_pairs={{0,6},{1,7},{2,4},{3,5},{4,2},{5,3},{6,0},{7,1},{8,14},{9,15},{10,... | collective-permute-start | bytes 688136 | tf_op jit(solution)/shard_map/ppermute | solution.py:19

commit v3 on v2

--- a/solution.py
+++ b/solution.py
@@ -10,6 +10,7 @@
 route_scale = 2.5
 epsilon = 1e-06
 CHUNKS = 1
+EXPERT_VMEM = 50
 F32 = jnp.float32
 BF16 = jnp.bfloat16
 
@@ -27,7 +28,7 @@
 def slot_columns(picks, where, geometry):
     tok_count, capacity, room, chips = geometry
     tokens = picks.shape[0]
-    base, chip = where[0], where[1]
+    base = where[0]
     down = lax.broadcasted_iota(jnp.int32, (tokens, tokens), 0)
     across = lax.broadcasted_iota(jnp.int32, (tokens, tokens), 1)
     earlier = (down // tok_count == across // tok_count) & (across < down)
@@ -39,7 +40,7 @@
         before = sum(jnp.where(earlier & (own == row), 1.0, 0.0) for row in rows)
         place = jnp.sum(before, axis=1, keepdims=True).astype(jnp.int32)
         local = picks[:, k : k + 1] - base
-        column = (local ^ chip) * room + turn * capacity + place
+        column = local * room + turn * capacity + place
         columns.append(jnp.where((local >= 0) & (local < chips), column, -1))
     return columns
 
@@ -48,31 +49,30 @@
     return jnp.sum(jnp.where(diagonal, column, 0.0), axis=0, keepdims=True)
 
 
-def pack_rows(normed_ref, picks, where, block_refs, geometry):
+def pack_rows(normed_ref, picks, where, packed, geometry):
     tokens, features = normed_ref.shape
-    room = geometry[2]
     down = lax.broadcasted_iota(jnp.int32, (tokens, tokens), 0)
     across = lax.broadcasted_iota(jnp.int32, (tokens, tokens), 1)
-    slots = lax.broadcasted_iota(jnp.int32, (len(block_refs) * room, tokens), 0).astype(F32)
+    slots = lax.broadcasted_iota(jnp.int32, (packed.shape[0], tokens), 0).astype(F32)
     sender = jnp.zeros(slots.shape, F32)
     for column in slot_columns(picks, where, geometry):
         sender += jnp.where(slots == as_row(column.astype(F32), down == across), 1.0, 0.0)
     sender = sender.astype(BF16)
     for part in tiles_of(features):
-        rows = jnp.dot(sender, normed_ref[:, part], preferred_element_type=F32).astype(BF16)
-        for k, block in enumerate(block_refs):
-            block[:, part] = rows[k * room : (k + 1) * room]
-
-
-def start_kernel(geometry, where, current, picks, gain, normed, *blocks):
+        packed[:, part] = jnp.dot(
+            sender, normed_ref[:, part], preferred_element_type=F32
+        ).astype(BF16)
+
+
+def start_kernel(geometry, where, current, picks, gain, normed, packed):
     wide = current[...].astype(F32)
     scale = lax.rsqrt(jnp.mean(wide * wide, axis=-1, keepdims=True) + epsilon)
     normed[...] = (wide * scale * gain[...]).astype(BF16)
-    pack_rows(normed, picks[...], where, blocks, geometry)
-
-
-def relay_kernel(geometry, where, normed, picks, *blocks):
-    pack_rows(normed, picks[...], where, blocks, geometry)
+    pack_rows(normed, picks[...], where, packed, geometry)
+
+
+def relay_kernel(geometry, where, normed, picks, packed):
+    pack_rows(normed, picks[...], where, packed, geometry)
 
 
 def gate_kernel(geometry, where, near, near_picks, far, far_picks, scorer, mixing):
@@ -99,34 +99,29 @@
         mixing[place, 1] = (mixed - high.astype(F32)).astype(BF16)
 
 
-def mixed_rows(mixing, place, blocks, part):
-    rows = jnp.concatenate([block[:, part] for block in blocks], axis=0)
+def mixed_rows(mixing, place, returned, part):
+    rows = returned[:, part]
     return jnp.dot(mixing[place, 0], rows, preferred_element_type=F32) + jnp.dot(
         mixing[place, 1], rows, preferred_element_type=F32
     )
 
 
-def far_mix_kernel(mixing, *refs):
-    *blocks, out = refs
+def far_mix_kernel(mixing, returned, out):
     for part in tiles_of(out.shape[1]):
-        out[:, part] = mixed_rows(mixing, 1, blocks, part).astype(BF16)
-
-
-def finish_kernel(mixing, current, beyond, *refs):
-    *blocks, out = refs
+        out[:, part] = mixed_rows(mixing, 1, returned, part).astype(BF16)
+
+
+def finish_kernel(mixing, current, beyond, returned, out):
     for part in tiles_of(out.shape[1]):
-        near = mixed_rows(mixing, 0, blocks, part)
+        near = mixed_rows(mixing, 0, returned, part)
         out[:, part] = (
             current[:, part].astype(F32) + (near + beyond[:, part].astype(F32))
         ).astype(BF16)
 
 
-def expert_kernel(count, *refs):
-    blocks, weights = refs[:count], refs[count : count + 6]
-    outs = refs[count + 6 : 2 * count + 6]
-    gate_buf, up_buf, down_buf, hidden, sems = refs[2 * count + 6 :]
+def expert_kernel(arrived, *refs):
+    weights, (out, gate_buf, up_buf, down_buf, hidden, sems) = refs[:6], refs[6:]
     features, units = gate_buf.shape[1:]
-    room = blocks[0].shape[0]
     inner = tiles_of(units, 256)
     copies = []
     for side in range(2):
@@ -140,7 +135,7 @@
     for copy in copies:
         copy.start()
     pending = iter(copies)
-    rows = jnp.concatenate([block[...] for block in blocks], axis=0)
+    rows = arrived[...]
     for side in range(2):
         for part in inner:
             next(pending).wait()
@@ -154,9 +149,7 @@
         total = jnp.dot(hidden[0], down_buf[0, :, part], preferred_element_type=F32) + jnp.dot(
             hidden[1], down_buf[1, :, part], preferred_element_type=F32
         )
-        total = total.astype(BF16)
-        for k, out in enumerate(outs):
-            out[:, part] = total[k * room : (k + 1) * room]
+        out[:, part] = total.astype(BF16)
 
 
 VMEM = pl.BlockSpec(memory_space=pltpu.VMEM)
@@ -187,7 +180,7 @@
     capacity = 2 * max(1, tok_count * top_count // experts)
     half = n_ep // 2
     chips = half // sharers
-    where = jnp.stack([ep_index // half * chips, ep_index % half // sharers]).astype(jnp.int32)
+    where = (ep_index // half * chips).astype(jnp.int32)[None]
     scorer = router[0].T
     own = (w_gate[0], w_up[0], w_down[0])
     weights = own + tuple(flipped(w, "ep", 1) for w in own)
@@ -197,18 +190,17 @@
     tokens = group * tok_count
     room = group * capacity
     geometry = (tok_count, capacity, room, chips)
-    block = jax.ShapeDtypeStruct((room, features), BF16)
+    packed = jax.ShapeDtypeStruct((chips * room, features), BF16)
     state = jax.ShapeDtypeStruct((tokens, features), BF16)
-    params = pltpu.CompilerParams(vmem_limit_bytes=48 << 20)
-
-    def call(kernel, out_shape, in_specs, flops, moved, scratch=()):
+
+    def call(kernel, out_shape, in_specs, flops, moved, scratch=(), vmem=24):
         return pl.pallas_call(
             kernel,
             out_shape=out_shape,
             in_specs=in_specs,
             out_specs=jax.tree.map(lambda _: VMEM, out_shape),
             scratch_shapes=scratch,
-            compiler_params=params,
+            compiler_params=pltpu.CompilerParams(vmem_limit_bytes=vmem << 20),
             cost_estimate=pl.CostEstimate(flops=flops, bytes_accessed=moved, transcendentals=0),
         )
 
@@ -216,13 +208,13 @@
     pack_flops = 2 * chips * room * tokens * features
     start = call(
         functools.partial(start_kernel, geometry),
-        [state] + [block] * chips,
+        [state, packed],
         [SMEM, VMEM, VMEM, VMEM],
         pack_flops,
         4 * row_bytes,
     )
     relay = call(
-        functools.partial(relay_kernel, geometry), [block] * chips, [SMEM, VMEM, VMEM], pack_flops, 3 * row_bytes
+        functools.partial(relay_kernel, geometry), packed, [SMEM, VMEM, VMEM], pack_flops, 3 * row_bytes
     )
     gates = call(
         functools.partial(gate_kernel, geometry),
@@ -231,12 +223,12 @@
         4 * tokens * features * 128,
         2 * row_bytes,
     )
-    far_mix = call(far_mix_kernel, state, [VMEM] * (1 + chips), 2 * pack_flops, 3 * row_bytes)
-    finish = call(finish_kernel, state, [VMEM] * (3 + chips), 2 * pack_flops, 5 * row_bytes)
+    far_mix = call(far_mix_kernel, state, [VMEM, VMEM], 2 * pack_flops, 3 * row_bytes)
+    finish = call(finish_kernel, state, [VMEM] * 4, 2 * pack_flops, 5 * row_bytes)
     expert = call(
-        functools.partial(expert_kernel, chips),
-        [block] * chips,
-        [VMEM] * chips + [HBM] * 6,
+        expert_kernel,
+        packed,
+        [VMEM] + [HBM] * 6,
         12 * chips * room * features * units,
         12 * features * units,
         [
@@ -246,19 +238,27 @@
             pltpu.VMEM((2, chips * room, units), BF16),
             pltpu.SemaphoreType.DMA((4 * len(tiles_of(units, 256)) + 2,)),
         ],
-    )
-
-    def spread(blocks):
-        return [blocks[0]] + [flipped(blocks[k], "ep", sharers * k) for k in range(1, chips)]
+        EXPERT_VMEM,
+    )
+
+    circles = [
+        [low + core + sharers * k for k in range(chips)] for low in (0, half) for core in range(sharers)
+    ]
+
+    def spread(rows):
+        return lax.all_to_all(
+            rows, "ep", split_axis=0, concat_axis=0, tiled=True, axis_index_groups=circles
+        )
 
     def layer(current, picks, far_picks):
-        normed, *near_rows = start(where, current, picks, norm_gain)
+        normed, near_rows = start(where, current, picks, norm_gain)
         far_normed = flipped(normed, "ep", half)
-        near_out = expert(*spread(near_rows), *weights)
-        far_out = expert(*spread(relay(where, far_normed, far_picks)), *weights)
+        near_out = expert(spread(near_rows), *weights)
+        far_normed, near_out = lax.optimization_barrier((far_normed, near_out))
+        far_out = expert(spread(relay(where, far_normed, far_picks)), *weights)
         mixing = gates(where, normed, picks, far_normed, far_picks, scorer)
-        beyond = flipped(far_mix(mixing, *spread(far_out)), "ep", half)
-        return finish(mixing, current, beyond, *spread(near_out))
+        beyond = flipped(far_mix(mixing, spread(far_out)), "ep", half)
+        return finish(mixing, current, beyond, spread(near_out))
 
     ticks = jnp.arange(n_section, dtype=jnp.int32)[:, None, None, None]
     picks = jnp.where(section_index == ticks, routes_rising, routes_falling)

time: 211 us -> 204 us (0.967)
  blocking collectives: 0 us -> 53.1 us
  waiting for transfers between devices: 121 us -> 77.5 us
  starting transfers between devices: 40.5 us -> 22.6 us
  Pallas kernels: 40.2 us -> 44.1 us
  local copies, waits for them, and re-layouts: 6.12 us -> 3.06 us
    ppermute x33 -> x9, waiting for transfers between devices: 121 us -> 26.6 us  [flipped(): return lax.ppermute(value, axis, [(i, i ^ mask) for i in range(count)])]
    all_to_all x0 -> x4, blocking collectives: none -> 53.1 us  [spread(): lax.all_to_all(rows, 'ep', split_axis=0, concat_axis=0, tiled=True, axis_...]
    all_to_all x0 -> x4, waiting for transfers between devices: none -> 51 us  [spread(): lax.all_to_all(rows, 'ep', split_axis=0, concat_axis=0, tiled=True, axis_...]
    ppermute x33 -> x9, starting transfers between devices: 40.5 us -> 6.94 us  [flipped(): return lax.ppermute(value, axis, [(i, i ^ mask) for i in range(count)])]
    all_to_all x0 -> x4, starting transfers between devices: none -> 15.7 us  [spread(): lax.all_to_all(rows, 'ep', split_axis=0, concat_axis=0, tiled=True, axis_...]
    pallas_call x12, Pallas kernels: 38 us -> 42.9 us  [the longest x2 19 us: layer(): near_out = expert(spread(near_rows), *weights)]
    unnamed x14 -> x10, local copies, waits for them, and re-layouts: 4.79 us -> 1.73 us
  transfers between devices with their start and end apart: 33 -> 13, of which waited for: 23 -> 8; matrix products, arithmetic and copies ran while one was open for 1% -> 1% of each run, Pallas kernels for 10% -> 11%
where the time goes in v3:
time: 204 us; the launch traced here: 203 us
  waiting for transfers between devices  77.5 us (38%)
  blocking collectives  53.1 us (26%)
  Pallas kernels  44.1 us (22%)
  starting transfers between devices  22.6 us (11%)
  local copies, waits for them, and re-layouts  3.06 us (2%)
  other arithmetic  2.21 us (1%)
    all_to_all x4, blocking collectives, spread(): lax.all_to_all(rows, 'ep', split_axis=0, concat_axis=0, tiled=True, axis_...  53.1 us
    all_to_all x4, waiting for transfers between devices, spread(): lax.all_to_all(rows, 'ep', split_axis=0, concat_axis=0, tiled=True, axis_...  51 us
    ppermute x9, waiting for transfers between devices, flipped(): return lax.ppermute(value, axis, [(i, i ^ mask) for i in range(count)])  26.6 us
    pallas_call x2, Pallas kernels, layer(): near_out = expert(spread(near_rows), *weights)  19 us
    pallas_call x4, Pallas kernels, layer(): far_out = expert(spread(relay(where, far_normed, far_picks)), *weights)  18.4 us
    all_to_all x4, starting transfers between devices, spread(): lax.all_to_all(rows, 'ep', split_axis=0, concat_axis=0, tiled=True, axis_...  15.7 us
    ppermute x9, starting transfers between devices, flipped(): return lax.ppermute(value, axis, [(i, i ^ mask) for i in range(count)])  6.94 us
  transfers between devices with their start and end apart: 13, of which 8 were waited for; matrix products, arithmetic and copies ran while one was open for 1% of the time, Pallas kernels for 11%

profile of v3, /device:TPU:0, one launch (start us, length us, event | category | flops | bytes accessed | tf_op | source)
XLA Modules:
  0.0 203.4 jit_solution(11860761128111958736)
XLA Ops:
  0.6 0.5 collective-permute-start.1
  1.1 0.1 collective-permute-start.2
  1.2 0.4 collective-permute-start.3
  1.7 0.7 copy_bitcast_fusion
  2.4 0.1 broadcast_in_dim.49
  2.5 0.1 broadcast_in_dim.47
  2.5 0.1 broadcast_select_fusion.1
  2.6 0.1 copy.13.picks.near_picks
  2.7 1.1 select_bitcast_fusion.2.current
  3.8 0.0 copy-start.3
  3.8 0.7 copy-done.3
  4.5 1.6 shard_map.104
  6.1 4.8 %all-to-all-start = ((bf16[4,32,3584]{2,1,0:T(8,128)(2,1)}), bf16[4,32,3584]{2,1,0:T(8,128)(2,1)S(1)}, u32[]{:S(2)}, u32[]{:S(2)}) async-start(bf16[4,32,3584]{2,1,0:T(8,128)(2,1)} %bitcast.3), calls=%async_computation | async-start | bytes 1835008 | tf_op jit(solution)/shard_map/all_to_all | solution.py:249
  10.9 0.1 broadcast_select_fusion
  11.0 2.6 %collective-permute-start.4 = (s32[2,8,8,2]{2,1,3,0:T(8,128)S(1)}, s32[2,8,8,2]{2,1,3,0:T(8,128)S(1)}, u32[]{:S(2)}, u32[]{:S(2)}) collective-permute-start(s32[2,8,8,2]{2,1,3,0:T(8,128)S(1)} %broadcast_select_fusion), channel_id=1, source_target_pairs={{0,8},{1,9},{2,10},{3,11},{4,12},{5,13},{6,14},{7,15},{8,0},{9,1},... | collective-permute-start | bytes 3080 | tf_op jit(solution)/shard_map/ppermute | solution.py:20
  13.6 0.3 collective-permute-start
  14.0 8.4 %collective-permute-done.4 = s32[2,8,8,2]{2,1,3,0:T(8,128)S(1)} collective-permute-done((s32[2,8,8,2]{2,1,3,0:T(8,128)S(1)}, s32[2,8,8,2]{2,1,3,0:T(8,128)S(1)}, u32[]{:S(2)}, u32[]{:S(2)}) %collective-permute-start.4) | collective-permute-done | bytes 1056 | tf_op jit(solution)/shard_map/ppermute | solution.py:20
  22.4 0.1 copy.23
  22.5 10.4 %all-to-all-done = bf16[4,32,3584]{2,1,0:T(8,128)(2,1)S(1)} async-done(((bf16[4,32,3584]{2,1,0:T(8,128)(2,1)}), bf16[4,32,3584]{2,1,0:T(8,128)(2,1)S(1)}, u32[]{:S(2)}, u32[]{:S(2)}) %all-to-all-start) | async-done | bytes 917536 | tf_op jit(solution)/shard_map/all_to_all | solution.py:249
  33.0 0.0 collective-permute-done.1.refs_3_
  33.0 0.0 collective-permute-done.2.refs_4_
  33.0 0.0 collective-permute-done.3.refs_5_
  33.0 9.5 %shard_map.105 = bf16[128,3584]{1,0:T(8,128)(2,1)} custom-call(bf16[128,3584]{1,0:T(8,128)(2,1)S(1)} %bitcast.53, bf16[3584,512]{1,0:T(8,128)(2,1)} %bitcast.66, bf16[3584,512]{1,0:T(8,128)(2,1)} %bitcast.71, bf16[512,3584]{1,0:T(8,128)(2,1)} %bitcast.76, bf16[3584,512]{1,0:T(8,128)(2,1)} %collective-permute-done.1.refs_3_, ...), custom_call_target="tpu_custom_call" | custom-call | flops 2818572288 | bytes 22020096 | tf_op jit(solution)/shard_map/pallas_call | solution.py:256
  42.5 0.0 collective-permute-done.far.normed
  42.5 0.6 shard_map.107
  43.1 15.0 %all_to_all.88 = bf16[4,32,3584]{2,1,0:T(8,128)(2,1)S(1)} all-to-all(bf16[4,32,3584]{2,1,0:T(8,128)(2,1)S(1)} %bitcast.49), channel_id=1, replica_groups={{0,2,4,6},{1,3,5,7},{8,10,12,14},{9,11,13,15},{16,18,20,22},{17,19,21,2..., dimensions={0} | all-to-all | bytes 1835008 | tf_op jit(solution)/shard_map/all_to_all | solution.py:249
  58.1 8.6 %shard_map.108 = bf16[128,3584]{1,0:T(8,128)(2,1)S(1)} custom-call(bf16[128,3584]{1,0:T(8,128)(2,1)S(1)} %bitcast.57, bf16[3584,512]{1,0:T(8,128)(2,1)} %bitcast.67, bf16[3584,512]{1,0:T(8,128)(2,1)} %bitcast.72, bf16[512,3584]{1,0:T(8,128)(2,1)} %bitcast.77, bf16[3584,512]{1,0:T(8,128)(2,1)} %collective-permute-done.1.refs_3_, ...), custom_call_target="tpu_custom_call" | custom-call | flops 2818572288 | bytes 22020096 | tf_op jit(solution)/shard_map/pallas_call | solution.py:258
  66.7 0.0 copy-start.2
  66.7 13.8 %all_to_all.89 = bf16[4,32,3584]{2,1,0:T(8,128)(2,1)S(1)} all-to-all(bf16[4,32,3584]{2,1,0:T(8,128)(2,1)S(1)} %bitcast.58), channel_id=1, replica_groups={{0,2,4,6},{1,3,5,7},{8,10,12,14},{9,11,13,15},{16,18,20,22},{17,19,21,2..., dimensions={0} | all-to-all | bytes 1835008 | tf_op jit(solution)/shard_map/all_to_all | solution.py:249
  80.5 0.0 copy-start.4
  80.5 3.6 %all-to-all-start.3 = ((bf16[4,32,3584]{2,1,0:T(8,128)(2,1)}), bf16[4,32,3584]{2,1,0:T(8,128)(2,1)S(1)}, u32[]{:S(2)}, u32[]{:S(2)}) async-start(bf16[4,32,3584]{2,1,0:T(8,128)(2,1)} %bitcast.17), calls=%async_computation.3 | async-start | bytes 1835008 | tf_op jit(solution)/shard_map/all_to_all | solution.py:249
  84.1 0.0 copy-done.2
  84.1 0.6 shard_map.106.mixing
  84.7 0.4 shard_map.109
  85.1 0.7 collective-permute-start.5
  85.8 15.5 %all-to-all-done.3 = bf16[4,32,3584]{2,1,0:T(8,128)(2,1)S(1)} async-done(((bf16[4,32,3584]{2,1,0:T(8,128)(2,1)}), bf16[4,32,3584]{2,1,0:T(8,128)(2,1)S(1)}, u32[]{:S(2)}, u32[]{:S(2)}) %all-to-all-start.3) | async-done | bytes 917536 | tf_op jit(solution)/shard_map/all_to_all | solution.py:249
  101.4 3.8 %collective-permute-done.5.beyond = bf16[64,3584]{1,0:T(8,128)(2,1)S(1)} collective-permute-done((bf16[64,3584]{1,0:T(8,128)(2,1)S(1)}, bf16[64,3584]{1,0:T(8,128)(2,1)S(1)}, u32[]{:S(2)}, u32[]{:S(2)}) %collective-permute-start.5) | collective-permute-done | bytes 458784 | tf_op jit(solution)/shard_map/ppermute | solution.py:20
  105.2 0.4 shard_map.110
  105.6 1.6 collective-permute-start.6
  107.2 0.1 copy.19.picks.near_picks
  107.3 6.9 %collective-permute-done.6.current = bf16[64,3584]{1,0:T(8,128)(2,1)S(1)} collective-permute-done((bf16[64,3584]{1,0:T(8,128)(2,1)S(1)}, bf16[64,3584]{1,0:T(8,128)(2,1)S(1)}, u32[]{:S(2)}, u32[]{:S(2)}) %collective-permute-start.6) | collective-permute-done | bytes 458784 | tf_op jit(solution)/shard_map/ppermute | solution.py:20
  114.1 0.0 copy-done.4
  114.1 1.6 shard_map.111
  115.7 3.7 %all-to-all-start.4 = ((bf16[4,32,3584]{2,1,0:T(8,128)(2,1)}), bf16[4,32,3584]{2,1,0:T(8,128)(2,1)S(1)}, u32[]{:S(2)}, u32[]{:S(2)}) async-start(bf16[4,32,3584]{2,1,0:T(8,128)(2,1)} %bitcast.20), calls=%async_computation.4 | async-start | bytes 1835008 | tf_op jit(solution)/shard_map/all_to_all | solution.py:249
  119.4 0.5 collective-permute-start.7
  119.9 0.1 copy.24
  120.0 14.5 %all-to-all-done.4 = bf16[4,32,3584]{2,1,0:T(8,128)(2,1)S(1)} async-done(((bf16[4,32,3584]{2,1,0:T(8,128)(2,1)}), bf16[4,32,3584]{2,1,0:T(8,128)(2,1)S(1)}, u32[]{:S(2)}, u32[]{:S(2)}) %all-to-all-start.4) | async-done | bytes 917536 | tf_op jit(solution)/shard_map/all_to_all | solution.py:249
  134.5 9.5 %shard_map.112 = bf16[128,3584]{1,0:T(8,128)(2,1)} custom-call(bf16[128,3584]{1,0:T(8,128)(2,1)S(1)} %bitcast.54, bf16[3584,512]{1,0:T(8,128)(2,1)} %bitcast.68, bf16[3584,512]{1,0:T(8,128)(2,1)} %bitcast.73, bf16[512,3584]{1,0:T(8,128)(2,1)} %bitcast.78, bf16[3584,512]{1,0:T(8,128)(2,1)} %collective-permute-done.1.refs_3_, ...), custom_call_target="tpu_custom_call" | custom-call | flops 2818572288 | bytes 22020096 | tf_op jit(solution)/shard_map/pallas_call | solution.py:256
  144.0 0.0 copy-done
  144.0 0.0 collective-permute-done.7.far.normed
  144.1 0.6 shard_map.114
  144.7 12.7 %all_to_all.90 = bf16[4,32,3584]{2,1,0:T(8,128)(2,1)S(1)} all-to-all(bf16[4,32,3584]{2,1,0:T(8,128)(2,1)S(1)} %bitcast.50), channel_id=1, replica_groups={{0,2,4,6},{1,3,5,7},{8,10,12,14},{9,11,13,15},{16,18,20,22},{17,19,21,2..., dimensions={0} | all-to-all | bytes 1835008 | tf_op jit(solution)/shard_map/all_to_all | solution.py:249
  157.4 8.6 %shard_map.115 = bf16[128,3584]{1,0:T(8,128)(2,1)S(1)} custom-call(bf16[128,3584]{1,0:T(8,128)(2,1)S(1)} %bitcast.55, bf16[3584,512]{1,0:T(8,128)(2,1)} %bitcast.69, bf16[3584,512]{1,0:T(8,128)(2,1)} %bitcast.74, bf16[512,3584]{1,0:T(8,128)(2,1)} %bitcast.79, bf16[3584,512]{1,0:T(8,128)(2,1)} %collective-permute-done.1.refs_3_, ...), custom_call_target="tpu_custom_call" | custom-call | flops 2818572288 | bytes 22020096 | tf_op jit(solution)/shard_map/pallas_call | solution.py:258
  165.9 11.7 %all_to_all.91 = bf16[4,32,3584]{2,1,0:T(8,128)(2,1)S(1)} all-to-all(bf16[4,32,3584]{2,1,0:T(8,128)(2,1)S(1)} %bitcast.56), channel_id=1, replica_groups={{0,2,4,6},{1,3,5,7},{8,10,12,14},{9,11,13,15},{16,18,20,22},{17,19,21,2..., dimensions={0} | all-to-all | bytes 1835008 | tf_op jit(solution)/shard_map/all_to_all | solution.py:249
  177.6 3.5 %all-to-all-start.7 = ((bf16[4,32,3584]{2,1,0:T(8,128)(2,1)}), bf16[4,32,3584]{2,1,0:T(8,128)(2,1)S(1)}, u32[]{:S(2)}, u32[]{:S(2)}) async-start(bf16[4,32,3584]{2,1,0:T(8,128)(2,1)} %bitcast.27), calls=%async_computation.7 | async-start | bytes 1835008 | tf_op jit(solution)/shard_map/all_to_all | solution.py:249
  181.1 0.0 copy-start.1
  181.1 1.0 copy-done.1
  182.1 0.6 shard_map.113.mixing
  182.7 1.2 shard_map.116
  183.9 0.2 collective-permute-start.8
  184.1 10.5 %all-to-all-done.7 = bf16[4,32,3584]{2,1,0:T(8,128)(2,1)S(1)} async-done(((bf16[4,32,3584]{2,1,0:T(8,128)(2,1)}), bf16[4,32,3584]{2,1,0:T(8,128)(2,1)S(1)}, u32[]{:S(2)}, u32[]{:S(2)}) %all-to-all-start.7) | async-done | bytes 917536 | tf_op jit(solution)/shard_map/all_to_all | solution.py:249
  194.6 7.4 %collective-permute-done.8.beyond = bf16[64,3584]{1,0:T(8,128)(2,1)S(1)} collective-permute-done((bf16[64,3584]{1,0:T(8,128)(2,1)}, bf16[64,3584]{1,0:T(8,128)(2,1)S(1)}, u32[]{:S(2)}, u32[]{:S(2)}) %collective-permute-start.8) | collective-permute-done | bytes 458784 | tf_op jit(solution)/shard_map/ppermute | solution.py:20
  202.0 0.4 shard_map.117
  202.4 1.0 select_bitcast_fusion
  (4 shorter events, 0.0 us)
Async XLA Ops:
  0.6 32.3 %collective-permute-start.1 = (bf16[3584,512]{1,0:T(8,128)(2,1)}, bf16[3584,512]{1,0:T(8,128)(2,1)}, u32[]{:S(2)}, u32[]{:S(2)}) collective-permute-start(bf16[3584,512]{1,0:T(8,128)(2,1)} %bitcast.65), channel_id=1, source_target_pairs={{0,1},{1,0},{2,3},{3,2},{4,5},{5,4},{6,7},{7,6},{8,9},{9,8},{10,11... | collective-permute-start | bytes 11010056 | tf_op jit(solution)/shard_map/ppermute | solution.py:20
  1.1 31.8 %collective-permute-start.2 = (bf16[3584,512]{1,0:T(8,128)(2,1)}, bf16[3584,512]{1,0:T(8,128)(2,1)}, u32[]{:S(2)}, u32[]{:S(2)}) collective-permute-start(bf16[3584,512]{1,0:T(8,128)(2,1)} %bitcast.70), channel_id=1, source_target_pairs={{0,1},{1,0},{2,3},{3,2},{4,5},{5,4},{6,7},{7,6},{8,9},{9,8},{10,11... | collective-permute-start | bytes 11010056 | tf_op jit(solution)/shard_map/ppermute | solution.py:20
  1.2 31.7 %collective-permute-start.3 = (bf16[512,3584]{1,0:T(8,128)(2,1)}, bf16[512,3584]{1,0:T(8,128)(2,1)}, u32[]{:S(2)}, u32[]{:S(2)}) collective-permute-start(bf16[512,3584]{1,0:T(8,128)(2,1)} %bitcast.75), channel_id=1, source_target_pairs={{0,1},{1,0},{2,3},{3,2},{4,5},{5,4},{6,7},{7,6},{8,9},{9,8},{10,11... | collective-permute-start | bytes 11010056 | tf_op jit(solution)/shard_map/ppermute | solution.py:20
  3.8 0.7 copy-start.3
  6.1 26.9 %all-to-all-start = ((bf16[4,32,3584]{2,1,0:T(8,128)(2,1)}), bf16[4,32,3584]{2,1,0:T(8,128)(2,1)S(1)}, u32[]{:S(2)}, u32[]{:S(2)}) async-start(bf16[4,32,3584]{2,1,0:T(8,128)(2,1)} %bitcast.3), calls=%async_computation | async-start | bytes 1835008 | tf_op jit(solution)/shard_map/all_to_all | solution.py:249
  11.0 11.4 %collective-permute-start.4 = (s32[2,8,8,2]{2,1,3,0:T(8,128)S(1)}, s32[2,8,8,2]{2,1,3,0:T(8,128)S(1)}, u32[]{:S(2)}, u32[]{:S(2)}) collective-permute-start(s32[2,8,8,2]{2,1,3,0:T(8,128)S(1)} %broadcast_select_fusion), channel_id=1, source_target_pairs={{0,8},{1,9},{2,10},{3,11},{4,12},{5,13},{6,14},{7,15},{8,0},{9,1},... | collective-permute-start | bytes 3080 | tf_op jit(solution)/shard_map/ppermute | solution.py:20
  13.6 28.9 %collective-permute-start = (bf16[64,3584]{1,0:T(8,128)(2,1)S(1)}, bf16[64,3584]{1,0:T(8,128)(2,1)S(1)}, u32[]{:S(2)}, u32[]{:S(2)}) collective-permute-start(bf16[64,3584]{1,0:T(8,128)(2,1)S(1)} %get-tuple-element.10.near), channel_id=1, source_target_pairs={{0,8},{1,9},{2,10},{3,11},{4,12},{5,13},{6,14},{7,15},{8,0},{9,1},... | collective-permute-start | bytes 1376264 | tf_op jit(solution)/shard_map/ppermute | solution.py:20
  66.7 17.5 %copy-start.2 = (bf16[1,3584,8]{1,2,0:T(8,128)(2,1)S(1)}, bf16[1,3584,8]{1,2,0:T(8,128)(2,1)}, u32[]{:S(2)}) copy-start(bf16[1,3584,8]{1,2,0:T(8,128)(2,1)} %param.12) | copy-start | bytes 172036
  80.5 33.7 %copy-start.4 = (f32[1,3584]{1,0:T(1,128)S(1)}, f32[1,3584]{1,0:T(1,128)}, u32[]{:S(2)}) copy-start(f32[1,3584]{1,0:T(1,128)} %gain.3) | copy-start | bytes 43012
  80.5 20.9 %all-to-all-start.3 = ((bf16[4,32,3584]{2,1,0:T(8,128)(2,1)}), bf16[4,32,3584]{2,1,0:T(8,128)(2,1)S(1)}, u32[]{:S(2)}, u32[]{:S(2)}) async-start(bf16[4,32,3584]{2,1,0:T(8,128)(2,1)} %bitcast.17), calls=%async_computation.3 | async-start | bytes 1835008 | tf_op jit(solution)/shard_map/all_to_all | solution.py:249
  85.1 20.1 %collective-permute-start.5 = (bf16[64,3584]{1,0:T(8,128)(2,1)S(1)}, bf16[64,3584]{1,0:T(8,128)(2,1)S(1)}, u32[]{:S(2)}, u32[]{:S(2)}) collective-permute-start(bf16[64,3584]{1,0:T(8,128)(2,1)S(1)} %shard_map.109), channel_id=1, source_target_pairs={{0,8},{1,9},{2,10},{3,11},{4,12},{5,13},{6,14},{7,15},{8,0},{9,1},... | collective-permute-start | bytes 1376264 | tf_op jit(solution)/shard_map/ppermute | solution.py:20
  105.6 8.5 %collective-permute-start.6 = (bf16[64,3584]{1,0:T(8,128)(2,1)S(1)}, bf16[64,3584]{1,0:T(8,128)(2,1)S(1)}, u32[]{:S(2)}, u32[]{:S(2)}) collective-permute-start(bf16[64,3584]{1,0:T(8,128)(2,1)S(1)} %shard_map.110), channel_id=1, source_target_pairs={{0,16},{16,0},{1,17},{17,1},{2,18},{18,2},{3,19},{19,3},{4,20},{20... | collective-permute-start | bytes 1376264 | tf_op jit(solution)/shard_map/ppermute | solution.py:20
  115.7 28.3 %copy-start = (bf16[64,3584]{1,0:T(8,128)(2,1)}, bf16[64,3584]{1,0:T(8,128)(2,1)S(1)}, u32[]{:S(2)}) copy-start(bf16[64,3584]{1,0:T(8,128)(2,1)S(1)} %get-tuple-element.14.near) | copy-start | bytes 1376260
  115.7 18.8 %all-to-all-start.4 = ((bf16[4,32,3584]{2,1,0:T(8,128)(2,1)}), bf16[4,32,3584]{2,1,0:T(8,128)(2,1)S(1)}, u32[]{:S(2)}, u32[]{:S(2)}) async-start(bf16[4,32,3584]{2,1,0:T(8,128)(2,1)} %bitcast.20), calls=%async_computation.4 | async-start | bytes 1835008 | tf_op jit(solution)/shard_map/all_to_all | solution.py:249
  119.4 24.6 %collective-permute-start.7 = (bf16[64,3584]{1,0:T(8,128)(2,1)S(1)}, bf16[64,3584]{1,0:T(8,128)(2,1)S(1)}, u32[]{:S(2)}, u32[]{:S(2)}) collective-permute-start(bf16[64,3584]{1,0:T(8,128)(2,1)S(1)} %get-tuple-element.14.near), channel_id=1, source_target_pairs={{0,8},{1,9},{2,10},{3,11},{4,12},{5,13},{6,14},{7,15},{8,0},{9,1},... | collective-permute-start | bytes 1376264 | tf_op jit(solution)/shard_map/ppermute | solution.py:20
  177.6 17.0 %all-to-all-start.7 = ((bf16[4,32,3584]{2,1,0:T(8,128)(2,1)}), bf16[4,32,3584]{2,1,0:T(8,128)(2,1)S(1)}, u32[]{:S(2)}, u32[]{:S(2)}) async-start(bf16[4,32,3584]{2,1,0:T(8,128)(2,1)} %bitcast.27), calls=%async_computation.7 | async-start | bytes 1835008 | tf_op jit(solution)/shard_map/all_to_all | solution.py:249
  181.1 1.0 copy-start.1
  183.9 18.1 %collective-permute-start.8 = (bf16[64,3584]{1,0:T(8,128)(2,1)}, bf16[64,3584]{1,0:T(8,128)(2,1)S(1)}, u32[]{:S(2)}, u32[]{:S(2)}) collective-permute-start(bf16[64,3584]{1,0:T(8,128)(2,1)} %shard_map.116), channel_id=1, source_target_pairs={{0,8},{1,9},{2,10},{3,11},{4,12},{5,13},{6,14},{7,15},{8,0},{9,1},... | collective-permute-start | bytes 1376264 | tf_op jit(solution)/shard_map/ppermute | solution.py:20

commit v4 on v3

v4 whole, which is shorter than its diff:
```python
import functools

import jax
import jax.numpy as jnp
from jax import lax
from jax.experimental import pallas as pl
from jax.experimental.pallas import tpu as pltpu
from jax.sharding import PartitionSpec as P

route_scale = 2.5
epsilon = 1e-06
CHUNKS = 1
EXPERT_VMEM = 50
F32 = jnp.float32
BF16 = jnp.bfloat16


def flipped(value, axis, mask):
    count = lax.axis_size(axis)
    return lax.ppermute(value, axis, [(i, i ^ mask) for i in range(count)])


def tied(*values):
    return lax.optimization_barrier(values)


def tiles_of(width, wanted=512):
    step = wanted if width % wanted == 0 else width
    return [pl.ds(low, step) for low in range(0, width, step)]


def slot_columns(picks, where, near, geometry):
    tok_count, capacity, room, chips = geometry
    tokens = picks.shape[0]
    base, chip = where[0], where[1] if near else 0
    down = lax.broadcasted_iota(jnp.int32, (tokens, tokens), 0)
    across = lax.broadcasted_iota(jnp.int32, (tokens, tokens), 1)
    earlier = (down // tok_count == across // tok_count) & (across < down)
    chosen = [picks[:, k : k + 1].astype(F32) for k in range(picks.shape[1])]
    rows = [as_row(c, down == across) for c in chosen]
    turn = lax.broadcasted_iota(jnp.int32, (tokens, 1), 0) // tok_count
    columns = []
    for k, own in enumerate(chosen):
        before = sum(jnp.where(earlier & (own == row), 1.0, 0.0) for row in rows)
        place = jnp.sum(before, axis=1, keepdims=True).astype(jnp.int32)
        local = picks[:, k : k + 1] - base
        column = (local ^ chip) * room + turn * capacity + place
        columns.append(jnp.where((local >= 0) & (local < chips), column, -1))
    return columns


def as_row(column, diagonal):
    return jnp.sum(jnp.where(diagonal, column, 0.0), axis=0, keepdims=True)


def start_kernel(near, geometry, where, current, picks, gain, normed, *packed):
    tokens, features = normed.shape
    wide = current[...].astype(F32)
    scale = lax.rsqrt(jnp.mean(wide * wide, axis=-1, keepdims=True) + epsilon)
    normed[...] = (wide * scale * gain[...]).astype(BF16)
    room, chips = geometry[2:]
    down = lax.broadcasted_iota(jnp.int32, (tokens, tokens), 0)
    across = lax.broadcasted_iota(jnp.int32, (tokens, tokens), 1)
    slots = lax.broadcasted_iota(jnp.int32, (chips * room, tokens), 0).astype(F32)
    sender = jnp.zeros(slots.shape, F32)
    for column in slot_columns(picks[...], where, near, geometry):
        sender += jnp.where(slots == as_row(column.astype(F32), down == across), 1.0, 0.0)
    sender = sender.astype(BF16)
    for part in tiles_of(features):
        rows = jnp.dot(sender, normed[:, part], preferred_element_type=F32)
        put_blocks(packed, part, rows.astype(BF16))


def put_blocks(blocks, part, rows):
    room = rows.shape[0] // len(blocks)
    for k, block in enumerate(blocks):
        block[:, part] = rows[k * room : (k + 1) * room]


def get_blocks(blocks, part):
    return jnp.concatenate([block[:, part] for block in blocks], axis=0)


def gate_kernel(geometry, where, near, near_picks, far, far_picks, scorer, mixing):
    room, chips = geometry[2:]
    for place, (normed, picks_ref) in enumerate(((near, near_picks), (far, far_picks))):
        picks = picks_ref[...]
        tokens, top_count = picks.shape
        raw = lax.dot_general(
            normed[...], scorer[...], (((1,), (1,)), ((), ())), preferred_element_type=F32
        )
        scores = jax.nn.sigmoid(raw)
        ids = lax.broadcasted_iota(jnp.int32, scores.shape, 1)
        chosen = [
            jnp.sum(jnp.where(ids == picks[:, k : k + 1], scores, 0.0), axis=1, keepdims=True)
            for k in range(top_count)
        ]
        total = sum(chosen)
        slots = lax.broadcasted_iota(jnp.int32, (tokens, chips * room), 1)
        mixed = jnp.zeros(slots.shape, F32)
        for score, column in zip(chosen, slot_columns(picks, where, place == 0, geometry)):
            mixed += jnp.where(slots == column, route_scale * score / total, 0.0)
        high = mixed.astype(BF16)
        mixing[place, 0] = high
        mixing[place, 1] = (mixed - high.astype(F32)).astype(BF16)


def mixed_rows(mixing, place, returned, part):
    rows = get_blocks(returned, part)
    return jnp.dot(mixing[place, 0], rows, preferred_element_type=F32) + jnp.dot(
        mixing[place, 1], rows, preferred_element_type=F32
    )


def far_mix_kernel(mixing, returned, out):
    for part in tiles_of(out.shape[1]):
        out[:, part] = mixed_rows(mixing, 1, [returned], part).astype(BF16)


def finish_kernel(mixing, current, beyond, *refs):
    *returned, out = refs
    for part in tiles_of(out.shape[1]):
        near = mixed_rows(mixing, 0, returned, part)
        out[:, part] = (
            current[:, part].astype(F32) + (near + beyond[:, part].astype(F32))
        ).astype(BF16)


def expert_kernel(count, *refs):
    arrived, weights, outs = refs[:count], refs[count : count + 6], refs[count + 6 : 2 * count + 6]
    gate_buf, up_buf, down_buf, hidden, sems = refs[2 * count + 6 :]
    features, units = gate_buf.shape[1:]
    inner = tiles_of(units, 256)
    copies = []
    for side in range(2):
        gate_w, up_w, _ = weights[3 * side : 3 * side + 3]
        for part in inner:
            copies.append((gate_w.at[:, part], gate_buf.at[side, :, part]))
            copies.append((up_w.at[:, part], up_buf.at[side, :, part]))
    for part in tiles_of(features):
        for side in range(2):
            copies.append((weights[3 * side + 2].at[:, part], down_buf.at[side, :, part]))
    copies = [pltpu.make_async_copy(a, b, sems.at[n]) for n, (a, b) in enumerate(copies)]
    for copy in copies:
        copy.start()
    pending = iter(copies)
    rows = get_blocks(arrived, slice(None))
    for side in range(2):
        for part in inner:
            next(pending).wait()
            next(pending).wait()
            gate_act = jnp.dot(rows, gate_buf[side, :, part], preferred_element_type=F32)
            upward = jnp.dot(rows, up_buf[side, :, part], preferred_element_type=F32)
            hidden[side, :, part] = (jax.nn.silu(gate_act) * upward).astype(BF16)
    for part in tiles_of(features):
        next(pending).wait()
        next(pending).wait()
        total = jnp.dot(hidden[0], down_buf[0, :, part], preferred_element_type=F32) + jnp.dot(
            hidden[1], down_buf[1, :, part], preferred_element_type=F32
        )
        put_blocks(outs, part, total.astype(BF16))


VMEM = pl.BlockSpec(memory_space=pltpu.VMEM)
SMEM = pl.BlockSpec(memory_space=pltpu.SMEM)
HBM = pl.BlockSpec(memory_space=pl.ANY)


def shards(
    entering_rising,
    entering_falling,
    norm_gain,
    router,
    w_gate,
    w_up,
    w_down,
    routes_rising,
    routes_falling,
):
    n_section = lax.axis_size("section")
    n_ep = lax.axis_size("ep")
    section_index = lax.axis_index("section")
    ep_index = lax.axis_index("ep")
    micro_count, tok_count, features = entering_rising.shape
    experts = router.shape[2]
    units = w_gate.shape[2]
    top_count = routes_rising.shape[3]
    sharers = n_ep // experts
    capacity = 2 * max(1, tok_count * top_count // experts)
    half = n_ep // 2
    chips = half // sharers
    where = jnp.stack([ep_index // half * chips, ep_index % half // sharers]).astype(jnp.int32)
    scorer = router[0].T
    ticks = jnp.arange(n_section, dtype=jnp.int32)[:, None, None, None]
    picks = jnp.where(section_index == ticks, routes_rising, routes_falling)
    own = (w_gate[0], w_up[0], w_down[0])
    picks, far_picks, *own = tied(picks, flipped(picks, "ep", half), *own)
    weights = (*own, *[flipped(w, "ep", 1) for w in own])

    chunks = CHUNKS if micro_count // CHUNKS * capacity % 16 == 0 else 1
    group = micro_count // chunks
    tokens = group * tok_count
    room = group * capacity
    geometry = (tok_count, capacity, room, chips)
    block = jax.ShapeDtypeStruct((room, features), BF16)
    packed = jax.ShapeDtypeStruct((chips * room, features), BF16)
    state = jax.ShapeDtypeStruct((tokens, features), BF16)

    def call(kernel, out_shape, in_specs, flops, moved, scratch=(), vmem=24):
        return pl.pallas_call(
            kernel,
            out_shape=out_shape,
            in_specs=in_specs,
            out_specs=jax.tree.map(lambda _: VMEM, out_shape),
            scratch_shapes=scratch,
            compiler_params=pltpu.CompilerParams(vmem_limit_bytes=vmem << 20),
            cost_estimate=pl.CostEstimate(flops=flops, bytes_accessed=moved, transcendentals=0),
        )

    row_bytes = 2 * tokens * features
    pack_flops = 2 * chips * room * tokens * features
    start, far_start = [
        call(
            functools.partial(start_kernel, near, geometry),
            [state] + shapes,
            [SMEM, VMEM, VMEM, VMEM],
            pack_flops,
            4 * row_bytes,
        )
        for near, shapes in ((True, [block] * chips), (False, [packed]))
    ]
    gates = call(
        functools.partial(gate_kernel, geometry),
        jax.ShapeDtypeStruct((2, 2, tokens, chips * room), BF16),
        [SMEM, VMEM, VMEM, VMEM, VMEM, VMEM],
        4 * tokens * features * 128,
        2 * row_bytes,
    )
    far_mix = call(far_mix_kernel, state, [VMEM, VMEM], 2 * pack_flops, 3 * row_bytes)
    finish = call(finish_kernel, state, [VMEM] * (3 + chips), 2 * pack_flops, 5 * row_bytes)
    expert, far_expert = [
        call(
            functools.partial(expert_kernel, len(shapes)),
            shapes,
            [VMEM] * len(shapes) + [HBM] * 6,
            12 * chips * room * features * units,
            12 * features * units,
            [
                pltpu.VMEM((2, features, units), BF16),
                pltpu.VMEM((2, features, units), BF16),
                pltpu.VMEM((2, units, features), BF16),
                pltpu.VMEM((2, chips * room, units), BF16),
                pltpu.SemaphoreType.DMA(
                    (4 * len(tiles_of(units, 256)) + 2 * len(tiles_of(features)),)
                ),
            ],
            EXPERT_VMEM,
        )
        for shapes in ([block] * chips, [packed])
    ]

    circles = [
        [low + core + sharers * k for k in range(chips)] for low in (0, half) for core in range(sharers)
    ]

    def spread(rows):
        return lax.all_to_all(
            rows, "ep", split_axis=0, concat_axis=0, tiled=True, axis_index_groups=circles
        )

    def pass_on(blocks):
        return [blocks[0]] + [flipped(blocks[k], "ep", sharers * k) for k in range(1, chips)]

    def layer(current, far_current, picks, far_picks):
        normed, *near_rows = start(where, current, picks, norm_gain)
        far_current, *near_rows = tied(far_current, *near_rows)
        far_normed, far_rows = far_start(where, far_current, far_picks, norm_gain)
        mixing = gates(where, normed, picks, far_normed, far_picks, scorer)
        far_in, mixing = tied(spread(far_rows), mixing)
        (far_out,) = far_expert(far_in, *weights)
        far_out, *near_in = tied(far_out, *pass_on(near_rows))
        near_out = expert(*near_in, *weights)
        far_part, *near_out = tied(far_mix(mixing, spread(far_out)), *near_out)
        beyond = flipped(far_part, "ep", half)
        return finish(mixing, current, beyond, *pass_on(near_out))

    tables = [a.reshape(n_section, chunks, tokens, top_count) for a in (picks, far_picks)]

    def swapped(done, tick):
        across = [(i, (i + n_ep) % (2 * n_ep) ^ half) for i in range(2 * n_ep)]
        return flipped(done, "section", 1), lax.ppermute(done, ("section", "ep"), across)

    def advance(tick, carry, moved):
        current, far_current, kept_rising, kept_falling = carry
        rising, falling = section_index == tick, section_index == n_section - 1 - tick
        here = [lax.dynamic_index_in_dim(a, tick, 0, keepdims=False) for a in tables]
        done = [layer(current[c], far_current[c], *[a[c] for a in here]) for c in range(chunks)]
        kept_rising = [jnp.where(rising, d, k) for d, k in zip(done, kept_rising)]
        kept_falling = [jnp.where(falling, d, k) for d, k in zip(done, kept_falling)]
        moves = [moved(d, tick) for d in done]
        return [m[0] for m in moves], [m[1] for m in moves], kept_rising, kept_falling

    def shifted(done, tick):
        up = lax.ppermute(done, "section", [(i, i + 1) for i in range(n_section - 1)])
        down = lax.ppermute(done, "section", [(i + 1, i) for i in range(n_section - 1)])
        here = jnp.where(section_index == tick + 1, up, down)
        return here, flipped(here, "ep", half)

    shape = (chunks, tokens, features)
    entered = jnp.where(section_index == 0, entering_rising, entering_falling).reshape(shape)
    empty = [jnp.zeros((tokens, features), BF16)] * chunks
    entered = [entered[c] for c in range(chunks)]
    carry = (entered, [flipped(e, "ep", half) for e in entered], empty, empty)
    if n_section == 2:
        carry = advance(0, carry, swapped)
        carry = advance(1, carry, lambda done, tick: (done, done))
    else:
        carry = lax.fori_loop(0, n_section, lambda t, c: advance(t, c, shifted), carry)
    _, _, kept_rising, kept_falling = carry
    out = (1, micro_count, tok_count, features)
    return (
        jnp.concatenate(kept_rising, axis=0).reshape(out),
        jnp.concatenate(kept_falling, axis=0).reshape(out),
    )


def solution(mesh):
    return jax.shard_map(
        shards,
        mesh=mesh,
        in_specs=(
            P(None, "ep", None),
            P(None, "ep", None),
            P("section", None),
            P("section", None, None),
            P("section", None, "ep"),
            P("section", None, "ep"),
            P("section", "ep", None),
            P("section", None, "ep", None),
            P("section", None, "ep", None),
        ),
        out_specs=(P("section", None, "ep", None), P("section", None, "ep", None)),
        check_vma=False,
    )
```

time: 204 us -> 195 us (0.956)
  blocking collectives: 53.1 us -> 0 us
  starting transfers between devices: 22.6 us -> 45.9 us
  waiting for transfers between devices: 77.5 us -> 93.3 us
  Pallas kernels: 44.1 us -> 48 us
    all_to_all x4 -> x0, blocking collectives: 53.1 us -> none  [spread(): lax.all_to_all(rows, 'ep', split_axis=0, concat_axis=0, tiled=True, axis_...]
    ppermute x9 -> x20, waiting for transfers between devices: 26.6 us -> 63.7 us  [flipped(): return lax.ppermute(value, axis, [(i, i ^ mask) for i in range(count)])]
    all_to_all x4, waiting for transfers between devices: 51 us -> 19.8 us  [spread(): lax.all_to_all(rows, 'ep', split_axis=0, concat_axis=0, tiled=True, axis_...]
    ppermute x9 -> x20, starting transfers between devices: 6.94 us -> 30.4 us  [flipped(): return lax.ppermute(value, axis, [(i, i ^ mask) for i in range(count)])]
    ppermute x0 -> x1, waiting for transfers between devices: none -> 9.72 us  [swapped(): lax.ppermute(done, ('section', 'ep'), across)]
    pallas_call x12, Pallas kernels: 42.9 us -> 45.8 us  [the longest x2 18.5 us: layer(): far_out, = far_expert(far_in, *weights)]
  transfers between devices with their start and end apart: 13 -> 25, of which waited for: 8 -> 13; matrix products, arithmetic and copies ran while one was open for 1% -> 1% of each run, Pallas kernels for 11% -> 23%
where the time goes in v4:
time: 195 us; the launch traced here: 194 us
  waiting for transfers between devices  93.3 us (48%)
  Pallas kernels  48 us (25%)
  starting transfers between devices  45.9 us (24%)
  local copies, waits for them, and re-layouts  4.05 us (2%)
  other arithmetic  2.21 us (1%)
    ppermute x20, waiting for transfers between devices, flipped(): return lax.ppermute(value, axis, [(i, i ^ mask) for i in range(count)])  63.7 us
    ppermute x20, starting transfers between devices, flipped(): return lax.ppermute(value, axis, [(i, i ^ mask) for i in range(count)])  30.4 us
    all_to_all x4, waiting for transfers between devices, spread(): lax.all_to_all(rows, 'ep', split_axis=0, concat_axis=0, tiled=True, axis_...  19.8 us
    pallas_call x2, Pallas kernels, layer(): far_out, = far_expert(far_in, *weights)  18.5 us
    pallas_call x2, Pallas kernels, layer(): near_out = expert(*near_in, *weights)  18.4 us
    all_to_all x4, starting transfers between devices, spread(): lax.all_to_all(rows, 'ep', split_axis=0, concat_axis=0, tiled=True, axis_...  14.2 us
    ppermute x1, waiting for transfers between devices, swapped(): lax.ppermute(done, ('section', 'ep'), across)  9.72 us
    pallas_call x2, Pallas kernels, layer(): far_normed, far_rows = far_start(where, far_current, far_picks, norm_gain)  4.31 us
  transfers between devices with their start and end apart: 25, of which 13 were waited for; matrix products, arithmetic and copies ran while one was open for 1% of the time, Pallas kernels for 23%

profile of v4, /device:TPU:0, one launch (start us, length us, event | category | flops | bytes accessed | tf_op | source)
XLA Modules:
  0.0 194.3 jit_solution(9838416884180689309)
XLA Ops:
  0.7 0.7 copy_bitcast_fusion
  1.4 0.1 broadcast_select_fusion
  1.5 4.0 %collective-permute-start.1 = (s32[2,8,8,2]{2,1,3,0:T(8,128)S(1)}, s32[2,8,8,2]{2,1,3,0:T(8,128)S(1)}, u32[]{:S(2)}, u32[]{:S(2)}) collective-permute-start(s32[2,8,8,2]{2,1,3,0:T(8,128)S(1)} %broadcast_select_fusion), channel_id=1, source_target_pairs={{0,8},{1,9},{2,10},{3,11},{4,12},{5,13},{6,14},{7,15},{8,0},{9,1},... | collective-permute-start | bytes 3080 | tf_op jit(solution)/shard_map/ppermute | solution.py:20
  5.5 1.7 collective-permute-done.1
  7.2 0.5 collective-permute-start.3
  7.7 1.1 select_bitcast_fusion.2.current
  8.8 3.0 %collective-permute-start = (bf16[64,3584]{1,0:T(8,128)(2,1)S(1)}, bf16[64,3584]{1,0:T(8,128)(2,1)S(1)}, u32[]{:S(2)}, u32[]{:S(2)}) collective-permute-start(bf16[64,3584]{1,0:T(8,128)(2,1)S(1)} %select_bitcast_fusion.2.current), channel_id=1, source_target_pairs={{0,8},{1,9},{2,10},{3,11},{4,12},{5,13},{6,14},{7,15},{8,0},{9,1},... | collective-permute-start | bytes 1376264 | tf_op jit(solution)/shard_map/ppermute | solution.py:20
  11.8 0.1 pad_add_fusion.where
  11.9 0.1 copy.22
  12.0 0.1 copy.21
  12.1 0.7 copy-done.1
  12.8 1.9 shard_map.104
  14.7 18.1 %collective-permute-done.current = bf16[64,3584]{1,0:T(8,128)(2,1)S(1)} collective-permute-done((bf16[64,3584]{1,0:T(8,128)(2,1)S(1)}, bf16[64,3584]{1,0:T(8,128)(2,1)S(1)}, u32[]{:S(2)}, u32[]{:S(2)}) %collective-permute-start) | collective-permute-done | bytes 458784 | tf_op jit(solution)/shard_map/ppermute | solution.py:20
  32.8 0.7 copy-done.2
  33.5 2.2 %shard_map.105 = (bf16[64,3584]{1,0:T(8,128)(2,1)S(1)}, bf16[128,3584]{1,0:T(8,128)(2,1)}) custom-call(s32[2]{0:T(128)S(1)} %pad_add_fusion.where, bf16[64,3584]{1,0:T(8,128)(2,1)S(1)} %collective-permute-done.current, s32[64,2]{1,0:T(8,128)S(1)} %bitcast.38, f32[1,3584]{1,0:T(1,128)S(1)} %copy-done.2), custom_call_target="tpu_custom_call" | custom-call | flops 58720256 | bytes 1835008 | tf_op jit(solution)/shard_map/pallas_call | solution.py:277
  35.7 3.5 %all-to-all-start = ((bf16[4,32,3584]{2,1,0:T(8,128)(2,1)}), bf16[4,32,3584]{2,1,0:T(8,128)(2,1)S(1)}, u32[]{:S(2)}, u32[]{:S(2)}) async-start(bf16[4,32,3584]{2,1,0:T(8,128)(2,1)} %bitcast.10), calls=%async_computation | async-start | bytes 1835008 | tf_op jit(solution)/shard_map/all_to_all | solution.py:267
  39.2 2.0 %collective-permute-start.5 = (bf16[32,3584]{1,0:T(8,128)(2,1)}, bf16[32,3584]{1,0:T(8,128)(2,1)S(1)}, u32[]{:S(2)}, u32[]{:S(2)}) collective-permute-start(bf16[32,3584]{1,0:T(8,128)(2,1)} %get-tuple-element.79), channel_id=1, source_target_pairs={{0,2},{1,3},{2,0},{3,1},{4,6},{5,7},{6,4},{7,5},{8,10},{9,11},{10,... | collective-permute-start | bytes 688136 | tf_op jit(solution)/shard_map/ppermute | solution.py:20
  41.2 1.5 collective-permute-start.6
  42.6 1.1 shard_map.106.mixing
  43.8 9.0 %all-to-all-done = bf16[4,32,3584]{2,1,0:T(8,128)(2,1)S(1)} async-done(((bf16[4,32,3584]{2,1,0:T(8,128)(2,1)}), bf16[4,32,3584]{2,1,0:T(8,128)(2,1)S(1)}, u32[]{:S(2)}, u32[]{:S(2)}) %all-to-all-start) | async-done | bytes 917536 | tf_op jit(solution)/shard_map/all_to_all | solution.py:267
  52.8 1.5 collective-permute-start.7
  54.3 9.2 %shard_map.107 = bf16[128,3584]{1,0:T(8,128)(2,1)} custom-call(bf16[128,3584]{1,0:T(8,128)(2,1)S(1)} %bitcast.32, bf16[3584,512]{1,0:T(8,128)(2,1)} %bitcast.45, bf16[3584,512]{1,0:T(8,128)(2,1)} %bitcast.50, bf16[512,3584]{1,0:T(8,128)(2,1)} %bitcast.55, bf16[3584,512]{1,0:T(8,128)(2,1)} %collective-permute-done.2.refs_4_.refs_7_, ...), custom_call_target="tpu_custom_call" | custom-call | flops 2818572288 | bytes 22020096 | tf_op jit(solution)/shard_map/pallas_call | solution.py:280
  63.5 3.5 %all-to-all-start.1 = ((bf16[4,32,3584]{2,1,0:T(8,128)(2,1)}), bf16[4,32,3584]{2,1,0:T(8,128)(2,1)S(1)}, u32[]{:S(2)}, u32[]{:S(2)}) async-start(bf16[4,32,3584]{2,1,0:T(8,128)(2,1)} %bitcast.14), calls=%async_computation.1 | async-start | bytes 1835008 | tf_op jit(solution)/shard_map/all_to_all | solution.py:267
  67.1 8.3 %shard_map.109 = (bf16[32,3584]{1,0:T(8,128)(2,1)S(1)}, bf16[32,3584]{1,0:T(8,128)(2,1)S(1)}, bf16[32,3584]{1,0:T(8,128)(2,1)S(1)}, bf16[32,3584]{1,0:T(8,128)(2,1)S(1)}) custom-call(bf16[32,3584]{1,0:T(8,128)(2,1)S(1)} %get-tuple-element.83.refs_0_, bf16[32,3584]{1,0:T(8,128)(2,1)S(1)} %collective-permute-done.5.refs_1_, ...), custom_call_target="tpu_custom_call" | custom-call | flops 2818572288 | bytes 22020096 | tf_op jit(solution)/shard_map/pallas_call | solution.py:282
  75.4 0.7 copy-done.9
  76.0 2.1 %all-to-all-done.1 = bf16[4,32,3584]{2,1,0:T(8,128)(2,1)S(1)} async-done(((bf16[4,32,3584]{2,1,0:T(8,128)(2,1)}), bf16[4,32,3584]{2,1,0:T(8,128)(2,1)S(1)}, u32[]{:S(2)}, u32[]{:S(2)}) %all-to-all-start.1) | async-done | bytes 917536 | tf_op jit(solution)/shard_map/all_to_all | solution.py:267
  78.1 0.4 shard_map.108
  78.5 2.7 %collective-permute-start.8 = (bf16[64,3584]{1,0:T(8,128)(2,1)S(1)}, bf16[64,3584]{1,0:T(8,128)(2,1)S(1)}, u32[]{:S(2)}, u32[]{:S(2)}) collective-permute-start(bf16[64,3584]{1,0:T(8,128)(2,1)S(1)} %shard_map.108), channel_id=1, source_target_pairs={{0,8},{1,9},{2,10},{3,11},{4,12},{5,13},{6,14},{7,15},{8,0},{9,1},... | collective-permute-start | bytes 1376264 | tf_op jit(solution)/shard_map/ppermute | solution.py:20
  81.2 1.5 collective-permute-start.9
  82.7 0.6 collective-permute-start.10
  83.2 1.5 collective-permute-start.11
  84.7 4.0 %collective-permute-done.9.refs_1_ = bf16[32,3584]{1,0:T(8,128)(2,1)S(1)} collective-permute-done((bf16[32,3584]{1,0:T(8,128)(2,1)}, bf16[32,3584]{1,0:T(8,128)(2,1)S(1)}, u32[]{:S(2)}, u32[]{:S(2)}) %collective-permute-start.9) | collective-permute-done | bytes 229408 | tf_op jit(solution)/shard_map/ppermute | solution.py:20
  88.7 8.4 %collective-permute-done.10.refs_2_ = bf16[32,3584]{1,0:T(8,128)(2,1)S(1)} collective-permute-done((bf16[32,3584]{1,0:T(8,128)(2,1)S(1)}, bf16[32,3584]{1,0:T(8,128)(2,1)S(1)}, u32[]{:S(2)}, u32[]{:S(2)}) %collective-permute-start.10) | collective-permute-done | bytes 229408 | tf_op jit(solution)/shard_map/ppermute | solution.py:20
  97.2 4.5 %collective-permute-done.11.refs_3_ = bf16[32,3584]{1,0:T(8,128)(2,1)S(1)} collective-permute-done((bf16[32,3584]{1,0:T(8,128)(2,1)S(1)}, bf16[32,3584]{1,0:T(8,128)(2,1)S(1)}, u32[]{:S(2)}, u32[]{:S(2)}) %collective-permute-start.11) | collective-permute-done | bytes 229408 | tf_op jit(solution)/shard_map/ppermute | solution.py:20
  101.6 0.4 shard_map.110
  102.0 1.6 collective-permute-start.13
  103.6 1.2 collective-permute-start.12
  104.8 0.1 copy.24
  105.0 0.1 copy.23
  105.1 8.8 %collective-permute-done.13.current = bf16[64,3584]{1,0:T(8,128)(2,1)S(1)} collective-permute-done((bf16[64,3584]{1,0:T(8,128)(2,1)S(1)}, bf16[64,3584]{1,0:T(8,128)(2,1)S(1)}, u32[]{:S(2)}, u32[]{:S(2)}) %collective-permute-start.13) | collective-permute-done | bytes 458784 | tf_op jit(solution)/shard_map/ppermute | solution.py:20
  113.9 1.2 shard_map.111
  115.1 0.0 copy-start.8
  115.2 9.7 %collective-permute-done.12.current = bf16[64,3584]{1,0:T(8,128)(2,1)S(1)} collective-permute-done((bf16[64,3584]{1,0:T(8,128)(2,1)S(1)}, bf16[64,3584]{1,0:T(8,128)(2,1)S(1)}, u32[]{:S(2)}, u32[]{:S(2)}) %collective-permute-start.12) | collective-permute-done | bytes 458784 | tf_op jit(solution)/shard_map/ppermute | solution.py:291
  124.9 2.2 %shard_map.112 = (bf16[64,3584]{1,0:T(8,128)(2,1)S(1)}, bf16[128,3584]{1,0:T(8,128)(2,1)}) custom-call(s32[2]{0:T(128)S(1)} %pad_add_fusion.where, bf16[64,3584]{1,0:T(8,128)(2,1)S(1)} %collective-permute-done.12.current, s32[64,2]{1,0:T(8,128)S(1)} %bitcast.34, f32[1,3584]{1,0:T(1,128)S(1)} %copy-done.3), custom_call_target="tpu_custom_call" | custom-call | flops 58720256 | bytes 1835008 | tf_op jit(solution)/shard_map/pallas_call | solution.py:277
  127.0 3.7 %all-to-all-start.2 = ((bf16[4,32,3584]{2,1,0:T(8,128)(2,1)}), bf16[4,32,3584]{2,1,0:T(8,128)(2,1)S(1)}, u32[]{:S(2)}, u32[]{:S(2)}) async-start(bf16[4,32,3584]{2,1,0:T(8,128)(2,1)} %bitcast.18), calls=%async_computation.2 | async-start | bytes 1835008 | tf_op jit(solution)/shard_map/all_to_all | solution.py:267
  130.7 1.8 collective-permute-start.14
  132.5 1.5 collective-permute-start.15
  134.0 0.3 collective-permute-start.16
  134.3 1.1 shard_map.113.mixing
  135.4 8.8 %all-to-all-done.2 = bf16[4,32,3584]{2,1,0:T(8,128)(2,1)S(1)} async-done(((bf16[4,32,3584]{2,1,0:T(8,128)(2,1)}), bf16[4,32,3584]{2,1,0:T(8,128)(2,1)S(1)}, u32[]{:S(2)}, u32[]{:S(2)}) %all-to-all-start.2) | async-done | bytes 917536 | tf_op jit(solution)/shard_map/all_to_all | solution.py:267
  144.2 9.2 %shard_map.114 = bf16[128,3584]{1,0:T(8,128)(2,1)} custom-call(bf16[128,3584]{1,0:T(8,128)(2,1)S(1)} %bitcast.33, bf16[3584,512]{1,0:T(8,128)(2,1)} %bitcast.47, bf16[3584,512]{1,0:T(8,128)(2,1)} %bitcast.52, bf16[512,3584]{1,0:T(8,128)(2,1)} %bitcast.57, bf16[3584,512]{1,0:T(8,128)(2,1)} %collective-permute-done.2.refs_4_.refs_7_, ...), custom_call_target="tpu_custom_call" | custom-call | flops 2818572288 | bytes 22020096 | tf_op jit(solution)/shard_map/pallas_call | solution.py:280
  153.4 3.5 %all-to-all-start.3 = ((bf16[4,32,3584]{2,1,0:T(8,128)(2,1)}), bf16[4,32,3584]{2,1,0:T(8,128)(2,1)S(1)}, u32[]{:S(2)}, u32[]{:S(2)}) async-start(bf16[4,32,3584]{2,1,0:T(8,128)(2,1)} %bitcast.21), calls=%async_computation.3 | async-start | bytes 1835008 | tf_op jit(solution)/shard_map/all_to_all | solution.py:267
  157.0 10.1 %shard_map.116 = (bf16[32,3584]{1,0:T(8,128)(2,1)S(1)}, bf16[32,3584]{1,0:T(8,128)(2,1)}, bf16[32,3584]{1,0:T(8,128)(2,1)}, bf16[32,3584]{1,0:T(8,128)(2,1)S(1)}) custom-call(bf16[32,3584]{1,0:T(8,128)(2,1)S(1)} %get-tuple-element.111.refs_0_, bf16[32,3584]{1,0:T(8,128)(2,1)S(1)} %collective-permute-done.14.refs_1_, ...), custom_call_target="tpu_custom_call" | custom-call | flops 2818572288 | bytes 22020096 | tf_op jit(solution)/shard_map/pallas_call | solution.py:282
  167.1 0.7 copy-done.7
  167.8 0.4 shard_map.115
  168.2 3.1 %collective-permute-start.17 = (bf16[64,3584]{1,0:T(8,128)(2,1)S(1)}, bf16[64,3584]{1,0:T(8,128)(2,1)S(1)}, u32[]{:S(2)}, u32[]{:S(2)}) collective-permute-start(bf16[64,3584]{1,0:T(8,128)(2,1)S(1)} %shard_map.115), channel_id=1, source_target_pairs={{0,8},{1,9},{2,10},{3,11},{4,12},{5,13},{6,14},{7,15},{8,0},{9,1},... | collective-permute-start | bytes 1376264 | tf_op jit(solution)/shard_map/ppermute | solution.py:20
  171.3 1.7 collective-permute-start.18
  173.0 1.5 collective-permute-start.19
  174.5 0.3 collective-permute-start.20
  174.8 4.2 %collective-permute-done.18.refs_1_ = bf16[32,3584]{1,0:T(8,128)(2,1)S(1)} collective-permute-done((bf16[32,3584]{1,0:T(8,128)(2,1)}, bf16[32,3584]{1,0:T(8,128)(2,1)S(1)}, u32[]{:S(2)}, u32[]{:S(2)}) %collective-permute-start.18) | collective-permute-done | bytes 229408 | tf_op jit(solution)/shard_map/ppermute | solution.py:20
  179.0 8.3 %collective-permute-done.19.refs_2_ = bf16[32,3584]{1,0:T(8,128)(2,1)S(1)} collective-permute-done((bf16[32,3584]{1,0:T(8,128)(2,1)}, bf16[32,3584]{1,0:T(8,128)(2,1)S(1)}, u32[]{:S(2)}, u32[]{:S(2)}) %collective-permute-start.19) | collective-permute-done | bytes 229408 | tf_op jit(solution)/shard_map/ppermute | solution.py:20
  187.3 5.6 %collective-permute-done.20.refs_3_ = bf16[32,3584]{1,0:T(8,128)(2,1)S(1)} collective-permute-done((bf16[32,3584]{1,0:T(8,128)(2,1)}, bf16[32,3584]{1,0:T(8,128)(2,1)S(1)}, u32[]{:S(2)}, u32[]{:S(2)}) %collective-permute-start.20) | collective-permute-done | bytes 229408 | tf_op jit(solution)/shard_map/ppermute | solution.py:20
  192.9 0.4 shard_map.117
  193.3 1.0 select_bitcast_fusion
  (32 shorter events, 0.1 us)
Async XLA Ops:
  0.6 42.0 %copy-start = (bf16[1,3584,8]{1,2,0:T(8,128)(2,1)S(1)}, bf16[1,3584,8]{1,2,0:T(8,128)(2,1)}, u32[]{:S(2)}) copy-start(bf16[1,3584,8]{1,2,0:T(8,128)(2,1)} %param.12) | copy-start | bytes 172036
  1.5 5.8 %collective-permute-start.1 = (s32[2,8,8,2]{2,1,3,0:T(8,128)S(1)}, s32[2,8,8,2]{2,1,3,0:T(8,128)S(1)}, u32[]{:S(2)}, u32[]{:S(2)}) collective-permute-start(s32[2,8,8,2]{2,1,3,0:T(8,128)S(1)} %broadcast_select_fusion), channel_id=1, source_target_pairs={{0,8},{1,9},{2,10},{3,11},{4,12},{5,13},{6,14},{7,15},{8,0},{9,1},... | collective-permute-start | bytes 3080 | tf_op jit(solution)/shard_map/ppermute | solution.py:20
  7.2 45.6 %collective-permute-start.2 = (bf16[3584,512]{1,0:T(8,128)(2,1)}, bf16[3584,512]{1,0:T(8,128)(2,1)}, u32[]{:S(2)}, u32[]{:S(2)}) collective-permute-start(bf16[3584,512]{1,0:T(8,128)(2,1)} %bitcast.44), channel_id=1, source_target_pairs={{0,1},{1,0},{2,3},{3,2},{4,5},{5,4},{6,7},{7,6},{8,9},{9,8},{10,11... | collective-permute-start | bytes 11010056 | tf_op jit(solution)/shard_map/ppermute | solution.py:20
  7.2 47.1 %collective-permute-start.3 = (bf16[3584,512]{1,0:T(8,128)(2,1)}, bf16[3584,512]{1,0:T(8,128)(2,1)}, u32[]{:S(2)}, u32[]{:S(2)}) collective-permute-start(bf16[3584,512]{1,0:T(8,128)(2,1)} %bitcast.49), channel_id=1, source_target_pairs={{0,1},{1,0},{2,3},{3,2},{4,5},{5,4},{6,7},{7,6},{8,9},{9,8},{10,11... | collective-permute-start | bytes 11010056 | tf_op jit(solution)/shard_map/ppermute | solution.py:20
  7.7 46.6 %collective-permute-start.4 = (bf16[512,3584]{1,0:T(8,128)(2,1)}, bf16[512,3584]{1,0:T(8,128)(2,1)}, u32[]{:S(2)}, u32[]{:S(2)}) collective-permute-start(bf16[512,3584]{1,0:T(8,128)(2,1)} %bitcast.54), channel_id=1, source_target_pairs={{0,1},{1,0},{2,3},{3,2},{4,5},{5,4},{6,7},{7,6},{8,9},{9,8},{10,11... | collective-permute-start | bytes 11010056 | tf_op jit(solution)/shard_map/ppermute | solution.py:20
  8.8 24.0 %collective-permute-start = (bf16[64,3584]{1,0:T(8,128)(2,1)S(1)}, bf16[64,3584]{1,0:T(8,128)(2,1)S(1)}, u32[]{:S(2)}, u32[]{:S(2)}) collective-permute-start(bf16[64,3584]{1,0:T(8,128)(2,1)S(1)} %select_bitcast_fusion.2.current), channel_id=1, source_target_pairs={{0,8},{1,9},{2,10},{3,11},{4,12},{5,13},{6,14},{7,15},{8,0},{9,1},... | collective-permute-start | bytes 1376264 | tf_op jit(solution)/shard_map/ppermute | solution.py:20
  12.1 0.7 copy-start.1
  14.7 18.1 %copy-start.4 = (bf16[32,3584]{1,0:T(8,128)(2,1)}, bf16[32,3584]{1,0:T(8,128)(2,1)S(1)}, u32[]{:S(2)}) copy-start(bf16[32,3584]{1,0:T(8,128)(2,1)S(1)} %get-tuple-element.80) | copy-start | bytes 688132
  32.8 0.7 copy-start.2
  35.7 17.1 %all-to-all-start = ((bf16[4,32,3584]{2,1,0:T(8,128)(2,1)}), bf16[4,32,3584]{2,1,0:T(8,128)(2,1)S(1)}, u32[]{:S(2)}, u32[]{:S(2)}) async-start(bf16[4,32,3584]{2,1,0:T(8,128)(2,1)} %bitcast.10), calls=%async_computation | async-start | bytes 1835008 | tf_op jit(solution)/shard_map/all_to_all | solution.py:267
  39.2 24.3 %collective-permute-start.5 = (bf16[32,3584]{1,0:T(8,128)(2,1)}, bf16[32,3584]{1,0:T(8,128)(2,1)S(1)}, u32[]{:S(2)}, u32[]{:S(2)}) collective-permute-start(bf16[32,3584]{1,0:T(8,128)(2,1)} %get-tuple-element.79), channel_id=1, source_target_pairs={{0,2},{1,3},{2,0},{3,1},{4,6},{5,7},{6,4},{7,5},{8,10},{9,11},{10,... | collective-permute-start | bytes 688136 | tf_op jit(solution)/shard_map/ppermute | solution.py:20
  41.2 22.3 %collective-permute-start.6 = (bf16[32,3584]{1,0:T(8,128)(2,1)}, bf16[32,3584]{1,0:T(8,128)(2,1)S(1)}, u32[]{:S(2)}, u32[]{:S(2)}) collective-permute-start(bf16[32,3584]{1,0:T(8,128)(2,1)} %copy-done.4), channel_id=1, source_target_pairs={{0,4},{1,5},{2,6},{3,7},{4,0},{5,1},{6,2},{7,3},{8,12},{9,13},{10,... | collective-permute-start | bytes 688136 | tf_op jit(solution)/shard_map/ppermute | solution.py:20
  52.8 10.8 %collective-permute-start.7 = (bf16[32,3584]{1,0:T(8,128)(2,1)S(1)}, bf16[32,3584]{1,0:T(8,128)(2,1)S(1)}, u32[]{:S(2)}, u32[]{:S(2)}) collective-permute-start(bf16[32,3584]{1,0:T(8,128)(2,1)S(1)} %get-tuple-element.81), channel_id=1, source_target_pairs={{0,6},{1,7},{2,4},{3,5},{4,2},{5,3},{6,0},{7,1},{8,14},{9,15},{10,... | collective-permute-start | bytes 688136 | tf_op jit(solution)/shard_map/ppermute | solution.py:20
  63.5 14.6 %all-to-all-start.1 = ((bf16[4,32,3584]{2,1,0:T(8,128)(2,1)}), bf16[4,32,3584]{2,1,0:T(8,128)(2,1)S(1)}, u32[]{:S(2)}, u32[]{:S(2)}) async-start(bf16[4,32,3584]{2,1,0:T(8,128)(2,1)} %bitcast.14), calls=%async_computation.1 | async-start | bytes 1835008 | tf_op jit(solution)/shard_map/all_to_all | solution.py:267
  75.3 0.7 copy-start.9
  76.0 37.9 %copy-start.3 = (f32[1,3584]{1,0:T(1,128)S(1)}, f32[1,3584]{1,0:T(1,128)}, u32[]{:S(2)}) copy-start(f32[1,3584]{1,0:T(1,128)} %gain.7) | copy-start | bytes 43012
  78.5 23.1 %collective-permute-start.8 = (bf16[64,3584]{1,0:T(8,128)(2,1)S(1)}, bf16[64,3584]{1,0:T(8,128)(2,1)S(1)}, u32[]{:S(2)}, u32[]{:S(2)}) collective-permute-start(bf16[64,3584]{1,0:T(8,128)(2,1)S(1)} %shard_map.108), channel_id=1, source_target_pairs={{0,8},{1,9},{2,10},{3,11},{4,12},{5,13},{6,14},{7,15},{8,0},{9,1},... | collective-permute-start | bytes 1376264 | tf_op jit(solution)/shard_map/ppermute | solution.py:20
  81.2 7.5 %collective-permute-start.9 = (bf16[32,3584]{1,0:T(8,128)(2,1)}, bf16[32,3584]{1,0:T(8,128)(2,1)S(1)}, u32[]{:S(2)}, u32[]{:S(2)}) collective-permute-start(bf16[32,3584]{1,0:T(8,128)(2,1)} %copy-done.9), channel_id=1, source_target_pairs={{0,2},{1,3},{2,0},{3,1},{4,6},{5,7},{6,4},{7,5},{8,10},{9,11},{10,... | collective-permute-start | bytes 688136 | tf_op jit(solution)/shard_map/ppermute | solution.py:20
  82.7 14.5 %collective-permute-start.10 = (bf16[32,3584]{1,0:T(8,128)(2,1)S(1)}, bf16[32,3584]{1,0:T(8,128)(2,1)S(1)}, u32[]{:S(2)}, u32[]{:S(2)}) collective-permute-start(bf16[32,3584]{1,0:T(8,128)(2,1)S(1)} %get-tuple-element.94), channel_id=1, source_target_pairs={{0,4},{1,5},{2,6},{3,7},{4,0},{5,1},{6,2},{7,3},{8,12},{9,13},{10,... | collective-permute-start | bytes 688136 | tf_op jit(solution)/shard_map/ppermute | solution.py:20
  83.2 18.4 %collective-permute-start.11 = (bf16[32,3584]{1,0:T(8,128)(2,1)S(1)}, bf16[32,3584]{1,0:T(8,128)(2,1)S(1)}, u32[]{:S(2)}, u32[]{:S(2)}) collective-permute-start(bf16[32,3584]{1,0:T(8,128)(2,1)S(1)} %get-tuple-element.95), channel_id=1, source_target_pairs={{0,6},{1,7},{2,4},{3,5},{4,2},{5,3},{6,0},{7,1},{8,14},{9,15},{10,... | collective-permute-start | bytes 688136 | tf_op jit(solution)/shard_map/ppermute | solution.py:20
  102.0 11.9 %collective-permute-start.13 = (bf16[64,3584]{1,0:T(8,128)(2,1)S(1)}, bf16[64,3584]{1,0:T(8,128)(2,1)S(1)}, u32[]{:S(2)}, u32[]{:S(2)}) collective-permute-start(bf16[64,3584]{1,0:T(8,128)(2,1)S(1)} %shard_map.110), channel_id=1, source_target_pairs={{0,16},{16,0},{1,17},{17,1},{2,18},{18,2},{3,19},{19,3},{4,20},{20... | collective-permute-start | bytes 1376264 | tf_op jit(solution)/shard_map/ppermute | solution.py:20
  103.6 21.3 %collective-permute-start.12 = (bf16[64,3584]{1,0:T(8,128)(2,1)S(1)}, bf16[64,3584]{1,0:T(8,128)(2,1)S(1)}, u32[]{:S(2)}, u32[]{:S(2)}) collective-permute-start(bf16[64,3584]{1,0:T(8,128)(2,1)S(1)} %shard_map.110), channel_id=1, source_target_pairs={{0,24},{1,25},{2,26},{3,27},{4,28},{5,29},{6,30},{7,31},{8,16},{9,... | collective-permute-start | bytes 1376264 | tf_op jit(solution)/shard_map/ppermute | solution.py:291
  115.1 9.8 %copy-start.8 = (bf16[32,3584]{1,0:T(8,128)(2,1)}, bf16[32,3584]{1,0:T(8,128)(2,1)S(1)}, u32[]{:S(2)}) copy-start(bf16[32,3584]{1,0:T(8,128)(2,1)S(1)} %get-tuple-element.107) | copy-start | bytes 688132
  115.1 11.9 %copy-start.5 = (bf16[32,3584]{1,0:T(8,128)(2,1)}, bf16[32,3584]{1,0:T(8,128)(2,1)S(1)}, u32[]{:S(2)}) copy-start(bf16[32,3584]{1,0:T(8,128)(2,1)S(1)} %get-tuple-element.109) | copy-start | bytes 688132
  115.1 11.9 %copy-start.6 = (bf16[32,3584]{1,0:T(8,128)(2,1)}, bf16[32,3584]{1,0:T(8,128)(2,1)S(1)}, u32[]{:S(2)}) copy-start(bf16[32,3584]{1,0:T(8,128)(2,1)S(1)} %get-tuple-element.108) | copy-start | bytes 688132
  127.0 17.1 %all-to-all-start.2 = ((bf16[4,32,3584]{2,1,0:T(8,128)(2,1)}), bf16[4,32,3584]{2,1,0:T(8,128)(2,1)S(1)}, u32[]{:S(2)}, u32[]{:S(2)}) async-start(bf16[4,32,3584]{2,1,0:T(8,128)(2,1)} %bitcast.18), calls=%async_computation.2 | async-start | bytes 1835008 | tf_op jit(solution)/shard_map/all_to_all | solution.py:267
  130.7 22.7 %collective-permute-start.14 = (bf16[32,3584]{1,0:T(8,128)(2,1)}, bf16[32,3584]{1,0:T(8,128)(2,1)S(1)}, u32[]{:S(2)}, u32[]{:S(2)}) collective-permute-start(bf16[32,3584]{1,0:T(8,128)(2,1)} %copy-done.8), channel_id=1, source_target_pairs={{0,2},{1,3},{2,0},{3,1},{4,6},{5,7},{6,4},{7,5},{8,10},{9,11},{10,... | collective-permute-start | bytes 688136 | tf_op jit(solution)/shard_map/ppermute | solution.py:20
  132.5 20.9 %collective-permute-start.15 = (bf16[32,3584]{1,0:T(8,128)(2,1)}, bf16[32,3584]{1,0:T(8,128)(2,1)}, u32[]{:S(2)}, u32[]{:S(2)}) collective-permute-start(bf16[32,3584]{1,0:T(8,128)(2,1)} %copy-done.6), channel_id=1, source_target_pairs={{0,4},{1,5},{2,6},{3,7},{4,0},{5,1},{6,2},{7,3},{8,12},{9,13},{10,... | collective-permute-start | bytes 688136 | tf_op jit(solution)/shard_map/ppermute | solution.py:20
  134.0 19.4 %collective-permute-start.16 = (bf16[32,3584]{1,0:T(8,128)(2,1)}, bf16[32,3584]{1,0:T(8,128)(2,1)}, u32[]{:S(2)}, u32[]{:S(2)}) collective-permute-start(bf16[32,3584]{1,0:T(8,128)(2,1)} %copy-done.5), channel_id=1, source_target_pairs={{0,6},{1,7},{2,4},{3,5},{4,2},{5,3},{6,0},{7,1},{8,14},{9,15},{10,... | collective-permute-start | bytes 688136 | tf_op jit(solution)/shard_map/ppermute | solution.py:20
  153.4 14.3 %all-to-all-start.3 = ((bf16[4,32,3584]{2,1,0:T(8,128)(2,1)}), bf16[4,32,3584]{2,1,0:T(8,128)(2,1)S(1)}, u32[]{:S(2)}, u32[]{:S(2)}) async-start(bf16[4,32,3584]{2,1,0:T(8,128)(2,1)} %bitcast.21), calls=%async_computation.3 | async-start | bytes 1835008 | tf_op jit(solution)/shard_map/all_to_all | solution.py:267
  167.0 0.7 copy-start.7
  168.2 24.8 %collective-permute-start.17 = (bf16[64,3584]{1,0:T(8,128)(2,1)S(1)}, bf16[64,3584]{1,0:T(8,128)(2,1)S(1)}, u32[]{:S(2)}, u32[]{:S(2)}) collective-permute-start(bf16[64,3584]{1,0:T(8,128)(2,1)S(1)} %shard_map.115), channel_id=1, source_target_pairs={{0,8},{1,9},{2,10},{3,11},{4,12},{5,13},{6,14},{7,15},{8,0},{9,1},... | collective-permute-start | bytes 1376264 | tf_op jit(solution)/shard_map/ppermute | solution.py:20
  171.3 7.7 %collective-permute-start.18 = (bf16[32,3584]{1,0:T(8,128)(2,1)}, bf16[32,3584]{1,0:T(8,128)(2,1)S(1)}, u32[]{:S(2)}, u32[]{:S(2)}) collective-permute-start(bf16[32,3584]{1,0:T(8,128)(2,1)} %get-tuple-element.121), channel_id=1, source_target_pairs={{0,2},{1,3},{2,0},{3,1},{4,6},{5,7},{6,4},{7,5},{8,10},{9,11},{10,... | collective-permute-start | bytes 688136 | tf_op jit(solution)/shard_map/ppermute | solution.py:20
  173.0 14.3 %collective-permute-start.19 = (bf16[32,3584]{1,0:T(8,128)(2,1)}, bf16[32,3584]{1,0:T(8,128)(2,1)S(1)}, u32[]{:S(2)}, u32[]{:S(2)}) collective-permute-start(bf16[32,3584]{1,0:T(8,128)(2,1)} %get-tuple-element.122), channel_id=1, source_target_pairs={{0,4},{1,5},{2,6},{3,7},{4,0},{5,1},{6,2},{7,3},{8,12},{9,13},{10,... | collective-permute-start | bytes 688136 | tf_op jit(solution)/shard_map/ppermute | solution.py:20
  174.5 18.4 %collective-permute-start.20 = (bf16[32,3584]{1,0:T(8,128)(2,1)}, bf16[32,3584]{1,0:T(8,128)(2,1)S(1)}, u32[]{:S(2)}, u32[]{:S(2)}) collective-permute-start(bf16[32,3584]{1,0:T(8,128)(2,1)} %copy-done.7), channel_id=1, source_target_pairs={{0,6},{1,7},{2,4},{3,5},{4,2},{5,3},{6,0},{7,1},{8,14},{9,15},{10,... | collective-permute-start | bytes 688136 | tf_op jit(solution)/shard_map/ppermute | solution.py:20

commit v5 on v4

--- a/solution.py
+++ b/solution.py
@@ -9,7 +9,6 @@
 
 route_scale = 2.5
 epsilon = 1e-06
-CHUNKS = 1
 EXPERT_VMEM = 50
 F32 = jnp.float32
 BF16 = jnp.bfloat16
@@ -22,6 +21,10 @@
 
 def tied(*values):
     return lax.optimization_barrier(values)
+
+
+def after(first, *values):
+    return lax.optimization_barrier((first, *values))[1:]
 
 
 def tiles_of(width, wanted=512):
@@ -81,14 +84,19 @@
     return jnp.concatenate([block[:, part] for block in blocks], axis=0)
 
 
-def gate_kernel(geometry, where, near, near_picks, far, far_picks, scorer, mixing):
+def gate_kernel(geometry, where, near, near_picks, far_picks, scorer, *refs):
     room, chips = geometry[2:]
-    for place, (normed, picks_ref) in enumerate(((near, near_picks), (far, far_picks))):
+    *far, mixing = refs
+    for place, (parts, picks_ref) in enumerate((((near,), near_picks), (far, far_picks))):
         picks = picks_ref[...]
         tokens, top_count = picks.shape
-        raw = lax.dot_general(
-            normed[...], scorer[...], (((1,), (1,)), ((), ())), preferred_element_type=F32
-        )
+        raw = [
+            lax.dot_general(
+                normed[...], scorer[...], (((1,), (1,)), ((), ())), preferred_element_type=F32
+            )
+            for normed in parts
+        ]
+        raw = jnp.concatenate(raw, axis=0)
         scores = jax.nn.sigmoid(raw)
         ids = lax.broadcasted_iota(jnp.int32, scores.shape, 1)
         chosen = [
@@ -121,14 +129,23 @@
     *returned, out = refs
     for part in tiles_of(out.shape[1]):
         near = mixed_rows(mixing, 0, returned, part)
-        out[:, part] = (
-            current[:, part].astype(F32) + (near + beyond[:, part].astype(F32))
-        ).astype(BF16)
-
-
-def expert_kernel(count, *refs):
-    arrived, weights, outs = refs[:count], refs[count : count + 6], refs[count + 6 : 2 * count + 6]
-    gate_buf, up_buf, down_buf, hidden, sems = refs[2 * count + 6 :]
+        total = current[:, part].astype(F32) + (near + beyond[:, part].astype(F32))
+        out[:, part] = total.astype(BF16)
+
+
+def last_kernel(section, mixing, current, beyond, first, *refs):
+    *returned, rising, falling = refs
+    for part in tiles_of(first.shape[1]):
+        near = mixed_rows(mixing, 0, returned, part)
+        last = current[:, part].astype(F32) + (near + beyond[:, part].astype(F32))
+        earlier = first[:, part].astype(F32)
+        rising[:, part] = jnp.where(section[0] == 0, earlier, last).astype(BF16)
+        falling[:, part] = jnp.where(section[0] == 0, last, earlier).astype(BF16)
+
+
+def expert_kernel(sources, chips, *refs):
+    arrived, weights, refs = refs[:sources], refs[sources : sources + 6], refs[sources + 6 :]
+    *outs, gate_buf, up_buf, down_buf, hidden, sems = refs
     features, units = gate_buf.shape[1:]
     inner = tiles_of(units, 256)
     copies = []
@@ -144,7 +161,13 @@
     for copy in copies:
         copy.start()
     pending = iter(copies)
-    rows = get_blocks(arrived, slice(None))
+    if chips:
+        share = arrived[0].shape[0] // chips
+        rows = jnp.concatenate(
+            [piece[k * share : (k + 1) * share] for k in range(chips) for piece in arrived], axis=0
+        )
+    else:
+        rows = get_blocks(arrived, slice(None))
     for side in range(2):
         for part in inner:
             next(pending).wait()
@@ -194,13 +217,10 @@
     ticks = jnp.arange(n_section, dtype=jnp.int32)[:, None, None, None]
     picks = jnp.where(section_index == ticks, routes_rising, routes_falling)
     own = (w_gate[0], w_up[0], w_down[0])
-    picks, far_picks, *own = tied(picks, flipped(picks, "ep", half), *own)
-    weights = (*own, *[flipped(w, "ep", 1) for w in own])
-
-    chunks = CHUNKS if micro_count // CHUNKS * capacity % 16 == 0 else 1
-    group = micro_count // chunks
-    tokens = group * tok_count
-    room = group * capacity
+    far_picks = flipped(picks, "ep", half)
+
+    tokens = micro_count * tok_count
+    room = micro_count * capacity
     geometry = (tok_count, capacity, room, chips)
     block = jax.ShapeDtypeStruct((room, features), BF16)
     packed = jax.ShapeDtypeStruct((chips * room, features), BF16)
@@ -219,30 +239,39 @@
 
     row_bytes = 2 * tokens * features
     pack_flops = 2 * chips * room * tokens * features
-    start, far_start = [
-        call(
-            functools.partial(start_kernel, near, geometry),
-            [state] + shapes,
+    start = call(
+        functools.partial(start_kernel, True, geometry),
+        [state] + [block] * chips,
+        [SMEM, VMEM, VMEM, VMEM],
+        pack_flops,
+        4 * row_bytes,
+    )
+
+    def far_start(cut):
+        piece = jax.ShapeDtypeStruct((tokens // cut, features), BF16)
+        some = jax.ShapeDtypeStruct((chips * room // cut, features), BF16)
+        return call(
+            functools.partial(start_kernel, False, (tok_count, capacity, room // cut, chips)),
+            [piece, some],
             [SMEM, VMEM, VMEM, VMEM],
-            pack_flops,
-            4 * row_bytes,
-        )
-        for near, shapes in ((True, [block] * chips), (False, [packed]))
-    ]
-    gates = call(
-        functools.partial(gate_kernel, geometry),
-        jax.ShapeDtypeStruct((2, 2, tokens, chips * room), BF16),
-        [SMEM, VMEM, VMEM, VMEM, VMEM, VMEM],
-        4 * tokens * features * 128,
-        2 * row_bytes,
-    )
-    far_mix = call(far_mix_kernel, state, [VMEM, VMEM], 2 * pack_flops, 3 * row_bytes)
-    finish = call(finish_kernel, state, [VMEM] * (3 + chips), 2 * pack_flops, 5 * row_bytes)
-    expert, far_expert = [
-        call(
-            functools.partial(expert_kernel, len(shapes)),
+            pack_flops // cut,
+            4 * row_bytes // cut,
+        )
+
+    def gates(cut):
+        return call(
+            functools.partial(gate_kernel, geometry),
+            jax.ShapeDtypeStruct((2, 2, tokens, chips * room), BF16),
+            [SMEM] + [VMEM] * (4 + cut),
+            4 * tokens * features * 128,
+            2 * row_bytes,
+        )
+
+    def expert(sources, joined, shapes):
+        return call(
+            functools.partial(expert_kernel, sources, joined),
             shapes,
-            [VMEM] * len(shapes) + [HBM] * 6,
+            [VMEM] * sources + [HBM] * 6,
             12 * chips * room * features * units,
             12 * features * units,
             [
@@ -256,9 +285,13 @@
             ],
             EXPERT_VMEM,
         )
-        for shapes in ([block] * chips, [packed])
-    ]
-
+
+    far_mix = call(far_mix_kernel, state, [VMEM, VMEM], 2 * pack_flops, 3 * row_bytes)
+    finish_last = call(
+        last_kernel, [state] * 2, [SMEM] + [VMEM] * (4 + chips), 2 * pack_flops, 7 * row_bytes
+    )
+    finish = call(
+        finish_kernel, state, [VMEM] * (3 + chips), 2 * pack_flops, 5 * row_bytes)
     circles = [
         [low + core + sharers * k for k in range(chips)] for low in (0, half) for core in range(sharers)
     ]
@@ -271,56 +304,69 @@
     def pass_on(blocks):
         return [blocks[0]] + [flipped(blocks[k], "ep", sharers * k) for k in range(1, chips)]
 
-    def layer(current, far_current, picks, far_picks):
+    def layer(current, far_current, picks, far_picks, weights):
         normed, *near_rows = start(where, current, picks, norm_gain)
-        far_current, *near_rows = tied(far_current, *near_rows)
-        far_normed, far_rows = far_start(where, far_current, far_picks, norm_gain)
-        mixing = gates(where, normed, picks, far_normed, far_picks, scorer)
-        far_in, mixing = tied(spread(far_rows), mixing)
-        (far_out,) = far_expert(far_in, *weights)
+        far_current = list(far_current)
+        pieces = len(far_current)
+        far_current[-1], *near_rows = tied(far_current[-1], *near_rows)
+        far_in, far_normed = [], []
+        for states, chosen in zip(far_current, jnp.split(far_picks, pieces)):
+            part, rows = far_start(pieces)(where, states, chosen, norm_gain)
+            far_normed.append(part)
+            far_in.append(spread(rows))
+        mixing = gates(pieces)(where, normed, picks, far_picks, scorer, *far_normed)
+        far_in[-1], mixing, *near_rows = tied(far_in[-1], mixing, *near_rows)
+        (far_out,) = expert(pieces, chips, [packed])(*far_in, *weights)
         far_out, *near_in = tied(far_out, *pass_on(near_rows))
-        near_out = expert(*near_in, *weights)
+        near_out = expert(chips, 0, [block] * chips)(*near_in, *weights)
         far_part, *near_out = tied(far_mix(mixing, spread(far_out)), *near_out)
         beyond = flipped(far_part, "ep", half)
-        return finish(mixing, current, beyond, *pass_on(near_out))
-
-    tables = [a.reshape(n_section, chunks, tokens, top_count) for a in (picks, far_picks)]
-
-    def swapped(done, tick):
+        return mixing, current, beyond, pass_on(near_out)
+
+    tables = [a.reshape(n_section, tokens, top_count) for a in (picks, far_picks)]
+
+    def advance(tick, current, far_current, weights):
+        here = [lax.dynamic_index_in_dim(a, tick, 0, keepdims=False) for a in tables]
+        return layer(current, far_current, *here, weights)
+
+    def whole_weights(*own):
+        return (*own, *[flipped(w, "ep", 1) for w in own])
+
+    entered = jnp.where(section_index == 0, entering_rising, entering_falling)
+    entered = entered.reshape(tokens, features)
+    pieces = 2 if room % 32 == 0 and n_section == 2 else 1
+    far = [flipped(e, "ep", half) for e in jnp.split(entered, pieces)]
+    weights = whole_weights(*own)
+    if n_section == 2:
+        mixing, current, beyond, returned = advance(0, entered, far, weights)
+        first = finish(mixing, current, beyond, *returned)
         across = [(i, (i + n_ep) % (2 * n_ep) ^ half) for i in range(2 * n_ep)]
-        return flipped(done, "section", 1), lax.ppermute(done, ("section", "ep"), across)
-
-    def advance(tick, carry, moved):
-        current, far_current, kept_rising, kept_falling = carry
-        rising, falling = section_index == tick, section_index == n_section - 1 - tick
-        here = [lax.dynamic_index_in_dim(a, tick, 0, keepdims=False) for a in tables]
-        done = [layer(current[c], far_current[c], *[a[c] for a in here]) for c in range(chunks)]
-        kept_rising = [jnp.where(rising, d, k) for d, k in zip(done, kept_rising)]
-        kept_falling = [jnp.where(falling, d, k) for d, k in zip(done, kept_falling)]
-        moves = [moved(d, tick) for d in done]
-        return [m[0] for m in moves], [m[1] for m in moves], kept_rising, kept_falling
-
-    def shifted(done, tick):
-        up = lax.ppermute(done, "section", [(i, i + 1) for i in range(n_section - 1)])
-        down = lax.ppermute(done, "section", [(i + 1, i) for i in range(n_section - 1)])
-        here = jnp.where(section_index == tick + 1, up, down)
-        return here, flipped(here, "ep", half)
-
-    shape = (chunks, tokens, features)
-    entered = jnp.where(section_index == 0, entering_rising, entering_falling).reshape(shape)
-    empty = [jnp.zeros((tokens, features), BF16)] * chunks
-    entered = [entered[c] for c in range(chunks)]
-    carry = (entered, [flipped(e, "ep", half) for e in entered], empty, empty)
-    if n_section == 2:
-        carry = advance(0, carry, swapped)
-        carry = advance(1, carry, lambda done, tick: (done, done))
+        far = [lax.ppermute(first, ("section", "ep"), across)]
+        mixing, current, beyond, returned = advance(1, flipped(first, "section", 1), far, weights)
+        here = section_index.astype(jnp.int32)[None]
+        kept_rising, kept_falling = finish_last(here, mixing, current, beyond, first, *returned)
     else:
-        carry = lax.fori_loop(0, n_section, lambda t, c: advance(t, c, shifted), carry)
-    _, _, kept_rising, kept_falling = carry
+
+        def body(tick, carry):
+            current, far, kept_rising, kept_falling = carry
+            mixing, current, beyond, returned = advance(tick, current, far, weights)
+            done = finish(mixing, current, beyond, *returned)
+            kept_rising = jnp.where(section_index == tick, done, kept_rising)
+            kept_falling = jnp.where(section_index == n_section - 1 - tick, done, kept_falling)
+            up = lax.ppermute(done, "section", [(i, i + 1) for i in range(n_section - 1)])
+            down = lax.ppermute(done, "section", [(i + 1, i) for i in range(n_section - 1)])
+            current = jnp.where(section_index == tick + 1, up, down)
+            far = [flipped(current, "ep", half)]
+            return current, far, kept_rising, kept_falling
+
+        empty = jnp.zeros((tokens, features), BF16)
+        _, _, kept_rising, kept_falling = lax.fori_loop(
+            0, n_section, body, (entered, far, empty, empty)
+        )
     out = (1, micro_count, tok_count, features)
     return (
-        jnp.concatenate(kept_rising, axis=0).reshape(out),
-        jnp.concatenate(kept_falling, axis=0).reshape(out),
+        kept_rising.reshape(out),
+        kept_falling.reshape(out),
     )
 
 

time: 195 us -> 186 us (0.954)
  waiting for transfers between devices: 93.3 us -> 87.9 us
  starting transfers between devices: 45.9 us -> 42.3 us
    ppermute x20 -> x21, starting transfers between devices: 30.4 us -> 23 us  [flipped(): return lax.ppermute(value, axis, [(i, i ^ mask) for i in range(count)])]
    all_to_all x4 -> x5, starting transfers between devices: 14.2 us -> 18.4 us  [spread(): lax.all_to_all(rows, 'ep', split_axis=0, concat_axis=0, tiled=True, axis_...]
    all_to_all x4 -> x5, waiting for transfers between devices: 19.8 us -> 16.6 us  [spread(): lax.all_to_all(rows, 'ep', split_axis=0, concat_axis=0, tiled=True, axis_...]
    ppermute x20 -> x21, waiting for transfers between devices: 63.7 us -> 62.8 us  [flipped(): return lax.ppermute(value, axis, [(i, i ^ mask) for i in range(count)])]
    pallas_call x10 -> x11, Pallas kernels: 44.2 us -> 44.9 us  [the longest x2 18.5 us: layer(): far_out, = expert(pieces, chips, [packed])(*far_in, *weights)]
  transfers between devices with their start and end apart: 25 -> 27, of which waited for: 13 -> 16; matrix products, arithmetic and copies ran while one was open for 1% -> 1% of each run, Pallas kernels for 23% -> 23%
where the time goes in v5:
time: 186 us
  waiting for transfers between devices  87.9 us (47%)
  Pallas kernels  48 us (26%)
  starting transfers between devices  42.3 us (23%)
  local copies, waits for them, and re-layouts  5.2 us (3%)
    ppermute x21, waiting for transfers between devices, flipped(): return lax.ppermute(value, axis, [(i, i ^ mask) for i in range(count)])  62.8 us
    ppermute x21, starting transfers between devices, flipped(): return lax.ppermute(value, axis, [(i, i ^ mask) for i in range(count)])  23 us
    pallas_call x2, Pallas kernels, layer(): far_out, = expert(pieces, chips, [packed])(*far_in, *weights)  18.5 us
    all_to_all x5, starting transfers between devices, spread(): lax.all_to_all(rows, 'ep', split_axis=0, concat_axis=0, tiled=True, axis_...  18.4 us
    all_to_all x5, waiting for transfers between devices, spread(): lax.all_to_all(rows, 'ep', split_axis=0, concat_axis=0, tiled=True, axis_...  16.6 us
    pallas_call x2, Pallas kernels, layer(): near_out = expert(chips, 0, [block] * chips)(*near_in, *weights)  16.6 us
    ppermute x1, waiting for transfers between devices, shards(): far = [lax.ppermute(first, ('section', 'ep'), across)]  8.43 us
    pallas_call x3, Pallas kernels, layer(): part, rows = far_start(pieces)(where, states, chosen, norm_gain)  5.78 us
  transfers between devices with their start and end apart: 27, of which 16 were waited for; matrix products, arithmetic and copies ran while one was open for 1% of the time, Pallas kernels for 23%

profile of v5, /device:TPU:0, one launch (start us, length us, event | category | flops | bytes accessed | tf_op | source)
XLA Modules:
  0.0 185.7 jit_solution(12747247628658941351)
XLA Ops:
  0.7 0.7 copy_bitcast_fusion
  1.5 4.0 %collective-permute-start.1 = (s32[2,8,8,2]{2,1,3,0:T(8,128)S(1)}, s32[2,8,8,2]{2,1,3,0:T(8,128)S(1)}, u32[]{:S(2)}, u32[]{:S(2)}) collective-permute-start(s32[2,8,8,2]{2,1,3,0:T(8,128)S(1)} %broadcast_select_fusion.1), channel_id=1, source_target_pairs={{0,8},{1,9},{2,10},{3,11},{4,12},{5,13},{6,14},{7,15},{8,0},{9,1},... | collective-permute-start | bytes 3080 | tf_op jit(solution)/shard_map/ppermute | solution.py:19
  5.5 0.5 collective-permute-start.4
  6.0 1.1 broadcast_select_fusion
  7.1 0.2 collective-permute-start
  7.6 0.1 copy.13.picks.near_picks
  7.8 0.7 copy-done
  8.5 1.2 shard_map.104
  10.0 11.1 %collective-permute-done.current = bf16[32,3584]{1,0:T(8,128)(2,1)S(1)} collective-permute-done((bf16[32,3584]{1,0:T(8,128)(2,1)S(1)}, bf16[32,3584]{1,0:T(8,128)(2,1)S(1)}, u32[]{:S(2)}, u32[]{:S(2)}) %collective-permute-start) | collective-permute-done | bytes 229408 | tf_op jit(solution)/shard_map/ppermute | solution.py:19
  21.0 0.7 copy-done.1
  21.7 1.8 shard_map.105
  23.6 3.5 %all-to-all-start = ((bf16[4,16,3584]{2,1,0:T(8,128)(2,1)}), bf16[4,16,3584]{2,1,0:T(8,128)(2,1)S(1)}, u32[]{:S(2)}, u32[]{:S(2)}) async-start(bf16[4,16,3584]{2,1,0:T(8,128)(2,1)} %bitcast.9), calls=%async_computation | async-start | bytes 917504 | tf_op jit(solution)/shard_map/all_to_all | solution.py:300
  27.0 0.5 collective-permute-start.2
  27.6 12.6 %collective-permute-done.2.current = bf16[32,3584]{1,0:T(8,128)(2,1)S(1)} collective-permute-done((bf16[32,3584]{1,0:T(8,128)(2,1)S(1)}, bf16[32,3584]{1,0:T(8,128)(2,1)S(1)}, u32[]{:S(2)}, u32[]{:S(2)}) %collective-permute-start.2) | collective-permute-done | bytes 229408 | tf_op jit(solution)/shard_map/ppermute | solution.py:19
  40.2 1.8 shard_map.106
  42.0 3.5 %all-to-all-start.1 = ((bf16[4,16,3584]{2,1,0:T(8,128)(2,1)}), bf16[4,16,3584]{2,1,0:T(8,128)(2,1)S(1)}, u32[]{:S(2)}, u32[]{:S(2)}) async-start(bf16[4,16,3584]{2,1,0:T(8,128)(2,1)} %bitcast.16), calls=%async_computation.1 | async-start | bytes 917504 | tf_op jit(solution)/shard_map/all_to_all | solution.py:300
  45.5 0.1 copy.24
  45.6 1.1 shard_map.107.mixing
  46.7 2.0 %collective-permute-start.6 = (bf16[32,3584]{1,0:T(8,128)(2,1)}, bf16[32,3584]{1,0:T(8,128)(2,1)S(1)}, u32[]{:S(2)}, u32[]{:S(2)}) collective-permute-start(bf16[32,3584]{1,0:T(8,128)(2,1)} %copy-done.4), channel_id=1, source_target_pairs={{0,2},{1,3},{2,0},{3,1},{4,6},{5,7},{6,4},{7,5},{8,10},{9,11},{10,... | collective-permute-start | bytes 688136 | tf_op jit(solution)/shard_map/ppermute | solution.py:19
  48.8 1.5 collective-permute-start.7
  50.3 3.8 %all-to-all-done.1 = bf16[4,16,3584]{2,1,0:T(8,128)(2,1)S(1)} async-done(((bf16[4,16,3584]{2,1,0:T(8,128)(2,1)}), bf16[4,16,3584]{2,1,0:T(8,128)(2,1)S(1)}, u32[]{:S(2)}, u32[]{:S(2)}) %all-to-all-start.1) | async-done | bytes 458784 | tf_op jit(solution)/shard_map/all_to_all | solution.py:300
  54.2 9.2 %shard_map.108 = bf16[128,3584]{1,0:T(8,128)(2,1)} custom-call(bf16[64,3584]{1,0:T(8,128)(2,1)S(1)} %bitcast.58, bf16[64,3584]{1,0:T(8,128)(2,1)S(1)} %bitcast.57, bf16[3584,512]{1,0:T(8,128)(2,1)} %bitcast.65, bf16[3584,512]{1,0:T(8,128)(2,1)} %bitcast.70, bf16[512,3584]{1,0:T(8,128)(2,1)} %bitcast.75, ...), custom_call_target="tpu_custom_call" | custom-call | flops 2818572288 | bytes 22020096 | tf_op jit(solution)/shard_map/pallas_call | solution.py:319
  63.4 3.7 %all-to-all-start.2 = ((bf16[4,32,3584]{2,1,0:T(8,128)(2,1)}), bf16[4,32,3584]{2,1,0:T(8,128)(2,1)S(1)}, u32[]{:S(2)}, u32[]{:S(2)}) async-start(bf16[4,32,3584]{2,1,0:T(8,128)(2,1)} %bitcast.21), calls=%async_computation.2 | async-start | bytes 1835008 | tf_op jit(solution)/shard_map/all_to_all | solution.py:300
  67.1 8.3 %shard_map.110 = (bf16[32,3584]{1,0:T(8,128)(2,1)S(1)}, bf16[32,3584]{1,0:T(8,128)(2,1)S(1)}, bf16[32,3584]{1,0:T(8,128)(2,1)S(1)}, bf16[32,3584]{1,0:T(8,128)(2,1)S(1)}) custom-call(bf16[32,3584]{1,0:T(8,128)(2,1)S(1)} %get-tuple-element.91.refs_0_, bf16[32,3584]{1,0:T(8,128)(2,1)S(1)} %collective-permute-done.6.refs_1_, ...), custom_call_target="tpu_custom_call" | custom-call | flops 2818572288 | bytes 22020096 | tf_op jit(solution)/shard_map/pallas_call | solution.py:321
  75.4 0.7 copy-done.9
  76.1 2.3 %all-to-all-done.2 = bf16[4,32,3584]{2,1,0:T(8,128)(2,1)S(1)} async-done(((bf16[4,32,3584]{2,1,0:T(8,128)(2,1)}), bf16[4,32,3584]{2,1,0:T(8,128)(2,1)S(1)}, u32[]{:S(2)}, u32[]{:S(2)}) %all-to-all-start.2) | async-done | bytes 917536 | tf_op jit(solution)/shard_map/all_to_all | solution.py:300
  78.4 0.4 shard_map.109
  78.9 0.6 collective-permute-start.10
  79.4 1.3 collective-permute-start.11
  80.8 1.6 collective-permute-start.12
  82.4 3.9 %collective-permute-done.10.refs_1_ = bf16[32,3584]{1,0:T(8,128)(2,1)S(1)} collective-permute-done((bf16[32,3584]{1,0:T(8,128)(2,1)}, bf16[32,3584]{1,0:T(8,128)(2,1)S(1)}, u32[]{:S(2)}, u32[]{:S(2)}) %collective-permute-start.10) | collective-permute-done | bytes 229408 | tf_op jit(solution)/shard_map/ppermute | solution.py:19
  86.3 5.4 %collective-permute-done.11.refs_2_ = bf16[32,3584]{1,0:T(8,128)(2,1)S(1)} collective-permute-done((bf16[32,3584]{1,0:T(8,128)(2,1)S(1)}, bf16[32,3584]{1,0:T(8,128)(2,1)S(1)}, u32[]{:S(2)}, u32[]{:S(2)}) %collective-permute-start.11) | collective-permute-done | bytes 229408 | tf_op jit(solution)/shard_map/ppermute | solution.py:19
  91.7 5.5 %collective-permute-done.12.refs_3_ = bf16[32,3584]{1,0:T(8,128)(2,1)S(1)} collective-permute-done((bf16[32,3584]{1,0:T(8,128)(2,1)S(1)}, bf16[32,3584]{1,0:T(8,128)(2,1)S(1)}, u32[]{:S(2)}, u32[]{:S(2)}) %collective-permute-start.12) | collective-permute-done | bytes 229408 | tf_op jit(solution)/shard_map/ppermute | solution.py:19
  97.2 0.4 shard_map.111.first
  97.6 1.6 collective-permute-start.14
  99.2 0.9 collective-permute-start.13
  100.2 0.1 copy.25
  100.3 7.8 %collective-permute-done.14.current = bf16[64,3584]{1,0:T(8,128)(2,1)S(1)} collective-permute-done((bf16[64,3584]{1,0:T(8,128)(2,1)S(1)}, bf16[64,3584]{1,0:T(8,128)(2,1)S(1)}, u32[]{:S(2)}, u32[]{:S(2)}) %collective-permute-start.14) | collective-permute-done | bytes 458784 | tf_op jit(solution)/shard_map/ppermute | solution.py:19
  108.1 1.2 shard_map.112
  109.3 8.4 %collective-permute-done.13.current = bf16[64,3584]{1,0:T(8,128)(2,1)S(1)} collective-permute-done((bf16[64,3584]{1,0:T(8,128)(2,1)S(1)}, bf16[64,3584]{1,0:T(8,128)(2,1)S(1)}, u32[]{:S(2)}, u32[]{:S(2)}) %collective-permute-start.13) | collective-permute-done | bytes 458784 | tf_op jit(solution)/shard_map/ppermute | solution.py:344
  117.7 2.2 %shard_map.113 = (bf16[64,3584]{1,0:T(8,128)(2,1)S(1)}, bf16[128,3584]{1,0:T(8,128)(2,1)}) custom-call(s32[2]{0:T(128)S(1)} %pad_add_fusion.where, bf16[64,3584]{1,0:T(8,128)(2,1)S(1)} %collective-permute-done.13.current, s32[64,2]{1,0:T(8,128)S(1)} %bitcast.59, f32[1,3584]{1,0:T(1,128)S(1)} %copy-done.2), custom_call_target="tpu_custom_call" | custom-call | flops 58720256 | bytes 1835008 | tf_op jit(solution)/shard_map/pallas_call | solution.py:314
  119.9 4.1 %all-to-all-start.3 = ((bf16[4,32,3584]{2,1,0:T(8,128)(2,1)}), bf16[4,32,3584]{2,1,0:T(8,128)(2,1)S(1)}, u32[]{:S(2)}, u32[]{:S(2)}) async-start(bf16[4,32,3584]{2,1,0:T(8,128)(2,1)} %bitcast.25), calls=%async_computation.3 | async-start | bytes 1835008 | tf_op jit(solution)/shard_map/all_to_all | solution.py:300
  124.0 1.1 shard_map.114.mixing
  125.1 9.4 %all-to-all-done.3 = bf16[4,32,3584]{2,1,0:T(8,128)(2,1)S(1)} async-done(((bf16[4,32,3584]{2,1,0:T(8,128)(2,1)}), bf16[4,32,3584]{2,1,0:T(8,128)(2,1)S(1)}, u32[]{:S(2)}, u32[]{:S(2)}) %all-to-all-start.3) | async-done | bytes 917536 | tf_op jit(solution)/shard_map/all_to_all | solution.py:300
  134.5 1.5 collective-permute-start.15
  136.0 0.6 collective-permute-start.16
  136.5 1.5 collective-permute-start.17
  138.0 9.2 %shard_map.115 = bf16[128,3584]{1,0:T(8,128)(2,1)} custom-call(bf16[128,3584]{1,0:T(8,128)(2,1)S(1)} %bitcast.56, bf16[3584,512]{1,0:T(8,128)(2,1)} %bitcast.67, bf16[3584,512]{1,0:T(8,128)(2,1)} %bitcast.72, bf16[512,3584]{1,0:T(8,128)(2,1)} %bitcast.77, bf16[3584,512]{1,0:T(8,128)(2,1)} %collective-permute-done.3.refs_5_.refs_7_.refs_4_, ...), custom_call_target="tpu_custom_call" | custom-call | flops 2818572288 | bytes 22020096 | tf_op jit(solution)/shard_map/pallas_call | solution.py:319
  147.3 0.1 collective-permute-done.17.refs_3_
  147.4 3.7 %all-to-all-start.4 = ((bf16[4,32,3584]{2,1,0:T(8,128)(2,1)}), bf16[4,32,3584]{2,1,0:T(8,128)(2,1)S(1)}, u32[]{:S(2)}, u32[]{:S(2)}) async-start(bf16[4,32,3584]{2,1,0:T(8,128)(2,1)} %bitcast.28), calls=%async_computation.4 | async-start | bytes 1835008 | tf_op jit(solution)/shard_map/all_to_all | solution.py:300
  151.1 8.3 %shard_map.117 = (bf16[32,3584]{1,0:T(8,128)(2,1)S(1)}, bf16[32,3584]{1,0:T(8,128)(2,1)S(1)}, bf16[32,3584]{1,0:T(8,128)(2,1)S(1)}, bf16[32,3584]{1,0:T(8,128)(2,1)S(1)}) custom-call(bf16[32,3584]{1,0:T(8,128)(2,1)S(1)} %get-tuple-element.123.refs_0_, bf16[32,3584]{1,0:T(8,128)(2,1)S(1)} %collective-permute-done.15.refs_1_, ...), custom_call_target="tpu_custom_call" | custom-call | flops 2818572288 | bytes 22020096 | tf_op jit(solution)/shard_map/pallas_call | solution.py:321
  159.4 0.7 copy-done.7
  160.1 0.7 copy-done.8
  160.8 1.2 all-to-all-done.4
  161.9 0.4 shard_map.116
  162.3 1.9 %collective-permute-start.18 = (bf16[64,3584]{1,0:T(8,128)(2,1)S(1)}, bf16[64,3584]{1,0:T(8,128)(2,1)S(1)}, u32[]{:S(2)}, u32[]{:S(2)}) collective-permute-start(bf16[64,3584]{1,0:T(8,128)(2,1)S(1)} %shard_map.116), channel_id=1, source_target_pairs={{0,8},{1,9},{2,10},{3,11},{4,12},{5,13},{6,14},{7,15},{8,0},{9,1},... | collective-permute-start | bytes 1376264 | tf_op jit(solution)/shard_map/ppermute | solution.py:19
  164.3 1.8 collective-permute-start.19
  166.0 1.5 collective-permute-start.20
  167.5 0.3 collective-permute-start.21
  167.7 5.2 %collective-permute-done.19.refs_1_ = bf16[32,3584]{1,0:T(8,128)(2,1)S(1)} collective-permute-done((bf16[32,3584]{1,0:T(8,128)(2,1)}, bf16[32,3584]{1,0:T(8,128)(2,1)S(1)}, u32[]{:S(2)}, u32[]{:S(2)}) %collective-permute-start.19) | collective-permute-done | bytes 229408 | tf_op jit(solution)/shard_map/ppermute | solution.py:19
  172.9 5.9 %collective-permute-done.20.refs_2_ = bf16[32,3584]{1,0:T(8,128)(2,1)S(1)} collective-permute-done((bf16[32,3584]{1,0:T(8,128)(2,1)}, bf16[32,3584]{1,0:T(8,128)(2,1)S(1)}, u32[]{:S(2)}, u32[]{:S(2)}) %collective-permute-start.20) | collective-permute-done | bytes 229408 | tf_op jit(solution)/shard_map/ppermute | solution.py:19
  178.9 2.4 %collective-permute-done.21.refs_3_ = bf16[32,3584]{1,0:T(8,128)(2,1)S(1)} collective-permute-done((bf16[32,3584]{1,0:T(8,128)(2,1)S(1)}, bf16[32,3584]{1,0:T(8,128)(2,1)S(1)}, u32[]{:S(2)}, u32[]{:S(2)}) %collective-permute-start.21) | collective-permute-done | bytes 229408 | tf_op jit(solution)/shard_map/ppermute | solution.py:19
  181.2 3.1 %collective-permute-done.18.beyond = bf16[64,3584]{1,0:T(8,128)(2,1)S(1)} collective-permute-done((bf16[64,3584]{1,0:T(8,128)(2,1)S(1)}, bf16[64,3584]{1,0:T(8,128)(2,1)S(1)}, u32[]{:S(2)}, u32[]{:S(2)}) %collective-permute-start.18) | collective-permute-done | bytes 458784 | tf_op jit(solution)/shard_map/ppermute | solution.py:19
  184.3 1.4 shard_map.118
  (44 shorter events, 1.1 us)
Async XLA Ops:
  0.6 39.6 %copy-start.2 = (f32[1,3584]{1,0:T(1,128)S(1)}, f32[1,3584]{1,0:T(1,128)}, u32[]{:S(2)}) copy-start(f32[1,3584]{1,0:T(1,128)} %gain.9) | copy-start | bytes 43012
  0.6 45.0 %copy-start.3 = (bf16[1,3584,8]{1,2,0:T(8,128)(2,1)S(1)}, bf16[1,3584,8]{1,2,0:T(8,128)(2,1)}, u32[]{:S(2)}) copy-start(bf16[1,3584,8]{1,2,0:T(8,128)(2,1)} %param.12) | copy-start | bytes 172036
  1.5 8.2 %collective-permute-start.1 = (s32[2,8,8,2]{2,1,3,0:T(8,128)S(1)}, s32[2,8,8,2]{2,1,3,0:T(8,128)S(1)}, u32[]{:S(2)}, u32[]{:S(2)}) collective-permute-start(s32[2,8,8,2]{2,1,3,0:T(8,128)S(1)} %broadcast_select_fusion.1), channel_id=1, source_target_pairs={{0,8},{1,9},{2,10},{3,11},{4,12},{5,13},{6,14},{7,15},{8,0},{9,1},... | collective-permute-start | bytes 3080 | tf_op jit(solution)/shard_map/ppermute | solution.py:19
  5.5 44.8 %collective-permute-start.3 = (bf16[3584,512]{1,0:T(8,128)(2,1)}, bf16[3584,512]{1,0:T(8,128)(2,1)}, u32[]{:S(2)}, u32[]{:S(2)}) collective-permute-start(bf16[3584,512]{1,0:T(8,128)(2,1)} %bitcast.64), channel_id=1, source_target_pairs={{0,1},{1,0},{2,3},{3,2},{4,5},{5,4},{6,7},{7,6},{8,9},{9,8},{10,11... | collective-permute-start | bytes 11010056 | tf_op jit(solution)/shard_map/ppermute | solution.py:19
  5.5 48.6 %collective-permute-start.4 = (bf16[3584,512]{1,0:T(8,128)(2,1)}, bf16[3584,512]{1,0:T(8,128)(2,1)}, u32[]{:S(2)}, u32[]{:S(2)}) collective-permute-start(bf16[3584,512]{1,0:T(8,128)(2,1)} %bitcast.69), channel_id=1, source_target_pairs={{0,1},{1,0},{2,3},{3,2},{4,5},{5,4},{6,7},{7,6},{8,9},{9,8},{10,11... | collective-permute-start | bytes 11010056 | tf_op jit(solution)/shard_map/ppermute | solution.py:19
  6.0 48.1 %collective-permute-start.5 = (bf16[512,3584]{1,0:T(8,128)(2,1)}, bf16[512,3584]{1,0:T(8,128)(2,1)}, u32[]{:S(2)}, u32[]{:S(2)}) collective-permute-start(bf16[512,3584]{1,0:T(8,128)(2,1)} %bitcast.74), channel_id=1, source_target_pairs={{0,1},{1,0},{2,3},{3,2},{4,5},{5,4},{6,7},{7,6},{8,9},{9,8},{10,11... | collective-permute-start | bytes 11010056 | tf_op jit(solution)/shard_map/ppermute | solution.py:19
  7.1 13.9 %collective-permute-start = (bf16[32,3584]{1,0:T(8,128)(2,1)S(1)}, bf16[32,3584]{1,0:T(8,128)(2,1)S(1)}, u32[]{:S(2)}, u32[]{:S(2)}) collective-permute-start(bf16[32,3584]{1,0:T(8,128)(2,1)S(1)} %get-tuple-element.139), channel_id=1, source_target_pairs={{0,8},{1,9},{2,10},{3,11},{4,12},{5,13},{6,14},{7,15},{8,0},{9,1},... | collective-permute-start | bytes 688136 | tf_op jit(solution)/shard_map/ppermute | solution.py:19
  7.8 0.7 copy-start
  9.7 11.3 %copy-start.4 = (bf16[32,3584]{1,0:T(8,128)(2,1)}, bf16[32,3584]{1,0:T(8,128)(2,1)S(1)}, u32[]{:S(2)}) copy-start(bf16[32,3584]{1,0:T(8,128)(2,1)S(1)} %get-tuple-element.87) | copy-start | bytes 688132
  21.0 0.7 copy-start.1
  23.6 18.5 %all-to-all-start = ((bf16[4,16,3584]{2,1,0:T(8,128)(2,1)}), bf16[4,16,3584]{2,1,0:T(8,128)(2,1)S(1)}, u32[]{:S(2)}, u32[]{:S(2)}) async-start(bf16[4,16,3584]{2,1,0:T(8,128)(2,1)} %bitcast.9), calls=%async_computation | async-start | bytes 917504 | tf_op jit(solution)/shard_map/all_to_all | solution.py:300
  27.0 13.2 %collective-permute-start.2 = (bf16[32,3584]{1,0:T(8,128)(2,1)S(1)}, bf16[32,3584]{1,0:T(8,128)(2,1)S(1)}, u32[]{:S(2)}, u32[]{:S(2)}) collective-permute-start(bf16[32,3584]{1,0:T(8,128)(2,1)S(1)} %get-tuple-element.138), channel_id=1, source_target_pairs={{0,8},{1,9},{2,10},{3,11},{4,12},{5,13},{6,14},{7,15},{8,0},{9,1},... | collective-permute-start | bytes 688136 | tf_op jit(solution)/shard_map/ppermute | solution.py:19
  42.0 12.1 %all-to-all-start.1 = ((bf16[4,16,3584]{2,1,0:T(8,128)(2,1)}), bf16[4,16,3584]{2,1,0:T(8,128)(2,1)S(1)}, u32[]{:S(2)}, u32[]{:S(2)}) async-start(bf16[4,16,3584]{2,1,0:T(8,128)(2,1)} %bitcast.16), calls=%async_computation.1 | async-start | bytes 917504 | tf_op jit(solution)/shard_map/all_to_all | solution.py:300
  46.7 16.6 %collective-permute-start.6 = (bf16[32,3584]{1,0:T(8,128)(2,1)}, bf16[32,3584]{1,0:T(8,128)(2,1)S(1)}, u32[]{:S(2)}, u32[]{:S(2)}) collective-permute-start(bf16[32,3584]{1,0:T(8,128)(2,1)} %copy-done.4), channel_id=1, source_target_pairs={{0,2},{1,3},{2,0},{3,1},{4,6},{5,7},{6,4},{7,5},{8,10},{9,11},{10,... | collective-permute-start | bytes 688136 | tf_op jit(solution)/shard_map/ppermute | solution.py:19
  48.8 14.6 %collective-permute-start.7 = (bf16[32,3584]{1,0:T(8,128)(2,1)S(1)}, bf16[32,3584]{1,0:T(8,128)(2,1)S(1)}, u32[]{:S(2)}, u32[]{:S(2)}) collective-permute-start(bf16[32,3584]{1,0:T(8,128)(2,1)S(1)} %get-tuple-element.88), channel_id=1, source_target_pairs={{0,4},{1,5},{2,6},{3,7},{4,0},{5,1},{6,2},{7,3},{8,12},{9,13},{10,... | collective-permute-start | bytes 688136 | tf_op jit(solution)/shard_map/ppermute | solution.py:19
  50.3 13.1 %collective-permute-start.8 = (bf16[32,3584]{1,0:T(8,128)(2,1)S(1)}, bf16[32,3584]{1,0:T(8,128)(2,1)S(1)}, u32[]{:S(2)}, u32[]{:S(2)}) collective-permute-start(bf16[32,3584]{1,0:T(8,128)(2,1)S(1)} %get-tuple-element.89), channel_id=1, source_target_pairs={{0,6},{1,7},{2,4},{3,5},{4,2},{5,3},{6,0},{7,1},{8,14},{9,15},{10,... | collective-permute-start | bytes 688136 | tf_op jit(solution)/shard_map/ppermute | solution.py:19
  63.4 15.0 %all-to-all-start.2 = ((bf16[4,32,3584]{2,1,0:T(8,128)(2,1)}), bf16[4,32,3584]{2,1,0:T(8,128)(2,1)S(1)}, u32[]{:S(2)}, u32[]{:S(2)}) async-start(bf16[4,32,3584]{2,1,0:T(8,128)(2,1)} %bitcast.21), calls=%async_computation.2 | async-start | bytes 1835008 | tf_op jit(solution)/shard_map/all_to_all | solution.py:300
  75.4 0.7 copy-start.9
  78.8 18.4 %collective-permute-start.9 = (bf16[64,3584]{1,0:T(8,128)(2,1)S(1)}, bf16[64,3584]{1,0:T(8,128)(2,1)S(1)}, u32[]{:S(2)}, u32[]{:S(2)}) collective-permute-start(bf16[64,3584]{1,0:T(8,128)(2,1)S(1)} %shard_map.109), channel_id=1, source_target_pairs={{0,8},{1,9},{2,10},{3,11},{4,12},{5,13},{6,14},{7,15},{8,0},{9,1},... | collective-permute-start | bytes 1376264 | tf_op jit(solution)/shard_map/ppermute | solution.py:19
  78.9 7.5 %collective-permute-start.10 = (bf16[32,3584]{1,0:T(8,128)(2,1)}, bf16[32,3584]{1,0:T(8,128)(2,1)S(1)}, u32[]{:S(2)}, u32[]{:S(2)}) collective-permute-start(bf16[32,3584]{1,0:T(8,128)(2,1)} %copy-done.9), channel_id=1, source_target_pairs={{0,2},{1,3},{2,0},{3,1},{4,6},{5,7},{6,4},{7,5},{8,10},{9,11},{10,... | collective-permute-start | bytes 688136 | tf_op jit(solution)/shard_map/ppermute | solution.py:19
  79.4 12.2 %collective-permute-start.11 = (bf16[32,3584]{1,0:T(8,128)(2,1)S(1)}, bf16[32,3584]{1,0:T(8,128)(2,1)S(1)}, u32[]{:S(2)}, u32[]{:S(2)}) collective-permute-start(bf16[32,3584]{1,0:T(8,128)(2,1)S(1)} %get-tuple-element.102), channel_id=1, source_target_pairs={{0,4},{1,5},{2,6},{3,7},{4,0},{5,1},{6,2},{7,3},{8,12},{9,13},{10,... | collective-permute-start | bytes 688136 | tf_op jit(solution)/shard_map/ppermute | solution.py:19
  80.8 16.4 %collective-permute-start.12 = (bf16[32,3584]{1,0:T(8,128)(2,1)S(1)}, bf16[32,3584]{1,0:T(8,128)(2,1)S(1)}, u32[]{:S(2)}, u32[]{:S(2)}) collective-permute-start(bf16[32,3584]{1,0:T(8,128)(2,1)S(1)} %get-tuple-element.103), channel_id=1, source_target_pairs={{0,6},{1,7},{2,4},{3,5},{4,2},{5,3},{6,0},{7,1},{8,14},{9,15},{10,... | collective-permute-start | bytes 688136 | tf_op jit(solution)/shard_map/ppermute | solution.py:19
  97.6 10.4 %collective-permute-start.14 = (bf16[64,3584]{1,0:T(8,128)(2,1)S(1)}, bf16[64,3584]{1,0:T(8,128)(2,1)S(1)}, u32[]{:S(2)}, u32[]{:S(2)}) collective-permute-start(bf16[64,3584]{1,0:T(8,128)(2,1)S(1)} %shard_map.111.first), channel_id=1, source_target_pairs={{0,16},{16,0},{1,17},{17,1},{2,18},{18,2},{3,19},{19,3},{4,20},{20... | collective-permute-start | bytes 1376264 | tf_op jit(solution)/shard_map/ppermute | solution.py:19
  99.2 18.5 %collective-permute-start.13 = (bf16[64,3584]{1,0:T(8,128)(2,1)S(1)}, bf16[64,3584]{1,0:T(8,128)(2,1)S(1)}, u32[]{:S(2)}, u32[]{:S(2)}) collective-permute-start(bf16[64,3584]{1,0:T(8,128)(2,1)S(1)} %shard_map.111.first), channel_id=1, source_target_pairs={{0,24},{1,25},{2,26},{3,27},{4,28},{5,29},{6,30},{7,31},{8,16},{9,... | collective-permute-start | bytes 1376264 | tf_op jit(solution)/shard_map/ppermute | solution.py:344
  109.3 10.6 %copy-start.5 = (bf16[32,3584]{1,0:T(8,128)(2,1)}, bf16[32,3584]{1,0:T(8,128)(2,1)S(1)}, u32[]{:S(2)}) copy-start(bf16[32,3584]{1,0:T(8,128)(2,1)S(1)} %get-tuple-element.120) | copy-start | bytes 688132
  109.3 10.6 %copy-start.6 = (bf16[32,3584]{1,0:T(8,128)(2,1)}, bf16[32,3584]{1,0:T(8,128)(2,1)S(1)}, u32[]{:S(2)}) copy-start(bf16[32,3584]{1,0:T(8,128)(2,1)S(1)} %get-tuple-element.119) | copy-start | bytes 688132
  119.9 14.6 %all-to-all-start.3 = ((bf16[4,32,3584]{2,1,0:T(8,128)(2,1)}), bf16[4,32,3584]{2,1,0:T(8,128)(2,1)S(1)}, u32[]{:S(2)}, u32[]{:S(2)}) async-start(bf16[4,32,3584]{2,1,0:T(8,128)(2,1)} %bitcast.25), calls=%async_computation.3 | async-start | bytes 1835008 | tf_op jit(solution)/shard_map/all_to_all | solution.py:300
  134.5 12.7 %collective-permute-start.15 = (bf16[32,3584]{1,0:T(8,128)(2,1)}, bf16[32,3584]{1,0:T(8,128)(2,1)S(1)}, u32[]{:S(2)}, u32[]{:S(2)}) collective-permute-start(bf16[32,3584]{1,0:T(8,128)(2,1)} %copy-done.6), channel_id=1, source_target_pairs={{0,2},{1,3},{2,0},{3,1},{4,6},{5,7},{6,4},{7,5},{8,10},{9,11},{10,... | collective-permute-start | bytes 688136 | tf_op jit(solution)/shard_map/ppermute | solution.py:19
  136.0 11.3 %collective-permute-start.16 = (bf16[32,3584]{1,0:T(8,128)(2,1)}, bf16[32,3584]{1,0:T(8,128)(2,1)S(1)}, u32[]{:S(2)}, u32[]{:S(2)}) collective-permute-start(bf16[32,3584]{1,0:T(8,128)(2,1)} %copy-done.5), channel_id=1, source_target_pairs={{0,4},{1,5},{2,6},{3,7},{4,0},{5,1},{6,2},{7,3},{8,12},{9,13},{10,... | collective-permute-start | bytes 688136 | tf_op jit(solution)/shard_map/ppermute | solution.py:19
  136.5 10.8 %collective-permute-start.17 = (bf16[32,3584]{1,0:T(8,128)(2,1)S(1)}, bf16[32,3584]{1,0:T(8,128)(2,1)S(1)}, u32[]{:S(2)}, u32[]{:S(2)}) collective-permute-start(bf16[32,3584]{1,0:T(8,128)(2,1)S(1)} %get-tuple-element.121), channel_id=1, source_target_pairs={{0,6},{1,7},{2,4},{3,5},{4,2},{5,3},{6,0},{7,1},{8,14},{9,15},{10,... | collective-permute-start | bytes 688136 | tf_op jit(solution)/shard_map/ppermute | solution.py:19
  147.4 14.6 %all-to-all-start.4 = ((bf16[4,32,3584]{2,1,0:T(8,128)(2,1)}), bf16[4,32,3584]{2,1,0:T(8,128)(2,1)S(1)}, u32[]{:S(2)}, u32[]{:S(2)}) async-start(bf16[4,32,3584]{2,1,0:T(8,128)(2,1)} %bitcast.28), calls=%async_computation.4 | async-start | bytes 1835008 | tf_op jit(solution)/shard_map/all_to_all | solution.py:300
  159.4 0.7 copy-start.7
  160.1 0.7 copy-start.8
  162.3 22.0 %collective-permute-start.18 = (bf16[64,3584]{1,0:T(8,128)(2,1)S(1)}, bf16[64,3584]{1,0:T(8,128)(2,1)S(1)}, u32[]{:S(2)}, u32[]{:S(2)}) collective-permute-start(bf16[64,3584]{1,0:T(8,128)(2,1)S(1)} %shard_map.116), channel_id=1, source_target_pairs={{0,8},{1,9},{2,10},{3,11},{4,12},{5,13},{6,14},{7,15},{8,0},{9,1},... | collective-permute-start | bytes 1376264 | tf_op jit(solution)/shard_map/ppermute | solution.py:19
  164.3 8.7 %collective-permute-start.19 = (bf16[32,3584]{1,0:T(8,128)(2,1)}, bf16[32,3584]{1,0:T(8,128)(2,1)S(1)}, u32[]{:S(2)}, u32[]{:S(2)}) collective-permute-start(bf16[32,3584]{1,0:T(8,128)(2,1)} %copy-done.8), channel_id=1, source_target_pairs={{0,2},{1,3},{2,0},{3,1},{4,6},{5,7},{6,4},{7,5},{8,10},{9,11},{10,... | collective-permute-start | bytes 688136 | tf_op jit(solution)/shard_map/ppermute | solution.py:19
  166.0 12.8 %collective-permute-start.20 = (bf16[32,3584]{1,0:T(8,128)(2,1)}, bf16[32,3584]{1,0:T(8,128)(2,1)S(1)}, u32[]{:S(2)}, u32[]{:S(2)}) collective-permute-start(bf16[32,3584]{1,0:T(8,128)(2,1)} %copy-done.7), channel_id=1, source_target_pairs={{0,4},{1,5},{2,6},{3,7},{4,0},{5,1},{6,2},{7,3},{8,12},{9,13},{10,... | collective-permute-start | bytes 688136 | tf_op jit(solution)/shard_map/ppermute | solution.py:19
  167.5 13.7 %collective-permute-start.21 = (bf16[32,3584]{1,0:T(8,128)(2,1)S(1)}, bf16[32,3584]{1,0:T(8,128)(2,1)S(1)}, u32[]{:S(2)}, u32[]{:S(2)}) collective-permute-start(bf16[32,3584]{1,0:T(8,128)(2,1)S(1)} %get-tuple-element.135), channel_id=1, source_target_pairs={{0,6},{1,7},{2,4},{3,5},{4,2},{5,3},{6,0},{7,1},{8,14},{9,15},{10,... | collective-permute-start | bytes 688136 | tf_op jit(solution)/shard_map/ppermute | solution.py:19

commit v6 on v5

--- a/solution.py
+++ b/solution.py
@@ -84,7 +84,7 @@
     return jnp.concatenate([block[:, part] for block in blocks], axis=0)
 
 
-def gate_kernel(geometry, where, near, near_picks, far_picks, scorer, *refs):
+def gate_kernel(turned, geometry, where, near, near_picks, far_picks, scorer, *refs):
     room, chips = geometry[2:]
     *far, mixing = refs
     for place, (parts, picks_ref) in enumerate((((near,), near_picks), (far, far_picks))):
@@ -106,7 +106,7 @@
         total = sum(chosen)
         slots = lax.broadcasted_iota(jnp.int32, (tokens, chips * room), 1)
         mixed = jnp.zeros(slots.shape, F32)
-        for score, column in zip(chosen, slot_columns(picks, where, place == 0, geometry)):
+        for score, column in zip(chosen, slot_columns(picks, where, turned or place == 0, geometry)):
             mixed += jnp.where(slots == column, route_scale * score / total, 0.0)
         high = mixed.astype(BF16)
         mixing[place, 0] = high
@@ -120,9 +120,10 @@
     )
 
 
-def far_mix_kernel(mixing, returned, out):
+def far_mix_kernel(mixing, *refs):
+    *returned, out = refs
     for part in tiles_of(out.shape[1]):
-        out[:, part] = mixed_rows(mixing, 1, [returned], part).astype(BF16)
+        out[:, part] = mixed_rows(mixing, 1, returned, part).astype(BF16)
 
 
 def finish_kernel(mixing, current, beyond, *refs):
@@ -143,15 +144,23 @@
         falling[:, part] = jnp.where(section[0] == 0, last, earlier).astype(BF16)
 
 
+def joined_rows(arrived, chips):
+    if not chips:
+        return get_blocks(arrived, slice(None))
+    share = arrived[0].shape[0] // chips
+    return jnp.concatenate(
+        [piece[k * share : (k + 1) * share] for k in range(chips) for piece in arrived], axis=0
+    )
+
+
 def expert_kernel(sources, chips, *refs):
     arrived, weights, refs = refs[:sources], refs[sources : sources + 6], refs[sources + 6 :]
     *outs, gate_buf, up_buf, down_buf, hidden, sems = refs
     features, units = gate_buf.shape[1:]
-    inner = tiles_of(units, 256)
     copies = []
     for side in range(2):
         gate_w, up_w, _ = weights[3 * side : 3 * side + 3]
-        for part in inner:
+        for part in tiles_of(units, 256):
             copies.append((gate_w.at[:, part], gate_buf.at[side, :, part]))
             copies.append((up_w.at[:, part], up_buf.at[side, :, part]))
     for part in tiles_of(features):
@@ -161,25 +170,27 @@
     for copy in copies:
         copy.start()
     pending = iter(copies)
-    if chips:
-        share = arrived[0].shape[0] // chips
-        rows = jnp.concatenate(
-            [piece[k * share : (k + 1) * share] for k in range(chips) for piece in arrived], axis=0
-        )
-    else:
-        rows = get_blocks(arrived, slice(None))
-    for side in range(2):
-        for part in inner:
-            next(pending).wait()
-            next(pending).wait()
-            gate_act = jnp.dot(rows, gate_buf[side, :, part], preferred_element_type=F32)
-            upward = jnp.dot(rows, up_buf[side, :, part], preferred_element_type=F32)
-            hidden[side, :, part] = (jax.nn.silu(gate_act) * upward).astype(BF16)
-    for part in tiles_of(features):
+
+    def ready():
         next(pending).wait()
         next(pending).wait()
-        total = jnp.dot(hidden[0], down_buf[0, :, part], preferred_element_type=F32) + jnp.dot(
-            hidden[1], down_buf[1, :, part], preferred_element_type=F32
+
+    held = [buf.at[side] for side in range(2) for buf in (gate_buf, up_buf, down_buf)]
+    serve(joined_rows(arrived, chips), held, hidden, outs, ready)
+
+
+def serve(rows, weights, hidden, outs, ready):
+    for side in range(2):
+        gate_w, up_w, _ = weights[3 * side : 3 * side + 3]
+        for part in tiles_of(hidden.shape[2], 256):
+            ready()
+            gate_act = jnp.dot(rows, gate_w[:, part], preferred_element_type=F32)
+            upward = jnp.dot(rows, up_w[:, part], preferred_element_type=F32)
+            hidden[side, :, part] = (jax.nn.silu(gate_act) * upward).astype(BF16)
+    for part in tiles_of(outs[0].shape[1]):
+        ready()
+        total = jnp.dot(hidden[0], weights[2][:, part], preferred_element_type=F32) + jnp.dot(
+            hidden[1], weights[5][:, part], preferred_element_type=F32
         )
         put_blocks(outs, part, total.astype(BF16))
 
@@ -260,7 +271,7 @@
 
     def gates(cut):
         return call(
-            functools.partial(gate_kernel, geometry),
+            functools.partial(gate_kernel, cut == 1, geometry),
             jax.ShapeDtypeStruct((2, 2, tokens, chips * room), BF16),
             [SMEM] + [VMEM] * (4 + cut),
             4 * tokens * features * 128,
@@ -286,7 +297,10 @@
             EXPERT_VMEM,
         )
 
-    far_mix = call(far_mix_kernel, state, [VMEM, VMEM], 2 * pack_flops, 3 * row_bytes)
+    def far_mix(mixing, *returned):
+        specs = [VMEM] * (1 + len(returned))
+        return call(far_mix_kernel, state, specs, 2 * pack_flops, 3 * row_bytes)(mixing, *returned)
+
     finish_last = call(
         last_kernel, [state] * 2, [SMEM] + [VMEM] * (4 + chips), 2 * pack_flops, 7 * row_bytes
     )
@@ -309,17 +323,27 @@
         far_current = list(far_current)
         pieces = len(far_current)
         far_current[-1], *near_rows = tied(far_current[-1], *near_rows)
-        far_in, far_normed = [], []
-        for states, chosen in zip(far_current, jnp.split(far_picks, pieces)):
-            part, rows = far_start(pieces)(where, states, chosen, norm_gain)
-            far_normed.append(part)
-            far_in.append(spread(rows))
-        mixing = gates(pieces)(where, normed, picks, far_picks, scorer, *far_normed)
-        far_in[-1], mixing, *near_rows = tied(far_in[-1], mixing, *near_rows)
-        (far_out,) = expert(pieces, chips, [packed])(*far_in, *weights)
-        far_out, *near_in = tied(far_out, *pass_on(near_rows))
-        near_out = expert(chips, 0, [block] * chips)(*near_in, *weights)
-        far_part, *near_out = tied(far_mix(mixing, spread(far_out)), *near_out)
+        if pieces == 1:
+            normed_far, *rows = start(where, far_current[0], far_picks, norm_gain)
+            mixing = gates(1)(where, normed, picks, far_picks, scorer, normed_far)
+            far_in = pass_on(rows)
+            far_in[-1], mixing, *near_rows = tied(far_in[-1], mixing, *near_rows)
+            far_out = list(expert(chips, 0, [block] * chips)(*far_in, *weights))
+            far_out[-1], *near_in = tied(far_out[-1], *pass_on(near_rows))
+            near_out = expert(chips, 0, [block] * chips)(*near_in, *weights)
+            far_part, *near_out = tied(far_mix(mixing, *pass_on(far_out)), *near_out)
+        else:
+            far_in, far_normed = [], []
+            for states, chosen in zip(far_current, jnp.split(far_picks, pieces)):
+                part, rows = far_start(pieces)(where, states, chosen, norm_gain)
+                far_normed.append(part)
+                far_in.append(spread(rows))
+            mixing = gates(pieces)(where, normed, picks, far_picks, scorer, *far_normed)
+            far_in[-1], mixing, *near_rows = tied(far_in[-1], mixing, *near_rows)
+            (far_out,) = expert(pieces, chips, [packed])(*far_in, *weights)
+            far_out, *near_in = tied(far_out, *pass_on(near_rows))
+            near_out = expert(chips, 0, [block] * chips)(*near_in, *weights)
+            far_part, *near_out = tied(far_mix(mixing, spread(far_out)), *near_out)
         beyond = flipped(far_part, "ep", half)
         return mixing, current, beyond, pass_on(near_out)
 

time: 186 us -> 174 us (0.935)
  waiting for transfers between devices: 87.9 us -> 77.7 us
  starting transfers between devices: 42.3 us -> 44.7 us
  local copies, waits for them, and re-layouts: 5.2 us -> 3.13 us
  Pallas kernels: 48 us -> 46.1 us
    pallas_call x2 -> x5, Pallas kernels: 0.78 us -> 11.4 us  [the longest x1 8.27 us: layer(): far_out = list(expert(chips, 0, [block] * chips)(*far_in, *weights))]
    ppermute x21 -> x27, starting transfers between devices: 23 us -> 32.9 us  [flipped(): return lax.ppermute(value, axis, [(i, i ^ mask) for i in range(count)])]
    all_to_all x5 -> x3, waiting for transfers between devices: 16.6 us -> 7.11 us  [spread(): lax.all_to_all(rows, 'ep', split_axis=0, concat_axis=0, tiled=True, axis_...]
    pallas_call x2 -> x1, Pallas kernels: 18.5 us -> 9.22 us  [layer(): far_out, = expert(pieces, chips, [packed])(*far_in, *weights)]
    all_to_all x5 -> x3, starting transfers between devices: 18.4 us -> 10.6 us  [spread(): lax.all_to_all(rows, 'ep', split_axis=0, concat_axis=0, tiled=True, axis_...]
    pallas_call x3 -> x2, Pallas kernels: 5.78 us -> 3.62 us  [layer(): part, rows = far_start(pieces)(where, states, chosen, norm_gain)]
    unnamed x20 -> x8, local copies, waits for them, and re-layouts: 3.51 us -> 1.44 us
    ppermute x21 -> x27, waiting for transfers between devices: 62.8 us -> 63 us  [flipped(): return lax.ppermute(value, axis, [(i, i ^ mask) for i in range(count)])]
  transfers between devices with their start and end apart: 27 -> 31, of which waited for: 16 -> 14; matrix products, arithmetic and copies ran while one was open for 1% -> 1% of each run, Pallas kernels for 23% -> 24%
where the time goes in v6:
time: 174 us
  waiting for transfers between devices  77.7 us (45%)
  Pallas kernels  46.1 us (26%)
  starting transfers between devices  44.7 us (26%)
  local copies, waits for them, and re-layouts  3.13 us (2%)
    ppermute x27, waiting for transfers between devices, flipped(): return lax.ppermute(value, axis, [(i, i ^ mask) for i in range(count)])  63 us
    ppermute x27, starting transfers between devices, flipped(): return lax.ppermute(value, axis, [(i, i ^ mask) for i in range(count)])  32.9 us
    pallas_call x2, Pallas kernels, layer(): near_out = expert(chips, 0, [block] * chips)(*near_in, *weights)  16.5 us
    all_to_all x3, starting transfers between devices, spread(): lax.all_to_all(rows, 'ep', split_axis=0, concat_axis=0, tiled=True, axis_...  10.6 us
    pallas_call x1, Pallas kernels, layer(): far_out, = expert(pieces, chips, [packed])(*far_in, *weights)  9.22 us
    pallas_call x1, Pallas kernels, layer(): far_out = list(expert(chips, 0, [block] * chips)(*far_in, *weights))  8.27 us
    ppermute x1, waiting for transfers between devices, shards(): far = [lax.ppermute(first, ('section', 'ep'), across)]  7.61 us
    all_to_all x3, waiting for transfers between devices, spread(): lax.all_to_all(rows, 'ep', split_axis=0, concat_axis=0, tiled=True, axis_...  7.11 us
  transfers between devices with their start and end apart: 31, of which 14 were waited for; matrix products, arithmetic and copies ran while one was open for 1% of the time, Pallas kernels for 24%

profile of v6, /device:TPU:0, one launch (start us, length us, event | category | flops | bytes accessed | tf_op | source)
XLA Modules:
  0.0 173.8 jit_solution(12469003337600418327)
XLA Ops:
  0.7 0.7 copy_bitcast_fusion
  1.5 4.0 %collective-permute-start.1 = (s32[2,8,8,2]{2,1,3,0:T(8,128)S(1)}, s32[2,8,8,2]{2,1,3,0:T(8,128)S(1)}, u32[]{:S(2)}, u32[]{:S(2)}) collective-permute-start(s32[2,8,8,2]{2,1,3,0:T(8,128)S(1)} %broadcast_select_fusion.1), channel_id=1, source_target_pairs={{0,8},{1,9},{2,10},{3,11},{4,12},{5,13},{6,14},{7,15},{8,0},{9,1},... | collective-permute-start | bytes 3080 | tf_op jit(solution)/shard_map/ppermute | solution.py:19
  5.5 0.5 collective-permute-start.4
  6.0 1.1 broadcast_select_fusion
  7.1 0.2 collective-permute-start
  7.6 0.1 copy.13.picks.near_picks
  7.8 0.7 copy-done
  8.5 1.2 shard_map.104
  9.9 0.1 copy.16.picks
  10.0 11.1 %collective-permute-done.current = bf16[32,3584]{1,0:T(8,128)(2,1)S(1)} collective-permute-done((bf16[32,3584]{1,0:T(8,128)(2,1)S(1)}, bf16[32,3584]{1,0:T(8,128)(2,1)S(1)}, u32[]{:S(2)}, u32[]{:S(2)}) %collective-permute-start) | collective-permute-done | bytes 229408 | tf_op jit(solution)/shard_map/ppermute | solution.py:19
  21.0 0.7 copy-done.1
  21.7 1.8 %shard_map.105 = (bf16[32,3584]{1,0:T(8,128)(2,1)S(1)}, bf16[64,3584]{1,0:T(8,128)(2,1)}) custom-call(s32[2]{0:T(128)S(1)} %pad_add_fusion.where, bf16[32,3584]{1,0:T(8,128)(2,1)S(1)} %collective-permute-done.current, s32[32,2]{1,0:T(8,128)S(1)} %copy.16.picks, f32[1,3584]{1,0:T(1,128)S(1)} %copy-done.1), custom_call_target="tpu_custom_call" | custom-call | flops 29360128 | bytes 917504 | tf_op jit(solution)/shard_map/pallas_call | solution.py:338
  23.6 3.5 %all-to-all-start = ((bf16[4,16,3584]{2,1,0:T(8,128)(2,1)}), bf16[4,16,3584]{2,1,0:T(8,128)(2,1)S(1)}, u32[]{:S(2)}, u32[]{:S(2)}) async-start(bf16[4,16,3584]{2,1,0:T(8,128)(2,1)} %bitcast.9), calls=%async_computation | async-start | bytes 917504 | tf_op jit(solution)/shard_map/all_to_all | solution.py:314
  27.0 0.5 collective-permute-start.2
  27.6 12.6 %collective-permute-done.2.current = bf16[32,3584]{1,0:T(8,128)(2,1)S(1)} collective-permute-done((bf16[32,3584]{1,0:T(8,128)(2,1)S(1)}, bf16[32,3584]{1,0:T(8,128)(2,1)S(1)}, u32[]{:S(2)}, u32[]{:S(2)}) %collective-permute-start.2) | collective-permute-done | bytes 229408 | tf_op jit(solution)/shard_map/ppermute | solution.py:19
  40.2 1.8 %shard_map.106 = (bf16[32,3584]{1,0:T(8,128)(2,1)S(1)}, bf16[64,3584]{1,0:T(8,128)(2,1)}) custom-call(s32[2]{0:T(128)S(1)} %pad_add_fusion.where, bf16[32,3584]{1,0:T(8,128)(2,1)S(1)} %collective-permute-done.2.current, s32[32,2]{1,0:T(8,128)S(1)} %copy.17.picks, f32[1,3584]{1,0:T(1,128)S(1)} %copy-done.2), custom_call_target="tpu_custom_call" | custom-call | flops 29360128 | bytes 917504 | tf_op jit(solution)/shard_map/pallas_call | solution.py:338
  42.0 3.5 %all-to-all-start.1 = ((bf16[4,16,3584]{2,1,0:T(8,128)(2,1)}), bf16[4,16,3584]{2,1,0:T(8,128)(2,1)S(1)}, u32[]{:S(2)}, u32[]{:S(2)}) async-start(bf16[4,16,3584]{2,1,0:T(8,128)(2,1)} %bitcast.16), calls=%async_computation.1 | async-start | bytes 917504 | tf_op jit(solution)/shard_map/all_to_all | solution.py:314
  45.5 0.1 copy.24
  45.6 1.1 shard_map.107.mixing
  46.7 2.0 %collective-permute-start.6 = (bf16[32,3584]{1,0:T(8,128)(2,1)S(1)}, bf16[32,3584]{1,0:T(8,128)(2,1)S(1)}, u32[]{:S(2)}, u32[]{:S(2)}) collective-permute-start(bf16[32,3584]{1,0:T(8,128)(2,1)S(1)} %get-tuple-element.94), channel_id=1, source_target_pairs={{0,2},{1,3},{2,0},{3,1},{4,6},{5,7},{6,4},{7,5},{8,10},{9,11},{10,... | collective-permute-start | bytes 688136 | tf_op jit(solution)/shard_map/ppermute | solution.py:19
  48.8 1.5 collective-permute-start.7
  50.3 3.8 %all-to-all-done.1 = bf16[4,16,3584]{2,1,0:T(8,128)(2,1)S(1)} async-done(((bf16[4,16,3584]{2,1,0:T(8,128)(2,1)}), bf16[4,16,3584]{2,1,0:T(8,128)(2,1)S(1)}, u32[]{:S(2)}, u32[]{:S(2)}) %all-to-all-start.1) | async-done | bytes 458784 | tf_op jit(solution)/shard_map/all_to_all | solution.py:314
  54.2 9.2 %shard_map.108 = bf16[128,3584]{1,0:T(8,128)(2,1)} custom-call(bf16[64,3584]{1,0:T(8,128)(2,1)S(1)} %bitcast.52, bf16[64,3584]{1,0:T(8,128)(2,1)S(1)} %bitcast.51, bf16[3584,512]{1,0:T(8,128)(2,1)} %bitcast.59, bf16[3584,512]{1,0:T(8,128)(2,1)} %bitcast.64, bf16[512,3584]{1,0:T(8,128)(2,1)} %bitcast.69, ...), custom_call_target="tpu_custom_call" | custom-call | flops 2818572288 | bytes 22020096 | tf_op jit(solution)/shard_map/pallas_call | solution.py:343
  63.4 3.7 %all-to-all-start.2 = ((bf16[4,32,3584]{2,1,0:T(8,128)(2,1)}), bf16[4,32,3584]{2,1,0:T(8,128)(2,1)S(1)}, u32[]{:S(2)}, u32[]{:S(2)}) async-start(bf16[4,32,3584]{2,1,0:T(8,128)(2,1)} %bitcast.21), calls=%async_computation.2 | async-start | bytes 1835008 | tf_op jit(solution)/shard_map/all_to_all | solution.py:314
  67.1 8.3 %shard_map.110 = (bf16[32,3584]{1,0:T(8,128)(2,1)S(1)}, bf16[32,3584]{1,0:T(8,128)(2,1)S(1)}, bf16[32,3584]{1,0:T(8,128)(2,1)S(1)}, bf16[32,3584]{1,0:T(8,128)(2,1)S(1)}) custom-call(bf16[32,3584]{1,0:T(8,128)(2,1)S(1)} %get-tuple-element.98.refs_0_, bf16[32,3584]{1,0:T(8,128)(2,1)S(1)} %collective-permute-done.6.refs_1_, ...), custom_call_target="tpu_custom_call" | custom-call | flops 2818572288 | bytes 22020096 | tf_op jit(solution)/shard_map/pallas_call | solution.py:345
  75.4 3.3 %all-to-all-done.2 = bf16[4,32,3584]{2,1,0:T(8,128)(2,1)S(1)} async-done(((bf16[4,32,3584]{2,1,0:T(8,128)(2,1)}), bf16[4,32,3584]{2,1,0:T(8,128)(2,1)S(1)}, u32[]{:S(2)}, u32[]{:S(2)}) %all-to-all-start.2) | async-done | bytes 917536 | tf_op jit(solution)/shard_map/all_to_all | solution.py:314
  78.7 0.4 shard_map.109
  79.2 0.7 collective-permute-start.10
  79.9 0.2 collective-permute-start.11
  80.1 2.7 %collective-permute-start.12 = (bf16[32,3584]{1,0:T(8,128)(2,1)S(1)}, bf16[32,3584]{1,0:T(8,128)(2,1)S(1)}, u32[]{:S(2)}, u32[]{:S(2)}) collective-permute-start(bf16[32,3584]{1,0:T(8,128)(2,1)S(1)} %get-tuple-element.110), channel_id=1, source_target_pairs={{0,6},{1,7},{2,4},{3,5},{4,2},{5,3},{6,0},{7,1},{8,14},{9,15},{10,... | collective-permute-start | bytes 688136 | tf_op jit(solution)/shard_map/ppermute | solution.py:19
  82.7 3.8 %collective-permute-done.10.refs_1_ = bf16[32,3584]{1,0:T(8,128)(2,1)S(1)} collective-permute-done((bf16[32,3584]{1,0:T(8,128)(2,1)S(1)}, bf16[32,3584]{1,0:T(8,128)(2,1)S(1)}, u32[]{:S(2)}, u32[]{:S(2)}) %collective-permute-start.10) | collective-permute-done | bytes 229408 | tf_op jit(solution)/shard_map/ppermute | solution.py:19
  86.5 5.1 %collective-permute-done.11.refs_2_ = bf16[32,3584]{1,0:T(8,128)(2,1)S(1)} collective-permute-done((bf16[32,3584]{1,0:T(8,128)(2,1)S(1)}, bf16[32,3584]{1,0:T(8,128)(2,1)S(1)}, u32[]{:S(2)}, u32[]{:S(2)}) %collective-permute-start.11) | collective-permute-done | bytes 229408 | tf_op jit(solution)/shard_map/ppermute | solution.py:19
  91.6 5.2 %collective-permute-done.12.refs_3_ = bf16[32,3584]{1,0:T(8,128)(2,1)S(1)} collective-permute-done((bf16[32,3584]{1,0:T(8,128)(2,1)S(1)}, bf16[32,3584]{1,0:T(8,128)(2,1)S(1)}, u32[]{:S(2)}, u32[]{:S(2)}) %collective-permute-start.12) | collective-permute-done | bytes 229408 | tf_op jit(solution)/shard_map/ppermute | solution.py:19
  96.8 0.4 shard_map.111.first
  97.2 1.6 collective-permute-start.14
  98.8 1.2 collective-permute-start.13
  99.9 0.1 copy.20.picks.near_picks
  100.0 0.1 copy.25
  100.2 7.8 %collective-permute-done.14.current = bf16[64,3584]{1,0:T(8,128)(2,1)S(1)} collective-permute-done((bf16[64,3584]{1,0:T(8,128)(2,1)S(1)}, bf16[64,3584]{1,0:T(8,128)(2,1)S(1)}, u32[]{:S(2)}, u32[]{:S(2)}) %collective-permute-start.14) | collective-permute-done | bytes 458784 | tf_op jit(solution)/shard_map/ppermute | solution.py:19
  108.0 1.2 shard_map.112
  109.2 7.6 %collective-permute-done.13.current = bf16[64,3584]{1,0:T(8,128)(2,1)S(1)} collective-permute-done((bf16[64,3584]{1,0:T(8,128)(2,1)S(1)}, bf16[64,3584]{1,0:T(8,128)(2,1)S(1)}, u32[]{:S(2)}, u32[]{:S(2)}) %collective-permute-start.13) | collective-permute-done | bytes 458784 | tf_op jit(solution)/shard_map/ppermute | solution.py:368
  116.8 1.2 shard_map.113
  118.0 3.2 %collective-permute-start.15 = (bf16[32,3584]{1,0:T(8,128)(2,1)S(1)}, bf16[32,3584]{1,0:T(8,128)(2,1)S(1)}, u32[]{:S(2)}, u32[]{:S(2)}) collective-permute-start(bf16[32,3584]{1,0:T(8,128)(2,1)S(1)} %get-tuple-element.116), channel_id=1, source_target_pairs={{0,6},{1,7},{2,4},{3,5},{4,2},{5,3},{6,0},{7,1},{8,14},{9,15},{10,... | collective-permute-start | bytes 688136 | tf_op jit(solution)/shard_map/ppermute | solution.py:19
  121.2 1.0 collective-permute-start.16
  122.2 1.1 shard_map.114.mixing
  123.4 4.2 %collective-permute-done.15.refs_3_ = bf16[32,3584]{1,0:T(8,128)(2,1)S(1)} collective-permute-done((bf16[32,3584]{1,0:T(8,128)(2,1)S(1)}, bf16[32,3584]{1,0:T(8,128)(2,1)S(1)}, u32[]{:S(2)}, u32[]{:S(2)}) %collective-permute-start.15) | collective-permute-done | bytes 229408 | tf_op jit(solution)/shard_map/ppermute | solution.py:19
  127.6 1.7 collective-permute-start.20
  129.3 2.0 %collective-permute-start.21 = (bf16[32,3584]{1,0:T(8,128)(2,1)S(1)}, bf16[32,3584]{1,0:T(8,128)(2,1)S(1)}, u32[]{:S(2)}, u32[]{:S(2)}) collective-permute-start(bf16[32,3584]{1,0:T(8,128)(2,1)S(1)} %get-tuple-element.134), channel_id=1, source_target_pairs={{0,4},{1,5},{2,6},{3,7},{4,0},{5,1},{6,2},{7,3},{8,12},{9,13},{10,... | collective-permute-start | bytes 688136 | tf_op jit(solution)/shard_map/ppermute | solution.py:19
  131.2 0.5 collective-permute-start.22
  131.7 1.0 collective-permute-done.17.refs_2_
  132.7 8.3 %shard_map.115 = (bf16[32,3584]{1,0:T(8,128)(2,1)S(1)}, bf16[32,3584]{1,0:T(8,128)(2,1)S(1)}, bf16[32,3584]{1,0:T(8,128)(2,1)S(1)}, bf16[32,3584]{1,0:T(8,128)(2,1)S(1)}) custom-call(bf16[32,3584]{1,0:T(8,128)(2,1)S(1)} %get-tuple-element.124.refs_0_, bf16[32,3584]{1,0:T(8,128)(2,1)S(1)} %collective-permute-done.16.refs_1_, ...), custom_call_target="tpu_custom_call" | custom-call | flops 2818572288 | bytes 22020096 | tf_op jit(solution)/shard_map/pallas_call | solution.py:331
  141.0 0.6 collective-permute-start.18
  141.6 2.5 %collective-permute-start.19 = (bf16[32,3584]{1,0:T(8,128)(2,1)S(1)}, bf16[32,3584]{1,0:T(8,128)(2,1)S(1)}, u32[]{:S(2)}, u32[]{:S(2)}) collective-permute-start(bf16[32,3584]{1,0:T(8,128)(2,1)S(1)} %get-tuple-element.130), channel_id=1, source_target_pairs={{0,4},{1,5},{2,6},{3,7},{4,0},{5,1},{6,2},{7,3},{8,12},{9,13},{10,... | collective-permute-start | bytes 688136 | tf_op jit(solution)/shard_map/ppermute | solution.py:19
  144.1 0.6 collective-permute-start.23
  144.6 8.3 %shard_map.117 = (bf16[32,3584]{1,0:T(8,128)(2,1)S(1)}, bf16[32,3584]{1,0:T(8,128)(2,1)S(1)}, bf16[32,3584]{1,0:T(8,128)(2,1)S(1)}, bf16[32,3584]{1,0:T(8,128)(2,1)S(1)}) custom-call(bf16[32,3584]{1,0:T(8,128)(2,1)S(1)} %get-tuple-element.137.refs_0_, bf16[32,3584]{1,0:T(8,128)(2,1)S(1)} %collective-permute-done.20.refs_1_, ...), custom_call_target="tpu_custom_call" | custom-call | flops 2818572288 | bytes 22020096 | tf_op jit(solution)/shard_map/pallas_call | solution.py:333
  152.9 0.4 shard_map.116
  153.3 3.0 %collective-permute-start.24 = (bf16[64,3584]{1,0:T(8,128)(2,1)S(1)}, bf16[64,3584]{1,0:T(8,128)(2,1)S(1)}, u32[]{:S(2)}, u32[]{:S(2)}) collective-permute-start(bf16[64,3584]{1,0:T(8,128)(2,1)S(1)} %shard_map.116), channel_id=1, source_target_pairs={{0,8},{1,9},{2,10},{3,11},{4,12},{5,13},{6,14},{7,15},{8,0},{9,1},... | collective-permute-start | bytes 1376264 | tf_op jit(solution)/shard_map/ppermute | solution.py:19
  156.3 0.9 collective-permute-start.25
  157.2 1.5 collective-permute-start.26
  158.7 1.5 collective-permute-start.27
  160.2 2.2 %collective-permute-done.25.refs_1_ = bf16[32,3584]{1,0:T(8,128)(2,1)S(1)} collective-permute-done((bf16[32,3584]{1,0:T(8,128)(2,1)S(1)}, bf16[32,3584]{1,0:T(8,128)(2,1)S(1)}, u32[]{:S(2)}, u32[]{:S(2)}) %collective-permute-start.25) | collective-permute-done | bytes 229408 | tf_op jit(solution)/shard_map/ppermute | solution.py:19
  162.4 5.0 %collective-permute-done.26.refs_2_ = bf16[32,3584]{1,0:T(8,128)(2,1)S(1)} collective-permute-done((bf16[32,3584]{1,0:T(8,128)(2,1)S(1)}, bf16[32,3584]{1,0:T(8,128)(2,1)S(1)}, u32[]{:S(2)}, u32[]{:S(2)}) %collective-permute-start.26) | collective-permute-done | bytes 229408 | tf_op jit(solution)/shard_map/ppermute | solution.py:19
  167.3 5.1 %collective-permute-done.27.refs_3_ = bf16[32,3584]{1,0:T(8,128)(2,1)S(1)} collective-permute-done((bf16[32,3584]{1,0:T(8,128)(2,1)S(1)}, bf16[32,3584]{1,0:T(8,128)(2,1)S(1)}, u32[]{:S(2)}, u32[]{:S(2)}) %collective-permute-start.27) | collective-permute-done | bytes 229408 | tf_op jit(solution)/shard_map/ppermute | solution.py:19
  172.4 1.4 shard_map.118
  (40 shorter events, 0.9 us)
Async XLA Ops:
  0.6 39.6 %copy-start.2 = (f32[1,3584]{1,0:T(1,128)S(1)}, f32[1,3584]{1,0:T(1,128)}, u32[]{:S(2)}) copy-start(f32[1,3584]{1,0:T(1,128)} %gain.9) | copy-start | bytes 43012
  0.6 45.0 %copy-start.3 = (bf16[1,3584,8]{1,2,0:T(8,128)(2,1)S(1)}, bf16[1,3584,8]{1,2,0:T(8,128)(2,1)}, u32[]{:S(2)}) copy-start(bf16[1,3584,8]{1,2,0:T(8,128)(2,1)} %param.12) | copy-start | bytes 172036
  1.5 8.2 %collective-permute-start.1 = (s32[2,8,8,2]{2,1,3,0:T(8,128)S(1)}, s32[2,8,8,2]{2,1,3,0:T(8,128)S(1)}, u32[]{:S(2)}, u32[]{:S(2)}) collective-permute-start(s32[2,8,8,2]{2,1,3,0:T(8,128)S(1)} %broadcast_select_fusion.1), channel_id=1, source_target_pairs={{0,8},{1,9},{2,10},{3,11},{4,12},{5,13},{6,14},{7,15},{8,0},{9,1},... | collective-permute-start | bytes 3080 | tf_op jit(solution)/shard_map/ppermute | solution.py:19
  5.5 44.8 %collective-permute-start.3 = (bf16[3584,512]{1,0:T(8,128)(2,1)}, bf16[3584,512]{1,0:T(8,128)(2,1)}, u32[]{:S(2)}, u32[]{:S(2)}) collective-permute-start(bf16[3584,512]{1,0:T(8,128)(2,1)} %bitcast.58), channel_id=1, source_target_pairs={{0,1},{1,0},{2,3},{3,2},{4,5},{5,4},{6,7},{7,6},{8,9},{9,8},{10,11... | collective-permute-start | bytes 11010056 | tf_op jit(solution)/shard_map/ppermute | solution.py:19
  5.5 48.6 %collective-permute-start.4 = (bf16[3584,512]{1,0:T(8,128)(2,1)}, bf16[3584,512]{1,0:T(8,128)(2,1)}, u32[]{:S(2)}, u32[]{:S(2)}) collective-permute-start(bf16[3584,512]{1,0:T(8,128)(2,1)} %bitcast.63), channel_id=1, source_target_pairs={{0,1},{1,0},{2,3},{3,2},{4,5},{5,4},{6,7},{7,6},{8,9},{9,8},{10,11... | collective-permute-start | bytes 11010056 | tf_op jit(solution)/shard_map/ppermute | solution.py:19
  6.0 48.1 %collective-permute-start.5 = (bf16[512,3584]{1,0:T(8,128)(2,1)}, bf16[512,3584]{1,0:T(8,128)(2,1)}, u32[]{:S(2)}, u32[]{:S(2)}) collective-permute-start(bf16[512,3584]{1,0:T(8,128)(2,1)} %bitcast.68), channel_id=1, source_target_pairs={{0,1},{1,0},{2,3},{3,2},{4,5},{5,4},{6,7},{7,6},{8,9},{9,8},{10,11... | collective-permute-start | bytes 11010056 | tf_op jit(solution)/shard_map/ppermute | solution.py:19
  7.1 13.9 %collective-permute-start = (bf16[32,3584]{1,0:T(8,128)(2,1)S(1)}, bf16[32,3584]{1,0:T(8,128)(2,1)S(1)}, u32[]{:S(2)}, u32[]{:S(2)}) collective-permute-start(bf16[32,3584]{1,0:T(8,128)(2,1)S(1)} %get-tuple-element.153), channel_id=1, source_target_pairs={{0,8},{1,9},{2,10},{3,11},{4,12},{5,13},{6,14},{7,15},{8,0},{9,1},... | collective-permute-start | bytes 688136 | tf_op jit(solution)/shard_map/ppermute | solution.py:19
  7.8 0.7 copy-start
  21.0 0.7 copy-start.1
  23.6 18.5 %all-to-all-start = ((bf16[4,16,3584]{2,1,0:T(8,128)(2,1)}), bf16[4,16,3584]{2,1,0:T(8,128)(2,1)S(1)}, u32[]{:S(2)}, u32[]{:S(2)}) async-start(bf16[4,16,3584]{2,1,0:T(8,128)(2,1)} %bitcast.9), calls=%async_computation | async-start | bytes 917504 | tf_op jit(solution)/shard_map/all_to_all | solution.py:314
  27.0 13.2 %collective-permute-start.2 = (bf16[32,3584]{1,0:T(8,128)(2,1)S(1)}, bf16[32,3584]{1,0:T(8,128)(2,1)S(1)}, u32[]{:S(2)}, u32[]{:S(2)}) collective-permute-start(bf16[32,3584]{1,0:T(8,128)(2,1)S(1)} %get-tuple-element.152), channel_id=1, source_target_pairs={{0,8},{1,9},{2,10},{3,11},{4,12},{5,13},{6,14},{7,15},{8,0},{9,1},... | collective-permute-start | bytes 688136 | tf_op jit(solution)/shard_map/ppermute | solution.py:19
  42.0 12.1 %all-to-all-start.1 = ((bf16[4,16,3584]{2,1,0:T(8,128)(2,1)}), bf16[4,16,3584]{2,1,0:T(8,128)(2,1)S(1)}, u32[]{:S(2)}, u32[]{:S(2)}) async-start(bf16[4,16,3584]{2,1,0:T(8,128)(2,1)} %bitcast.16), calls=%async_computation.1 | async-start | bytes 917504 | tf_op jit(solution)/shard_map/all_to_all | solution.py:314
  46.7 16.6 %collective-permute-start.6 = (bf16[32,3584]{1,0:T(8,128)(2,1)S(1)}, bf16[32,3584]{1,0:T(8,128)(2,1)S(1)}, u32[]{:S(2)}, u32[]{:S(2)}) collective-permute-start(bf16[32,3584]{1,0:T(8,128)(2,1)S(1)} %get-tuple-element.94), channel_id=1, source_target_pairs={{0,2},{1,3},{2,0},{3,1},{4,6},{5,7},{6,4},{7,5},{8,10},{9,11},{10,... | collective-permute-start | bytes 688136 | tf_op jit(solution)/shard_map/ppermute | solution.py:19
  48.8 14.6 %collective-permute-start.7 = (bf16[32,3584]{1,0:T(8,128)(2,1)S(1)}, bf16[32,3584]{1,0:T(8,128)(2,1)S(1)}, u32[]{:S(2)}, u32[]{:S(2)}) collective-permute-start(bf16[32,3584]{1,0:T(8,128)(2,1)S(1)} %get-tuple-element.95), channel_id=1, source_target_pairs={{0,4},{1,5},{2,6},{3,7},{4,0},{5,1},{6,2},{7,3},{8,12},{9,13},{10,... | collective-permute-start | bytes 688136 | tf_op jit(solution)/shard_map/ppermute | solution.py:19
  50.3 13.1 %collective-permute-start.8 = (bf16[32,3584]{1,0:T(8,128)(2,1)S(1)}, bf16[32,3584]{1,0:T(8,128)(2,1)S(1)}, u32[]{:S(2)}, u32[]{:S(2)}) collective-permute-start(bf16[32,3584]{1,0:T(8,128)(2,1)S(1)} %get-tuple-element.96), channel_id=1, source_target_pairs={{0,6},{1,7},{2,4},{3,5},{4,2},{5,3},{6,0},{7,1},{8,14},{9,15},{10,... | collective-permute-start | bytes 688136 | tf_op jit(solution)/shard_map/ppermute | solution.py:19
  63.4 15.3 %all-to-all-start.2 = ((bf16[4,32,3584]{2,1,0:T(8,128)(2,1)}), bf16[4,32,3584]{2,1,0:T(8,128)(2,1)S(1)}, u32[]{:S(2)}, u32[]{:S(2)}) async-start(bf16[4,32,3584]{2,1,0:T(8,128)(2,1)} %bitcast.21), calls=%async_computation.2 | async-start | bytes 1835008 | tf_op jit(solution)/shard_map/all_to_all | solution.py:314
  79.1 17.7 %collective-permute-start.9 = (bf16[64,3584]{1,0:T(8,128)(2,1)S(1)}, bf16[64,3584]{1,0:T(8,128)(2,1)S(1)}, u32[]{:S(2)}, u32[]{:S(2)}) collective-permute-start(bf16[64,3584]{1,0:T(8,128)(2,1)S(1)} %shard_map.109), channel_id=1, source_target_pairs={{0,8},{1,9},{2,10},{3,11},{4,12},{5,13},{6,14},{7,15},{8,0},{9,1},... | collective-permute-start | bytes 1376264 | tf_op jit(solution)/shard_map/ppermute | solution.py:19
  79.2 7.3 %collective-permute-start.10 = (bf16[32,3584]{1,0:T(8,128)(2,1)S(1)}, bf16[32,3584]{1,0:T(8,128)(2,1)S(1)}, u32[]{:S(2)}, u32[]{:S(2)}) collective-permute-start(bf16[32,3584]{1,0:T(8,128)(2,1)S(1)} %get-tuple-element.108), channel_id=1, source_target_pairs={{0,2},{1,3},{2,0},{3,1},{4,6},{5,7},{6,4},{7,5},{8,10},{9,11},{10,... | collective-permute-start | bytes 688136 | tf_op jit(solution)/shard_map/ppermute | solution.py:19
  79.9 11.7 %collective-permute-start.11 = (bf16[32,3584]{1,0:T(8,128)(2,1)S(1)}, bf16[32,3584]{1,0:T(8,128)(2,1)S(1)}, u32[]{:S(2)}, u32[]{:S(2)}) collective-permute-start(bf16[32,3584]{1,0:T(8,128)(2,1)S(1)} %get-tuple-element.109), channel_id=1, source_target_pairs={{0,4},{1,5},{2,6},{3,7},{4,0},{5,1},{6,2},{7,3},{8,12},{9,13},{10,... | collective-permute-start | bytes 688136 | tf_op jit(solution)/shard_map/ppermute | solution.py:19
  80.1 16.7 %collective-permute-start.12 = (bf16[32,3584]{1,0:T(8,128)(2,1)S(1)}, bf16[32,3584]{1,0:T(8,128)(2,1)S(1)}, u32[]{:S(2)}, u32[]{:S(2)}) collective-permute-start(bf16[32,3584]{1,0:T(8,128)(2,1)S(1)} %get-tuple-element.110), channel_id=1, source_target_pairs={{0,6},{1,7},{2,4},{3,5},{4,2},{5,3},{6,0},{7,1},{8,14},{9,15},{10,... | collective-permute-start | bytes 688136 | tf_op jit(solution)/shard_map/ppermute | solution.py:19
  97.2 10.8 %collective-permute-start.14 = (bf16[64,3584]{1,0:T(8,128)(2,1)S(1)}, bf16[64,3584]{1,0:T(8,128)(2,1)S(1)}, u32[]{:S(2)}, u32[]{:S(2)}) collective-permute-start(bf16[64,3584]{1,0:T(8,128)(2,1)S(1)} %shard_map.111.first), channel_id=1, source_target_pairs={{0,16},{16,0},{1,17},{17,1},{2,18},{18,2},{3,19},{19,3},{4,20},{20... | collective-permute-start | bytes 1376264 | tf_op jit(solution)/shard_map/ppermute | solution.py:19
  98.8 18.0 %collective-permute-start.13 = (bf16[64,3584]{1,0:T(8,128)(2,1)S(1)}, bf16[64,3584]{1,0:T(8,128)(2,1)S(1)}, u32[]{:S(2)}, u32[]{:S(2)}) collective-permute-start(bf16[64,3584]{1,0:T(8,128)(2,1)S(1)} %shard_map.111.first), channel_id=1, source_target_pairs={{0,24},{1,25},{2,26},{3,27},{4,28},{5,29},{6,30},{7,31},{8,16},{9,... | collective-permute-start | bytes 1376264 | tf_op jit(solution)/shard_map/ppermute | solution.py:368
  118.0 9.6 %collective-permute-start.15 = (bf16[32,3584]{1,0:T(8,128)(2,1)S(1)}, bf16[32,3584]{1,0:T(8,128)(2,1)S(1)}, u32[]{:S(2)}, u32[]{:S(2)}) collective-permute-start(bf16[32,3584]{1,0:T(8,128)(2,1)S(1)} %get-tuple-element.116), channel_id=1, source_target_pairs={{0,6},{1,7},{2,4},{3,5},{4,2},{5,3},{6,0},{7,1},{8,14},{9,15},{10,... | collective-permute-start | bytes 688136 | tf_op jit(solution)/shard_map/ppermute | solution.py:19
  121.2 10.5 %collective-permute-start.16 = (bf16[32,3584]{1,0:T(8,128)(2,1)S(1)}, bf16[32,3584]{1,0:T(8,128)(2,1)S(1)}, u32[]{:S(2)}, u32[]{:S(2)}) collective-permute-start(bf16[32,3584]{1,0:T(8,128)(2,1)S(1)} %get-tuple-element.125), channel_id=1, source_target_pairs={{0,2},{1,3},{2,0},{3,1},{4,6},{5,7},{6,4},{7,5},{8,10},{9,11},{10,... | collective-permute-start | bytes 688136 | tf_op jit(solution)/shard_map/ppermute | solution.py:19
  122.2 10.5 %collective-permute-start.17 = (bf16[32,3584]{1,0:T(8,128)(2,1)S(1)}, bf16[32,3584]{1,0:T(8,128)(2,1)S(1)}, u32[]{:S(2)}, u32[]{:S(2)}) collective-permute-start(bf16[32,3584]{1,0:T(8,128)(2,1)S(1)} %get-tuple-element.126), channel_id=1, source_target_pairs={{0,4},{1,5},{2,6},{3,7},{4,0},{5,1},{6,2},{7,3},{8,12},{9,13},{10,... | collective-permute-start | bytes 688136 | tf_op jit(solution)/shard_map/ppermute | solution.py:19
  127.6 16.5 %collective-permute-start.20 = (bf16[32,3584]{1,0:T(8,128)(2,1)S(1)}, bf16[32,3584]{1,0:T(8,128)(2,1)S(1)}, u32[]{:S(2)}, u32[]{:S(2)}) collective-permute-start(bf16[32,3584]{1,0:T(8,128)(2,1)S(1)} %get-tuple-element.133), channel_id=1, source_target_pairs={{0,2},{1,3},{2,0},{3,1},{4,6},{5,7},{6,4},{7,5},{8,10},{9,11},{10,... | collective-permute-start | bytes 688136 | tf_op jit(solution)/shard_map/ppermute | solution.py:19
  129.3 14.8 %collective-permute-start.21 = (bf16[32,3584]{1,0:T(8,128)(2,1)S(1)}, bf16[32,3584]{1,0:T(8,128)(2,1)S(1)}, u32[]{:S(2)}, u32[]{:S(2)}) collective-permute-start(bf16[32,3584]{1,0:T(8,128)(2,1)S(1)} %get-tuple-element.134), channel_id=1, source_target_pairs={{0,4},{1,5},{2,6},{3,7},{4,0},{5,1},{6,2},{7,3},{8,12},{9,13},{10,... | collective-permute-start | bytes 688136 | tf_op jit(solution)/shard_map/ppermute | solution.py:19
  131.2 12.8 %collective-permute-start.22 = (bf16[32,3584]{1,0:T(8,128)(2,1)S(1)}, bf16[32,3584]{1,0:T(8,128)(2,1)S(1)}, u32[]{:S(2)}, u32[]{:S(2)}) collective-permute-start(bf16[32,3584]{1,0:T(8,128)(2,1)S(1)} %get-tuple-element.135), channel_id=1, source_target_pairs={{0,6},{1,7},{2,4},{3,5},{4,2},{5,3},{6,0},{7,1},{8,14},{9,15},{10,... | collective-permute-start | bytes 688136 | tf_op jit(solution)/shard_map/ppermute | solution.py:19
  141.0 11.9 %collective-permute-start.18 = (bf16[32,3584]{1,0:T(8,128)(2,1)S(1)}, bf16[32,3584]{1,0:T(8,128)(2,1)S(1)}, u32[]{:S(2)}, u32[]{:S(2)}) collective-permute-start(bf16[32,3584]{1,0:T(8,128)(2,1)S(1)} %get-tuple-element.129), channel_id=1, source_target_pairs={{0,2},{1,3},{2,0},{3,1},{4,6},{5,7},{6,4},{7,5},{8,10},{9,11},{10,... | collective-permute-start | bytes 688136 | tf_op jit(solution)/shard_map/ppermute | solution.py:19
  141.6 11.4 %collective-permute-start.19 = (bf16[32,3584]{1,0:T(8,128)(2,1)S(1)}, bf16[32,3584]{1,0:T(8,128)(2,1)S(1)}, u32[]{:S(2)}, u32[]{:S(2)}) collective-permute-start(bf16[32,3584]{1,0:T(8,128)(2,1)S(1)} %get-tuple-element.130), channel_id=1, source_target_pairs={{0,4},{1,5},{2,6},{3,7},{4,0},{5,1},{6,2},{7,3},{8,12},{9,13},{10,... | collective-permute-start | bytes 688136 | tf_op jit(solution)/shard_map/ppermute | solution.py:19
  144.1 8.9 %collective-permute-start.23 = (bf16[32,3584]{1,0:T(8,128)(2,1)S(1)}, bf16[32,3584]{1,0:T(8,128)(2,1)S(1)}, u32[]{:S(2)}, u32[]{:S(2)}) collective-permute-start(bf16[32,3584]{1,0:T(8,128)(2,1)S(1)} %get-tuple-element.136), channel_id=1, source_target_pairs={{0,6},{1,7},{2,4},{3,5},{4,2},{5,3},{6,0},{7,1},{8,14},{9,15},{10,... | collective-permute-start | bytes 688136 | tf_op jit(solution)/shard_map/ppermute | solution.py:19
  153.3 19.1 %collective-permute-start.24 = (bf16[64,3584]{1,0:T(8,128)(2,1)S(1)}, bf16[64,3584]{1,0:T(8,128)(2,1)S(1)}, u32[]{:S(2)}, u32[]{:S(2)}) collective-permute-start(bf16[64,3584]{1,0:T(8,128)(2,1)S(1)} %shard_map.116), channel_id=1, source_target_pairs={{0,8},{1,9},{2,10},{3,11},{4,12},{5,13},{6,14},{7,15},{8,0},{9,1},... | collective-permute-start | bytes 1376264 | tf_op jit(solution)/shard_map/ppermute | solution.py:19
  156.3 6.0 %collective-permute-start.25 = (bf16[32,3584]{1,0:T(8,128)(2,1)S(1)}, bf16[32,3584]{1,0:T(8,128)(2,1)S(1)}, u32[]{:S(2)}, u32[]{:S(2)}) collective-permute-start(bf16[32,3584]{1,0:T(8,128)(2,1)S(1)} %get-tuple-element.147), channel_id=1, source_target_pairs={{0,2},{1,3},{2,0},{3,1},{4,6},{5,7},{6,4},{7,5},{8,10},{9,11},{10,... | collective-permute-start | bytes 688136 | tf_op jit(solution)/shard_map/ppermute | solution.py:19
  157.2 10.1 %collective-permute-start.26 = (bf16[32,3584]{1,0:T(8,128)(2,1)S(1)}, bf16[32,3584]{1,0:T(8,128)(2,1)S(1)}, u32[]{:S(2)}, u32[]{:S(2)}) collective-permute-start(bf16[32,3584]{1,0:T(8,128)(2,1)S(1)} %get-tuple-element.148), channel_id=1, source_target_pairs={{0,4},{1,5},{2,6},{3,7},{4,0},{5,1},{6,2},{7,3},{8,12},{9,13},{10,... | collective-permute-start | bytes 688136 | tf_op jit(solution)/shard_map/ppermute | solution.py:19
  158.7 13.7 %collective-permute-start.27 = (bf16[32,3584]{1,0:T(8,128)(2,1)S(1)}, bf16[32,3584]{1,0:T(8,128)(2,1)S(1)}, u32[]{:S(2)}, u32[]{:S(2)}) collective-permute-start(bf16[32,3584]{1,0:T(8,128)(2,1)S(1)} %get-tuple-element.149), channel_id=1, source_target_pairs={{0,6},{1,7},{2,4},{3,5},{4,2},{5,3},{6,0},{7,1},{8,14},{9,15},{10,... | collective-permute-start | bytes 688136 | tf_op jit(solution)/shard_map/ppermute | solution.py:19

commit v7 on v6

--- a/solution.py
+++ b/solution.py
@@ -260,10 +260,10 @@
 
     def far_start(cut):
         piece = jax.ShapeDtypeStruct((tokens // cut, features), BF16)
-        some = jax.ShapeDtypeStruct((chips * room // cut, features), BF16)
+        some = jax.ShapeDtypeStruct((room // cut, features), BF16)
         return call(
-            functools.partial(start_kernel, False, (tok_count, capacity, room // cut, chips)),
-            [piece, some],
+            functools.partial(start_kernel, True, (tok_count, capacity, room // cut, chips)),
+            [piece] + [some] * chips,
             [SMEM, VMEM, VMEM, VMEM],
             pack_flops // cut,
             4 * row_bytes // cut,
@@ -271,7 +271,7 @@
 
     def gates(cut):
         return call(
-            functools.partial(gate_kernel, cut == 1, geometry),
+            functools.partial(gate_kernel, True, geometry),
             jax.ShapeDtypeStruct((2, 2, tokens, chips * room), BF16),
             [SMEM] + [VMEM] * (4 + cut),
             4 * tokens * features * 128,
@@ -323,27 +323,18 @@
         far_current = list(far_current)
         pieces = len(far_current)
         far_current[-1], *near_rows = tied(far_current[-1], *near_rows)
-        if pieces == 1:
-            normed_far, *rows = start(where, far_current[0], far_picks, norm_gain)
-            mixing = gates(1)(where, normed, picks, far_picks, scorer, normed_far)
-            far_in = pass_on(rows)
-            far_in[-1], mixing, *near_rows = tied(far_in[-1], mixing, *near_rows)
-            far_out = list(expert(chips, 0, [block] * chips)(*far_in, *weights))
-            far_out[-1], *near_in = tied(far_out[-1], *pass_on(near_rows))
-            near_out = expert(chips, 0, [block] * chips)(*near_in, *weights)
-            far_part, *near_out = tied(far_mix(mixing, *pass_on(far_out)), *near_out)
-        else:
-            far_in, far_normed = [], []
-            for states, chosen in zip(far_current, jnp.split(far_picks, pieces)):
-                part, rows = far_start(pieces)(where, states, chosen, norm_gain)
-                far_normed.append(part)
-                far_in.append(spread(rows))
-            mixing = gates(pieces)(where, normed, picks, far_picks, scorer, *far_normed)
-            far_in[-1], mixing, *near_rows = tied(far_in[-1], mixing, *near_rows)
-            (far_out,) = expert(pieces, chips, [packed])(*far_in, *weights)
-            far_out, *near_in = tied(far_out, *pass_on(near_rows))
-            near_out = expert(chips, 0, [block] * chips)(*near_in, *weights)
-            far_part, *near_out = tied(far_mix(mixing, spread(far_out)), *near_out)
+        far_in, far_normed = [], []
+        for states, chosen in zip(far_current, jnp.split(far_picks, pieces)):
+            part, *rows = far_start(pieces)(where, states, chosen, norm_gain)
+            far_normed.append(part)
+            far_in.append(pass_on(rows))
+        mixing = gates(pieces)(where, normed, picks, far_picks, scorer, *far_normed)
+        far_in = [piece[k] for k in range(chips) for piece in far_in]
+        far_in[-1], mixing, *near_rows = tied(far_in[-1], mixing, *near_rows)
+        far_out = list(expert(len(far_in), 0, [block] * chips)(*far_in, *weights))
+        far_out[-1], *near_in = tied(far_out[-1], *pass_on(near_rows))
+        near_out = expert(chips, 0, [block] * chips)(*near_in, *weights)
+        far_part, *near_out = tied(far_mix(mixing, *pass_on(far_out)), *near_out)
         beyond = flipped(far_part, "ep", half)
         return mixing, current, beyond, pass_on(near_out)
 

time: 174 us -> 174 us (level)
    ppermute x27 -> x36, starting transfers between devices: 32.9 us -> 45.6 us  [flipped(): return lax.ppermute(value, axis, [(i, i ^ mask) for i in range(count)])]
    all_to_all x3 -> x0, starting transfers between devices: 10.6 us -> none  [spread(): lax.all_to_all(rows, 'ep', split_axis=0, concat_axis=0, tiled=True, axis_...]
    all_to_all x3 -> x0, waiting for transfers between devices: 7.11 us -> none  [spread(): lax.all_to_all(rows, 'ep', split_axis=0, concat_axis=0, tiled=True, axis_...]
    ppermute x1, waiting for transfers between devices: 7.61 us -> 11 us  [shards(): far = [lax.ppermute(first, ('section', 'ep'), across)]]
    ppermute x27 -> x36, waiting for transfers between devices: 63 us -> 65.9 us  [flipped(): return lax.ppermute(value, axis, [(i, i ^ mask) for i in range(count)])]
    pallas_call x6 -> x5, Pallas kernels: 23.4 us -> 21.3 us  [the longest x2 16.6 us: layer(): far_out = list(expert(len(far_in), 0, [block] * chips)(*far_in, *weights))]
  transfers between devices with their start and end apart: 31 -> 37, of which waited for: 14 -> 16; matrix products, arithmetic and copies ran while one was open for 1% -> 2% of each run, Pallas kernels for 24% -> 24%
where the time goes in v7:
time: 174 us
  waiting for transfers between devices  76.9 us (44%)
  starting transfers between devices  45.6 us (26%)
  Pallas kernels  45.1 us (26%)
  local copies, waits for them, and re-layouts  3.83 us (2%)
    ppermute x36, waiting for transfers between devices, flipped(): return lax.ppermute(value, axis, [(i, i ^ mask) for i in range(count)])  65.9 us
    ppermute x36, starting transfers between devices, flipped(): return lax.ppermute(value, axis, [(i, i ^ mask) for i in range(count)])  45.6 us
    pallas_call x2, Pallas kernels, layer(): far_out = list(expert(len(far_in), 0, [block] * chips)(*far_in, *weights))  16.6 us
    pallas_call x2, Pallas kernels, layer(): near_out = expert(chips, 0, [block] * chips)(*near_in, *weights)  16.5 us
    ppermute x1, waiting for transfers between devices, shards(): far = [lax.ppermute(first, ('section', 'ep'), across)]  11 us
    pallas_call x3, Pallas kernels, layer(): part, *rows = far_start(pieces)(where, states, chosen, norm_gain)  4.76 us
  transfers between devices with their start and end apart: 37, of which 16 were waited for; matrix products, arithmetic and copies ran while one was open for 2% of the time, Pallas kernels for 24%

profile of v7, /device:TPU:0, one launch (start us, length us, event | category | flops | bytes accessed | tf_op | source)
XLA Modules:
  0.0 173.6 jit_solution(14562562175548826011)
XLA Ops:
  0.6 0.5 collective-permute-start.9
  1.2 0.4 collective-permute-start.11
  1.7 0.7 copy_bitcast_fusion
  2.5 3.7 %collective-permute-start.1 = (s32[2,8,8,2]{2,1,3,0:T(8,128)S(1)}, s32[2,8,8,2]{2,1,3,0:T(8,128)S(1)}, u32[]{:S(2)}, u32[]{:S(2)}) collective-permute-start(s32[2,8,8,2]{2,1,3,0:T(8,128)S(1)} %broadcast_select_fusion.1), channel_id=1, source_target_pairs={{0,8},{1,9},{2,10},{3,11},{4,12},{5,13},{6,14},{7,15},{8,0},{9,1},... | collective-permute-start | bytes 3080 | tf_op jit(solution)/shard_map/ppermute | solution.py:19
  6.1 1.1 broadcast_select_fusion
  7.7 0.2 collective-permute-done.1
  7.9 2.9 %collective-permute-start = (bf16[32,3584]{1,0:T(8,128)(2,1)S(1)}, bf16[32,3584]{1,0:T(8,128)(2,1)S(1)}, u32[]{:S(2)}, u32[]{:S(2)}) collective-permute-start(bf16[32,3584]{1,0:T(8,128)(2,1)S(1)} %get-tuple-element.173), channel_id=1, source_target_pairs={{0,8},{1,9},{2,10},{3,11},{4,12},{5,13},{6,14},{7,15},{8,0},{9,1},... | collective-permute-start | bytes 688136 | tf_op jit(solution)/shard_map/ppermute | solution.py:19
  11.0 15.5 %collective-permute-done.3.current = bf16[32,3584]{1,0:T(8,128)(2,1)S(1)} collective-permute-done((bf16[32,3584]{1,0:T(8,128)(2,1)S(1)}, bf16[32,3584]{1,0:T(8,128)(2,1)S(1)}, u32[]{:S(2)}, u32[]{:S(2)}) %collective-permute-start.3) | collective-permute-done | bytes 229408 | tf_op jit(solution)/shard_map/ppermute | solution.py:19
  26.5 0.7 copy-done
  27.2 1.7 shard_map.106
  28.9 1.5 collective-permute-start.4
  30.4 0.2 collective-permute-done.current
  30.7 0.7 copy-done.1
  31.4 1.2 shard_map.104
  32.7 0.7 copy-done.2
  33.5 1.7 shard_map.105
  35.1 3.0 %collective-permute-start.8 = (bf16[16,3584]{1,0:T(8,128)(2,1)S(1)}, bf16[16,3584]{1,0:T(8,128)(2,1)S(1)}, u32[]{:S(2)}, u32[]{:S(2)}) collective-permute-start(bf16[16,3584]{1,0:T(8,128)(2,1)S(1)} %get-tuple-element.107), channel_id=1, source_target_pairs={{0,6},{1,7},{2,4},{3,5},{4,2},{5,3},{6,0},{7,1},{8,14},{9,15},{10,... | collective-permute-start | bytes 344072 | tf_op jit(solution)/shard_map/ppermute | solution.py:19
  38.2 3.2 %collective-permute-done.8.refs_6_ = bf16[16,3584]{1,0:T(8,128)(2,1)S(1)} collective-permute-done((bf16[16,3584]{1,0:T(8,128)(2,1)S(1)}, bf16[16,3584]{1,0:T(8,128)(2,1)S(1)}, u32[]{:S(2)}, u32[]{:S(2)}) %collective-permute-start.8) | collective-permute-done | bytes 114720 | tf_op jit(solution)/shard_map/ppermute | solution.py:19
  41.4 2.0 %collective-permute-start.5 = (bf16[16,3584]{1,0:T(8,128)(2,1)}, bf16[16,3584]{1,0:T(8,128)(2,1)S(1)}, u32[]{:S(2)}, u32[]{:S(2)}) collective-permute-start(bf16[16,3584]{1,0:T(8,128)(2,1)} %get-tuple-element.104), channel_id=1, source_target_pairs={{0,2},{1,3},{2,0},{3,1},{4,6},{5,7},{6,4},{7,5},{8,10},{9,11},{10,... | collective-permute-start | bytes 344072 | tf_op jit(solution)/shard_map/ppermute | solution.py:19
  43.4 0.5 collective-permute-done.2.refs_7_
  43.9 1.0 collective-permute-start.7
  44.9 0.1 copy.24
  45.0 1.1 shard_map.107.mixing
  46.2 0.2 collective-permute-done.5.refs_3_
  46.4 2.1 %collective-permute-start.14 = (bf16[32,3584]{1,0:T(8,128)(2,1)S(1)}, bf16[32,3584]{1,0:T(8,128)(2,1)S(1)}, u32[]{:S(2)}, u32[]{:S(2)}) collective-permute-start(bf16[32,3584]{1,0:T(8,128)(2,1)S(1)} %get-tuple-element.114), channel_id=1, source_target_pairs={{0,2},{1,3},{2,0},{3,1},{4,6},{5,7},{6,4},{7,5},{8,10},{9,11},{10,... | collective-permute-start | bytes 688136 | tf_op jit(solution)/shard_map/ppermute | solution.py:19
  48.5 0.4 collective-permute-done.7.refs_5_
  48.9 1.1 collective-permute-start.15
  50.0 1.0 collective-permute-start.16
  51.0 8.3 %shard_map.108 = (bf16[32,3584]{1,0:T(8,128)(2,1)S(1)}, bf16[32,3584]{1,0:T(8,128)(2,1)S(1)}, bf16[32,3584]{1,0:T(8,128)(2,1)S(1)}, bf16[32,3584]{1,0:T(8,128)(2,1)S(1)}) custom-call(bf16[16,3584]{1,0:T(8,128)(2,1)S(1)} %get-tuple-element.101.refs_0_, bf16[16,3584]{1,0:T(8,128)(2,1)S(1)} %get-tuple-element.102.refs_1_, ...), custom_call_target="tpu_custom_call" | custom-call | flops 2818572288 | bytes 22020096 | tf_op jit(solution)/shard_map/pallas_call | solution.py:334
  59.4 2.0 %collective-permute-start.17 = (bf16[32,3584]{1,0:T(8,128)(2,1)S(1)}, bf16[32,3584]{1,0:T(8,128)(2,1)S(1)}, u32[]{:S(2)}, u32[]{:S(2)}) collective-permute-start(bf16[32,3584]{1,0:T(8,128)(2,1)S(1)} %get-tuple-element.117), channel_id=1, source_target_pairs={{0,6},{1,7},{2,4},{3,5},{4,2},{5,3},{6,0},{7,1},{8,14},{9,15},{10,... | collective-permute-start | bytes 688136 | tf_op jit(solution)/shard_map/ppermute | solution.py:19
  61.3 1.6 collective-permute-start.12
  62.9 8.3 %shard_map.110 = (bf16[32,3584]{1,0:T(8,128)(2,1)S(1)}, bf16[32,3584]{1,0:T(8,128)(2,1)S(1)}, bf16[32,3584]{1,0:T(8,128)(2,1)S(1)}, bf16[32,3584]{1,0:T(8,128)(2,1)S(1)}) custom-call(bf16[32,3584]{1,0:T(8,128)(2,1)S(1)} %get-tuple-element.118.refs_0_, bf16[32,3584]{1,0:T(8,128)(2,1)S(1)} %collective-permute-done.14.refs_1_, ...), custom_call_target="tpu_custom_call" | custom-call | flops 2818572288 | bytes 22020096 | tf_op jit(solution)/shard_map/pallas_call | solution.py:336
  71.2 0.4 shard_map.109
  71.6 2.0 %collective-permute-start.18 = (bf16[64,3584]{1,0:T(8,128)(2,1)S(1)}, bf16[64,3584]{1,0:T(8,128)(2,1)S(1)}, u32[]{:S(2)}, u32[]{:S(2)}) collective-permute-start(bf16[64,3584]{1,0:T(8,128)(2,1)S(1)} %shard_map.109), channel_id=1, source_target_pairs={{0,8},{1,9},{2,10},{3,11},{4,12},{5,13},{6,14},{7,15},{8,0},{9,1},... | collective-permute-start | bytes 1376264 | tf_op jit(solution)/shard_map/ppermute | solution.py:19
  73.6 1.0 collective-permute-start.19
  74.7 2.4 %collective-permute-start.21 = (bf16[32,3584]{1,0:T(8,128)(2,1)S(1)}, bf16[32,3584]{1,0:T(8,128)(2,1)S(1)}, u32[]{:S(2)}, u32[]{:S(2)}) collective-permute-start(bf16[32,3584]{1,0:T(8,128)(2,1)S(1)} %get-tuple-element.130), channel_id=1, source_target_pairs={{0,6},{1,7},{2,4},{3,5},{4,2},{5,3},{6,0},{7,1},{8,14},{9,15},{10,... | collective-permute-start | bytes 688136 | tf_op jit(solution)/shard_map/ppermute | solution.py:19
  77.1 3.5 %collective-permute-done.19.refs_1_ = bf16[32,3584]{1,0:T(8,128)(2,1)S(1)} collective-permute-done((bf16[32,3584]{1,0:T(8,128)(2,1)S(1)}, bf16[32,3584]{1,0:T(8,128)(2,1)S(1)}, u32[]{:S(2)}, u32[]{:S(2)}) %collective-permute-start.19) | collective-permute-done | bytes 229408 | tf_op jit(solution)/shard_map/ppermute | solution.py:19
  80.6 6.9 %collective-permute-done.20.refs_2_ = bf16[32,3584]{1,0:T(8,128)(2,1)S(1)} collective-permute-done((bf16[32,3584]{1,0:T(8,128)(2,1)S(1)}, bf16[32,3584]{1,0:T(8,128)(2,1)S(1)}, u32[]{:S(2)}, u32[]{:S(2)}) %collective-permute-start.20) | collective-permute-done | bytes 229408 | tf_op jit(solution)/shard_map/ppermute | solution.py:19
  87.5 5.3 %collective-permute-done.21.refs_3_ = bf16[32,3584]{1,0:T(8,128)(2,1)S(1)} collective-permute-done((bf16[32,3584]{1,0:T(8,128)(2,1)S(1)}, bf16[32,3584]{1,0:T(8,128)(2,1)S(1)}, u32[]{:S(2)}, u32[]{:S(2)}) %collective-permute-start.21) | collective-permute-done | bytes 229408 | tf_op jit(solution)/shard_map/ppermute | solution.py:19
  92.8 0.4 shard_map.111.first
  93.2 1.6 collective-permute-start.23
  95.0 8.6 %collective-permute-done.23.current = bf16[64,3584]{1,0:T(8,128)(2,1)S(1)} collective-permute-done((bf16[64,3584]{1,0:T(8,128)(2,1)S(1)}, bf16[64,3584]{1,0:T(8,128)(2,1)S(1)}, u32[]{:S(2)}, u32[]{:S(2)}) %collective-permute-start.23) | collective-permute-done | bytes 458784 | tf_op jit(solution)/shard_map/ppermute | solution.py:19
  103.7 1.2 shard_map.112
  104.9 11.0 %collective-permute-done.22.current = bf16[64,3584]{1,0:T(8,128)(2,1)S(1)} collective-permute-done((bf16[64,3584]{1,0:T(8,128)(2,1)S(1)}, bf16[64,3584]{1,0:T(8,128)(2,1)S(1)}, u32[]{:S(2)}, u32[]{:S(2)}) %collective-permute-start.22) | collective-permute-done | bytes 458784 | tf_op jit(solution)/shard_map/ppermute | solution.py:359
  115.9 1.4 shard_map.113
  117.4 0.7 collective-permute-start.25
  118.1 2.8 %collective-permute-start.26 = (bf16[32,3584]{1,0:T(8,128)(2,1)S(1)}, bf16[32,3584]{1,0:T(8,128)(2,1)S(1)}, u32[]{:S(2)}, u32[]{:S(2)}) collective-permute-start(bf16[32,3584]{1,0:T(8,128)(2,1)S(1)} %get-tuple-element.146), channel_id=1, source_target_pairs={{0,4},{1,5},{2,6},{3,7},{4,0},{5,1},{6,2},{7,3},{8,12},{9,13},{10,... | collective-permute-start | bytes 688136 | tf_op jit(solution)/shard_map/ppermute | solution.py:19
  120.9 1.1 shard_map.114.mixing
  122.0 4.8 %collective-permute-done.24.refs_3_ = bf16[32,3584]{1,0:T(8,128)(2,1)S(1)} collective-permute-done((bf16[32,3584]{1,0:T(8,128)(2,1)S(1)}, bf16[32,3584]{1,0:T(8,128)(2,1)S(1)}, u32[]{:S(2)}, u32[]{:S(2)}) %collective-permute-start.24) | collective-permute-done | bytes 229408 | tf_op jit(solution)/shard_map/ppermute | solution.py:19
  126.8 0.6 collective-permute-start.30
  127.4 2.9 %collective-permute-start.31 = (bf16[32,3584]{1,0:T(8,128)(2,1)S(1)}, bf16[32,3584]{1,0:T(8,128)(2,1)S(1)}, u32[]{:S(2)}, u32[]{:S(2)}) collective-permute-start(bf16[32,3584]{1,0:T(8,128)(2,1)S(1)} %get-tuple-element.155), channel_id=1, source_target_pairs={{0,6},{1,7},{2,4},{3,5},{4,2},{5,3},{6,0},{7,1},{8,14},{9,15},{10,... | collective-permute-start | bytes 688136 | tf_op jit(solution)/shard_map/ppermute | solution.py:19
  130.3 8.3 %shard_map.115 = (bf16[32,3584]{1,0:T(8,128)(2,1)S(1)}, bf16[32,3584]{1,0:T(8,128)(2,1)S(1)}, bf16[32,3584]{1,0:T(8,128)(2,1)S(1)}, bf16[32,3584]{1,0:T(8,128)(2,1)S(1)}) custom-call(bf16[32,3584]{1,0:T(8,128)(2,1)S(1)} %get-tuple-element.144.refs_0_, bf16[32,3584]{1,0:T(8,128)(2,1)S(1)} %collective-permute-done.25.refs_1_, ...), custom_call_target="tpu_custom_call" | custom-call | flops 2818572288 | bytes 22020096 | tf_op jit(solution)/shard_map/pallas_call | solution.py:334
  138.6 2.0 %collective-permute-start.27 = (bf16[32,3584]{1,0:T(8,128)(2,1)S(1)}, bf16[32,3584]{1,0:T(8,128)(2,1)S(1)}, u32[]{:S(2)}, u32[]{:S(2)}) collective-permute-start(bf16[32,3584]{1,0:T(8,128)(2,1)S(1)} %get-tuple-element.149), channel_id=1, source_target_pairs={{0,2},{1,3},{2,0},{3,1},{4,6},{5,7},{6,4},{7,5},{8,10},{9,11},{10,... | collective-permute-start | bytes 688136 | tf_op jit(solution)/shard_map/ppermute | solution.py:19
  140.7 1.6 collective-permute-start.32
  142.3 8.3 %shard_map.117 = (bf16[32,3584]{1,0:T(8,128)(2,1)S(1)}, bf16[32,3584]{1,0:T(8,128)(2,1)S(1)}, bf16[32,3584]{1,0:T(8,128)(2,1)S(1)}, bf16[32,3584]{1,0:T(8,128)(2,1)S(1)}) custom-call(bf16[32,3584]{1,0:T(8,128)(2,1)S(1)} %get-tuple-element.157.refs_0_, bf16[32,3584]{1,0:T(8,128)(2,1)S(1)} %collective-permute-done.29.refs_1_, ...), custom_call_target="tpu_custom_call" | custom-call | flops 2818572288 | bytes 22020096 | tf_op jit(solution)/shard_map/pallas_call | solution.py:336
  150.6 0.4 shard_map.116
  151.0 1.4 collective-permute-start.33
  152.4 1.0 collective-permute-start.34
  153.4 2.0 %collective-permute-start.35 = (bf16[32,3584]{1,0:T(8,128)(2,1)S(1)}, bf16[32,3584]{1,0:T(8,128)(2,1)S(1)}, u32[]{:S(2)}, u32[]{:S(2)}) collective-permute-start(bf16[32,3584]{1,0:T(8,128)(2,1)S(1)} %get-tuple-element.168), channel_id=1, source_target_pairs={{0,4},{1,5},{2,6},{3,7},{4,0},{5,1},{6,2},{7,3},{8,12},{9,13},{10,... | collective-permute-start | bytes 688136 | tf_op jit(solution)/shard_map/ppermute | solution.py:19
  155.4 0.4 collective-permute-start.36
  155.8 5.0 %collective-permute-done.34.refs_1_ = bf16[32,3584]{1,0:T(8,128)(2,1)S(1)} collective-permute-done((bf16[32,3584]{1,0:T(8,128)(2,1)S(1)}, bf16[32,3584]{1,0:T(8,128)(2,1)S(1)}, u32[]{:S(2)}, u32[]{:S(2)}) %collective-permute-start.34) | collective-permute-done | bytes 229408 | tf_op jit(solution)/shard_map/ppermute | solution.py:19
  160.8 6.8 %collective-permute-done.35.refs_2_ = bf16[32,3584]{1,0:T(8,128)(2,1)S(1)} collective-permute-done((bf16[32,3584]{1,0:T(8,128)(2,1)S(1)}, bf16[32,3584]{1,0:T(8,128)(2,1)S(1)}, u32[]{:S(2)}, u32[]{:S(2)}) %collective-permute-start.35) | collective-permute-done | bytes 229408 | tf_op jit(solution)/shard_map/ppermute | solution.py:19
  167.6 4.6 %collective-permute-done.36.refs_3_ = bf16[32,3584]{1,0:T(8,128)(2,1)S(1)} collective-permute-done((bf16[32,3584]{1,0:T(8,128)(2,1)S(1)}, bf16[32,3584]{1,0:T(8,128)(2,1)S(1)}, u32[]{:S(2)}, u32[]{:S(2)}) %collective-permute-start.36) | collective-permute-done | bytes 229408 | tf_op jit(solution)/shard_map/ppermute | solution.py:19
  172.2 1.4 shard_map.118
  (54 shorter events, 1.5 us)
Async XLA Ops:
  0.6 44.4 %copy-start.4 = (bf16[1,3584,8]{1,2,0:T(8,128)(2,1)S(1)}, bf16[1,3584,8]{1,2,0:T(8,128)(2,1)}, u32[]{:S(2)}) copy-start(bf16[1,3584,8]{1,2,0:T(8,128)(2,1)} %param.12) | copy-start | bytes 172036
  0.6 49.4 %collective-permute-start.9 = (bf16[3584,512]{1,0:T(8,128)(2,1)}, bf16[3584,512]{1,0:T(8,128)(2,1)}, u32[]{:S(2)}, u32[]{:S(2)}) collective-permute-start(bf16[3584,512]{1,0:T(8,128)(2,1)} %bitcast.49), channel_id=1, source_target_pairs={{0,1},{1,0},{2,3},{3,2},{4,5},{5,4},{6,7},{7,6},{8,9},{9,8},{10,11... | collective-permute-start | bytes 11010056 | tf_op jit(solution)/shard_map/ppermute | solution.py:19
  1.2 49.9 %collective-permute-start.10 = (bf16[3584,512]{1,0:T(8,128)(2,1)}, bf16[3584,512]{1,0:T(8,128)(2,1)}, u32[]{:S(2)}, u32[]{:S(2)}) collective-permute-start(bf16[3584,512]{1,0:T(8,128)(2,1)} %bitcast.54), channel_id=1, source_target_pairs={{0,1},{1,0},{2,3},{3,2},{4,5},{5,4},{6,7},{7,6},{8,9},{9,8},{10,11... | collective-permute-start | bytes 11010056 | tf_op jit(solution)/shard_map/ppermute | solution.py:19
  1.2 49.8 %collective-permute-start.11 = (bf16[512,3584]{1,0:T(8,128)(2,1)}, bf16[512,3584]{1,0:T(8,128)(2,1)}, u32[]{:S(2)}, u32[]{:S(2)}) collective-permute-start(bf16[512,3584]{1,0:T(8,128)(2,1)} %bitcast.59), channel_id=1, source_target_pairs={{0,1},{1,0},{2,3},{3,2},{4,5},{5,4},{6,7},{7,6},{8,9},{9,8},{10,11... | collective-permute-start | bytes 11010056 | tf_op jit(solution)/shard_map/ppermute | solution.py:19
  2.5 5.4 %collective-permute-start.1 = (s32[2,8,8,2]{2,1,3,0:T(8,128)S(1)}, s32[2,8,8,2]{2,1,3,0:T(8,128)S(1)}, u32[]{:S(2)}, u32[]{:S(2)}) collective-permute-start(s32[2,8,8,2]{2,1,3,0:T(8,128)S(1)} %broadcast_select_fusion.1), channel_id=1, source_target_pairs={{0,8},{1,9},{2,10},{3,11},{4,12},{5,13},{6,14},{7,15},{8,0},{9,1},... | collective-permute-start | bytes 3080 | tf_op jit(solution)/shard_map/ppermute | solution.py:19
  7.2 19.2 %collective-permute-start.3 = (bf16[32,3584]{1,0:T(8,128)(2,1)S(1)}, bf16[32,3584]{1,0:T(8,128)(2,1)S(1)}, u32[]{:S(2)}, u32[]{:S(2)}) collective-permute-start(bf16[32,3584]{1,0:T(8,128)(2,1)S(1)} %get-tuple-element.172), channel_id=1, source_target_pairs={{0,8},{1,9},{2,10},{3,11},{4,12},{5,13},{6,14},{7,15},{8,0},{9,1},... | collective-permute-start | bytes 688136 | tf_op jit(solution)/shard_map/ppermute | solution.py:19
  7.9 22.8 %collective-permute-start = (bf16[32,3584]{1,0:T(8,128)(2,1)S(1)}, bf16[32,3584]{1,0:T(8,128)(2,1)S(1)}, u32[]{:S(2)}, u32[]{:S(2)}) collective-permute-start(bf16[32,3584]{1,0:T(8,128)(2,1)S(1)} %get-tuple-element.173), channel_id=1, source_target_pairs={{0,8},{1,9},{2,10},{3,11},{4,12},{5,13},{6,14},{7,15},{8,0},{9,1},... | collective-permute-start | bytes 688136 | tf_op jit(solution)/shard_map/ppermute | solution.py:19
  26.5 0.7 copy-start
  28.9 6.2 %collective-permute-start.4 = (bf16[16,3584]{1,0:T(8,128)(2,1)}, bf16[16,3584]{1,0:T(8,128)(2,1)S(1)}, u32[]{:S(2)}, u32[]{:S(2)}) collective-permute-start(bf16[16,3584]{1,0:T(8,128)(2,1)} %get-tuple-element.103), channel_id=1, source_target_pairs={{0,2},{1,3},{2,0},{3,1},{4,6},{5,7},{6,4},{7,5},{8,10},{9,11},{10,... | collective-permute-start | bytes 344072 | tf_op jit(solution)/shard_map/ppermute | solution.py:19
  30.6 7.5 %collective-permute-start.6 = (bf16[16,3584]{1,0:T(8,128)(2,1)S(1)}, bf16[16,3584]{1,0:T(8,128)(2,1)S(1)}, u32[]{:S(2)}, u32[]{:S(2)}) collective-permute-start(bf16[16,3584]{1,0:T(8,128)(2,1)S(1)} %get-tuple-element.105), channel_id=1, source_target_pairs={{0,4},{1,5},{2,6},{3,7},{4,0},{5,1},{6,2},{7,3},{8,12},{9,13},{10,... | collective-permute-start | bytes 344072 | tf_op jit(solution)/shard_map/ppermute | solution.py:19
  30.7 0.7 copy-start.1
  32.7 0.7 copy-start.2
  35.1 6.3 %collective-permute-start.8 = (bf16[16,3584]{1,0:T(8,128)(2,1)S(1)}, bf16[16,3584]{1,0:T(8,128)(2,1)S(1)}, u32[]{:S(2)}, u32[]{:S(2)}) collective-permute-start(bf16[16,3584]{1,0:T(8,128)(2,1)S(1)} %get-tuple-element.107), channel_id=1, source_target_pairs={{0,6},{1,7},{2,4},{3,5},{4,2},{5,3},{6,0},{7,1},{8,14},{9,15},{10,... | collective-permute-start | bytes 344072 | tf_op jit(solution)/shard_map/ppermute | solution.py:19
  38.1 5.8 %collective-permute-start.2 = (bf16[16,3584]{1,0:T(8,128)(2,1)S(1)}, bf16[16,3584]{1,0:T(8,128)(2,1)S(1)}, u32[]{:S(2)}, u32[]{:S(2)}) collective-permute-start(bf16[16,3584]{1,0:T(8,128)(2,1)S(1)} %get-tuple-element.92), channel_id=1, source_target_pairs={{0,6},{1,7},{2,4},{3,5},{4,2},{5,3},{6,0},{7,1},{8,14},{9,15},{10,... | collective-permute-start | bytes 344072 | tf_op jit(solution)/shard_map/ppermute | solution.py:19
  41.4 5.0 %collective-permute-start.5 = (bf16[16,3584]{1,0:T(8,128)(2,1)}, bf16[16,3584]{1,0:T(8,128)(2,1)S(1)}, u32[]{:S(2)}, u32[]{:S(2)}) collective-permute-start(bf16[16,3584]{1,0:T(8,128)(2,1)} %get-tuple-element.104), channel_id=1, source_target_pairs={{0,2},{1,3},{2,0},{3,1},{4,6},{5,7},{6,4},{7,5},{8,10},{9,11},{10,... | collective-permute-start | bytes 344072 | tf_op jit(solution)/shard_map/ppermute | solution.py:19
  43.9 5.0 %collective-permute-start.7 = (bf16[16,3584]{1,0:T(8,128)(2,1)S(1)}, bf16[16,3584]{1,0:T(8,128)(2,1)S(1)}, u32[]{:S(2)}, u32[]{:S(2)}) collective-permute-start(bf16[16,3584]{1,0:T(8,128)(2,1)S(1)} %get-tuple-element.106), channel_id=1, source_target_pairs={{0,4},{1,5},{2,6},{3,7},{4,0},{5,1},{6,2},{7,3},{8,12},{9,13},{10,... | collective-permute-start | bytes 344072 | tf_op jit(solution)/shard_map/ppermute | solution.py:19
  46.4 12.9 %collective-permute-start.14 = (bf16[32,3584]{1,0:T(8,128)(2,1)S(1)}, bf16[32,3584]{1,0:T(8,128)(2,1)S(1)}, u32[]{:S(2)}, u32[]{:S(2)}) collective-permute-start(bf16[32,3584]{1,0:T(8,128)(2,1)S(1)} %get-tuple-element.114), channel_id=1, source_target_pairs={{0,2},{1,3},{2,0},{3,1},{4,6},{5,7},{6,4},{7,5},{8,10},{9,11},{10,... | collective-permute-start | bytes 688136 | tf_op jit(solution)/shard_map/ppermute | solution.py:19
  48.9 10.4 %collective-permute-start.15 = (bf16[32,3584]{1,0:T(8,128)(2,1)S(1)}, bf16[32,3584]{1,0:T(8,128)(2,1)S(1)}, u32[]{:S(2)}, u32[]{:S(2)}) collective-permute-start(bf16[32,3584]{1,0:T(8,128)(2,1)S(1)} %get-tuple-element.115), channel_id=1, source_target_pairs={{0,4},{1,5},{2,6},{3,7},{4,0},{5,1},{6,2},{7,3},{8,12},{9,13},{10,... | collective-permute-start | bytes 688136 | tf_op jit(solution)/shard_map/ppermute | solution.py:19
  50.0 9.3 %collective-permute-start.16 = (bf16[32,3584]{1,0:T(8,128)(2,1)S(1)}, bf16[32,3584]{1,0:T(8,128)(2,1)S(1)}, u32[]{:S(2)}, u32[]{:S(2)}) collective-permute-start(bf16[32,3584]{1,0:T(8,128)(2,1)S(1)} %get-tuple-element.116), channel_id=1, source_target_pairs={{0,6},{1,7},{2,4},{3,5},{4,2},{5,3},{6,0},{7,1},{8,14},{9,15},{10,... | collective-permute-start | bytes 688136 | tf_op jit(solution)/shard_map/ppermute | solution.py:19
  59.4 11.9 %collective-permute-start.17 = (bf16[32,3584]{1,0:T(8,128)(2,1)S(1)}, bf16[32,3584]{1,0:T(8,128)(2,1)S(1)}, u32[]{:S(2)}, u32[]{:S(2)}) collective-permute-start(bf16[32,3584]{1,0:T(8,128)(2,1)S(1)} %get-tuple-element.117), channel_id=1, source_target_pairs={{0,6},{1,7},{2,4},{3,5},{4,2},{5,3},{6,0},{7,1},{8,14},{9,15},{10,... | collective-permute-start | bytes 688136 | tf_op jit(solution)/shard_map/ppermute | solution.py:19
  61.3 9.9 %collective-permute-start.12 = (bf16[32,3584]{1,0:T(8,128)(2,1)S(1)}, bf16[32,3584]{1,0:T(8,128)(2,1)S(1)}, u32[]{:S(2)}, u32[]{:S(2)}) collective-permute-start(bf16[32,3584]{1,0:T(8,128)(2,1)S(1)} %get-tuple-element.110), channel_id=1, source_target_pairs={{0,2},{1,3},{2,0},{3,1},{4,6},{5,7},{6,4},{7,5},{8,10},{9,11},{10,... | collective-permute-start | bytes 688136 | tf_op jit(solution)/shard_map/ppermute | solution.py:19
  62.9 8.3 %collective-permute-start.13 = (bf16[32,3584]{1,0:T(8,128)(2,1)S(1)}, bf16[32,3584]{1,0:T(8,128)(2,1)S(1)}, u32[]{:S(2)}, u32[]{:S(2)}) collective-permute-start(bf16[32,3584]{1,0:T(8,128)(2,1)S(1)} %get-tuple-element.111), channel_id=1, source_target_pairs={{0,4},{1,5},{2,6},{3,7},{4,0},{5,1},{6,2},{7,3},{8,12},{9,13},{10,... | collective-permute-start | bytes 688136 | tf_op jit(solution)/shard_map/ppermute | solution.py:19
  71.2 32.5 %copy-start.3 = (f32[1,3584]{1,0:T(1,128)S(1)}, f32[1,3584]{1,0:T(1,128)}, u32[]{:S(2)}) copy-start(f32[1,3584]{1,0:T(1,128)} %gain.9) | copy-start | bytes 43012
  71.6 21.1 %collective-permute-start.18 = (bf16[64,3584]{1,0:T(8,128)(2,1)S(1)}, bf16[64,3584]{1,0:T(8,128)(2,1)S(1)}, u32[]{:S(2)}, u32[]{:S(2)}) collective-permute-start(bf16[64,3584]{1,0:T(8,128)(2,1)S(1)} %shard_map.109), channel_id=1, source_target_pairs={{0,8},{1,9},{2,10},{3,11},{4,12},{5,13},{6,14},{7,15},{8,0},{9,1},... | collective-permute-start | bytes 1376264 | tf_op jit(solution)/shard_map/ppermute | solution.py:19
  73.6 7.0 %collective-permute-start.19 = (bf16[32,3584]{1,0:T(8,128)(2,1)S(1)}, bf16[32,3584]{1,0:T(8,128)(2,1)S(1)}, u32[]{:S(2)}, u32[]{:S(2)}) collective-permute-start(bf16[32,3584]{1,0:T(8,128)(2,1)S(1)} %get-tuple-element.128), channel_id=1, source_target_pairs={{0,2},{1,3},{2,0},{3,1},{4,6},{5,7},{6,4},{7,5},{8,10},{9,11},{10,... | collective-permute-start | bytes 688136 | tf_op jit(solution)/shard_map/ppermute | solution.py:19
  74.6 12.8 %collective-permute-start.20 = (bf16[32,3584]{1,0:T(8,128)(2,1)S(1)}, bf16[32,3584]{1,0:T(8,128)(2,1)S(1)}, u32[]{:S(2)}, u32[]{:S(2)}) collective-permute-start(bf16[32,3584]{1,0:T(8,128)(2,1)S(1)} %get-tuple-element.129), channel_id=1, source_target_pairs={{0,4},{1,5},{2,6},{3,7},{4,0},{5,1},{6,2},{7,3},{8,12},{9,13},{10,... | collective-permute-start | bytes 688136 | tf_op jit(solution)/shard_map/ppermute | solution.py:19
  74.7 18.1 %collective-permute-start.21 = (bf16[32,3584]{1,0:T(8,128)(2,1)S(1)}, bf16[32,3584]{1,0:T(8,128)(2,1)S(1)}, u32[]{:S(2)}, u32[]{:S(2)}) collective-permute-start(bf16[32,3584]{1,0:T(8,128)(2,1)S(1)} %get-tuple-element.130), channel_id=1, source_target_pairs={{0,6},{1,7},{2,4},{3,5},{4,2},{5,3},{6,0},{7,1},{8,14},{9,15},{10,... | collective-permute-start | bytes 688136 | tf_op jit(solution)/shard_map/ppermute | solution.py:19
  93.2 10.5 %collective-permute-start.23 = (bf16[64,3584]{1,0:T(8,128)(2,1)S(1)}, bf16[64,3584]{1,0:T(8,128)(2,1)S(1)}, u32[]{:S(2)}, u32[]{:S(2)}) collective-permute-start(bf16[64,3584]{1,0:T(8,128)(2,1)S(1)} %shard_map.111.first), channel_id=1, source_target_pairs={{0,16},{16,0},{1,17},{17,1},{2,18},{18,2},{3,19},{19,3},{4,20},{20... | collective-permute-start | bytes 1376264 | tf_op jit(solution)/shard_map/ppermute | solution.py:19
  94.8 21.1 %collective-permute-start.22 = (bf16[64,3584]{1,0:T(8,128)(2,1)S(1)}, bf16[64,3584]{1,0:T(8,128)(2,1)S(1)}, u32[]{:S(2)}, u32[]{:S(2)}) collective-permute-start(bf16[64,3584]{1,0:T(8,128)(2,1)S(1)} %shard_map.111.first), channel_id=1, source_target_pairs={{0,24},{1,25},{2,26},{3,27},{4,28},{5,29},{6,30},{7,31},{8,16},{9,... | collective-permute-start | bytes 1376264 | tf_op jit(solution)/shard_map/ppermute | solution.py:359
  117.3 9.5 %collective-permute-start.24 = (bf16[32,3584]{1,0:T(8,128)(2,1)S(1)}, bf16[32,3584]{1,0:T(8,128)(2,1)S(1)}, u32[]{:S(2)}, u32[]{:S(2)}) collective-permute-start(bf16[32,3584]{1,0:T(8,128)(2,1)S(1)} %get-tuple-element.136), channel_id=1, source_target_pairs={{0,6},{1,7},{2,4},{3,5},{4,2},{5,3},{6,0},{7,1},{8,14},{9,15},{10,... | collective-permute-start | bytes 688136 | tf_op jit(solution)/shard_map/ppermute | solution.py:19
  117.4 12.9 %collective-permute-start.25 = (bf16[32,3584]{1,0:T(8,128)(2,1)S(1)}, bf16[32,3584]{1,0:T(8,128)(2,1)S(1)}, u32[]{:S(2)}, u32[]{:S(2)}) collective-permute-start(bf16[32,3584]{1,0:T(8,128)(2,1)S(1)} %get-tuple-element.145), channel_id=1, source_target_pairs={{0,2},{1,3},{2,0},{3,1},{4,6},{5,7},{6,4},{7,5},{8,10},{9,11},{10,... | collective-permute-start | bytes 688136 | tf_op jit(solution)/shard_map/ppermute | solution.py:19
  118.1 12.2 %collective-permute-start.26 = (bf16[32,3584]{1,0:T(8,128)(2,1)S(1)}, bf16[32,3584]{1,0:T(8,128)(2,1)S(1)}, u32[]{:S(2)}, u32[]{:S(2)}) collective-permute-start(bf16[32,3584]{1,0:T(8,128)(2,1)S(1)} %get-tuple-element.146), channel_id=1, source_target_pairs={{0,4},{1,5},{2,6},{3,7},{4,0},{5,1},{6,2},{7,3},{8,12},{9,13},{10,... | collective-permute-start | bytes 688136 | tf_op jit(solution)/shard_map/ppermute | solution.py:19
  126.8 13.8 %collective-permute-start.29 = (bf16[32,3584]{1,0:T(8,128)(2,1)S(1)}, bf16[32,3584]{1,0:T(8,128)(2,1)S(1)}, u32[]{:S(2)}, u32[]{:S(2)}) collective-permute-start(bf16[32,3584]{1,0:T(8,128)(2,1)S(1)} %get-tuple-element.153), channel_id=1, source_target_pairs={{0,2},{1,3},{2,0},{3,1},{4,6},{5,7},{6,4},{7,5},{8,10},{9,11},{10,... | collective-permute-start | bytes 688136 | tf_op jit(solution)/shard_map/ppermute | solution.py:19
  126.8 13.8 %collective-permute-start.30 = (bf16[32,3584]{1,0:T(8,128)(2,1)S(1)}, bf16[32,3584]{1,0:T(8,128)(2,1)S(1)}, u32[]{:S(2)}, u32[]{:S(2)}) collective-permute-start(bf16[32,3584]{1,0:T(8,128)(2,1)S(1)} %get-tuple-element.154), channel_id=1, source_target_pairs={{0,4},{1,5},{2,6},{3,7},{4,0},{5,1},{6,2},{7,3},{8,12},{9,13},{10,... | collective-permute-start | bytes 688136 | tf_op jit(solution)/shard_map/ppermute | solution.py:19
  127.4 13.3 %collective-permute-start.31 = (bf16[32,3584]{1,0:T(8,128)(2,1)S(1)}, bf16[32,3584]{1,0:T(8,128)(2,1)S(1)}, u32[]{:S(2)}, u32[]{:S(2)}) collective-permute-start(bf16[32,3584]{1,0:T(8,128)(2,1)S(1)} %get-tuple-element.155), channel_id=1, source_target_pairs={{0,6},{1,7},{2,4},{3,5},{4,2},{5,3},{6,0},{7,1},{8,14},{9,15},{10,... | collective-permute-start | bytes 688136 | tf_op jit(solution)/shard_map/ppermute | solution.py:19
  138.6 11.9 %collective-permute-start.27 = (bf16[32,3584]{1,0:T(8,128)(2,1)S(1)}, bf16[32,3584]{1,0:T(8,128)(2,1)S(1)}, u32[]{:S(2)}, u32[]{:S(2)}) collective-permute-start(bf16[32,3584]{1,0:T(8,128)(2,1)S(1)} %get-tuple-element.149), channel_id=1, source_target_pairs={{0,2},{1,3},{2,0},{3,1},{4,6},{5,7},{6,4},{7,5},{8,10},{9,11},{10,... | collective-permute-start | bytes 688136 | tf_op jit(solution)/shard_map/ppermute | solution.py:19
  140.7 9.9 %collective-permute-start.28 = (bf16[32,3584]{1,0:T(8,128)(2,1)S(1)}, bf16[32,3584]{1,0:T(8,128)(2,1)S(1)}, u32[]{:S(2)}, u32[]{:S(2)}) collective-permute-start(bf16[32,3584]{1,0:T(8,128)(2,1)S(1)} %get-tuple-element.150), channel_id=1, source_target_pairs={{0,4},{1,5},{2,6},{3,7},{4,0},{5,1},{6,2},{7,3},{8,12},{9,13},{10,... | collective-permute-start | bytes 688136 | tf_op jit(solution)/shard_map/ppermute | solution.py:19
  140.7 9.9 %collective-permute-start.32 = (bf16[32,3584]{1,0:T(8,128)(2,1)S(1)}, bf16[32,3584]{1,0:T(8,128)(2,1)S(1)}, u32[]{:S(2)}, u32[]{:S(2)}) collective-permute-start(bf16[32,3584]{1,0:T(8,128)(2,1)S(1)} %get-tuple-element.156), channel_id=1, source_target_pairs={{0,6},{1,7},{2,4},{3,5},{4,2},{5,3},{6,0},{7,1},{8,14},{9,15},{10,... | collective-permute-start | bytes 688136 | tf_op jit(solution)/shard_map/ppermute | solution.py:19
  151.0 21.2 %collective-permute-start.33 = (bf16[64,3584]{1,0:T(8,128)(2,1)S(1)}, bf16[64,3584]{1,0:T(8,128)(2,1)S(1)}, u32[]{:S(2)}, u32[]{:S(2)}) collective-permute-start(bf16[64,3584]{1,0:T(8,128)(2,1)S(1)} %shard_map.116), channel_id=1, source_target_pairs={{0,8},{1,9},{2,10},{3,11},{4,12},{5,13},{6,14},{7,15},{8,0},{9,1},... | collective-permute-start | bytes 1376264 | tf_op jit(solution)/shard_map/ppermute | solution.py:19
  152.4 8.5 %collective-permute-start.34 = (bf16[32,3584]{1,0:T(8,128)(2,1)S(1)}, bf16[32,3584]{1,0:T(8,128)(2,1)S(1)}, u32[]{:S(2)}, u32[]{:S(2)}) collective-permute-start(bf16[32,3584]{1,0:T(8,128)(2,1)S(1)} %get-tuple-element.167), channel_id=1, source_target_pairs={{0,2},{1,3},{2,0},{3,1},{4,6},{5,7},{6,4},{7,5},{8,10},{9,11},{10,... | collective-permute-start | bytes 688136 | tf_op jit(solution)/shard_map/ppermute | solution.py:19
  153.4 14.2 %collective-permute-start.35 = (bf16[32,3584]{1,0:T(8,128)(2,1)S(1)}, bf16[32,3584]{1,0:T(8,128)(2,1)S(1)}, u32[]{:S(2)}, u32[]{:S(2)}) collective-permute-start(bf16[32,3584]{1,0:T(8,128)(2,1)S(1)} %get-tuple-element.168), channel_id=1, source_target_pairs={{0,4},{1,5},{2,6},{3,7},{4,0},{5,1},{6,2},{7,3},{8,12},{9,13},{10,... | collective-permute-start | bytes 688136 | tf_op jit(solution)/shard_map/ppermute | solution.py:19
  155.4 16.8 %collective-permute-start.36 = (bf16[32,3584]{1,0:T(8,128)(2,1)S(1)}, bf16[32,3584]{1,0:T(8,128)(2,1)S(1)}, u32[]{:S(2)}, u32[]{:S(2)}) collective-permute-start(bf16[32,3584]{1,0:T(8,128)(2,1)S(1)} %get-tuple-element.169), channel_id=1, source_target_pairs={{0,6},{1,7},{2,4},{3,5},{4,2},{5,3},{6,0},{7,1},{8,14},{9,15},{10,... | collective-permute-start | bytes 688136 | tf_op jit(solution)/shard_map/ppermute | solution.py:19
